TPU v7x, 128 devices: a whole 4x4x4 slice. The times are simulated.
128 devices in a mesh: leaf: 32 (over x, y, core), sub: 4 (over z).
Axes of the slice: x: 4, y: 4, z: 4, core: 2. Of those that a mesh axis runs over, the one named last changes fastest.
Arguments:
- points: float32 [2, 1048576], P(None, ('leaf', 'sub')), may hold values from 0 to 1
- probes: float32 [16, 1048576], P(None, ('leaf', 'sub')), may hold values from -6 to 6
- basis: float32 [4096, 256, 64], P(('leaf', 'sub')), may hold values from -0.375 to 0.375
- transfer_leaf: float32 [4096, 64, 64], P(('leaf', 'sub')), may hold values from -0.125 to 0.125
- transfer_box: float32 [128, 64, 64], P(('leaf', 'sub')), may hold values from -0.375 to 0.375
- couple_leaf: float32 [4096, 27, 64, 64], P(('leaf', 'sub')), may hold values from -0.15625 to 0.15625
- couple_box: float32 [128, 27, 64, 64], P(('leaf', 'sub')), may hold values from -0.15625 to 0.15625
- couple_column: float32 [32, 4, 64, 64], P('leaf'), may hold values from -0.375 to 0.375
- near_list: int32 [4096, 9], P(('leaf', 'sub')), may hold values from -1 to 4095, as said below
- far_list: int32 [4096, 27], P(('leaf', 'sub')), may hold values from -1 to 4095, as said below
- box_list: int32 [128, 27], P(('leaf', 'sub')), may hold values from -1 to 127, as said below
- column_list: int32 [32, 4], P('leaf'), may hold values from -1 to 31, as said below
Outputs:
- product: float32 [16, 1048576], P(None, ('leaf', 'sub'))
Inputs may be any that keep to these rules, and one draw needn't show every extreme that they name: `near_list`: each entry is a leaf whose index differs from the row's leaf by at most 8; entry 0 is the leaf itself; in every row some entries may be -1 and they stand after the valid ones; the first leaf of every box has no -1 and its entry 1 lies exactly 8 away. `far_list`: each valid entry is a leaf whose box (index // 32) differs from the row's box by at most 4, and entry 0 of every row lies exactly 4 boxes away; entries -1 stand after the valid ones; the first leaf of every box has none. Entries may repeat. `box_list`: valid entries are any boxes and may repeat; entries -1 stand after the valid ones; at least 13 entries of every row are valid. `column_list`: valid entries are any columns and may repeat; entries -1 stand after the valid ones; at least 2 entries of every row are valid.
All inputs are finite; a program needn't handle non-finite values.
Results may differ from a plain program's by a relative error of at most 0.0003.
Values sent between devices are 32-bit elements; how exact they have to be, the bound alone decides.
No kernel may reach another device: no remote copies, remote signals or barrier semaphores. Data moves between devices by JAX's collectives and lax.ppermute only.
A program may use at most 128 MiB of HBM per device.

v0:
```python
import math

import jax
import jax.numpy as jnp
from jax import lax
from jax.sharding import PartitionSpec as P

FAR_REACH = 4


topmost_level = lax.Precision.HIGHEST
matern_rate = math.sqrt(3.0) / 0.1


def from_behind(array, axis, by):
    devices = lax.axis_size(axis)
    pairs = [(i, i + by) for i in range(devices) if 0 <= i + by < devices]
    return lax.ppermute(array, axis, pairs)


def extended(cells, sides, width):
    for axis, dim in sides:
        count = lax.axis_size(axis)
        ends = count - 1
        head = lax.slice_in_dim(cells, 0, width, axis=dim)
        tail = lax.slice_in_dim(cells, cells.shape[dim] - width, cells.shape[dim], axis=dim)
        cells = jnp.concatenate(
            [
                lax.ppermute(tail, axis, [(i, (i + 1) % count) for i in range(ends)]),
                cells,
                lax.ppermute(head, axis, [((i + 1) % count, i) for i in range(ends)]),
            ],
            axis=dim,
        )
    return cells


def matern_tiles(target_points, source_points):
    delta_x = target_points[:, None, 0, :, None] - source_points[:, :, 0, None, :]
    delta_y = target_points[:, None, 1, :, None] - source_points[:, :, 1, None, :]
    scaled = matern_rate * jnp.sqrt(delta_x * delta_x + delta_y * delta_y)
    return (1.0 + scaled) * jnp.exp(-scaled)


def near_field(target_points, source_points, source_values, present):
    kernel_tiles = matern_tiles(target_points, source_points) * present[:, :, None, None]
    return jnp.einsum("bkij,bkpj->bpi", kernel_tiles, source_values, precision=topmost_level)


def pick_rows(table, entries, first):
    present = entries >= 0
    chosen = table[jnp.where(present, entries - first, 0)]
    return chosen * present.astype(table.dtype)[:, :, None]


def per_device(
    points,
    probes,
    basis,
    transfer_leaf,
    transfer_box,
    couple_leaf,
    couple_box,
    couple_column,
    near_list,
    far_list,
    box_list,
    column_list,
):
    leaves, leaf_size, rank = basis.shape
    probe_count = probes.shape[0]
    width = probe_count * rank
    devices = lax.axis_size(("leaf", "sub"))
    group_size = lax.axis_size("sub")
    columns = devices // group_size
    position = lax.axis_index(("leaf", "sub"))
    near_reach = leaves // 4
    grouped_cluster_values = probes.reshape(probe_count, leaves, leaf_size).transpose(1, 0, 2)
    skeleton_leaf = jnp.einsum(
        "gyz,gzk->gyk", grouped_cluster_values, basis, precision=topmost_level
    )
    skel_box = jnp.einsum("cpr,crs->ps", skeleton_leaf, transfer_leaf, precision=topmost_level)
    box_term = jnp.dot(skel_box, transfer_box[0], precision=topmost_level)
    flat_leaf = skeleton_leaf.reshape(leaves, width)

    def neighbour(offset):
        return from_behind(flat_leaf, ("leaf", "sub"), offset)

    pieces = (
        [neighbour(offset) for offset in range(FAR_REACH, 0, -1)]
        + [flat_leaf]
        + [neighbour(-offset) for offset in range(1, FAR_REACH + 1)]
    )
    first_leaf = (position - FAR_REACH) * leaves
    far_window = jnp.concatenate(pieces, axis=0)
    stacked = jnp.concatenate([points, probes], axis=0)
    window = extended(stacked, ((("leaf", "sub"), 1),), near_reach * leaf_size)
    window = window.reshape(2 + probe_count, leaves + 2 * near_reach, leaf_size).transpose(1, 0, 2)
    all_skel, all_terms = (
        lax.all_gather(skel_box.reshape(1, width), ("leaf", "sub"), axis=0, tiled=True),
        lax.all_gather(box_term.reshape(1, width), ("leaf", "sub"), axis=0, tiled=True),
    )
    far_rows = pick_rows(far_window, far_list, first_leaf).reshape(
        leaves, far_list.shape[1], probe_count, rank
    )
    far_leaf = jnp.einsum("ckpr,ckrs->cps", far_rows, couple_leaf, precision=topmost_level)
    skel_column = all_terms.reshape(columns, group_size, width).sum(axis=1)
    box_rows = pick_rows(all_skel, box_list, 0).reshape(1, box_list.shape[1], probe_count, rank)
    far_box = jnp.einsum("ckpr,ckrs->cps", box_rows, couple_box, precision=topmost_level)[0]
    column_rows = pick_rows(skel_column, column_list, 0).reshape(
        1, column_list.shape[1], probe_count, rank
    )
    far_column = jnp.einsum("ckpr,ckrs->cps", column_rows, couple_column, precision=topmost_level)[
        0
    ]
    down_box = far_box + jnp.dot(far_column, transfer_box[0].T, precision=topmost_level)
    downward_leaf = far_leaf + jnp.einsum(
        "ps,crs->cpr", down_box, transfer_leaf, precision=topmost_level
    )
    distant_values = jnp.einsum("wdq,wkq->wdk", downward_leaf, basis, precision=topmost_level)
    near_present = near_list >= 0
    near_index = jnp.where(near_present, near_list - (position * leaves - near_reach), 0)
    sources = window[near_index]
    target_points = points.reshape(2, leaves, leaf_size).transpose(1, 0, 2)
    nearby_span = 4

    def near_block(inputs):
        target_list, source_block, present = inputs
        return near_field(target_list, source_block[:, :, :2], source_block[:, :, 2:], present)

    near_values = lax.map(
        near_block,
        (
            target_points.reshape(leaves // nearby_span, nearby_span, 2, leaf_size),
            sources.reshape(
                leaves // nearby_span, nearby_span, near_list.shape[1], 2 + probe_count, leaf_size
            ),
            near_present.astype(points.dtype).reshape(
                leaves // nearby_span, nearby_span, near_list.shape[1]
            ),
        ),
    ).reshape(leaves, probe_count, leaf_size)
    return (
        (distant_values + near_values).transpose(1, 0, 2).reshape(probe_count, leaves * leaf_size)
    )


def solution(mesh):
    placed = (
        P(None, ("leaf", "sub")),
        P(None, ("leaf", "sub")),
        P(("leaf", "sub"), None, None),
        P(("leaf", "sub"), None, None),
        P(("leaf", "sub"), None, None),
        P(("leaf", "sub"), None, None, None),
        P(("leaf", "sub"), None, None, None),
        P("leaf", None, None, None),
        P(("leaf", "sub"), None),
        P(("leaf", "sub"), None),
        P(("leaf", "sub"), None),
        P("leaf", None),
    )
    return jax.shard_map(
        per_device, mesh=mesh, in_specs=placed, out_specs=P(None, ("leaf", "sub")), check_vma=False
    )
```

profile of v0, /device:TPU:2, one launch (start us, length us, event | category | flops | bytes accessed | tf_op | source)
XLA Modules:
  0.0 337.4 jit_solution(735826770532336750)
XLA Ops:
  0.0 1.5 copy-done
  1.6 2.9 fusion.41
  4.5 0.8 reshape.177
  5.2 1.9 collective-permute-start
  7.2 5.9 %collective-permute-start.1 = (f32[32,1024]{1,0:T(8,128)}, f32[32,1024]{1,0:T(8,128)}, u32[]{:S(2)}, u32[]{:S(2)}) collective-permute-start(f32[32,1024]{1,0:T(8,128)} %reshape.177), channel_id=1, source_target_pairs={{0,3},{1,4},{2,5},{3,6},{4,7},{5,8},{6,9},{7,10},{8,11},{9,12},{10... | collective-permute-start | bytes 393224 | tf_op jit(solution)/shard_map/ppermute | solution.py:18
  13.1 3.1 collective-permute-start.2
  16.3 3.2 collective-permute-start.3
  19.5 6.6 %collective-permute-start.4 = (f32[32,1024]{1,0:T(8,128)}, f32[32,1024]{1,0:T(8,128)}, u32[]{:S(2)}, u32[]{:S(2)}) collective-permute-start(f32[32,1024]{1,0:T(8,128)} %reshape.177), channel_id=1, source_target_pairs={{1,0},{2,1},{3,2},{4,3},{5,4},{6,5},{7,6},{8,7},{9,8},{10,9},{11,1... | collective-permute-start | bytes 393224 | tf_op jit(solution)/shard_map/ppermute | solution.py:18
  27.0 0.7 convolution_bitcast_fusion.3
  27.9 49.2 %all-gather.1 = f32[128,1,1024]{2,1,0:T(1,128)S(1)} all-gather(f32[1,1,1024]{2,1,0:T(1,128)S(1)} %reshape.237), channel_id=1, replica_groups=mesh['leaf'=32,'sub'=4] {'leaf','sub'}, dimensions={0}, use_global_device_ids=true | all-gather | bytes 528384 | tf_op jit(solution)/shard_map/all_gather | solution.py:101
  77.2 1.2 reduce
  80.2 52.2 %all-gather = f32[128,1,1024]{2,1,0:T(1,128)S(1)} all-gather(f32[1,1,1024]{2,1,0:T(1,128)S(1)} %reshape.235), channel_id=1, replica_groups=mesh['leaf'=32,'sub'=4] {'leaf','sub'}, dimensions={0}, use_global_device_ids=true | all-gather | bytes 528384 | tf_op jit(solution)/shard_map/all_gather | solution.py:100
  133.6 1.8 convolution_bitcast_fusion.2
  135.5 3.8 %convolution_bitcast_fusion = f32[32,16,64]{2,1,0:T(8,128)S(1)} fusion(f32[16,64,1]{1,0,2:T(8,128)S(1)} %fusion.39, f32[32,64,64]{2,1,0:T(8,128)} %param.17), kind=kOutput, calls=%fused_computation.44 | convolution fusion | flops 25165824 | bytes 659456 | tf_op jit(solution)/shard_map/ps,crs->cpr/dot_general | solution.py:117
  139.3 0.8 pad_maximum_fusion.2
  140.9 0.7 copy.47
  141.5 6.7 %collective-permute-start.5 = (f32[32,1024]{1,0:T(8,128)}, f32[32,1024]{1,0:T(8,128)S(1)}, u32[]{:S(2)}, u32[]{:S(2)}) collective-permute-start(f32[32,1024]{1,0:T(8,128)} %reshape.177), channel_id=1, source_target_pairs={{2,0},{3,1},{4,2},{5,3},{6,4},{7,5},{8,6},{9,7},{10,8},{11,9},{12,... | collective-permute-start | bytes 393224 | tf_op jit(solution)/shard_map/ppermute | solution.py:18
  148.2 0.9 constant_dynamic-update-slice_fusion.8
  149.2 1.9 collective-permute-start.6
  151.1 0.9 constant_dynamic-update-slice_fusion.7
  152.0 1.9 collective-permute-start.7
  154.0 0.9 constant_dynamic-update-slice_fusion.6
  154.9 3.6 %collective-permute-start.8 = (f32[18,2048]{1,0:T(8,128)}, f32[18,2048]{1,0:T(8,128)}, u32[]{:S(2)}, u32[]{:S(2)}) collective-permute-start(f32[18,2048]{1,0:T(8,128)} %get-tuple-element.64), channel_id=1, source_target_pairs={{0,1},{1,2},{2,3},{3,4},{4,5},{5,6},{6,7},{7,8},{8,9},{9,10},{10,1... | collective-permute-start | bytes 442376 | tf_op jit(solution)/shard_map/ppermute | solution.py:29
  158.5 0.9 constant_dynamic-update-slice_fusion.5
  159.5 0.9 constant_dynamic-update-slice_fusion.4
  160.4 6.3 %collective-permute-start.9 = (f32[18,2048]{1,0:T(8,128)}, f32[18,2048]{1,0:T(8,128)}, u32[]{:S(2)}, u32[]{:S(2)}) collective-permute-start(f32[18,2048]{1,0:T(8,128)} %get-tuple-element.65), channel_id=1, source_target_pairs={{1,0},{2,1},{3,2},{4,3},{5,4},{6,5},{7,6},{8,7},{9,8},{10,9},{11,1... | collective-permute-start | bytes 442376 | tf_op jit(solution)/shard_map/ppermute | solution.py:31
  166.7 0.9 constant_dynamic-update-slice_fusion.3
  167.7 4.3 %gather_fusion = f32[864,1024]{1,0:T(8,128)} fusion(f32[288,1024]{1,0:T(8,128)S(1)} %constant_dynamic-update-slice_fusion, s32[1024]{0:T(1024)} %pad_clamp_fusion.3), kind=kCustom, calls=%fused_computation | custom fusion | bytes 7081344 | tf_op jit(solution)/shard_map/gather | solution.py:52
  172.0 6.6 %gather.15 = f32[32,27,16,64]{3,2,1,0:T(8,128)} reshape(f32[864,1024]{1,0:T(8,128)} %gather_fusion) | data formatting | bytes 7077888 | tf_op jit(solution)/shard_map/gather | solution.py:52
  178.6 22.8 %fusion.36 = f32[32,16,64]{2,1,0:T(8,128)} fusion(f32[32,16,64]{2,1,0:T(8,128)S(1)} %convolution_bitcast_fusion, f32[32,27,64,64]{3,2,1,0:T(8,128)} %param.19, f32[32,27,16,64]{3,2,1,0:T(8,128)} %gather.15, f32[32,27]{1,0:T(8,128)S(1)} %fusion.47), kind=kOutput, calls=%fused_computation.46 | convolution fusion | flops 680394752 | bytes 17960320 | tf_op jit(solution)/shard_map/ckpr,ckrs->cps/dot_general | solution.py:106
  201.4 1.1 pad_maximum_fusion
  203.6 4.1 %gather_fusion.3 = f32[288,18,256]{2,1,0:T(8,128)} fusion(f32[48,18,256]{2,1,0:T(8,128)S(1)} %bitcast.111, s32[1024]{0:T(1024)S(1)} %copy-done.9), kind=kCustom, calls=%fused_computation.3 | custom fusion | bytes 10617984 | tf_op jit(solution)/shard_map/gather | solution.py:123
  207.7 126.6 %while.10 = (s32[]{:T(128)}, f32[8,4,16,256]{3,2,1,0:T(8,128)}, f32[8,4,9,18,256]{4,3,2,1,0:T(8,128)}, f32[8,4,2,256]{3,2,1,0:T(2,128)}, f32[8,4,9]{2,1,0:T(4,128)}, /*index=5*/s32[]{:T(128)}) while((s32[]{:T(128)}, f32[8,4,16,256]{3,2,1,0:T(8,128)}, f32[8,4,9,18,256]{4,3,2,1,0:T(8,128)}, f32[8,4,2,256]{3,2,1,0:T(2,128)}, ...), condition=%wide.region_2.3_spmd, body=%wide.region_1.2_spmd.sunk | while | flops 476577792 | bytes 2616177 | solution.py:131
  207.7 1.3 dynamic-slice_bitcast_fusion.5
  209.1 0.7 constant_dynamic-slice_fusion.2
  210.4 13.1 %fusion.73 = f32[8,4,16,256]{3,2,1,0:T(8,128)} fusion(f32[8,4,16,256]{3,2,1,0:T(8,128)} %get-tuple-element.118, s32[]{:T(128)} %get-tuple-element.117, f32[4,9]{1,0:T(4,128)S(1)} %dynamic-slice_bitcast_fusion.4, f32[4,9,256]{2,1,0:T(8,128)S(1)} %copy.75, f32[4,256]{1,0:T(4,128)S(1)} %get-tuple-element.108, f32[4,9,256]{2,1,0:T(8,128)S(1)} %copy.77, ...), kind=kOutput, calls=%fused_computation.25.clone.1 | convolution fusion | flops 476577792 | bytes 797184 | tf_op jit(solution)/shard_map/while/body/eval_jaxpr/bkij,bkpj->bpi/dot_general | solution.py:47
  223.5 1.2 dynamic-slice_bitcast_fusion.5
  224.9 0.7 constant_dynamic-slice_fusion.2
  225.6 0.7 dynamic-slice_bitcast_fusion.4
  226.3 13.1 %fusion.73 = f32[8,4,16,256]{3,2,1,0:T(8,128)} fusion(f32[8,4,16,256]{3,2,1,0:T(8,128)} %get-tuple-element.118, s32[]{:T(128)} %get-tuple-element.117, f32[4,9]{1,0:T(4,128)S(1)} %dynamic-slice_bitcast_fusion.4, f32[4,9,256]{2,1,0:T(8,128)S(1)} %copy.75, f32[4,256]{1,0:T(4,128)S(1)} %get-tuple-element.108, f32[4,9,256]{2,1,0:T(8,128)S(1)} %copy.77, ...), kind=kOutput, calls=%fused_computation.25.clone.1 | convolution fusion | flops 476577792 | bytes 797184 | tf_op jit(solution)/shard_map/while/body/eval_jaxpr/bkij,bkpj->bpi/dot_general | solution.py:47
  239.4 1.2 dynamic-slice_bitcast_fusion.5
  240.7 0.7 constant_dynamic-slice_fusion.2
  241.5 0.6 dynamic-slice_bitcast_fusion.4
  242.1 13.1 %fusion.73 = f32[8,4,16,256]{3,2,1,0:T(8,128)} fusion(f32[8,4,16,256]{3,2,1,0:T(8,128)} %get-tuple-element.118, s32[]{:T(128)} %get-tuple-element.117, f32[4,9]{1,0:T(4,128)S(1)} %dynamic-slice_bitcast_fusion.4, f32[4,9,256]{2,1,0:T(8,128)S(1)} %copy.75, f32[4,256]{1,0:T(4,128)S(1)} %get-tuple-element.108, f32[4,9,256]{2,1,0:T(8,128)S(1)} %copy.77, ...), kind=kOutput, calls=%fused_computation.25.clone.1 | convolution fusion | flops 476577792 | bytes 797184 | tf_op jit(solution)/shard_map/while/body/eval_jaxpr/bkij,bkpj->bpi/dot_general | solution.py:47
  255.2 1.2 dynamic-slice_bitcast_fusion.5
  256.5 0.7 constant_dynamic-slice_fusion.2
  257.3 0.7 dynamic-slice_bitcast_fusion.4
  257.9 13.1 %fusion.73 = f32[8,4,16,256]{3,2,1,0:T(8,128)} fusion(f32[8,4,16,256]{3,2,1,0:T(8,128)} %get-tuple-element.118, s32[]{:T(128)} %get-tuple-element.117, f32[4,9]{1,0:T(4,128)S(1)} %dynamic-slice_bitcast_fusion.4, f32[4,9,256]{2,1,0:T(8,128)S(1)} %copy.75, f32[4,256]{1,0:T(4,128)S(1)} %get-tuple-element.108, f32[4,9,256]{2,1,0:T(8,128)S(1)} %copy.77, ...), kind=kOutput, calls=%fused_computation.25.clone.1 | convolution fusion | flops 476577792 | bytes 797184 | tf_op jit(solution)/shard_map/while/body/eval_jaxpr/bkij,bkpj->bpi/dot_general | solution.py:47
  271.0 1.2 dynamic-slice_bitcast_fusion.5
  272.4 0.7 constant_dynamic-slice_fusion.2
  273.1 0.7 dynamic-slice_bitcast_fusion.4
  273.8 13.1 %fusion.73 = f32[8,4,16,256]{3,2,1,0:T(8,128)} fusion(f32[8,4,16,256]{3,2,1,0:T(8,128)} %get-tuple-element.118, s32[]{:T(128)} %get-tuple-element.117, f32[4,9]{1,0:T(4,128)S(1)} %dynamic-slice_bitcast_fusion.4, f32[4,9,256]{2,1,0:T(8,128)S(1)} %copy.75, f32[4,256]{1,0:T(4,128)S(1)} %get-tuple-element.108, f32[4,9,256]{2,1,0:T(8,128)S(1)} %copy.77, ...), kind=kOutput, calls=%fused_computation.25.clone.1 | convolution fusion | flops 476577792 | bytes 797184 | tf_op jit(solution)/shard_map/while/body/eval_jaxpr/bkij,bkpj->bpi/dot_general | solution.py:47
  286.9 1.2 dynamic-slice_bitcast_fusion.5
  288.2 0.7 constant_dynamic-slice_fusion.2
  289.6 13.1 %fusion.73 = f32[8,4,16,256]{3,2,1,0:T(8,128)} fusion(f32[8,4,16,256]{3,2,1,0:T(8,128)} %get-tuple-element.118, s32[]{:T(128)} %get-tuple-element.117, f32[4,9]{1,0:T(4,128)S(1)} %dynamic-slice_bitcast_fusion.4, f32[4,9,256]{2,1,0:T(8,128)S(1)} %copy.75, f32[4,256]{1,0:T(4,128)S(1)} %get-tuple-element.108, f32[4,9,256]{2,1,0:T(8,128)S(1)} %copy.77, ...), kind=kOutput, calls=%fused_computation.25.clone.1 | convolution fusion | flops 476577792 | bytes 797184 | tf_op jit(solution)/shard_map/while/body/eval_jaxpr/bkij,bkpj->bpi/dot_general | solution.py:47
  302.7 1.2 dynamic-slice_bitcast_fusion.5
  304.0 0.7 constant_dynamic-slice_fusion.2
  304.8 0.7 dynamic-slice_bitcast_fusion.4
  305.4 13.1 %fusion.73 = f32[8,4,16,256]{3,2,1,0:T(8,128)} fusion(f32[8,4,16,256]{3,2,1,0:T(8,128)} %get-tuple-element.118, s32[]{:T(128)} %get-tuple-element.117, f32[4,9]{1,0:T(4,128)S(1)} %dynamic-slice_bitcast_fusion.4, f32[4,9,256]{2,1,0:T(8,128)S(1)} %copy.75, f32[4,256]{1,0:T(4,128)S(1)} %get-tuple-element.108, f32[4,9,256]{2,1,0:T(8,128)S(1)} %copy.77, ...), kind=kOutput, calls=%fused_computation.25.clone.1 | convolution fusion | flops 476577792 | bytes 797184 | tf_op jit(solution)/shard_map/while/body/eval_jaxpr/bkij,bkpj->bpi/dot_general | solution.py:47
  318.5 1.2 dynamic-slice_bitcast_fusion.5
  319.9 0.7 constant_dynamic-slice_fusion.2
  321.2 13.1 %fusion.73 = f32[8,4,16,256]{3,2,1,0:T(8,128)} fusion(f32[8,4,16,256]{3,2,1,0:T(8,128)} %get-tuple-element.118, s32[]{:T(128)} %get-tuple-element.117, f32[4,9]{1,0:T(4,128)S(1)} %dynamic-slice_bitcast_fusion.4, f32[4,9,256]{2,1,0:T(8,128)S(1)} %copy.75, f32[4,256]{1,0:T(4,128)S(1)} %get-tuple-element.108, f32[4,9,256]{2,1,0:T(8,128)S(1)} %copy.77, ...), kind=kOutput, calls=%fused_computation.25.clone.1 | convolution fusion | flops 476577792 | bytes 797184 | tf_op jit(solution)/shard_map/while/body/eval_jaxpr/bkij,bkpj->bpi/dot_general | solution.py:47
  334.3 2.2 fusion.32
  336.5 0.8 copy.56
  (127 shorter events, 8.7 us)
Async XLA Ops:
  0.0 1.6 copy-start
  0.0 26.1 %copy-start.14 = (s32[1,4]{1,0:T(1,128)S(1)}, s32[1,4]{1,0:T(1,128)}, u32[]{:S(2)}) copy-start(s32[1,4]{1,0:T(1,128)} %param.25) | copy-start | bytes 52
  0.0 26.1 %copy-start.15 = (s32[1,27]{1,0:T(1,128)S(1)}, s32[1,27]{1,0:T(1,128)}, u32[]{:S(2)}) copy-start(s32[1,27]{1,0:T(1,128)} %param.24) | copy-start | bytes 328
  0.0 26.1 %copy-start.11 = (s32[32,27]{1,0:T(8,128)S(1)}, s32[32,27]{1,0:T(8,128)}, u32[]{:S(2)}) copy-start(s32[32,27]{1,0:T(8,128)} %param.23) | copy-start | bytes 10372
  0.0 26.8 %copy-start.12 = (s32[32,9]{0,1:T(8,128)S(1)}, s32[32,9]{0,1:T(8,128)}, u32[]{:S(2)}) copy-start(s32[32,9]{0,1:T(8,128)} %param.22) | copy-start | bytes 3460
  0.0 26.9 %copy-start.3 = (f32[32,64,64]{2,1,0:T(8,128)S(1)}, f32[32,64,64]{2,1,0:T(8,128)}, u32[]{:S(2)}) copy-start(f32[32,64,64]{2,1,0:T(8,128)} %param.17) | copy-start | bytes 1572868
  1.6 26.1 %copy-start.7 = (f32[1,64,64]{2,1,0:T(8,128)S(1)}, f32[1,64,64]{2,1,0:T(8,128)}, u32[]{:S(2)}) copy-start(f32[1,64,64]{2,1,0:T(8,128)} %param.18) | copy-start | bytes 49156
  5.2 136.3 %collective-permute-start = (f32[32,1024]{1,0:T(8,128)}, f32[32,1024]{1,0:T(8,128)}, u32[]{:S(2)}, u32[]{:S(2)}) collective-permute-start(f32[32,1024]{1,0:T(8,128)} %reshape.177), channel_id=1, source_target_pairs={{0,4},{1,5},{2,6},{3,7},{4,8},{5,9},{6,10},{7,11},{8,12},{9,13},{1... | collective-permute-start | bytes 393224 | tf_op jit(solution)/shard_map/ppermute | solution.py:18
  7.2 142.0 %collective-permute-start.1 = (f32[32,1024]{1,0:T(8,128)}, f32[32,1024]{1,0:T(8,128)}, u32[]{:S(2)}, u32[]{:S(2)}) collective-permute-start(f32[32,1024]{1,0:T(8,128)} %reshape.177), channel_id=1, source_target_pairs={{0,3},{1,4},{2,5},{3,6},{4,7},{5,8},{6,9},{7,10},{8,11},{9,12},{10... | collective-permute-start | bytes 393224 | tf_op jit(solution)/shard_map/ppermute | solution.py:18
  13.1 138.9 %collective-permute-start.2 = (f32[32,1024]{1,0:T(8,128)}, f32[32,1024]{1,0:T(8,128)}, u32[]{:S(2)}, u32[]{:S(2)}) collective-permute-start(f32[32,1024]{1,0:T(8,128)} %reshape.177), channel_id=1, source_target_pairs={{0,2},{1,3},{2,4},{3,5},{4,6},{5,7},{6,8},{7,9},{8,10},{9,11},{10,... | collective-permute-start | bytes 393224 | tf_op jit(solution)/shard_map/ppermute | solution.py:18
  16.3 138.6 %collective-permute-start.3 = (f32[32,1024]{1,0:T(8,128)}, f32[32,1024]{1,0:T(8,128)}, u32[]{:S(2)}, u32[]{:S(2)}) collective-permute-start(f32[32,1024]{1,0:T(8,128)} %reshape.177), channel_id=1, source_target_pairs={{0,1},{1,2},{2,3},{3,4},{4,5},{5,6},{6,7},{7,8},{8,9},{9,10},{10,1... | collective-permute-start | bytes 393224 | tf_op jit(solution)/shard_map/ppermute | solution.py:18
  19.5 140.9 %collective-permute-start.4 = (f32[32,1024]{1,0:T(8,128)}, f32[32,1024]{1,0:T(8,128)}, u32[]{:S(2)}, u32[]{:S(2)}) collective-permute-start(f32[32,1024]{1,0:T(8,128)} %reshape.177), channel_id=1, source_target_pairs={{1,0},{2,1},{3,2},{4,3},{5,4},{6,5},{7,6},{8,7},{9,8},{10,9},{11,1... | collective-permute-start | bytes 393224 | tf_op jit(solution)/shard_map/ppermute | solution.py:18
  79.2 54.2 %copy-start.8 = (f32[1,4,64,64]{3,2,1,0:T(8,128)S(1)}, f32[1,4,64,64]{3,2,1,0:T(8,128)}, u32[]{:S(2)}) copy-start(f32[1,4,64,64]{3,2,1,0:T(8,128)} %param.21) | copy-start | bytes 196612
  132.5 6.8 %copy-start.1 = (f32[16,8192]{1,0:T(8,128)S(1)}, f32[16,8192]{1,0:T(8,128)}, u32[]{:S(2)}) copy-start(f32[16,8192]{1,0:T(8,128)} %param.15) | copy-start | bytes 1572868
  133.1 6.2 %copy-start.5 = (f32[2,8192]{1,0:T(2,128)S(1)}, f32[2,8192]{1,0:T(2,128)}, u32[]{:S(2)}) copy-start(f32[2,8192]{1,0:T(2,128)} %param.14) | copy-start | bytes 196612
  133.2 7.0 %copy-start.13 = (s32[32,9]{0,1:T(8,128)S(1)}, s32[32,9]{0,1:T(8,128)}, u32[]{:S(2)}) copy-start(s32[32,9]{0,1:T(8,128)} %param.22) | copy-start | bytes 3460
  133.2 7.0 %copy-start.10 = (s32[32,27]{1,0:T(8,128)S(1)}, s32[32,27]{1,0:T(8,128)}, u32[]{:S(2)}) copy-start(s32[32,27]{1,0:T(8,128)} %compare_select_fusion) | copy-start | bytes 10372
  141.5 26.1 %collective-permute-start.5 = (f32[32,1024]{1,0:T(8,128)}, f32[32,1024]{1,0:T(8,128)S(1)}, u32[]{:S(2)}, u32[]{:S(2)}) collective-permute-start(f32[32,1024]{1,0:T(8,128)} %reshape.177), channel_id=1, source_target_pairs={{2,0},{3,1},{4,2},{5,3},{6,4},{7,5},{8,6},{9,7},{10,8},{11,9},{12,... | collective-permute-start | bytes 393224 | tf_op jit(solution)/shard_map/ppermute | solution.py:18
  149.2 18.5 %collective-permute-start.6 = (f32[32,1024]{1,0:T(8,128)}, f32[32,1024]{1,0:T(8,128)S(1)}, u32[]{:S(2)}, u32[]{:S(2)}) collective-permute-start(f32[32,1024]{1,0:T(8,128)} %reshape.177), channel_id=1, source_target_pairs={{3,0},{4,1},{5,2},{6,3},{7,4},{8,5},{9,6},{10,7},{11,8},{12,9},{13... | collective-permute-start | bytes 393224 | tf_op jit(solution)/shard_map/ppermute | solution.py:18
  152.0 15.7 %collective-permute-start.7 = (f32[32,1024]{1,0:T(8,128)}, f32[32,1024]{1,0:T(8,128)S(1)}, u32[]{:S(2)}, u32[]{:S(2)}) collective-permute-start(f32[32,1024]{1,0:T(8,128)} %reshape.177), channel_id=1, source_target_pairs={{4,0},{5,1},{6,2},{7,3},{8,4},{9,5},{10,6},{11,7},{12,8},{13,9},{1... | collective-permute-start | bytes 393224 | tf_op jit(solution)/shard_map/ppermute | solution.py:18
  154.9 46.5 %collective-permute-start.8 = (f32[18,2048]{1,0:T(8,128)}, f32[18,2048]{1,0:T(8,128)}, u32[]{:S(2)}, u32[]{:S(2)}) collective-permute-start(f32[18,2048]{1,0:T(8,128)} %get-tuple-element.64), channel_id=1, source_target_pairs={{0,1},{1,2},{2,3},{3,4},{4,5},{5,6},{6,7},{7,8},{8,9},{9,10},{10,1... | collective-permute-start | bytes 442376 | tf_op jit(solution)/shard_map/ppermute | solution.py:29
  160.4 41.0 %collective-permute-start.9 = (f32[18,2048]{1,0:T(8,128)}, f32[18,2048]{1,0:T(8,128)}, u32[]{:S(2)}, u32[]{:S(2)}) collective-permute-start(f32[18,2048]{1,0:T(8,128)} %get-tuple-element.65), channel_id=1, source_target_pairs={{1,0},{2,1},{3,2},{4,3},{5,4},{6,5},{7,6},{8,7},{9,8},{10,9},{11,1... | collective-permute-start | bytes 442376 | tf_op jit(solution)/shard_map/ppermute | solution.py:31
  178.6 22.8 %copy-start.2 = (f32[16,8192]{1,0:T(8,128)S(1)}, f32[16,8192]{1,0:T(8,128)}, u32[]{:S(2)}) copy-start(f32[16,8192]{1,0:T(8,128)} %param.15) | copy-start | bytes 1572868
  178.6 22.8 %copy-start.6 = (f32[2,8192]{1,0:T(2,128)S(1)}, f32[2,8192]{1,0:T(2,128)}, u32[]{:S(2)}) copy-start(f32[2,8192]{1,0:T(2,128)} %param.14) | copy-start | bytes 196612
  202.9 0.7 copy-start.9
  207.7 126.6 %copy-start.4 = (f32[32,16,64]{2,1,0:T(8,128)S(1)}, f32[32,16,64]{2,1,0:T(8,128)}, u32[]{:S(2)}) copy-start(f32[32,16,64]{2,1,0:T(8,128)} %fusion.36) | copy-start | bytes 393220
where the time goes:
time: 339 us; the launch traced here: 337 us
  matrix products  139 us (41%)
  blocking collectives  101 us (30%)
  local copies, waits for them, and re-layouts  49 us (14%)
  starting transfers between devices  41.3 us (12%)
  other arithmetic  5.49 us (2%)
    dot_general x8, matrix products, near_field(): jnp.einsum('bkij,bkpj->bpi', kernel_tiles, source_values, precision=topmo...  105 us
    all_gather x1, blocking collectives, per_device(): lax.all_gather(skel_box.reshape(1, width), ('leaf', 'sub'), axis=0, tiled...  52.2 us
    all_gather x1, blocking collectives, per_device(): lax.all_gather(box_term.reshape(1, width), ('leaf', 'sub'), axis=0, tiled...  49.2 us
    ppermute x8, starting transfers between devices, from_behind(): return lax.ppermute(array, axis, pairs)  31.3 us
    dot_general x1, matrix products, per_device(): jnp.einsum('ckpr,ckrs->cps', far_rows, couple_leaf, precision=topmost_level)  22.8 us
    gather x4, local copies, waits for them, and re-layouts, pick_rows(): chosen = table[jnp.where(present, entries - first, 0)]  12.1 us
    squeeze x8, local copies, waits for them, and re-layouts, per_device(): lax.map(near_block, (target_points.reshape(leaves // nearby_span, nearby_...  9.84 us
    unnamed x44, local copies, waits for them, and re-layouts  7.84 us
  transfers between devices with their start and end apart: 10, of which 0 were waited for; matrix products, arithmetic and copies ran while one was open for 16% of the time, Pallas kernels for 0%

commit v1 on v0

v1 whole, which is shorter than its diff:
```python
import functools
import math

import jax
import jax.numpy as jnp
from jax import lax
from jax.experimental import pallas as pl
from jax.experimental.pallas import tpu as pltpu
from jax.sharding import PartitionSpec as P

NEAR_REACH = 8
FAR_REACH = 4
FEATURES = 16
GROUP = 8
FAR_STEP = 2

matern_rate = math.sqrt(3.0) / 0.1
coordinate_scale = matern_rate * math.log2(math.e)
ln2 = math.log(2.0)
tiny = 1e-20
f32 = jnp.float32
bf16 = jnp.bfloat16
vmem_bytes = 60 * 2**20
ring = ("leaf", "sub")


def halves(array):
    high = array.astype(bf16)
    return high, (array - high.astype(f32)).astype(bf16)


def stacked_halves(array):
    return jnp.concatenate(halves(array), axis=0)


def contract(left, right, dims):
    return lax.dot_general(left, right, (dims, ((), ())), preferred_element_type=f32)


def product3(left, right, dims=((1,), (0,))):
    rows = left.shape[0]
    high, low = halves(right)
    both = stacked_halves(left)
    wide = contract(both, high, dims)
    return wide[:rows] + wide[rows:] + contract(both[:rows], low, dims)


def skeleton_kernel(probes, basis, transfer_leaf, transfer_box, out):
    leaves, rank, leaf_size = basis.shape
    low_lanes = lax.broadcasted_iota(jnp.int32, (16, 2 * rank), 1) < rank

    def leaf_skeleton(c):
        both = stacked_halves(probes[:, c * leaf_size : (c + 1) * leaf_size])
        weights = stacked_halves(basis[c])
        wide = contract(both, weights, ((1,), (1,)))
        rolled = jnp.concatenate([wide[:16, rank:], wide[:16, :rank]], axis=1)
        return wide[:16] + wide[16:] + rolled

    box = jnp.zeros((16, rank), f32)
    for m in range(leaves // 2):
        even, odd = leaf_skeleton(2 * m), leaf_skeleton(2 * m + 1)
        odd = jnp.concatenate([odd[:, rank:], odd[:, :rank]], axis=1)
        pair = jnp.where(low_lanes, even, odd)
        out[m] = pair
        box += product3(pair, transfer_leaf[2 * m : 2 * m + 2].reshape(2 * rank, rank))
    term = product3(box, transfer_box[0])
    out[leaves // 2] = jnp.concatenate([box, term], axis=1)


def near_kernel(
    near, points, probes, left, right, out, values, source, target, total, item_c, item_s, item_w
):
    slots, leaves = near.shape
    leaf_size = target.shape[2]
    window = leaves + 2 * NEAR_REACH
    base = near[0, 0] - NEAR_REACH

    count = jnp.int32(0)
    for c in range(leaves):
        entries = [near[k, c] for k in range(slots)]
        for k in range(slots):
            new = entries[k] >= 0
            for j in range(k):
                new = new & (entries[j] != entries[k])
            times = jnp.float32(1.0)
            for j in range(k + 1, slots):
                times = times + jnp.where(entries[j] == entries[k], 1.0, 0.0)
            item_c[count] = c
            item_s[count] = entries[k] - base
            item_w[count] = times * ln2
            count = count + jnp.where(new, 1, 0)
    for u in range(GROUP):
        item_c[count + u] = 0
        item_s[count + u] = 0
        item_w[count + u] = 0.0

    ones = jnp.ones((3, leaf_size), f32)
    pad = jnp.zeros((2, leaf_size), f32)
    for w in range(window):
        own = NEAR_REACH <= w < NEAR_REACH + leaves
        if own:
            lanes = slice((w - NEAR_REACH) * leaf_size, (w - NEAR_REACH + 1) * leaf_size)
            place, value = points[:, lanes], probes[:, lanes]
        else:
            side = left if w < NEAR_REACH else right
            first = w if w < NEAR_REACH else w - NEAR_REACH - leaves
            lanes = slice(first * leaf_size, (first + 1) * leaf_size)
            place, value = side[16:18, lanes], side[0:16, lanes]
        values[w] = stacked_halves(value)
        scaled = (place - 0.5) * coordinate_scale
        first = scaled.astype(bf16).astype(f32)
        second = (scaled - first).astype(bf16).astype(f32)
        kept = first + second
        norm = kept[0:1] * kept[0:1] + kept[1:2] * kept[1:2]
        norm1 = norm.astype(bf16).astype(f32)
        rest = norm - norm1
        norm2 = rest.astype(bf16).astype(f32)
        norms = jnp.concatenate([norm1, norm2, rest - norm2], axis=0)
        rows = jnp.concatenate([first, second, first, second, norms, ones, pad], axis=0)
        source[w] = rows.T.astype(bf16)
        if own:
            target[w - NEAR_REACH] = jnp.concatenate(
                [-2.0 * first, -2.0 * first, -2.0 * second, -2.0 * second, ones, norms, pad], axis=0
            ).astype(bf16)
    total[...] = jnp.zeros_like(total)

    def tile(i):
        c, s, weight = item_c[i], item_s[i], item_w[i]
        squared = jnp.dot(source[s], target[c], preferred_element_type=f32)
        squared = jnp.maximum(squared, tiny)
        distance = squared * lax.rsqrt(squared)
        high, low = halves((distance + 1.0 / ln2) * jnp.exp2(-distance))
        both = values[s]
        wide = jnp.dot(both, high, preferred_element_type=f32)
        rest = jnp.dot(both[:16], low, preferred_element_type=f32)
        return c, (wide[:16] + wide[16:] + rest) * weight

    def group(t, carry):
        for c, term in [tile(t * GROUP + u) for u in range(GROUP)]:
            total[c] += term
        return carry

    lax.fori_loop(0, (count + GROUP - 1) // GROUP, group, 0)
    for c in range(leaves):
        out[:, c * leaf_size : (c + 1) * leaf_size] = total[c]


def fill_table(table, blocks, start):
    count, _, lanes = blocks.shape
    half = lanes // 2
    for m in range(count):
        block = blocks[m]
        swapped = jnp.concatenate([block[:, half:], block[:, :half]], axis=1)
        table[start + 2 * m] = stacked_halves(block)
        table[start + 2 * m + 1] = stacked_halves(swapped)


def picked(table, rows, low_lanes):
    pieces = []
    for k in range(0, len(rows) - 1, 2):
        pieces.append(jnp.where(low_lanes, table[rows[k]], table[rows[k + 1] ^ 1]))
    if len(rows) % 2:
        pieces.append(table[rows[-1]][:, : low_lanes.shape[1] // 2])
    return jnp.concatenate(pieces, axis=1)


def coupled(both, couples):
    count, rank, _ = couples.shape
    high, low = halves(couples.reshape(count * rank, rank))
    wide = jnp.dot(both, jnp.concatenate([high, low], axis=1), preferred_element_type=f32)
    return wide[:16, :rank] + wide[16:, :rank] + wide[:16, rank:]


def far_kernel(far, near, before, middle, after, couples, out, table):
    step = pl.program_id(0)
    per_step, slots, rank, _ = couples.shape
    leaves = far.shape[0]
    boxes = 2 * FAR_REACH + 1
    empty = boxes * leaves
    low_lanes = lax.broadcasted_iota(jnp.int32, (32, 2 * rank), 1) < rank

    @pl.when(step == 0)
    def _():
        for b in range(3):
            for place, blocks in ((b, before), (3 + b, middle), (6 + b, after)):
                fill_table(table, blocks.at[b, : leaves // 2], place * leaves)
        table[empty] = jnp.zeros_like(table[empty])
        table[empty + 1] = jnp.zeros_like(table[empty])

    base = near[0, 0] - FAR_REACH * leaves
    for u in range(per_step):
        c = step * per_step + u
        rows = [far[c, k] for k in range(slots)]
        rows = [jnp.where(row >= 0, row - base, empty) for row in rows]
        out[u] = coupled(picked(table, rows, low_lanes), couples[u])


def down_kernel(
    box_list,
    column_list,
    gathered,
    couple_box,
    couple_column,
    transfer_box,
    transfer_leaf,
    basis,
    far_leaf,
    near_values,
    out,
    table,
):
    leaves, rank, leaf_size = basis.shape
    boxes = gathered.shape[0]
    slots, column_slots = box_list.shape[1], column_list.shape[1]
    group_size = 4
    low_lanes = lax.broadcasted_iota(jnp.int32, (32, 2 * rank), 1) < rank

    def pick(row, present):
        block = gathered[jnp.where(present, row, 0)] * jnp.where(present, 1.0, 0.0)
        return block

    def swap(block):
        return jnp.concatenate([block[:, rank:], block[:, :rank]], axis=1)

    pieces = []
    for k in range(0, slots, 2):
        first = pick(box_list[0, k], box_list[0, k] >= 0)
        if k + 1 < slots:
            second = pick(box_list[0, k + 1], box_list[0, k + 1] >= 0)
            pieces.append(stacked_halves(jnp.where(low_lanes[:16], first, swap(second))))
        else:
            pieces.append(stacked_halves(first)[:, :rank])
    far_box = coupled(jnp.concatenate(pieces, axis=1), couple_box[0])

    columns = []
    for k in range(column_slots):
        row = column_list[0, k]
        start = jnp.where(row >= 0, row, 0) * group_size
        block = gathered[start]
        for j in range(1, group_size):
            block = block + gathered[start + j]
        columns.append(block * jnp.where(row >= 0, 1.0, 0.0))
    pieces = [
        stacked_halves(jnp.where(low_lanes[:16], swap(columns[k]), columns[k + 1]))
        for k in range(0, column_slots, 2)
    ]
    far_column = coupled(jnp.concatenate(pieces, axis=1), couple_column[0])
    down_box = far_box + product3(far_column, transfer_box[0], ((1,), (1,)))

    for c in range(leaves):
        down = far_leaf[c] + product3(down_box, transfer_leaf[c], ((1,), (1,)))
        lanes = slice(c * leaf_size, (c + 1) * leaf_size)
        out[:, lanes] = near_values[:, lanes] + product3(down, basis[c])


def whole(count):
    return [pl.BlockSpec(memory_space=pltpu.VMEM)] * count


def scalars(count):
    return [pl.BlockSpec(memory_space=pltpu.SMEM)] * count


params = pltpu.CompilerParams(vmem_limit_bytes=vmem_bytes)


def shifted(array, by):
    devices = lax.axis_size(ring)
    return lax.ppermute(array, ring, [(i, (i + by) % devices) for i in range(devices)])


def near_call(near_slots, points, probes, halo_left, halo_right):
    slots, leaves = near_slots.shape
    probe_count = probes.shape[0]
    leaf_size = probes.shape[1] // leaves
    window = leaves + 2 * NEAR_REACH
    items = leaves * slots + 2 * GROUP
    return pl.pallas_call(
        near_kernel,
        out_shape=jax.ShapeDtypeStruct(probes.shape, f32),
        in_specs=scalars(1) + whole(4),
        out_specs=pl.BlockSpec(memory_space=pltpu.VMEM),
        scratch_shapes=[
            pltpu.VMEM((window, 2 * probe_count, leaf_size), bf16),
            pltpu.VMEM((window, leaf_size, FEATURES), bf16),
            pltpu.VMEM((leaves, FEATURES, leaf_size), bf16),
            pltpu.VMEM((leaves, probe_count, leaf_size), f32),
        ]
        + [pltpu.SMEM((items,), dtype) for dtype in (jnp.int32, jnp.int32, f32)],
        compiler_params=params,
        cost_estimate=pl.CostEstimate(flops=20_000_000_000, bytes_accessed=2**22, transcendentals=0),
        name="near",
    )(near_slots, points, probes, halo_left, halo_right)


def per_device(
    points,
    probes,
    basis,
    transfer_leaf,
    transfer_box,
    couple_leaf,
    couple_box,
    couple_column,
    near_list,
    far_list,
    box_list,
    column_list,
):
    leaves, leaf_size, rank = basis.shape
    probe_count = probes.shape[0]
    reach = NEAR_REACH * leaf_size
    near_slots = near_list.T
    basis = basis.transpose(0, 2, 1)

    blocks = leaves // 2 + 1
    skeletons = pl.pallas_call(
        skeleton_kernel,
        out_shape=jax.ShapeDtypeStruct((blocks, probe_count, 2 * rank), f32),
        in_specs=whole(4),
        out_specs=pl.BlockSpec(memory_space=pltpu.VMEM),
        compiler_params=params,
        name="skeletons",
    )(probes, basis, transfer_leaf, transfer_box)

    stacked = jnp.concatenate([probes, points], axis=0)
    halo_left = shifted(stacked[:, -reach:], 1)
    halo_right = shifted(stacked[:, :reach], -1)

    middle = jnp.stack([shifted(skeletons, 1), skeletons, shifted(skeletons, -1)])
    before, after = shifted(middle, 3), shifted(middle, -3)

    sub = lax.axis_index("sub")
    window = jnp.concatenate([before[:, -1], middle[:, -1], after[:, -1]])
    column = lax.dynamic_slice_in_dim(window, FAR_REACH - sub, lax.axis_size("sub"), 0)
    gathered = lax.all_gather(column, "leaf", axis=0, tiled=True)

    near_values = near_call(near_slots, points, probes, halo_left, halo_right)

    boxes = 2 * FAR_REACH + 1
    three = pl.BlockSpec((3, blocks, probe_count, 2 * rank), lambda i: (0, 0, 0, 0))
    far_leaf = pl.pallas_call(
        far_kernel,
        grid=(leaves // FAR_STEP,),
        out_shape=jax.ShapeDtypeStruct((leaves, probe_count, rank), f32),
        in_specs=scalars(2)
        + [three] * 3
        + [pl.BlockSpec((FAR_STEP,) + couple_leaf.shape[1:], lambda i: (i, 0, 0, 0))],
        out_specs=pl.BlockSpec((FAR_STEP, probe_count, rank), lambda i: (i, 0, 0)),
        scratch_shapes=[pltpu.VMEM((boxes * leaves + 2, 2 * probe_count, 2 * rank), bf16)],
        compiler_params=params,
        cost_estimate=pl.CostEstimate(flops=5_000_000_000, bytes_accessed=2**25, transcendentals=0),
        name="far",
    )(far_list, near_slots, before, middle, after, couple_leaf)

    return pl.pallas_call(
        down_kernel,
        out_shape=jax.ShapeDtypeStruct(probes.shape, f32),
        in_specs=scalars(2) + whole(8),
        out_specs=pl.BlockSpec(memory_space=pltpu.VMEM),
        scratch_shapes=[pltpu.VMEM((8, 128), f32)],
        compiler_params=params,
        name="down",
    )(
        box_list,
        column_list,
        gathered,
        couple_box,
        couple_column,
        transfer_box,
        transfer_leaf,
        basis,
        far_leaf,
        near_values,
    )


def solution(mesh):
    placed = (
        P(None, ring),
        P(None, ring),
        P(ring, None, None),
        P(ring, None, None),
        P(ring, None, None),
        P(ring, None, None, None),
        P(ring, None, None, None),
        P("leaf", None, None, None),
        P(ring, None),
        P(ring, None),
        P(ring, None),
        P("leaf", None),
    )
    return jax.shard_map(
        per_device, mesh=mesh, in_specs=placed, out_specs=P(None, ring), check_vma=False
    )
```

time: 339 us -> 118 us (0.35)
  the two profiles are of different devices: /device:TPU:2 before, /device:TPU:1 now
where the time goes in v1:
time: 118 us; the launch traced here: 119 us
  Pallas kernels  67.7 us (57%)
  starting transfers between devices  17 us (14%)
  waiting for transfers between devices  15.9 us (13%)
  between operations  13.5 us (11%)
  local copies, waits for them, and re-layouts  3.52 us (3%)
  other arithmetic  1.57 us (1%)
    pallas_call x1, Pallas kernels, near_call(): pl.pallas_call(near_kernel, out_shape=jax.ShapeDtypeStruct(probes.shape,...  32.5 us
    pallas_call x1, Pallas kernels, per_device(): pl.pallas_call(far_kernel, grid=(leaves // FAR_STEP,), out_shape=jax.Shap...  18.8 us
    ppermute x6, starting transfers between devices, shifted(): lax.ppermute(array, ring, [(i, (i + by) % devices) for i in range(devices)])  17 us
    ppermute x6, waiting for transfers between devices, shifted(): lax.ppermute(array, ring, [(i, (i + by) % devices) for i in range(devices)])  15.9 us
    pallas_call x1, Pallas kernels, per_device(): pl.pallas_call(down_kernel, out_shape=jax.ShapeDtypeStruct(probes.shape,...  8.81 us
    pallas_call x1, Pallas kernels, per_device(): pl.pallas_call(skeleton_kernel, out_shape=jax.ShapeDtypeStruct((blocks, p...  7.55 us
  transfers between devices with their start and end apart: 7, of which 3 were waited for; matrix products, arithmetic and copies ran while one was open for 3% of the time, Pallas kernels for 43%

profile of v1, /device:TPU:1, one launch (start us, length us, event | category | flops | bytes accessed | tf_op | source)
XLA Modules:
  0.0 119.1 jit_solution(14113697899030205008)
XLA Ops:
  6.5 0.0 all-gather.2.cloned.1.call-start
  6.5 7.6 %skeletons.1 = f32[17,16,128]{2,1,0:T(8,128)} custom-call(f32[16,8192]{1,0:T(8,128)} %probes.3, f32[32,64,256]{2,1,0:T(8,128)} %bitcast.11, f32[32,64,64]{2,1,0:T(8,128)} %transfer_leaf.3, f32[1,64,64]{2,1,0:T(8,128)} %transfer_box.3), custom_call_target="tpu_custom_call" | custom-call | tf_op jit(solution)/shard_map/skeletons/pallas_call | solution.py:317
  14.1 5.1 %collective-permute-start.1 = (f32[17,16,128]{2,1,0:T(8,128)}, f32[17,16,128]{2,1,0:T(8,128)S(1)}, u32[]{:S(2)}, u32[]{:S(2)}) collective-permute-start(f32[17,16,128]{2,1,0:T(8,128)} %skeletons.1), channel_id=1, source_target_pairs={{0,127},{1,0},{2,1},{3,2},{4,3},{5,4},{6,5},{7,6},{8,7},{9,8},{10,... | collective-permute-start | bytes 417800 | tf_op jit(solution)/shard_map/ppermute | solution.py:269
  19.2 0.0 collective-permute-start
  19.2 1.1 constant_dynamic-update-slice_fusion.1
  20.3 0.9 constant_dynamic-update-slice_fusion
  21.2 1.9 %collective-permute-done.1 = f32[17,16,128]{2,1,0:T(8,128)S(1)} collective-permute-done((f32[17,16,128]{2,1,0:T(8,128)}, f32[17,16,128]{2,1,0:T(8,128)S(1)}, u32[]{:S(2)}, u32[]{:S(2)}) %collective-permute-start.1) | collective-permute-done | bytes 139296 | tf_op jit(solution)/shard_map/ppermute | solution.py:269
  23.1 2.1 %collective-permute-done = f32[17,16,128]{2,1,0:T(8,128)S(1)} collective-permute-done((f32[17,16,128]{2,1,0:T(8,128)}, f32[17,16,128]{2,1,0:T(8,128)S(1)}, u32[]{:S(2)}, u32[]{:S(2)}) %collective-permute-start) | collective-permute-done | bytes 139296 | tf_op jit(solution)/shard_map/ppermute | solution.py:269
  25.1 1.0 pad_maximum_fusion
  26.1 0.0 copy-start
  26.1 3.6 %collective-permute-start.3 = (f32[3,17,16,128]{3,2,1,0:T(8,128)S(1)}, f32[3,17,16,128]{3,2,1,0:T(8,128)S(1)}, u32[]{:S(2)}, u32[]{:S(2)}) collective-permute-start(f32[3,17,16,128]{3,2,1,0:T(8,128)S(1)} %copy.16.middle), channel_id=1, source_target_pairs={{0,125},{1,126},{2,127},{3,0},{4,1},{5,2},{6,3},{7,4},{8,5},{9,6},... | collective-permute-start | bytes 1253384 | tf_op jit(solution)/shard_map/ppermute | solution.py:269
  29.7 8.2 %collective-permute-start.5 = (f32[18,2048]{1,0:T(8,128)S(1)}, f32[18,2048]{1,0:T(8,128)S(1)}, u32[]{:S(2)}, u32[]{:S(2)}) collective-permute-start(f32[18,2048]{1,0:T(8,128)S(1)} %get-tuple-element.5), channel_id=1, source_target_pairs={{0,127},{1,0},{2,1},{3,2},{4,3},{5,4},{6,5},{7,6},{8,7},{9,8},{10,... | collective-permute-start | bytes 442376 | tf_op jit(solution)/shard_map/ppermute | solution.py:269
  38.0 0.0 collective-permute-start.4
  38.0 0.0 collective-permute-start.2
  38.0 0.0 collective-permute-done.3.after
  38.0 0.0 copy-start.1
  38.0 11.9 %collective-permute-done.2 = f32[3,17,16,128]{3,2,0,1:T(8,128)S(1)} collective-permute-done((f32[3,17,16,128]{3,2,0,1:T(8,128)S(1)}, f32[3,17,16,128]{3,2,0,1:T(8,128)S(1)}, u32[]{:S(2)}, u32[]{:S(2)}) %collective-permute-start.2) | collective-permute-done | bytes 417824 | tf_op jit(solution)/shard_map/ppermute | solution.py:269
  49.9 0.6 fusion.1
  50.5 0.0 all-gather.2.cloned.1.call-update
  50.6 0.0 collective-permute-done.5.right
  50.6 0.0 copy-start.2
  50.6 0.0 collective-permute-done.4.left
  50.6 0.0 copy-start.3
  50.6 0.6 copy-done.2
  51.2 0.1 copy-done.3
  51.3 32.5 %near.1.near_values = f32[16,8192]{1,0:T(8,128)} custom-call(s32[9,32]{1,0:T(8,128)} %bitcast.16, f32[2,8192]{1,0:T(2,128)} %points.1, f32[16,8192]{1,0:T(8,128)} %probes.3, f32[18,2048]{1,0:T(8,128)} %copy-done.3, f32[18,2048]{1,0:T(8,128)} %copy-done.2), custom_call_target="tpu_custom_call" | custom-call | flops 20000000000 | bytes 4194304 | tf_op jit(solution)/shard_map/near/pallas_call | solution.py:278
  83.8 0.0 copy-done
  83.8 0.0 copy-done.1
  83.8 0.8 copy.17.before
  84.6 18.8 %far.2.far_leaf = f32[32,16,64]{2,1,0:T(8,128)} custom-call(s32[32,27]{1,0:T(8,128)} %far.3, s32[9,32]{1,0:T(8,128)} %bitcast.17, f32[3,17,16,128]{3,2,1,0:T(8,128)} %copy.17.before, f32[3,17,16,128]{3,2,1,0:T(8,128)} %copy-done, f32[3,17,16,128]{3,2,1,0:T(8,128)} %copy-done.1, f32[32,27,64,64]{3,2,1,0:T(8,128)} %couples.1), custom_call_target="tpu_custom_call" | custom-call | flops 5000000000 | bytes 33554432 | tf_op jit(solution)/shard_map/far/pallas_call | solution.py:342
  103.4 0.0 all-gather.2.cloned.1.call-done.gathered
  103.4 8.8 %down.1 = f32[16,8192]{1,0:T(8,128)} custom-call(s32[1,27]{1,0:T(1,128)} %box_list.1, s32[1,4]{1,0:T(1,128)} %column_list.1, f32[128,16,128]{2,1,0:T(8,128)} %all-gather.2.cloned.1.call-done.gathered, f32[1,27,64,64]{3,2,1,0:T(8,128)} %couple_box.1, f32[1,4,64,64]{3,2,1,0:T(8,128)} %couple_column.1, f32[1,64,64]{2,1,0:T(8,128)} %transfer_box.3, ...), custom_call_target="tpu_custom_call" | custom-call | tf_op jit(solution)/shard_map/down/pallas_call | solution.py:356
  (5 shorter events, 0.1 us)
Async XLA Ops:
  6.5 96.9 %all-gather.2.cloned.1.call-start = ((), (), s32[]{:S(2)}) async-start(), calls=%async_computation | async-start | bytes 1081344 | tf_op jit(solution)/shard_map/all_gather | solution.py:336
  14.1 9.0 %collective-permute-start.1 = (f32[17,16,128]{2,1,0:T(8,128)}, f32[17,16,128]{2,1,0:T(8,128)S(1)}, u32[]{:S(2)}, u32[]{:S(2)}) collective-permute-start(f32[17,16,128]{2,1,0:T(8,128)} %skeletons.1), channel_id=1, source_target_pairs={{0,127},{1,0},{2,1},{3,2},{4,3},{5,4},{6,5},{7,6},{8,7},{9,8},{10,... | collective-permute-start | bytes 417800 | tf_op jit(solution)/shard_map/ppermute | solution.py:269
  19.2 5.9 %collective-permute-start = (f32[17,16,128]{2,1,0:T(8,128)}, f32[17,16,128]{2,1,0:T(8,128)S(1)}, u32[]{:S(2)}, u32[]{:S(2)}) collective-permute-start(f32[17,16,128]{2,1,0:T(8,128)} %skeletons.1), channel_id=1, source_target_pairs={{0,1},{1,2},{2,3},{3,4},{4,5},{5,6},{6,7},{7,8},{8,9},{9,10},{10,1... | collective-permute-start | bytes 417800 | tf_op jit(solution)/shard_map/ppermute | solution.py:269
  26.1 57.6 %copy-start = (f32[3,17,16,128]{3,2,1,0:T(8,128)}, f32[3,17,16,128]{3,2,1,0:T(8,128)S(1)}, u32[]{:S(2)}) copy-start(f32[3,17,16,128]{3,2,1,0:T(8,128)S(1)} %copy.16.middle) | copy-start | bytes 1253380
  26.1 11.8 %collective-permute-start.3 = (f32[3,17,16,128]{3,2,1,0:T(8,128)S(1)}, f32[3,17,16,128]{3,2,1,0:T(8,128)S(1)}, u32[]{:S(2)}, u32[]{:S(2)}) collective-permute-start(f32[3,17,16,128]{3,2,1,0:T(8,128)S(1)} %copy.16.middle), channel_id=1, source_target_pairs={{0,125},{1,126},{2,127},{3,0},{4,1},{5,2},{6,3},{7,4},{8,5},{9,6},... | collective-permute-start | bytes 1253384 | tf_op jit(solution)/shard_map/ppermute | solution.py:269
  29.7 20.8 %collective-permute-start.5 = (f32[18,2048]{1,0:T(8,128)S(1)}, f32[18,2048]{1,0:T(8,128)S(1)}, u32[]{:S(2)}, u32[]{:S(2)}) collective-permute-start(f32[18,2048]{1,0:T(8,128)S(1)} %get-tuple-element.5), channel_id=1, source_target_pairs={{0,127},{1,0},{2,1},{3,2},{4,3},{5,4},{6,5},{7,6},{8,7},{9,8},{10,... | collective-permute-start | bytes 442376 | tf_op jit(solution)/shard_map/ppermute | solution.py:269
  38.0 12.6 %collective-permute-start.4 = (f32[18,2048]{1,0:T(8,128)S(1)}, f32[18,2048]{1,0:T(8,128)S(1)}, u32[]{:S(2)}, u32[]{:S(2)}) collective-permute-start(f32[18,2048]{1,0:T(8,128)S(1)} %get-tuple-element.6), channel_id=1, source_target_pairs={{0,1},{1,2},{2,3},{3,4},{4,5},{5,6},{6,7},{7,8},{8,9},{9,10},{10,1... | collective-permute-start | bytes 442376 | tf_op jit(solution)/shard_map/ppermute | solution.py:269
  38.0 11.9 %collective-permute-start.2 = (f32[3,17,16,128]{3,2,0,1:T(8,128)S(1)}, f32[3,17,16,128]{3,2,0,1:T(8,128)S(1)}, u32[]{:S(2)}, u32[]{:S(2)}) collective-permute-start(f32[3,17,16,128]{3,2,0,1:T(8,128)S(1)} %pad_maximum_fusion), channel_id=1, source_target_pairs={{0,3},{1,4},{2,5},{3,6},{4,7},{5,8},{6,9},{7,10},{8,11},{9,12},{10... | collective-permute-start | bytes 1253384 | tf_op jit(solution)/shard_map/ppermute | solution.py:269
  38.0 45.8 %copy-start.1 = (f32[3,17,16,128]{3,2,1,0:T(8,128)}, f32[3,17,16,128]{3,2,1,0:T(8,128)S(1)}, u32[]{:S(2)}) copy-start(f32[3,17,16,128]{3,2,1,0:T(8,128)S(1)} %collective-permute-done.3.after) | copy-start | bytes 1253380
  50.6 0.7 copy-start.2
  50.6 0.7 copy-start.3
Sparse Core Ops, SparseCore 0:
  50.7 39.5 all-gather.1

commit v2 on v1

v2 whole, which is shorter than its diff:
```python
import functools
import math

import jax
import jax.numpy as jnp
from jax import lax
from jax.experimental import pallas as pl
from jax.experimental.pallas import tpu as pltpu
from jax.sharding import PartitionSpec as P

NEAR_REACH = 8
FAR_REACH = 4
FEATURES = 16
GROUP = 8
FAR_STEP = 2

matern_rate = math.sqrt(3.0) / 0.1
coordinate_scale = matern_rate * math.log2(math.e)
ln2 = math.log(2.0)
tiny = 1e-20
f32 = jnp.float32
bf16 = jnp.bfloat16
vmem_bytes = 60 * 2**20
ring = ("leaf", "sub")


def halves(array):
    high = array.astype(bf16)
    return high, (array - high.astype(f32)).astype(bf16)


def stacked_halves(array):
    return jnp.concatenate(halves(array), axis=0)


def contract(left, right, dims):
    return lax.dot_general(left, right, (dims, ((), ())), preferred_element_type=f32)


def product3(left, right, dims=((1,), (0,))):
    rows = left.shape[0]
    high, low = halves(right)
    both = stacked_halves(left)
    wide = contract(both, high, dims)
    return wide[:rows] + wide[rows:] + contract(both[:rows], low, dims)


def exchanged(block):
    half = block.shape[1] // 2
    return jnp.concatenate([block[:, half:], block[:, :half]], axis=1)


def skeleton_kernel(near, points, probes, basis, transfer_leaf, transfer_box, out, box_out, items):
    leaves, rank, leaf_size = basis.shape
    slots = near.shape[0]
    pairs = leaves // 2
    low_lanes = lax.broadcasted_iota(jnp.int32, (16, 2 * rank), 1) < rank

    leaf = lax.broadcasted_iota(jnp.int32, (1, leaves), 1)
    rows = [near[k : k + 1, :] for k in range(slots)]
    for k in range(slots):
        new = rows[k] >= 0
        times = jnp.ones_like(leaf)
        for j in range(k):
            new = new & (rows[j] != rows[k])
        for j in range(k + 1, slots):
            times = times + jnp.where(rows[j] == rows[k], 1, 0)
        place = rows[k] - rows[0] + leaf + NEAR_REACH
        items[k : k + 1, :] = jnp.where(new, leaf + place * 64 + times * 4096, 0)

    width = probes.shape[1]
    edge = NEAR_REACH * leaf_size
    for side, start in ((0, width - edge), (1, 0)):
        for j in range(edge // 128):
            lanes = slice(start + j * 128, start + (j + 1) * 128)
            out[side, pairs + j] = probes[:, lanes]
            out[side, pairs + edge // 128, j : j + 1, :] = points[0:1, lanes]
            out[side, pairs + edge // 128 + 1, j : j + 1, :] = points[1:2, lanes]

    def leaf_skeleton(c):
        both = stacked_halves(probes[:, c * leaf_size : (c + 1) * leaf_size])
        weights = stacked_halves(basis[c])
        wide = contract(both, weights, ((1,), (1,)))
        return wide[:16] + wide[16:] + exchanged(wide[:16])

    box = jnp.zeros((16, rank), f32)
    for m in range(pairs):
        pair = jnp.where(low_lanes, leaf_skeleton(2 * m), exchanged(leaf_skeleton(2 * m + 1)))
        out[0, m] = pair
        out[1, m] = pair
        box += product3(pair, transfer_leaf[2 * m : 2 * m + 2].reshape(2 * rank, rank))
    box_out[...] = jnp.concatenate([box, product3(box, transfer_box[0])], axis=1)


def near_kernel(
    items, points, probes, left, right, out, values, source, target, total, listed, *, groups
):
    slots, leaves = items.shape
    leaf_size = target.shape[2]
    pieces = leaf_size // 128
    pairs = leaves // 2
    edge_blocks = NEAR_REACH * pieces

    count = jnp.int32(0)
    for begin, end in groups:
        for c in range(begin, end):
            for k in range(slots):
                item = items[k, c]
                listed[count] = item
                count = count + jnp.where(item != 0, 1, 0)
    for u in range(GROUP):
        listed[count + u] = groups[0][0] + NEAR_REACH * 64

    ones = jnp.ones((3, leaf_size), f32)
    pad = jnp.zeros((2, leaf_size), f32)
    window = sorted({w for begin, end in groups for w in range(begin, end + 2 * NEAR_REACH)})
    for w in window:
        own = NEAR_REACH <= w < NEAR_REACH + leaves
        if own:
            lanes = slice((w - NEAR_REACH) * leaf_size, (w - NEAR_REACH + 1) * leaf_size)
            place, value = points[:, lanes], probes[:, lanes]
        else:
            side = left if w < NEAR_REACH else right
            first = (w if w < NEAR_REACH else w - NEAR_REACH - leaves) * pieces
            parts = range(first, first + pieces)
            value = jnp.concatenate([side[pairs + j] for j in parts], axis=1)
            place = jnp.concatenate(
                [
                    jnp.concatenate(
                        [side[pairs + edge_blocks + d, j : j + 1, :] for j in parts], axis=1
                    )
                    for d in range(2)
                ],
                axis=0,
            )
        values[w] = stacked_halves(value)
        scaled = (place - 0.5) * coordinate_scale
        first = scaled.astype(bf16).astype(f32)
        second = (scaled - first).astype(bf16).astype(f32)
        kept = first + second
        norm = kept[0:1] * kept[0:1] + kept[1:2] * kept[1:2]
        norm1 = norm.astype(bf16).astype(f32)
        rest = norm - norm1
        norm2 = rest.astype(bf16).astype(f32)
        norms = jnp.concatenate([norm1, norm2, rest - norm2], axis=0)
        rows = jnp.concatenate([first, second, first, second, norms, ones, pad], axis=0)
        source[w] = rows.T.astype(bf16)
        if own and any(begin <= w - NEAR_REACH < end for begin, end in groups):
            target[w - NEAR_REACH] = jnp.concatenate(
                [-2.0 * first, -2.0 * first, -2.0 * second, -2.0 * second, ones, norms, pad], axis=0
            ).astype(bf16)
    total[...] = jnp.zeros_like(total)

    def tile(i):
        item = listed[i]
        c, s, times = item & 63, (item >> 6) & 63, item >> 12
        squared = jnp.dot(source[s], target[c], preferred_element_type=f32)
        squared = jnp.maximum(squared, tiny)
        distance = squared * lax.rsqrt(squared)
        high, low = halves((distance + 1.0 / ln2) * jnp.exp2(-distance))
        both = values[s]
        wide = jnp.dot(both, high, preferred_element_type=f32)
        rest = jnp.dot(both[:16], low, preferred_element_type=f32)
        return c, (wide[:16] + wide[16:] + rest) * (times.astype(f32) * ln2)

    def group(t, carry):
        for c, term in [tile(t * GROUP + u) for u in range(GROUP)]:
            total[c] += term
        return carry

    lax.fori_loop(0, (count + GROUP - 1) // GROUP, group, 0)
    place = 0
    for begin, end in groups:
        for c in range(begin, end):
            out[:, place * leaf_size : (place + 1) * leaf_size] = total[c]
            place += 1


def fill_table(table, blocks, start):
    count, _, lanes = blocks.shape
    half = lanes // 2
    for m in range(count):
        block = blocks[m]
        swapped = jnp.concatenate([block[:, half:], block[:, :half]], axis=1)
        table[start + 2 * m] = stacked_halves(block)
        table[start + 2 * m + 1] = stacked_halves(swapped)


def picked(table, rows, low_lanes):
    pieces = []
    for k in range(0, len(rows) - 1, 2):
        pieces.append(jnp.where(low_lanes, table[rows[k]], table[rows[k + 1] ^ 1]))
    if len(rows) % 2:
        pieces.append(table[rows[-1]][:, : low_lanes.shape[1] // 2])
    return jnp.concatenate(pieces, axis=1)


def coupled_pairs(picks, couples):
    slots, rank, _ = couples.shape
    result = jnp.zeros((16, rank), f32)
    low_lanes = lax.broadcasted_iota(jnp.int32, (rank, 2 * rank), 1) < rank
    for start in range(0, slots, 8):
        pairs = (min(slots - start, 8) + 1) // 2
        highs, lows = [], []
        for m in range(pairs):
            even = couples[start + m]
            if start + pairs + m < slots:
                odd = couples[start + pairs + m]
            else:
                odd = jnp.zeros_like(even)
            high, low = halves(jnp.concatenate([even, odd], axis=1))
            highs.append(high)
            lows.append(low)
        right = jnp.concatenate(
            [jnp.concatenate(highs, axis=0), jnp.concatenate(lows, axis=0)], axis=1
        )
        left = jnp.concatenate(
            [picks(start, pairs), picks(start + pairs, pairs)], axis=0
        )
        wide = jnp.dot(left, right, preferred_element_type=f32)
        first = wide[:16, : 2 * rank] + wide[16:32, : 2 * rank] + wide[:16, 2 * rank :]
        second = wide[32:48, : 2 * rank] + wide[48:, : 2 * rank] + wide[32:48, 2 * rank :]
        result = result + first[:, :rank] + second[:, rank:]
    return result


def coupled(both, couples):
    count, rank, _ = couples.shape
    high, low = halves(couples.reshape(count * rank, rank))
    wide = jnp.dot(both, jnp.concatenate([high, low], axis=1), preferred_element_type=f32)
    return wide[:16, :rank] + wide[16:, :rank] + wide[:16, rank:]


def far_kernel(far, near, before, middle, after, couples, out, table):
    step = pl.program_id(0)
    per_step, slots, rank, _ = couples.shape
    leaves = far.shape[0]
    empty = (2 * FAR_REACH + 1) * leaves
    low_lanes = lax.broadcasted_iota(jnp.int32, (32, 2 * rank), 1) < rank

    @pl.when(step == 0)
    def _():
        for b in range(3):
            for place, blocks in ((b, before), (3 + b, middle), (6 + b, after)):
                fill_table(table, blocks.at[b], place * leaves)
        table[empty] = jnp.zeros_like(table[empty])
        table[empty + 1] = jnp.zeros_like(table[empty])

    base = near[0, 0] - FAR_REACH * leaves
    for u in range(per_step):
        c = step * per_step + u

        def picks(start, count):
            rows = [far[c, k] if k < slots else -1 for k in range(start, start + count)]
            rows = [jnp.where(row >= 0, row - base, empty) for row in rows]
            return picked(table, rows, low_lanes)

        out[u] = coupled_pairs(picks, couples[u])


def down_kernel(
    near,
    box_list,
    column_list,
    gathered,
    couple_box,
    couple_column,
    transfer_box,
    transfer_leaf,
    basis,
    far_leaf,
    near_inner,
    near_outer,
    out,
):
    leaves, rank, leaf_size = basis.shape
    slots, column_slots = box_list.shape[1], column_list.shape[1]
    group_size = 4
    low_lanes = lax.broadcasted_iota(jnp.int32, (32, 2 * rank), 1) < rank

    sub = (near[0, 0] // leaves) & (group_size - 1)

    def box_row(entry):
        entry = jnp.where(entry >= 0, entry, 0)
        return entry - (entry & (group_size - 1)) + ((entry - sub) & (group_size - 1))

    def pick(k):
        entry = box_list[0, k]
        return gathered[box_row(entry)] * jnp.where(entry >= 0, 1.0, 0.0)

    pieces = []
    for k in range(0, slots, 2):
        if k + 1 < slots:
            pieces.append(stacked_halves(jnp.where(low_lanes[:16], pick(k), exchanged(pick(k + 1)))))
        else:
            pieces.append(stacked_halves(pick(k))[:, :rank])
    far_box = coupled(jnp.concatenate(pieces, axis=1), couple_box[0])

    columns = []
    for k in range(column_slots):
        row = column_list[0, k]
        start = jnp.where(row >= 0, row, 0) * group_size
        block = gathered[start]
        for j in range(1, group_size):
            block = block + gathered[start + j]
        columns.append(block * jnp.where(row >= 0, 1.0, 0.0))
    pieces = [
        stacked_halves(jnp.where(low_lanes[:16], exchanged(columns[k]), columns[k + 1]))
        for k in range(0, column_slots, 2)
    ]
    far_column = coupled(jnp.concatenate(pieces, axis=1), couple_column[0])
    down_box = far_box + product3(far_column, transfer_box[0], ((1,), (1,)))

    for c in range(leaves):
        down = far_leaf[c] + product3(down_box, transfer_leaf[c], ((1,), (1,)))
        lanes = slice(c * leaf_size, (c + 1) * leaf_size)
        inner = NEAR_REACH <= c < leaves - NEAR_REACH
        place = c - NEAR_REACH if inner else c if c < NEAR_REACH else c - leaves + 2 * NEAR_REACH
        held = near_inner if inner else near_outer
        near_value = held[:, place * leaf_size : (place + 1) * leaf_size]
        out[:, lanes] = near_value + product3(down, basis[c])


def whole(count):
    return [pl.BlockSpec(memory_space=pltpu.VMEM)] * count


def scalars(count):
    return [pl.BlockSpec(memory_space=pltpu.SMEM)] * count


def params(mebibytes):
    return pltpu.CompilerParams(vmem_limit_bytes=mebibytes * 2**20)


def cost(flops):
    return pl.CostEstimate(flops=flops, bytes_accessed=2**20, transcendentals=0)


def shifted(array, axis, by):
    devices = lax.axis_size(axis)
    return lax.ppermute(array, axis, [(i, (i + by) % devices) for i in range(devices)])


def near_call(name, groups, items, points, probes, left, right):
    slots, leaves = items.shape
    probe_count = probes.shape[0]
    leaf_size = probes.shape[1] // leaves
    window = leaves + 2 * NEAR_REACH
    width = sum(end - begin for begin, end in groups) * leaf_size
    return pl.pallas_call(
        functools.partial(near_kernel, groups=groups),
        out_shape=jax.ShapeDtypeStruct((probe_count, width), f32),
        in_specs=scalars(1) + whole(4),
        out_specs=pl.BlockSpec(memory_space=pltpu.VMEM),
        scratch_shapes=[
            pltpu.VMEM((window, 2 * probe_count, leaf_size), bf16),
            pltpu.VMEM((window, leaf_size, FEATURES), bf16),
            pltpu.VMEM((leaves, FEATURES, leaf_size), bf16),
            pltpu.VMEM((leaves, probe_count, leaf_size), f32),
            pltpu.SMEM((leaves * slots + 2 * GROUP,), jnp.int32),
        ],
        compiler_params=params(14),
        cost_estimate=cost(10_000_000_000),
        name=name,
    )(items, points, probes, left, right)


def per_device(
    points,
    probes,
    basis,
    transfer_leaf,
    transfer_box,
    couple_leaf,
    couple_box,
    couple_column,
    near_list,
    far_list,
    box_list,
    column_list,
):
    leaves, leaf_size, rank = basis.shape
    probe_count = probes.shape[0]
    near_slots = near_list.T
    basis = basis.transpose(0, 2, 1)
    pairs = leaves // 2
    blocks = pairs + NEAR_REACH * leaf_size // 128 + 2

    bundles, box, items = pl.pallas_call(
        skeleton_kernel,
        out_shape=(
            jax.ShapeDtypeStruct((2, blocks, probe_count, 2 * rank), f32),
            jax.ShapeDtypeStruct((probe_count, 2 * rank), f32),
            jax.ShapeDtypeStruct(near_slots.shape, jnp.int32),
        ),
        in_specs=whole(6),
        out_specs=tuple(whole(3)),
        compiler_params=params(14),
        name="skeletons",
    )(near_slots, points, probes, basis, transfer_leaf, transfer_box)

    box_next, box_last = shifted(box, "sub", -1), shifted(box, "sub", 1)
    box_second = shifted(box_next, "sub", -1)
    column = jnp.stack([box, box_next, box_second, box_last])
    gathered = lax.all_gather(column, "leaf", axis=0, tiled=True)

    left, right = shifted(bundles[0], ring, 1), shifted(bundles[1], ring, -1)
    near_inner = near_call(
        "near_inner", ((NEAR_REACH, leaves - NEAR_REACH),), items, points, probes, box, box
    )
    middle = jnp.stack([left[:pairs], bundles[0, :pairs], right[:pairs]])
    before, after = shifted(middle, ring, 3), shifted(middle, ring, -3)
    near_outer = near_call(
        "near_outer",
        ((0, NEAR_REACH), (leaves - NEAR_REACH, leaves)),
        items,
        points,
        probes,
        left,
        right,
    )

    three = pl.BlockSpec(middle.shape, lambda i: (0, 0, 0, 0))
    far_leaf = pl.pallas_call(
        far_kernel,
        grid=(leaves // FAR_STEP,),
        out_shape=jax.ShapeDtypeStruct((leaves, probe_count, rank), f32),
        in_specs=scalars(2)
        + [three] * 3
        + [pl.BlockSpec((FAR_STEP,) + couple_leaf.shape[1:], lambda i: (i, 0, 0, 0))],
        out_specs=pl.BlockSpec((FAR_STEP, probe_count, rank), lambda i: (i, 0, 0)),
        scratch_shapes=[
            pltpu.VMEM(
                ((2 * FAR_REACH + 1) * leaves + 2, 2 * probe_count, 2 * rank), bf16
            )
        ],
        compiler_params=params(20),
        cost_estimate=cost(5_000_000_000),
        name="far",
    )(far_list, near_slots, before, middle, after, couple_leaf)

    return pl.pallas_call(
        down_kernel,
        out_shape=jax.ShapeDtypeStruct(probes.shape, f32),
        in_specs=scalars(3) + whole(9),
        out_specs=pl.BlockSpec(memory_space=pltpu.VMEM),
        compiler_params=params(14),
        name="down",
    )(
        near_slots,
        box_list,
        column_list,
        gathered,
        couple_box,
        couple_column,
        transfer_box,
        transfer_leaf,
        basis,
        far_leaf,
        near_inner,
        near_outer,
    )


def solution(mesh):
    placed = (
        P(None, ring),
        P(None, ring),
        P(ring, None, None),
        P(ring, None, None),
        P(ring, None, None),
        P(ring, None, None, None),
        P(ring, None, None, None),
        P("leaf", None, None, None),
        P(ring, None),
        P(ring, None),
        P(ring, None),
        P("leaf", None),
    )
    return jax.shard_map(
        per_device, mesh=mesh, in_specs=placed, out_specs=P(None, ring), check_vma=False
    )
```

time: 118 us -> 100 us (0.85)
  the two profiles are of different devices: /device:TPU:1 before, /device:TPU:0 now
where the time goes in v2:
time: 100 us; the launch traced here: 99.5 us
  Pallas kernels  49.7 us (50%)
  local copies, waits for them, and re-layouts  17.3 us (17%)
  starting transfers between devices  16.7 us (17%)
  between operations  13.7 us (14%)
  waiting for transfers between devices  1.4 us (1%)
    pallas_call x2, Pallas kernels, near_call(): pl.pallas_call(functools.partial(near_kernel, groups=groups), out_shape=j...  28.3 us
    unnamed x66, local copies, waits for them, and re-layouts  17.3 us
    ppermute x7, starting transfers between devices, shifted(): lax.ppermute(array, axis, [(i, (i + by) % devices) for i in range(devices)])  16.7 us
    pallas_call x1, Pallas kernels, per_device(): pl.pallas_call(far_kernel, grid=(leaves // FAR_STEP,), out_shape=jax.Shap...  9.8 us
    pallas_call x1, Pallas kernels, per_device(): pl.pallas_call(down_kernel, out_shape=jax.ShapeDtypeStruct(probes.shape,...  6.79 us
    pallas_call x1, Pallas kernels, per_device(): pl.pallas_call(skeleton_kernel, out_shape=(jax.ShapeDtypeStruct((2, block...  4.86 us
  transfers between devices with their start and end apart: 8, of which 1 were waited for; matrix products, arithmetic and copies ran while one was open for 1% of the time, Pallas kernels for 38%

profile of v2, /device:TPU:0, one launch (start us, length us, event | category | flops | bytes accessed | tf_op | source)
XLA Modules:
  0.0 99.5 jit_solution(5634387613823162327)
XLA Ops:
  6.5 1.6 %copy-done = f32[32,256,64]{1,2,0:T(8,128)S(1)} copy-done((f32[32,256,64]{1,2,0:T(8,128)S(1)}, f32[32,256,64]{1,2,0:T(8,128)}, u32[]{:S(2)}) %copy-start) | copy-done | bytes 2097176
  8.1 1.2 %copy-done.2 = f32[32,64,64]{2,1,0:T(8,128)S(1)} copy-done((f32[32,64,64]{2,1,0:T(8,128)S(1)}, f32[32,64,64]{2,1,0:T(8,128)}, u32[]{:S(2)}) %copy-start.2) | copy-done | bytes 524312
  9.4 1.0 %copy-done.6 = f32[16,8192]{1,0:T(8,128)S(1)} copy-done((f32[16,8192]{1,0:T(8,128)S(1)}, f32[16,8192]{1,0:T(8,128)}, u32[]{:S(2)}) %copy-start.6) | copy-done | bytes 524312
  10.4 0.8 copy-done.12
  11.2 0.7 copy-done.15
  11.9 0.8 copy-done.17
  12.7 4.9 %skeletons.1 = (f32[2,34,16,128]{3,2,1,0:T(8,128)S(1)}, f32[16,128]{1,0:T(8,128)S(1)}, s32[9,32]{1,0:T(8,128)S(1)}) custom-call(s32[9,32]{1,0:T(8,128)S(1)} %bitcast.18, f32[2,8192]{1,0:T(2,128)S(1)} %copy-done.17, f32[16,8192]{1,0:T(8,128)S(1)} %copy-done.6, f32[32,64,256]{2,1,0:T(8,128)S(1)} %bitcast.16, f32[32,64,64]{2,1,0:T(8,128)S(1)} %copy-done.2, ...), custom_call_target="tpu_custom_call" | custom-call | tf_op jit(solution)/shard_map/skeletons/pallas_call | solution.py:390
  17.6 4.1 %collective-permute-start = (f32[16,128]{1,0:T(8,128)S(1)}, f32[16,128]{1,0:T(8,128)S(1)}, u32[]{:S(2)}, u32[]{:S(2)}) collective-permute-start(f32[16,128]{1,0:T(8,128)S(1)} %get-tuple-element.8.left.right), channel_id=1, source_target_pairs={{0,3},{1,0},{2,1},{3,2},{4,7},{5,4},{6,5},{7,6},{8,11},{9,8},{10,9... | collective-permute-start | bytes 24584 | tf_op jit(solution)/shard_map/ppermute | solution.py:342
  21.7 0.0 collective-permute-start.2
  21.7 1.4 %collective-permute-done = f32[16,128]{1,0:T(8,128)S(1)} collective-permute-done((f32[16,128]{1,0:T(8,128)S(1)}, f32[16,128]{1,0:T(8,128)S(1)}, u32[]{:S(2)}, u32[]{:S(2)}) %collective-permute-start) | collective-permute-done | bytes 8224 | tf_op jit(solution)/shard_map/ppermute | solution.py:342
  23.1 3.5 %collective-permute-start.1 = (f32[16,128]{1,0:T(8,128)S(1)}, f32[16,128]{1,0:T(8,128)S(1)}, u32[]{:S(2)}, u32[]{:S(2)}) collective-permute-start(f32[16,128]{1,0:T(8,128)S(1)} %collective-permute-done), channel_id=1, source_target_pairs={{0,3},{1,0},{2,1},{3,2},{4,7},{5,4},{6,5},{7,6},{8,11},{9,8},{10,9... | collective-permute-start | bytes 24584 | tf_op jit(solution)/shard_map/ppermute | solution.py:342
  26.6 3.0 %collective-permute-start.4 = (f32[34,16,128]{2,1,0:T(8,128)S(1)}, f32[34,16,128]{2,1,0:T(8,128)S(1)}, u32[]{:S(2)}, u32[]{:S(2)}) collective-permute-start(f32[34,16,128]{2,1,0:T(8,128)S(1)} %get-tuple-element.12), channel_id=1, source_target_pairs={{0,127},{1,0},{2,1},{3,2},{4,3},{5,4},{6,5},{7,6},{8,7},{9,8},{10,... | collective-permute-start | bytes 835592 | tf_op jit(solution)/shard_map/ppermute | solution.py:342
  29.6 0.0 collective-permute-start.3
  29.6 0.0 collective-permute-done.2
  29.6 0.0 collective-permute-done.1
  29.6 0.6 pad_maximum_fusion.1
  30.2 0.0 all-gather.2.cloned.1.call-update
  30.3 0.0 copy-start.7
  30.3 1.0 %copy-done.7 = f32[16,8192]{1,0:T(8,128)S(1)} copy-done((f32[16,8192]{1,0:T(8,128)S(1)}, f32[16,8192]{1,0:T(8,128)}, u32[]{:S(2)}) %copy-start.7) | copy-done | bytes 524312
  31.3 0.8 copy-done.18
  32.2 14.5 %near_inner.1 = f32[16,4096]{1,0:T(8,128)S(1)} custom-call(s32[9,32]{1,0:T(8,128)S(1)} %get-tuple-element.10.items, f32[2,8192]{1,0:T(2,128)S(1)} %copy-done.18, f32[16,8192]{1,0:T(8,128)S(1)} %copy-done.7, f32[16,128]{1,0:T(8,128)S(1)} %get-tuple-element.8.left.right, f32[16,128]{1,0:T(8,128)S(1)} %get-tuple-element.8.left.right), custom_call_target="tpu_custom_call" | custom-call | flops 10000000000 | bytes 1048576 | tf_op jit(solution)/shard_map/near_inner/pallas_call | solution.py:351
  46.7 0.0 copy-start.16
  46.7 0.0 copy-start.23
  46.8 0.0 collective-permute-done.4.right
  46.8 0.0 collective-permute-done.3.left
  46.8 0.6 copy-done.19
  47.5 0.7 copy-done.21
  48.2 0.0 slice-start.4
  48.2 0.0 slice-start.5
  48.3 0.0 slice-start.6
  48.3 0.0 copy-start.1
  48.3 0.0 copy-start.3
  48.3 0.0 copy-start.13
  48.3 0.8 collective-permute-start.5
  49.1 5.2 %collective-permute-start.6 = (f32[3,16,16,128]{3,2,1,0:T(8,128)S(1)}, f32[3,16,16,128]{3,2,1,0:T(8,128)S(1)}, u32[]{:S(2)}, u32[]{:S(2)}) collective-permute-start(f32[3,16,16,128]{3,2,1,0:T(8,128)S(1)} %pad_maximum_fusion.middle), channel_id=1, source_target_pairs={{0,125},{1,126},{2,127},{3,0},{4,1},{5,2},{6,3},{7,4},{8,5},{9,6},... | collective-permute-start | bytes 1179656 | tf_op jit(solution)/shard_map/ppermute | solution.py:342
  54.3 1.0 copy-done.20
  55.3 1.0 copy-done.22
  56.3 13.8 %near_outer.1 = f32[16,4096]{1,0:T(8,128)S(1)} custom-call(s32[9,32]{1,0:T(8,128)S(1)} %get-tuple-element.10.items, f32[2,8192]{1,0:T(2,128)S(1)} %copy-done.18, f32[16,8192]{1,0:T(8,128)S(1)} %copy-done.7, f32[34,16,128]{2,1,0:T(8,128)S(1)} %copy-done.22, f32[34,16,128]{2,1,0:T(8,128)S(1)} %copy-done.20), custom_call_target="tpu_custom_call" | custom-call | flops 10000000000 | bytes 1048576 | tf_op jit(solution)/shard_map/near_outer/pallas_call | solution.py:351
  70.0 0.0 copy-start.10
  70.0 0.7 copy-done.10
  70.7 0.0 collective-permute-done.5.before
  70.7 0.0 collective-permute-done.6.after
  70.7 0.0 slice-done
  70.7 0.0 slice-done.1
  70.8 0.0 slice-done.2
  70.8 0.0 slice-done.3
  70.8 0.0 copy-done.16
  70.8 0.0 copy-done.23
  70.8 0.0 slice-done.4
  70.8 0.0 slice-done.5
  70.8 0.0 slice-done.6
  70.8 9.8 %far.2.far_leaf = f32[32,16,64]{2,1,0:T(8,128)S(1)} custom-call(s32[32,27]{1,0:T(8,128)S(1)} %copy-done.23, s32[9,32]{1,0:T(8,128)S(1)} %bitcast.19, f32[3,16,16,128]{3,2,1,0:T(8,128)S(1)} %collective-permute-done.5.before, f32[3,16,16,128]{3,2,1,0:T(8,128)S(1)} %pad_maximum_fusion.middle, f32[3,16,16,128]{3,2,1,0:T(8,128)S(1)} %collective-permute-done.6.after, ...), custom_call_target="tpu_custom_call" | custom-call | flops 5000000000 | bytes 1048576 | tf_op jit(solution)/shard_map/far/pallas_call | solution.py:425
  80.6 0.0 copy-done.24
  80.6 0.0 copy-done.25
  80.7 0.0 copy-done.1
  80.7 0.0 copy-done.3
  80.7 0.0 copy-done.13
  80.7 0.0 copy-start.4
  80.7 1.2 %copy-done.4 = f32[128,16,128]{2,1,0:T(8,128)S(1)} copy-done((f32[128,16,128]{2,1,0:T(8,128)S(1)}, f32[128,16,128]{2,1,0:T(8,128)}, u32[]{:S(2)}) %copy-start.4) | copy-done | bytes 1048600
  81.9 1.2 %copy-done.5 = f32[1,27,64,64]{3,2,1,0:T(8,128)S(1)} copy-done((f32[1,27,64,64]{3,2,1,0:T(8,128)S(1)}, f32[1,27,64,64]{3,2,1,0:T(8,128)}, u32[]{:S(2)}) %copy-start.5) | copy-done | bytes 442392
  83.1 0.9 copy-done.9
  84.0 0.9 copy-done.11
  85.0 0.9 copy-done.14
  85.9 6.8 %down.1 = f32[16,8192]{1,0:T(8,128)} custom-call(s32[9,32]{1,0:T(8,128)S(1)} %bitcast.20, s32[1,27]{1,0:T(1,128)S(1)} %copy-done.24, s32[1,4]{1,0:T(1,128)S(1)} %copy-done.25, f32[128,16,128]{2,1,0:T(8,128)S(1)} %copy-done.4, f32[1,27,64,64]{3,2,1,0:T(8,128)S(1)} %copy-done.5, f32[1,4,64,64]{3,2,1,0:T(8,128)S(1)} %copy-done.14, f32[1,64,64]{2,1,0:T(8,128)S(1)} %copy-done.13, ...), custom_call_target="tpu_custom_call" | custom-call | tf_op jit(solution)/shard_map/down/pallas_call | solution.py:443
  (31 shorter events, 0.1 us)
Async XLA Ops:
  6.5 74.1 %all-gather.2.cloned.1.call-start = ((), (), s32[]{:S(2)}) async-start(), calls=%async_computation | async-start | bytes 1081344 | tf_op jit(solution)/shard_map/all_gather | solution.py:406
  6.5 1.6 %copy-start = (f32[32,256,64]{1,2,0:T(8,128)S(1)}, f32[32,256,64]{1,2,0:T(8,128)}, u32[]{:S(2)}) copy-start(f32[32,256,64]{1,2,0:T(8,128)} %param.14) | copy-start | bytes 6291460
  8.1 1.2 %copy-start.2 = (f32[32,64,64]{2,1,0:T(8,128)S(1)}, f32[32,64,64]{2,1,0:T(8,128)}, u32[]{:S(2)}) copy-start(f32[32,64,64]{2,1,0:T(8,128)} %transfer_leaf.3) | copy-start | bytes 1572868
  9.4 1.0 %copy-start.6 = (f32[16,8192]{1,0:T(8,128)S(1)}, f32[16,8192]{1,0:T(8,128)}, u32[]{:S(2)}) copy-start(f32[16,8192]{1,0:T(8,128)} %probes.5) | copy-start | bytes 1572868
  10.4 0.8 copy-start.12
  11.2 0.7 copy-start.15
  11.9 0.8 copy-start.17
  17.6 5.5 %collective-permute-start = (f32[16,128]{1,0:T(8,128)S(1)}, f32[16,128]{1,0:T(8,128)S(1)}, u32[]{:S(2)}, u32[]{:S(2)}) collective-permute-start(f32[16,128]{1,0:T(8,128)S(1)} %get-tuple-element.8.left.right), channel_id=1, source_target_pairs={{0,3},{1,0},{2,1},{3,2},{4,7},{5,4},{6,5},{7,6},{8,11},{9,8},{10,9... | collective-permute-start | bytes 24584 | tf_op jit(solution)/shard_map/ppermute | solution.py:342
  21.7 7.9 %collective-permute-start.2 = (f32[16,128]{1,0:T(8,128)S(1)}, f32[16,128]{1,0:T(8,128)S(1)}, u32[]{:S(2)}, u32[]{:S(2)}) collective-permute-start(f32[16,128]{1,0:T(8,128)S(1)} %get-tuple-element.8.left.right), channel_id=1, source_target_pairs={{0,1},{1,2},{2,3},{3,0},{4,5},{5,6},{6,7},{7,4},{8,9},{9,10},{10,1... | collective-permute-start | bytes 24584 | tf_op jit(solution)/shard_map/ppermute | solution.py:342
  23.1 6.6 %collective-permute-start.1 = (f32[16,128]{1,0:T(8,128)S(1)}, f32[16,128]{1,0:T(8,128)S(1)}, u32[]{:S(2)}, u32[]{:S(2)}) collective-permute-start(f32[16,128]{1,0:T(8,128)S(1)} %collective-permute-done), channel_id=1, source_target_pairs={{0,3},{1,0},{2,1},{3,2},{4,7},{5,4},{6,5},{7,6},{8,11},{9,8},{10,9... | collective-permute-start | bytes 24584 | tf_op jit(solution)/shard_map/ppermute | solution.py:342
  26.6 20.2 %collective-permute-start.4 = (f32[34,16,128]{2,1,0:T(8,128)S(1)}, f32[34,16,128]{2,1,0:T(8,128)S(1)}, u32[]{:S(2)}, u32[]{:S(2)}) collective-permute-start(f32[34,16,128]{2,1,0:T(8,128)S(1)} %get-tuple-element.12), channel_id=1, source_target_pairs={{0,127},{1,0},{2,1},{3,2},{4,3},{5,4},{6,5},{7,6},{8,7},{9,8},{10,... | collective-permute-start | bytes 835592 | tf_op jit(solution)/shard_map/ppermute | solution.py:342
  29.6 17.2 %collective-permute-start.3 = (f32[34,16,128]{2,1,0:T(8,128)S(1)}, f32[34,16,128]{2,1,0:T(8,128)S(1)}, u32[]{:S(2)}, u32[]{:S(2)}) collective-permute-start(f32[34,16,128]{2,1,0:T(8,128)S(1)} %get-tuple-element.11), channel_id=1, source_target_pairs={{0,1},{1,2},{2,3},{3,4},{4,5},{5,6},{6,7},{7,8},{8,9},{9,10},{10,1... | collective-permute-start | bytes 835592 | tf_op jit(solution)/shard_map/ppermute | solution.py:342
  30.3 1.0 %copy-start.7 = (f32[16,8192]{1,0:T(8,128)S(1)}, f32[16,8192]{1,0:T(8,128)}, u32[]{:S(2)}) copy-start(f32[16,8192]{1,0:T(8,128)} %probes.5) | copy-start | bytes 1572868
  31.3 0.8 copy-start.18
  32.2 38.6 %slice-start = ((s8[28311552]{0:T(1024)(128)(4,1)}), s8[4194304]{0:T(1024)(128)(4,1)S(1)}, s32[]{:S(2)}) async-start(s8[28311552]{0:T(1024)(128)(4,1)} %bitcast.14), calls=%async_computation.1 | async-start | bytes 8388608
  32.2 38.6 %slice-start.1 = ((s8[28311552]{0:T(1024)(128)(4,1)}), s8[4194304]{0:T(1024)(128)(4,1)S(1)}, s32[]{:S(2)}) async-start(s8[28311552]{0:T(1024)(128)(4,1)} %bitcast.14), calls=%async_computation.2 | async-start | bytes 8388608
  32.2 38.6 %slice-start.2 = ((s8[28311552]{0:T(1024)(128)(4,1)}), s8[4194304]{0:T(1024)(128)(4,1)S(1)}, s32[]{:S(2)}) async-start(s8[28311552]{0:T(1024)(128)(4,1)} %bitcast.14), calls=%async_computation.3 | async-start | bytes 8388608
  32.2 38.6 %slice-start.3 = ((s8[28311552]{0:T(1024)(128)(4,1)}), s8[4194304]{0:T(1024)(128)(4,1)S(1)}, s32[]{:S(2)}) async-start(s8[28311552]{0:T(1024)(128)(4,1)} %bitcast.14), calls=%async_computation.4 | async-start | bytes 8388608
  46.7 1.5 %copy-start.8 = (f32[16,4096]{1,0:T(8,128)}, f32[16,4096]{1,0:T(8,128)S(1)}, u32[]{:S(2)}) copy-start(f32[16,4096]{1,0:T(8,128)S(1)} %near_inner.1) | copy-start | bytes 786436
  46.7 24.1 %copy-start.16 = (s32[32,9]{0,1:T(8,128)S(1)}, s32[32,9]{0,1:T(8,128)}, u32[]{:S(2)}) copy-start(s32[32,9]{0,1:T(8,128)} %param.20) | copy-start | bytes 3460
  46.7 24.1 %copy-start.23 = (s32[32,27]{1,0:T(8,128)S(1)}, s32[32,27]{1,0:T(8,128)}, u32[]{:S(2)}) copy-start(s32[32,27]{1,0:T(8,128)} %far.3) | copy-start | bytes 10372
  46.8 0.7 copy-start.19
  47.5 0.7 copy-start.21
  48.2 32.5 %copy-start.24 = (s32[1,27]{1,0:T(1,128)S(1)}, s32[1,27]{1,0:T(1,128)}, u32[]{:S(2)}) copy-start(s32[1,27]{1,0:T(1,128)} %box_list.1) | copy-start | bytes 328
  48.2 32.5 %copy-start.25 = (s32[1,4]{1,0:T(1,128)S(1)}, s32[1,4]{1,0:T(1,128)}, u32[]{:S(2)}) copy-start(s32[1,4]{1,0:T(1,128)} %column_list.1) | copy-start | bytes 52
  48.2 22.6 %slice-start.4 = ((s8[28311552]{0:T(1024)(128)(4,1)}), s8[4194304]{0:T(1024)(128)(4,1)S(1)}, s32[]{:S(2)}) async-start(s8[28311552]{0:T(1024)(128)(4,1)} %bitcast.14), calls=%async_computation.5 | async-start | bytes 8388608
  48.2 22.6 %slice-start.5 = ((s8[28311552]{0:T(1024)(128)(4,1)}), s8[4194304]{0:T(1024)(128)(4,1)S(1)}, s32[]{:S(2)}) async-start(s8[28311552]{0:T(1024)(128)(4,1)} %bitcast.14), calls=%async_computation.6 | async-start | bytes 8388608
  48.3 22.6 %slice-start.6 = ((s8[28311552]{0:T(1024)(128)(4,1)}), s8[3145728]{0:T(1024)(128)(4,1)S(1)}, s32[]{:S(2)}) async-start(s8[28311552]{0:T(1024)(128)(4,1)} %bitcast.14), calls=%async_computation.7 | async-start | bytes 6291456
  48.3 32.4 %copy-start.1 = (f32[32,256,64]{1,2,0:T(8,128)S(1)}, f32[32,256,64]{1,2,0:T(8,128)}, u32[]{:S(2)}) copy-start(f32[32,256,64]{1,2,0:T(8,128)} %param.14) | copy-start | bytes 6291460
  48.3 32.4 %copy-start.3 = (f32[32,64,64]{2,1,0:T(8,128)S(1)}, f32[32,64,64]{2,1,0:T(8,128)}, u32[]{:S(2)}) copy-start(f32[32,64,64]{2,1,0:T(8,128)} %transfer_leaf.3) | copy-start | bytes 1572868
  48.3 32.4 %copy-start.13 = (f32[1,64,64]{2,1,0:T(8,128)S(1)}, f32[1,64,64]{2,1,0:T(8,128)}, u32[]{:S(2)}) copy-start(f32[1,64,64]{2,1,0:T(8,128)} %transfer_box.3) | copy-start | bytes 49156
  48.3 22.4 %collective-permute-start.5 = (f32[3,16,16,128]{3,2,1,0:T(8,128)S(1)}, f32[3,16,16,128]{3,2,1,0:T(8,128)S(1)}, u32[]{:S(2)}, u32[]{:S(2)}) collective-permute-start(f32[3,16,16,128]{3,2,1,0:T(8,128)S(1)} %pad_maximum_fusion.middle), channel_id=1, source_target_pairs={{0,3},{1,4},{2,5},{3,6},{4,7},{5,8},{6,9},{7,10},{8,11},{9,12},{10... | collective-permute-start | bytes 1179656 | tf_op jit(solution)/shard_map/ppermute | solution.py:342
  49.1 21.6 %collective-permute-start.6 = (f32[3,16,16,128]{3,2,1,0:T(8,128)S(1)}, f32[3,16,16,128]{3,2,1,0:T(8,128)S(1)}, u32[]{:S(2)}, u32[]{:S(2)}) collective-permute-start(f32[3,16,16,128]{3,2,1,0:T(8,128)S(1)} %pad_maximum_fusion.middle), channel_id=1, source_target_pairs={{0,125},{1,126},{2,127},{3,0},{4,1},{5,2},{6,3},{7,4},{8,5},{9,6},... | collective-permute-start | bytes 1179656 | tf_op jit(solution)/shard_map/ppermute | solution.py:342
  54.3 1.0 copy-start.20
  55.3 1.0 copy-start.22
  70.0 0.7 copy-start.10
  80.7 1.2 %copy-start.4 = (f32[128,16,128]{2,1,0:T(8,128)S(1)}, f32[128,16,128]{2,1,0:T(8,128)}, u32[]{:S(2)}) copy-start(f32[128,16,128]{2,1,0:T(8,128)} %all-gather.2.cloned.1.call-done.gathered) | copy-start | bytes 3145732
  81.9 1.2 %copy-start.5 = (f32[1,27,64,64]{3,2,1,0:T(8,128)S(1)}, f32[1,27,64,64]{3,2,1,0:T(8,128)}, u32[]{:S(2)}) copy-start(f32[1,27,64,64]{3,2,1,0:T(8,128)} %couple_box.1) | copy-start | bytes 1327108
  83.1 0.9 copy-start.9
  84.0 0.9 copy-start.11
  85.0 0.9 copy-start.14
Sparse Core Ops, SparseCore 0:
  30.4 43.1 all-gather.1

commit v3 on v2

--- a/solution.py
+++ b/solution.py
@@ -11,8 +11,9 @@
 NEAR_REACH = 8
 FAR_REACH = 4
 FEATURES = 16
-GROUP = 8
+GROUP = 12
 FAR_STEP = 2
+CHUNKS = 4
 
 matern_rate = math.sqrt(3.0) / 0.1
 coordinate_scale = matern_rate * math.log2(math.e)
@@ -45,13 +46,36 @@
     return wide[:rows] + wide[rows:] + contract(both[:rows], low, dims)
 
 
+def copies(pairs, semaphores):
+    made = [
+        pltpu.make_async_copy(source, held, semaphores.at[i])
+        for i, (source, held) in enumerate(pairs)
+    ]
+    for copy in made:
+        copy.start()
+    return made
+
+
+def parts(source, held):
+    length = source.shape[0] // CHUNKS
+    runs = [pl.ds(i * length, length) for i in range(CHUNKS)]
+    return [(source.at[run], held.at[run]) for run in runs]
+
+
 def exchanged(block):
     half = block.shape[1] // 2
     return jnp.concatenate([block[:, half:], block[:, :half]], axis=1)
 
 
-def skeleton_kernel(near, points, probes, basis, transfer_leaf, transfer_box, out, box_out, items):
+def skeleton_kernel(
+    near, points, probes_in, basis_in, transfer_in, transfer_box, out, box_out, items,
+    probes, basis, transfer_leaf, semaphores,
+):
     leaves, rank, leaf_size = basis.shape
+    arriving = copies(
+        [(probes_in, probes)] + parts(basis_in, basis) + parts(transfer_in, transfer_leaf),
+        semaphores,
+    )
     slots = near.shape[0]
     pairs = leaves // 2
     low_lanes = lax.broadcasted_iota(jnp.int32, (16, 2 * rank), 1) < rank
@@ -68,6 +92,7 @@
         place = rows[k] - rows[0] + leaf + NEAR_REACH
         items[k : k + 1, :] = jnp.where(new, leaf + place * 64 + times * 4096, 0)
 
+    arriving[0].wait()
     width = probes.shape[1]
     edge = NEAR_REACH * leaf_size
     for side, start in ((0, width - edge), (1, 0)):
@@ -85,11 +110,14 @@
 
     box = jnp.zeros((16, rank), f32)
     for m in range(pairs):
+        if m % (pairs // CHUNKS) == 0:
+            arriving[1 + m // (pairs // CHUNKS)].wait()
+            arriving[1 + CHUNKS + m // (pairs // CHUNKS)].wait()
         pair = jnp.where(low_lanes, leaf_skeleton(2 * m), exchanged(leaf_skeleton(2 * m + 1)))
         out[0, m] = pair
         out[1, m] = pair
         box += product3(pair, transfer_leaf[2 * m : 2 * m + 2].reshape(2 * rank, rank))
-    box_out[...] = jnp.concatenate([box, product3(box, transfer_box[0])], axis=1)
+    box_out[0] = jnp.concatenate([box, product3(box, transfer_box[0])], axis=1)
 
 
 def near_kernel(
@@ -231,58 +259,90 @@
     return wide[:16, :rank] + wide[16:, :rank] + wide[:16, rank:]
 
 
-def far_kernel(far, near, before, middle, after, couples, out, table):
-    step = pl.program_id(0)
-    per_step, slots, rank, _ = couples.shape
-    leaves = far.shape[0]
+def outer_kernel(
+    items, far, near, points, probes, left, right, before, middle, after, couples_in,
+    out, far_out, values, source, target, total, listed, table, couples, semaphores, *, groups
+):
+    leaves, slots, rank, _ = couples.shape
+    steps = leaves // FAR_STEP
+
+    def arriving(step):
+        run = pl.ds(step * FAR_STEP, FAR_STEP)
+        return pltpu.make_async_copy(couples_in.at[run], couples.at[run], semaphores.at[step])
+
+    def start(step, carry):
+        arriving(step).start()
+        return carry
+
+    lax.fori_loop(0, steps, start, 0)
+    near_kernel(
+        items, points, probes, left, right, out, values, source, target, total, listed, groups=groups
+    )
+
     empty = (2 * FAR_REACH + 1) * leaves
     low_lanes = lax.broadcasted_iota(jnp.int32, (32, 2 * rank), 1) < rank
-
-    @pl.when(step == 0)
-    def _():
-        for b in range(3):
-            for place, blocks in ((b, before), (3 + b, middle), (6 + b, after)):
-                fill_table(table, blocks.at[b], place * leaves)
-        table[empty] = jnp.zeros_like(table[empty])
-        table[empty + 1] = jnp.zeros_like(table[empty])
-
+    for b in range(3):
+        for place, blocks in ((b, before), (3 + b, middle), (6 + b, after)):
+            fill_table(table, blocks.at[b], place * leaves)
+    table[empty] = jnp.zeros_like(table[empty])
+    table[empty + 1] = jnp.zeros_like(table[empty])
     base = near[0, 0] - FAR_REACH * leaves
-    for u in range(per_step):
-        c = step * per_step + u
-
-        def picks(start, count):
-            rows = [far[c, k] if k < slots else -1 for k in range(start, start + count)]
-            rows = [jnp.where(row >= 0, row - base, empty) for row in rows]
-            return picked(table, rows, low_lanes)
-
-        out[u] = coupled_pairs(picks, couples[u])
+
+    def far_step(step, carry):
+        arriving(step).wait()
+        for u in range(FAR_STEP):
+            c = step * FAR_STEP + u
+
+            def picks(start, count):
+                rows = [far[c, k] if k < slots else -1 for k in range(start, start + count)]
+                rows = [jnp.where(row >= 0, row - base, empty) for row in rows]
+                return picked(table, rows, low_lanes)
+
+            far_out[c] = coupled_pairs(picks, couples.at[c])
+        return carry
+
+    lax.fori_loop(0, steps, far_step, 0)
 
 
 def down_kernel(
-    near,
-    box_list,
-    column_list,
-    gathered,
-    couple_box,
-    couple_column,
-    transfer_box,
-    transfer_leaf,
-    basis,
-    far_leaf,
-    near_inner,
-    near_outer,
-    out,
+    near, box_list, column_list, boxes0, boxes1, boxes2, boxes3, couple_box_in, couple_column_in,
+    transfer_box_in, transfer_in, basis_in, far_in, inner_in, outer_in, out,
+    gathered, couple_box, couple_column, transfer_box, transfer_leaf, basis, far_leaf,
+    near_inner, near_outer, semaphores,
 ):
     leaves, rank, leaf_size = basis.shape
     slots, column_slots = box_list.shape[1], column_list.shape[1]
-    group_size = 4
     low_lanes = lax.broadcasted_iota(jnp.int32, (32, 2 * rank), 1) < rank
-
-    sub = (near[0, 0] // leaves) & (group_size - 1)
+    length = boxes0.shape[0]
+    arriving = copies(
+        [
+            (boxes, gathered.at[pl.ds(i * length, length)])
+            for i, boxes in enumerate((boxes0, boxes1, boxes2, boxes3))
+        ]
+        + [
+            (couple_box_in, couple_box),
+            (couple_column_in, couple_column),
+            (transfer_box_in, transfer_box),
+            (far_in, far_leaf),
+            (inner_in, near_inner),
+            (outer_in, near_outer),
+        ]
+        + parts(transfer_in, transfer_leaf)
+        + parts(basis_in, basis),
+        semaphores,
+    )
+    for copy in arriving[:7]:
+        copy.wait()
+
+    own = near[0, 0] // leaves
+
+    def moved(entry, shift, bits):
+        mask = (1 << bits) - 1
+        return (((entry >> shift) - (own >> shift)) & mask) << shift
 
     def box_row(entry):
         entry = jnp.where(entry >= 0, entry, 0)
-        return entry - (entry & (group_size - 1)) + ((entry - sub) & (group_size - 1))
+        return moved(entry, 0, 2) + moved(entry, 2, 1) + moved(entry, 3, 2) + moved(entry, 5, 2)
 
     def pick(k):
         entry = box_list[0, k]
@@ -299,9 +359,9 @@
     columns = []
     for k in range(column_slots):
         row = column_list[0, k]
-        start = jnp.where(row >= 0, row, 0) * group_size
+        start = box_row(row * 4) & ~3
         block = gathered[start]
-        for j in range(1, group_size):
+        for j in range(1, 4):
             block = block + gathered[start + j]
         columns.append(block * jnp.where(row >= 0, 1.0, 0.0))
     pieces = [
@@ -311,7 +371,12 @@
     far_column = coupled(jnp.concatenate(pieces, axis=1), couple_column[0])
     down_box = far_box + product3(far_column, transfer_box[0], ((1,), (1,)))
 
+    for copy in arriving[7:10]:
+        copy.wait()
     for c in range(leaves):
+        if c % (leaves // CHUNKS) == 0:
+            arriving[10 + c // (leaves // CHUNKS)].wait()
+            arriving[10 + CHUNKS + c // (leaves // CHUNKS)].wait()
         down = far_leaf[c] + product3(down_box, transfer_leaf[c], ((1,), (1,)))
         lanes = slice(c * leaf_size, (c + 1) * leaf_size)
         inner = NEAR_REACH <= c < leaves - NEAR_REACH
@@ -329,8 +394,7 @@
     return [pl.BlockSpec(memory_space=pltpu.SMEM)] * count
 
 
-def params(mebibytes):
-    return pltpu.CompilerParams(vmem_limit_bytes=mebibytes * 2**20)
+params = pltpu.CompilerParams(vmem_limit_bytes=60 * 2**20)
 
 
 def cost(flops):
@@ -342,28 +406,38 @@
     return lax.ppermute(array, axis, [(i, (i + by) % devices) for i in range(devices)])
 
 
-def near_call(name, groups, items, points, probes, left, right):
+def hbm(count):
+    return [pl.BlockSpec(memory_space=pl.ANY)] * count
+
+
+def near_scratch(items, probe_count, leaf_size):
     slots, leaves = items.shape
-    probe_count = probes.shape[0]
-    leaf_size = probes.shape[1] // leaves
     window = leaves + 2 * NEAR_REACH
-    width = sum(end - begin for begin, end in groups) * leaf_size
-    return pl.pallas_call(
-        functools.partial(near_kernel, groups=groups),
-        out_shape=jax.ShapeDtypeStruct((probe_count, width), f32),
-        in_specs=scalars(1) + whole(4),
-        out_specs=pl.BlockSpec(memory_space=pltpu.VMEM),
-        scratch_shapes=[
-            pltpu.VMEM((window, 2 * probe_count, leaf_size), bf16),
-            pltpu.VMEM((window, leaf_size, FEATURES), bf16),
-            pltpu.VMEM((leaves, FEATURES, leaf_size), bf16),
-            pltpu.VMEM((leaves, probe_count, leaf_size), f32),
-            pltpu.SMEM((leaves * slots + 2 * GROUP,), jnp.int32),
-        ],
-        compiler_params=params(14),
-        cost_estimate=cost(10_000_000_000),
-        name=name,
-    )(items, points, probes, left, right)
+    return [
+        pltpu.VMEM((window, 2 * probe_count, leaf_size), bf16),
+        pltpu.VMEM((window, leaf_size, FEATURES), bf16),
+        pltpu.VMEM((leaves, FEATURES, leaf_size), bf16),
+        pltpu.VMEM((leaves, probe_count, leaf_size), f32),
+        pltpu.SMEM((leaves * slots + 2 * GROUP,), jnp.int32),
+    ]
+
+
+def like(array):
+    return pltpu.VMEM(array.shape, array.dtype)
+
+
+def copy_semaphores(count):
+    return pltpu.SemaphoreType.DMA((count,))
+
+
+def moved_along(array, shift, bits, by):
+    mask = (1 << bits) - 1
+
+    def target(i):
+        part = (i >> shift) & mask
+        return i + ((((part - by) & mask) - part) << shift)
+
+    return lax.ppermute(array, "leaf", [(i, target(i)) for i in range(lax.axis_size("leaf"))])
 
 
 def per_device(
@@ -391,76 +465,72 @@
         skeleton_kernel,
         out_shape=(
             jax.ShapeDtypeStruct((2, blocks, probe_count, 2 * rank), f32),
-            jax.ShapeDtypeStruct((probe_count, 2 * rank), f32),
+            jax.ShapeDtypeStruct((1, probe_count, 2 * rank), f32),
             jax.ShapeDtypeStruct(near_slots.shape, jnp.int32),
         ),
-        in_specs=whole(6),
+        in_specs=whole(2) + hbm(3) + whole(1),
         out_specs=tuple(whole(3)),
-        compiler_params=params(14),
+        scratch_shapes=[like(probes), like(basis), like(transfer_leaf)]
+        + [copy_semaphores(1 + 2 * CHUNKS)],
+        compiler_params=params,
         name="skeletons",
     )(near_slots, points, probes, basis, transfer_leaf, transfer_box)
 
     box_next, box_last = shifted(box, "sub", -1), shifted(box, "sub", 1)
+    left, right = shifted(bundles[0], ring, 1), shifted(bundles[1], ring, -1)
     box_second = shifted(box_next, "sub", -1)
-    column = jnp.stack([box, box_next, box_second, box_last])
-    gathered = lax.all_gather(column, "leaf", axis=0, tiled=True)
-
-    left, right = shifted(bundles[0], ring, 1), shifted(bundles[1], ring, -1)
-    near_inner = near_call(
-        "near_inner", ((NEAR_REACH, leaves - NEAR_REACH),), items, points, probes, box, box
-    )
+    column = jnp.concatenate([box, box_next, box_second, box_last])
+    both = jnp.concatenate([column, moved_along(column, 0, 1, 1)])
+    along_y = [both] + [moved_along(both, 1, 2, by) for by in (1, 2, 3)]
+    plane = jnp.concatenate(along_y)
+    planes = [plane] + [moved_along(plane, 3, 2, by) for by in (1, 2, 3)]
+
     middle = jnp.stack([left[:pairs], bundles[0, :pairs], right[:pairs]])
     before, after = shifted(middle, ring, 3), shifted(middle, ring, -3)
-    near_outer = near_call(
-        "near_outer",
-        ((0, NEAR_REACH), (leaves - NEAR_REACH, leaves)),
-        items,
-        points,
-        probes,
-        left,
-        right,
-    )
-
-    three = pl.BlockSpec(middle.shape, lambda i: (0, 0, 0, 0))
-    far_leaf = pl.pallas_call(
-        far_kernel,
-        grid=(leaves // FAR_STEP,),
-        out_shape=jax.ShapeDtypeStruct((leaves, probe_count, rank), f32),
-        in_specs=scalars(2)
-        + [three] * 3
-        + [pl.BlockSpec((FAR_STEP,) + couple_leaf.shape[1:], lambda i: (i, 0, 0, 0))],
-        out_specs=pl.BlockSpec((FAR_STEP, probe_count, rank), lambda i: (i, 0, 0)),
-        scratch_shapes=[
-            pltpu.VMEM(
-                ((2 * FAR_REACH + 1) * leaves + 2, 2 * probe_count, 2 * rank), bf16
-            )
+
+    inner = ((NEAR_REACH, leaves - NEAR_REACH),)
+    outer = ((0, NEAR_REACH), (leaves - NEAR_REACH, leaves))
+    half = jax.ShapeDtypeStruct((probe_count, probes.shape[1] // 2), f32)
+    near_inner = pl.pallas_call(
+        functools.partial(near_kernel, groups=inner),
+        out_shape=half,
+        in_specs=scalars(1) + whole(4),
+        out_specs=pl.BlockSpec(memory_space=pltpu.VMEM),
+        scratch_shapes=near_scratch(items, probe_count, leaf_size),
+        compiler_params=params,
+        cost_estimate=cost(10_000_000_000),
+        name="near_inner",
+    )(items, points, probes, box, box)
+
+    near_outer, far_leaf = pl.pallas_call(
+        functools.partial(outer_kernel, groups=outer),
+        out_shape=(half, jax.ShapeDtypeStruct((leaves, probe_count, rank), f32)),
+        in_specs=scalars(3) + whole(7) + hbm(1),
+        out_specs=tuple(whole(2)),
+        scratch_shapes=near_scratch(items, probe_count, leaf_size)
+        + [
+            pltpu.VMEM(((2 * FAR_REACH + 1) * leaves + 2, 2 * probe_count, 2 * rank), bf16),
+            like(couple_leaf),
+            copy_semaphores(leaves // FAR_STEP),
         ],
-        compiler_params=params(20),
-        cost_estimate=cost(5_000_000_000),
-        name="far",
-    )(far_list, near_slots, before, middle, after, couple_leaf)
-
+        compiler_params=params,
+        cost_estimate=cost(15_000_000_000),
+        name="near_outer_far",
+    )(items, far_list, near_slots, points, probes, left, right, before, middle, after, couple_leaf)
+
+    gathered = pltpu.VMEM((4 * plane.shape[0],) + plane.shape[1:], f32)
+    held = (couple_box, couple_column, transfer_box, transfer_leaf, basis, far_leaf)
+    held += (near_inner, near_outer)
     return pl.pallas_call(
         down_kernel,
         out_shape=jax.ShapeDtypeStruct(probes.shape, f32),
-        in_specs=scalars(3) + whole(9),
+        in_specs=scalars(3) + hbm(12),
         out_specs=pl.BlockSpec(memory_space=pltpu.VMEM),
-        compiler_params=params(14),
+        scratch_shapes=[gathered] + [like(array) for array in held]
+        + [copy_semaphores(10 + 2 * CHUNKS)],
+        compiler_params=params,
         name="down",
-    )(
-        near_slots,
-        box_list,
-        column_list,
-        gathered,
-        couple_box,
-        couple_column,
-        transfer_box,
-        transfer_leaf,
-        basis,
-        far_leaf,
-        near_inner,
-        near_outer,
-    )
+    )(near_slots, box_list, column_list, *planes, *held)
 
 
 def solution(mesh):

time: 100 us -> 99.6 us (level)
  the two profiles are of different devices: /device:TPU:0 before, /device:TPU:4 now
where the time goes in v3:
time: 99.6 us; the launch traced here: 98.5 us
  Pallas kernels  55.5 us (56%)
  starting transfers between devices  28.7 us (29%)
  waiting for transfers between devices  8.24 us (8%)
  local copies, waits for them, and re-layouts  5.07 us (5%)
    pallas_call x1, Pallas kernels, per_device(): pl.pallas_call(functools.partial(outer_kernel, groups=outer), out_shape=(...  24.6 us
    ppermute x7, starting transfers between devices, shifted(): lax.ppermute(array, axis, [(i, (i + by) % devices) for i in range(devices)])  15.3 us
    ppermute x7, starting transfers between devices, moved_along(): lax.ppermute(array, 'leaf', [(i, target(i)) for i in range(lax.axis_size(...  13.4 us
    pallas_call x1, Pallas kernels, per_device(): pl.pallas_call(functools.partial(near_kernel, groups=inner), out_shape=ha...  13.1 us
    pallas_call x1, Pallas kernels, per_device(): pl.pallas_call(down_kernel, out_shape=jax.ShapeDtypeStruct(probes.shape,...  9.21 us
    pallas_call x1, Pallas kernels, per_device(): pl.pallas_call(skeleton_kernel, out_shape=(jax.ShapeDtypeStruct((2, block...  8.51 us
    ppermute x7, waiting for transfers between devices, moved_along(): lax.ppermute(array, 'leaf', [(i, target(i)) for i in range(lax.axis_size(...  6.23 us
    unnamed x24, local copies, waits for them, and re-layouts  3.05 us
  transfers between devices with their start and end apart: 14, of which 4 were waited for; matrix products, arithmetic and copies ran while one was open for 4% of the time, Pallas kernels for 38%

profile of v3, /device:TPU:4, one launch (start us, length us, event | category | flops | bytes accessed | tf_op | source)
XLA Modules:
  0.0 98.5 jit_solution(11524354852725726629)
XLA Ops:
  0.0 8.5 %skeletons.1 = (f32[2,34,16,128]{3,2,1,0:T(8,128)}, f32[1,16,128]{2,1,0:T(8,128)}, s32[9,32]{1,0:T(8,128)}) custom-call(s32[9,32]{1,0:T(8,128)} %bitcast.12, f32[2,8192]{1,0:T(2,128)} %points.5, f32[16,8192]{1,0:T(8,128)} %probes.3, f32[32,64,256]{2,1,0:T(8,128)} %bitcast.10, f32[32,64,64]{2,1,0:T(8,128)} %transfer_in.3, f32[1,64,64]{2,1,0:T(8,128)} %transfer_box_in.1), custom_call_target="tpu_custom_call" | custom-call | tf_op jit(solution)/shard_map/skeletons/pallas_call | solution.py:464
  8.5 4.1 %collective-permute-start = (f32[1,16,128]{2,1,0:T(8,128)}, f32[1,16,128]{2,1,0:T(8,128)S(1)}, u32[]{:S(2)}, u32[]{:S(2)}) collective-permute-start(f32[1,16,128]{2,1,0:T(8,128)} %get-tuple-element.10.left.right), channel_id=1, source_target_pairs={{0,3},{1,0},{2,1},{3,2},{4,7},{5,4},{6,5},{7,6},{8,11},{9,8},{10,9... | collective-permute-start | bytes 24584 | tf_op jit(solution)/shard_map/ppermute | solution.py:406
  12.6 0.0 collective-permute-start.2
  12.6 1.1 %slice_bitcast_fusion = (f32[34,16,128]{2,1,0:T(8,128)S(1)}, f32[34,16,128]{2,1,0:T(8,128)S(1)}) fusion(f32[2,34,16,128]{3,2,1,0:T(8,128)} %get-tuple-element.12), kind=kLoop, calls=%fused_computation.1 | loop fusion | bytes 1114112 | tf_op jit(solution)/shard_map/squeeze | solution.py:480
  13.7 4.6 %collective-permute-start.11 = (f32[34,16,128]{2,1,0:T(8,128)S(1)}, f32[34,16,128]{2,1,0:T(8,128)S(1)}, u32[]{:S(2)}, u32[]{:S(2)}) collective-permute-start(f32[34,16,128]{2,1,0:T(8,128)S(1)} %get-tuple-element.15), channel_id=1, source_target_pairs={{0,127},{1,0},{2,1},{3,2},{4,3},{5,4},{6,5},{7,6},{8,7},{9,8},{10,... | collective-permute-start | bytes 835592 | tf_op jit(solution)/shard_map/ppermute | solution.py:406
  18.3 0.0 collective-permute-start.10
  18.3 0.7 constant_dynamic-update-slice_fusion.4
  19.0 0.9 slice.18
  19.9 0.0 collective-permute-done
  19.9 1.7 %collective-permute-start.1 = (f32[1,16,128]{2,1,0:T(8,128)S(1)}, f32[1,16,128]{2,1,0:T(8,128)S(1)}, u32[]{:S(2)}, u32[]{:S(2)}) collective-permute-start(f32[1,16,128]{2,1,0:T(8,128)S(1)} %collective-permute-done), channel_id=1, source_target_pairs={{0,3},{1,0},{2,1},{3,2},{4,7},{5,4},{6,5},{7,6},{8,11},{9,8},{10,9... | collective-permute-start | bytes 24584 | tf_op jit(solution)/shard_map/ppermute | solution.py:406
  21.7 0.0 collective-permute-done.2
  21.7 2.0 %collective-permute-done.1 = f32[1,16,128]{2,1,0:T(8,128)S(1)} collective-permute-done((f32[1,16,128]{2,1,0:T(8,128)S(1)}, f32[1,16,128]{2,1,0:T(8,128)S(1)}, u32[]{:S(2)}, u32[]{:S(2)}) %collective-permute-start.1) | collective-permute-done | bytes 8224 | tf_op jit(solution)/shard_map/ppermute | solution.py:406
  23.7 0.7 pad_maximum_fusion.1
  24.4 0.1 collective-permute-start.3
  24.5 1.1 %collective-permute-done.3 = f32[4,16,128]{2,1,0:T(8,128)S(1)} collective-permute-done((f32[4,16,128]{2,1,0:T(8,128)S(1)}, f32[4,16,128]{2,1,0:T(8,128)S(1)}, u32[]{:S(2)}, u32[]{:S(2)}) %collective-permute-start.3) | collective-permute-done | bytes 32800 | tf_op jit(solution)/shard_map/ppermute | solution.py:440
  25.6 3.5 %collective-permute-start.4 = (f32[8,16,128]{2,1,0:T(8,128)S(1)}, f32[8,16,128]{2,1,0:T(8,128)S(1)}, u32[]{:S(2)}, u32[]{:S(2)}) collective-permute-start(f32[8,16,128]{2,1,0:T(8,128)S(1)} %get-tuple-element.17), channel_id=1, source_target_pairs={{0,24},{4,28},{8,0},{12,4},{16,8},{20,12},{24,16},{28,20},{32,56},... | collective-permute-start | bytes 196616 | tf_op jit(solution)/shard_map/ppermute | solution.py:440
  29.0 0.0 collective-permute-done.11.right
  29.0 0.0 copy-start.5
  29.1 0.0 collective-permute-done.10.left
  29.1 0.0 copy-start.6
  29.1 0.0 copy-start
  29.1 3.3 %collective-permute-start.12 = (f32[3,16,16,128]{3,2,1,0:T(8,128)S(1)}, f32[3,16,16,128]{3,2,1,0:T(8,128)S(1)}, u32[]{:S(2)}, u32[]{:S(2)}) collective-permute-start(f32[3,16,16,128]{3,2,1,0:T(8,128)S(1)} %pad_maximum_fusion.middle), channel_id=1, source_target_pairs={{0,3},{1,4},{2,5},{3,6},{4,7},{5,8},{6,9},{7,10},{8,11},{9,12},{10... | collective-permute-start | bytes 1179656 | tf_op jit(solution)/shard_map/ppermute | solution.py:406
  32.4 1.6 %collective-permute-start.13 = (f32[3,16,16,128]{3,2,1,0:T(8,128)S(1)}, f32[3,16,16,128]{3,2,1,0:T(8,128)S(1)}, u32[]{:S(2)}, u32[]{:S(2)}) collective-permute-start(f32[3,16,16,128]{3,2,1,0:T(8,128)S(1)} %pad_maximum_fusion.middle), channel_id=1, source_target_pairs={{0,125},{1,126},{2,127},{3,0},{4,1},{5,2},{6,3},{7,4},{8,5},{9,6},... | collective-permute-start | bytes 1179656 | tf_op jit(solution)/shard_map/ppermute | solution.py:406
  34.0 13.1 %near_inner.1.inner_in = f32[16,4096]{1,0:T(8,128)} custom-call(s32[9,32]{1,0:T(8,128)} %get-tuple-element.11.items, f32[2,8192]{1,0:T(2,128)} %points.5, f32[16,8192]{1,0:T(8,128)} %probes.3, f32[1,16,128]{2,1,0:T(8,128)} %get-tuple-element.10.left.right, f32[1,16,128]{2,1,0:T(8,128)} %get-tuple-element.10.left.right), custom_call_target="tpu_custom_call" | custom-call | flops 10000000000 | bytes 1048576 | tf_op jit(solution)/shard_map/near_inner/pallas_call | solution.py:494
  47.1 0.0 collective-permute-start.5
  47.1 1.3 %collective-permute-start.6 = (f32[8,16,128]{2,1,0:T(8,128)S(1)}, f32[8,16,128]{2,1,0:T(8,128)S(1)}, u32[]{:S(2)}, u32[]{:S(2)}) collective-permute-start(f32[8,16,128]{2,1,0:T(8,128)S(1)} %get-tuple-element.17), channel_id=1, source_target_pairs={{0,8},{4,12},{8,16},{12,20},{16,24},{20,28},{24,0},{28,4},{32,40},... | collective-permute-start | bytes 196616 | tf_op jit(solution)/shard_map/ppermute | solution.py:440
  48.4 0.0 collective-permute-done.4
  48.4 4.7 %collective-permute-done.5 = f32[8,16,128]{2,1,0:T(8,128)S(1)} collective-permute-done((f32[8,16,128]{2,1,0:T(8,128)S(1)}, f32[8,16,128]{2,1,0:T(8,128)S(1)}, u32[]{:S(2)}, u32[]{:S(2)}) %collective-permute-start.5) | collective-permute-done | bytes 65568 | tf_op jit(solution)/shard_map/ppermute | solution.py:440
  53.1 0.4 collective-permute-done.6
  53.6 0.0 copy-start.1
  53.6 1.9 %collective-permute-start.7 = (f32[32,16,128]{2,1,0:T(8,128)S(1)}, f32[32,16,128]{2,1,0:T(8,128)S(1)}, u32[]{:S(2)}, u32[]{:S(2)}) collective-permute-start(f32[32,16,128]{2,1,0:T(8,128)S(1)} %constant_dynamic-update-slice_fusion.5.boxes0), channel_id=1, source_target_pairs={{0,96},{4,100},{8,104},{12,108},{16,112},{20,116},{24,120},{28,124... | collective-permute-start | bytes 786440 | tf_op jit(solution)/shard_map/ppermute | solution.py:440
  55.4 4.1 %collective-permute-start.8 = (f32[32,16,128]{2,1,0:T(8,128)S(1)}, f32[32,16,128]{2,1,0:T(8,128)S(1)}, u32[]{:S(2)}, u32[]{:S(2)}) collective-permute-start(f32[32,16,128]{2,1,0:T(8,128)S(1)} %constant_dynamic-update-slice_fusion.5.boxes0), channel_id=1, source_target_pairs={{0,64},{4,68},{8,72},{12,76},{16,80},{20,84},{24,88},{28,92},{32,9... | collective-permute-start | bytes 786440 | tf_op jit(solution)/shard_map/ppermute | solution.py:440
  59.6 2.5 %collective-permute-start.9 = (f32[32,16,128]{2,1,0:T(8,128)S(1)}, f32[32,16,128]{2,1,0:T(8,128)S(1)}, u32[]{:S(2)}, u32[]{:S(2)}) collective-permute-start(f32[32,16,128]{2,1,0:T(8,128)S(1)} %constant_dynamic-update-slice_fusion.5.boxes0), channel_id=1, source_target_pairs={{0,32},{4,36},{8,40},{12,44},{16,48},{20,52},{24,56},{28,60},{32,6... | collective-permute-start | bytes 786440 | tf_op jit(solution)/shard_map/ppermute | solution.py:440
  62.1 0.0 collective-permute-done.12.before
  62.1 0.0 copy-start.7
  62.1 0.0 collective-permute-done.13.after
  62.1 0.0 copy-done.5
  62.1 0.0 copy-done.6
  62.1 0.0 copy-done
  62.1 0.7 copy-done.7
  62.8 0.0 copy-start.8
  62.8 0.8 copy-done.8
  63.6 24.6 %near_outer_far.1 = (f32[16,4096]{1,0:T(8,128)}, f32[32,16,64]{2,1,0:T(8,128)}) custom-call(s32[9,32]{1,0:T(8,128)} %get-tuple-element.11.items, s32[32,27]{1,0:T(8,128)} %far.1, s32[9,32]{1,0:T(8,128)} %bitcast.13, f32[2,8192]{1,0:T(2,128)} %points.5, f32[16,8192]{1,0:T(8,128)} %probes.3, f32[34,16,128]{2,1,0:T(8,128)} %copy-done.6, ...), custom_call_target="tpu_custom_call" | custom-call | flops 15000000512 | bytes 1048576 | tf_op jit(solution)/shard_map/near_outer_far/pallas_call | solution.py:505
  88.3 0.0 collective-permute-done.7.boxes1
  88.3 0.0 copy-start.2
  88.3 0.0 collective-permute-done.8.boxes2
  88.3 0.0 copy-start.3
  88.3 0.0 collective-permute-done.9.boxes3
  88.3 0.0 copy-start.4
  88.3 0.0 copy-done.1
  88.3 0.6 copy-done.2
  89.0 0.1 copy-done.3
  89.1 0.1 copy-done.4
  89.2 9.2 %down.1 = f32[16,8192]{1,0:T(8,128)} custom-call(s32[9,32]{1,0:T(8,128)} %bitcast.14, s32[1,27]{1,0:T(1,128)} %box_list.1, s32[1,4]{1,0:T(1,128)} %column_list.1, f32[32,16,128]{2,1,0:T(8,128)} %copy-done.1, f32[32,16,128]{2,1,0:T(8,128)} %copy-done.2, f32[32,16,128]{2,1,0:T(8,128)} %copy-done.3, f32[32,16,128]{2,1,0:T(8,128)} %copy-done.4, ...), custom_call_target="tpu_custom_call" | custom-call | tf_op jit(solution)/shard_map/down/pallas_call | solution.py:524
  (10 shorter events, 0.1 us)
Async XLA Ops:
  8.5 11.4 %collective-permute-start = (f32[1,16,128]{2,1,0:T(8,128)}, f32[1,16,128]{2,1,0:T(8,128)S(1)}, u32[]{:S(2)}, u32[]{:S(2)}) collective-permute-start(f32[1,16,128]{2,1,0:T(8,128)} %get-tuple-element.10.left.right), channel_id=1, source_target_pairs={{0,3},{1,0},{2,1},{3,2},{4,7},{5,4},{6,5},{7,6},{8,11},{9,8},{10,9... | collective-permute-start | bytes 24584 | tf_op jit(solution)/shard_map/ppermute | solution.py:406
  12.6 9.1 %collective-permute-start.2 = (f32[1,16,128]{2,1,0:T(8,128)}, f32[1,16,128]{2,1,0:T(8,128)S(1)}, u32[]{:S(2)}, u32[]{:S(2)}) collective-permute-start(f32[1,16,128]{2,1,0:T(8,128)} %get-tuple-element.10.left.right), channel_id=1, source_target_pairs={{0,1},{1,2},{2,3},{3,0},{4,5},{5,6},{6,7},{7,4},{8,9},{9,10},{10,1... | collective-permute-start | bytes 24584 | tf_op jit(solution)/shard_map/ppermute | solution.py:406
  13.7 15.3 %collective-permute-start.11 = (f32[34,16,128]{2,1,0:T(8,128)S(1)}, f32[34,16,128]{2,1,0:T(8,128)S(1)}, u32[]{:S(2)}, u32[]{:S(2)}) collective-permute-start(f32[34,16,128]{2,1,0:T(8,128)S(1)} %get-tuple-element.15), channel_id=1, source_target_pairs={{0,127},{1,0},{2,1},{3,2},{4,3},{5,4},{6,5},{7,6},{8,7},{9,8},{10,... | collective-permute-start | bytes 835592 | tf_op jit(solution)/shard_map/ppermute | solution.py:406
  18.3 10.7 %collective-permute-start.10 = (f32[34,16,128]{2,1,0:T(8,128)S(1)}, f32[34,16,128]{2,1,0:T(8,128)S(1)}, u32[]{:S(2)}, u32[]{:S(2)}) collective-permute-start(f32[34,16,128]{2,1,0:T(8,128)S(1)} %get-tuple-element.16), channel_id=1, source_target_pairs={{0,1},{1,2},{2,3},{3,4},{4,5},{5,6},{6,7},{7,8},{8,9},{9,10},{10,1... | collective-permute-start | bytes 835592 | tf_op jit(solution)/shard_map/ppermute | solution.py:406
  19.9 3.7 %collective-permute-start.1 = (f32[1,16,128]{2,1,0:T(8,128)S(1)}, f32[1,16,128]{2,1,0:T(8,128)S(1)}, u32[]{:S(2)}, u32[]{:S(2)}) collective-permute-start(f32[1,16,128]{2,1,0:T(8,128)S(1)} %collective-permute-done), channel_id=1, source_target_pairs={{0,3},{1,0},{2,1},{3,2},{4,7},{5,4},{6,5},{7,6},{8,11},{9,8},{10,9... | collective-permute-start | bytes 24584 | tf_op jit(solution)/shard_map/ppermute | solution.py:406
  24.4 1.2 %collective-permute-start.3 = (f32[4,16,128]{2,1,0:T(8,128)S(1)}, f32[4,16,128]{2,1,0:T(8,128)S(1)}, u32[]{:S(2)}, u32[]{:S(2)}) collective-permute-start(f32[4,16,128]{2,1,0:T(8,128)S(1)} %pad_maximum_fusion.1), channel_id=1, source_target_pairs={{0,4},{4,0},{8,12},{12,8},{16,20},{20,16},{24,28},{28,24},{32,36},... | collective-permute-start | bytes 98312 | tf_op jit(solution)/shard_map/ppermute | solution.py:440
  25.6 22.8 %collective-permute-start.4 = (f32[8,16,128]{2,1,0:T(8,128)S(1)}, f32[8,16,128]{2,1,0:T(8,128)S(1)}, u32[]{:S(2)}, u32[]{:S(2)}) collective-permute-start(f32[8,16,128]{2,1,0:T(8,128)S(1)} %get-tuple-element.17), channel_id=1, source_target_pairs={{0,24},{4,28},{8,0},{12,4},{16,8},{20,12},{24,16},{28,20},{32,56},... | collective-permute-start | bytes 196616 | tf_op jit(solution)/shard_map/ppermute | solution.py:440
  29.0 33.1 %copy-start.5 = (f32[34,16,128]{2,1,0:T(8,128)}, f32[34,16,128]{2,1,0:T(8,128)S(1)}, u32[]{:S(2)}) copy-start(f32[34,16,128]{2,1,0:T(8,128)S(1)} %collective-permute-done.11.right) | copy-start | bytes 835588
  29.1 33.0 %copy-start.6 = (f32[34,16,128]{2,1,0:T(8,128)}, f32[34,16,128]{2,1,0:T(8,128)S(1)}, u32[]{:S(2)}) copy-start(f32[34,16,128]{2,1,0:T(8,128)S(1)} %collective-permute-done.10.left) | copy-start | bytes 835588
  29.1 33.0 %copy-start = (f32[3,16,16,128]{3,2,1,0:T(8,128)}, f32[3,16,16,128]{3,2,1,0:T(8,128)S(1)}, u32[]{:S(2)}) copy-start(f32[3,16,16,128]{3,2,1,0:T(8,128)S(1)} %pad_maximum_fusion.middle) | copy-start | bytes 1179652
  29.1 32.9 %collective-permute-start.12 = (f32[3,16,16,128]{3,2,1,0:T(8,128)S(1)}, f32[3,16,16,128]{3,2,1,0:T(8,128)S(1)}, u32[]{:S(2)}, u32[]{:S(2)}) collective-permute-start(f32[3,16,16,128]{3,2,1,0:T(8,128)S(1)} %pad_maximum_fusion.middle), channel_id=1, source_target_pairs={{0,3},{1,4},{2,5},{3,6},{4,7},{5,8},{6,9},{7,10},{8,11},{9,12},{10... | collective-permute-start | bytes 1179656 | tf_op jit(solution)/shard_map/ppermute | solution.py:406
  32.4 29.7 %collective-permute-start.13 = (f32[3,16,16,128]{3,2,1,0:T(8,128)S(1)}, f32[3,16,16,128]{3,2,1,0:T(8,128)S(1)}, u32[]{:S(2)}, u32[]{:S(2)}) collective-permute-start(f32[3,16,16,128]{3,2,1,0:T(8,128)S(1)} %pad_maximum_fusion.middle), channel_id=1, source_target_pairs={{0,125},{1,126},{2,127},{3,0},{4,1},{5,2},{6,3},{7,4},{8,5},{9,6},... | collective-permute-start | bytes 1179656 | tf_op jit(solution)/shard_map/ppermute | solution.py:406
  47.1 6.0 %collective-permute-start.5 = (f32[8,16,128]{2,1,0:T(8,128)S(1)}, f32[8,16,128]{2,1,0:T(8,128)S(1)}, u32[]{:S(2)}, u32[]{:S(2)}) collective-permute-start(f32[8,16,128]{2,1,0:T(8,128)S(1)} %get-tuple-element.17), channel_id=1, source_target_pairs={{0,16},{4,20},{8,24},{12,28},{16,0},{20,4},{24,8},{28,12},{32,48},... | collective-permute-start | bytes 196616 | tf_op jit(solution)/shard_map/ppermute | solution.py:440
  47.1 6.4 %collective-permute-start.6 = (f32[8,16,128]{2,1,0:T(8,128)S(1)}, f32[8,16,128]{2,1,0:T(8,128)S(1)}, u32[]{:S(2)}, u32[]{:S(2)}) collective-permute-start(f32[8,16,128]{2,1,0:T(8,128)S(1)} %get-tuple-element.17), channel_id=1, source_target_pairs={{0,8},{4,12},{8,16},{12,20},{16,24},{20,28},{24,0},{28,4},{32,40},... | collective-permute-start | bytes 196616 | tf_op jit(solution)/shard_map/ppermute | solution.py:440
  53.6 34.8 %copy-start.1 = (f32[32,16,128]{2,1,0:T(8,128)}, f32[32,16,128]{2,1,0:T(8,128)S(1)}, u32[]{:S(2)}) copy-start(f32[32,16,128]{2,1,0:T(8,128)S(1)} %constant_dynamic-update-slice_fusion.5.boxes0) | copy-start | bytes 786436
  53.6 34.7 %collective-permute-start.7 = (f32[32,16,128]{2,1,0:T(8,128)S(1)}, f32[32,16,128]{2,1,0:T(8,128)S(1)}, u32[]{:S(2)}, u32[]{:S(2)}) collective-permute-start(f32[32,16,128]{2,1,0:T(8,128)S(1)} %constant_dynamic-update-slice_fusion.5.boxes0), channel_id=1, source_target_pairs={{0,96},{4,100},{8,104},{12,108},{16,112},{20,116},{24,120},{28,124... | collective-permute-start | bytes 786440 | tf_op jit(solution)/shard_map/ppermute | solution.py:440
  55.4 32.9 %collective-permute-start.8 = (f32[32,16,128]{2,1,0:T(8,128)S(1)}, f32[32,16,128]{2,1,0:T(8,128)S(1)}, u32[]{:S(2)}, u32[]{:S(2)}) collective-permute-start(f32[32,16,128]{2,1,0:T(8,128)S(1)} %constant_dynamic-update-slice_fusion.5.boxes0), channel_id=1, source_target_pairs={{0,64},{4,68},{8,72},{12,76},{16,80},{20,84},{24,88},{28,92},{32,9... | collective-permute-start | bytes 786440 | tf_op jit(solution)/shard_map/ppermute | solution.py:440
  59.6 28.7 %collective-permute-start.9 = (f32[32,16,128]{2,1,0:T(8,128)S(1)}, f32[32,16,128]{2,1,0:T(8,128)S(1)}, u32[]{:S(2)}, u32[]{:S(2)}) collective-permute-start(f32[32,16,128]{2,1,0:T(8,128)S(1)} %constant_dynamic-update-slice_fusion.5.boxes0), channel_id=1, source_target_pairs={{0,32},{4,36},{8,40},{12,44},{16,48},{20,52},{24,56},{28,60},{32,6... | collective-permute-start | bytes 786440 | tf_op jit(solution)/shard_map/ppermute | solution.py:440
  62.1 0.7 copy-start.7
  62.8 0.8 copy-start.8
  88.3 0.7 copy-start.2
  88.3 0.8 copy-start.3
  88.3 0.9 copy-start.4

commit v4 on v3

--- a/solution.py
+++ b/solution.py
@@ -12,7 +12,7 @@
 FAR_REACH = 4
 FEATURES = 16
 GROUP = 12
-FAR_STEP = 2
+FAR_STEP = 4
 CHUNKS = 4
 
 matern_rate = math.sqrt(3.0) / 0.1
@@ -68,7 +68,7 @@
 
 
 def skeleton_kernel(
-    near, points, probes_in, basis_in, transfer_in, transfer_box, out, box_out, items,
+    near, points, probes_in, basis_in, transfer_in, transfer_box, out, out_first, box_out, items,
     probes, basis, transfer_leaf, semaphores,
 ):
     leaves, rank, leaf_size = basis.shape
@@ -95,28 +95,40 @@
     arriving[0].wait()
     width = probes.shape[1]
     edge = NEAR_REACH * leaf_size
-    for side, start in ((0, width - edge), (1, 0)):
+    for side, start in ((out, width - edge), (out_first, 0)):
         for j in range(edge // 128):
             lanes = slice(start + j * 128, start + (j + 1) * 128)
-            out[side, pairs + j] = probes[:, lanes]
-            out[side, pairs + edge // 128, j : j + 1, :] = points[0:1, lanes]
-            out[side, pairs + edge // 128 + 1, j : j + 1, :] = points[1:2, lanes]
-
-    def leaf_skeleton(c):
-        both = stacked_halves(probes[:, c * leaf_size : (c + 1) * leaf_size])
-        weights = stacked_halves(basis[c])
-        wide = contract(both, weights, ((1,), (1,)))
+            side[pairs + j] = probes[:, lanes]
+            side[pairs + edge // 128, j : j + 1, :] = points[0:1, lanes]
+            side[pairs + edge // 128 + 1, j : j + 1, :] = points[1:2, lanes]
+
+    def leaf_probes(c):
+        return stacked_halves(probes[:, c * leaf_size : (c + 1) * leaf_size])
+
+    def summed(wide):
         return wide[:16] + wide[16:] + exchanged(wide[:16])
 
-    box = jnp.zeros((16, rank), f32)
+    skeletons = []
     for m in range(pairs):
         if m % (pairs // CHUNKS) == 0:
             arriving[1 + m // (pairs // CHUNKS)].wait()
-            arriving[1 + CHUNKS + m // (pairs // CHUNKS)].wait()
-        pair = jnp.where(low_lanes, leaf_skeleton(2 * m), exchanged(leaf_skeleton(2 * m + 1)))
-        out[0, m] = pair
-        out[1, m] = pair
-        box += product3(pair, transfer_leaf[2 * m : 2 * m + 2].reshape(2 * rank, rank))
+        left = jnp.concatenate([leaf_probes(2 * m), leaf_probes(2 * m + 1)], axis=0)
+        right = jnp.concatenate([stacked_halves(basis[2 * m]), stacked_halves(basis[2 * m + 1])], axis=0)
+        wide = contract(left, right, ((1,), (1,)))
+        even, odd = summed(wide[:32, : 2 * rank]), summed(wide[32:, 2 * rank :])
+        pair = jnp.where(low_lanes, even, exchanged(odd))
+        out[m] = pair
+        out_first[m] = pair
+        skeletons.append(pair)
+    for copy in arriving[1 + CHUNKS :]:
+        copy.wait()
+    high, low = halves(transfer_leaf[...].reshape(leaves * rank, rank))
+    wide = jnp.dot(
+        stacked_halves(jnp.concatenate(skeletons, axis=1)),
+        jnp.concatenate([high, low], axis=1),
+        preferred_element_type=f32,
+    )
+    box = summed(wide)[:, :rank]
     box_out[0] = jnp.concatenate([box, product3(box, transfer_box[0])], axis=1)
 
 
@@ -259,9 +271,16 @@
     return wide[:16, :rank] + wide[16:, :rank] + wide[:16, rank:]
 
 
-def outer_kernel(
-    items, far, near, points, probes, left, right, before, middle, after, couples_in,
-    out, far_out, values, source, target, total, listed, table, couples, semaphores, *, groups
+def inner_kernel(
+    items, points, probes, bundle, column, out, skeletons_out, column_out, *scratch, groups
+):
+    skeletons_out[...] = bundle[: skeletons_out.shape[0]]
+    column_out[...] = column[...]
+    near_kernel(items, points, probes, bundle, bundle, out, *scratch, groups=groups)
+
+
+def far_kernel(
+    far, near, before, middle, after, couples_in, out, table, couples, semaphores
 ):
     leaves, slots, rank, _ = couples.shape
     steps = leaves // FAR_STEP
@@ -275,10 +294,6 @@
         return carry
 
     lax.fori_loop(0, steps, start, 0)
-    near_kernel(
-        items, points, probes, left, right, out, values, source, target, total, listed, groups=groups
-    )
-
     empty = (2 * FAR_REACH + 1) * leaves
     low_lanes = lax.broadcasted_iota(jnp.int32, (32, 2 * rank), 1) < rank
     for b in range(3):
@@ -288,17 +303,20 @@
     table[empty + 1] = jnp.zeros_like(table[empty])
     base = near[0, 0] - FAR_REACH * leaves
 
+    def far_leaf(c):
+        def picks(start, count):
+            rows = [far[c, k] if k < slots else -1 for k in range(start, start + count)]
+            rows = [jnp.where(row >= 0, row - base, empty) for row in rows]
+            return picked(table, rows, low_lanes)
+
+        return coupled_pairs(picks, couples.at[c])
+
     def far_step(step, carry):
         arriving(step).wait()
-        for u in range(FAR_STEP):
+        for u in range(0, FAR_STEP, 2):
             c = step * FAR_STEP + u
-
-            def picks(start, count):
-                rows = [far[c, k] if k < slots else -1 for k in range(start, start + count)]
-                rows = [jnp.where(row >= 0, row - base, empty) for row in rows]
-                return picked(table, rows, low_lanes)
-
-            far_out[c] = coupled_pairs(picks, couples.at[c])
+            pair = jnp.concatenate([far_leaf(c), far_leaf(c + 1)], axis=1)
+            out[(step * FAR_STEP + u) // 2] = pair
         return carry
 
     lax.fori_loop(0, steps, far_step, 0)
@@ -371,19 +389,34 @@
     far_column = coupled(jnp.concatenate(pieces, axis=1), couple_column[0])
     down_box = far_box + product3(far_column, transfer_box[0], ((1,), (1,)))
 
-    for copy in arriving[7:10]:
+    for copy in arriving[7 : 10 + CHUNKS]:
         copy.wait()
-    for c in range(leaves):
-        if c % (leaves // CHUNKS) == 0:
-            arriving[10 + c // (leaves // CHUNKS)].wait()
-            arriving[10 + CHUNKS + c // (leaves // CHUNKS)].wait()
-        down = far_leaf[c] + product3(down_box, transfer_leaf[c], ((1,), (1,)))
-        lanes = slice(c * leaf_size, (c + 1) * leaf_size)
-        inner = NEAR_REACH <= c < leaves - NEAR_REACH
-        place = c - NEAR_REACH if inner else c if c < NEAR_REACH else c - leaves + 2 * NEAR_REACH
-        held = near_inner if inner else near_outer
-        near_value = held[:, place * leaf_size : (place + 1) * leaf_size]
-        out[:, lanes] = near_value + product3(down, basis[c])
+    high, low = halves(transfer_leaf[...].reshape(leaves * rank, rank))
+    both = stacked_halves(down_box)
+    wide = contract(both, high, ((1,), (1,)))
+    from_box = wide[:16] + wide[16:] + contract(both[:16], low, ((1,), (1,)))
+
+    lane = lax.broadcasted_iota(jnp.int32, (16, 4 * rank), 1)
+    for m in range(leaves // 4):
+        if m % (leaves // 4 // CHUNKS) == 0:
+            arriving[10 + CHUNKS + m // (leaves // 4 // CHUNKS)].wait()
+        down = from_box[:, m * 4 * rank : (m + 1) * 4 * rank]
+        down = down + jnp.concatenate([far_leaf[2 * m], far_leaf[2 * m + 1]], axis=1)
+        own_rows = [
+            jnp.where((lane >= j * rank) & (lane < (j + 1) * rank), down, 0.0) for j in range(4)
+        ]
+        left = stacked_halves(jnp.concatenate(own_rows, axis=0))
+        high, low = halves(basis[4 * m : 4 * m + 4].reshape(4 * rank, leaf_size))
+        wide = jnp.dot(left, high, preferred_element_type=f32)
+        rest = jnp.dot(left[:64], low, preferred_element_type=f32)
+        result = wide[:64] + wide[64:] + rest
+        for j in range(4):
+            c = 4 * m + j
+            inner = NEAR_REACH <= c < leaves - NEAR_REACH
+            place = c - NEAR_REACH if inner else c if c < NEAR_REACH else c - leaves + 2 * NEAR_REACH
+            held = near_inner if inner else near_outer
+            near_value = held[:, place * leaf_size : (place + 1) * leaf_size]
+            out[:, c * leaf_size : (c + 1) * leaf_size] = near_value + result[16 * j : 16 * j + 16]
 
 
 def whole(count):
@@ -461,62 +494,76 @@
     pairs = leaves // 2
     blocks = pairs + NEAR_REACH * leaf_size // 128 + 2
 
-    bundles, box, items = pl.pallas_call(
+    edges = jax.ShapeDtypeStruct((blocks, probe_count, 2 * rank), f32)
+    bundle_last, bundle_first, box, items = pl.pallas_call(
         skeleton_kernel,
         out_shape=(
-            jax.ShapeDtypeStruct((2, blocks, probe_count, 2 * rank), f32),
+            edges,
+            edges,
             jax.ShapeDtypeStruct((1, probe_count, 2 * rank), f32),
             jax.ShapeDtypeStruct(near_slots.shape, jnp.int32),
         ),
         in_specs=whole(2) + hbm(3) + whole(1),
-        out_specs=tuple(whole(3)),
+        out_specs=tuple(whole(4)),
         scratch_shapes=[like(probes), like(basis), like(transfer_leaf)]
         + [copy_semaphores(1 + 2 * CHUNKS)],
         compiler_params=params,
         name="skeletons",
     )(near_slots, points, probes, basis, transfer_leaf, transfer_box)
 
-    box_next, box_last = shifted(box, "sub", -1), shifted(box, "sub", 1)
-    left, right = shifted(bundles[0], ring, 1), shifted(bundles[1], ring, -1)
-    box_second = shifted(box_next, "sub", -1)
-    column = jnp.concatenate([box, box_next, box_second, box_last])
-    both = jnp.concatenate([column, moved_along(column, 0, 1, 1)])
-    along_y = [both] + [moved_along(both, 1, 2, by) for by in (1, 2, 3)]
-    plane = jnp.concatenate(along_y)
-    planes = [plane] + [moved_along(plane, 3, 2, by) for by in (1, 2, 3)]
-
-    middle = jnp.stack([left[:pairs], bundles[0, :pairs], right[:pairs]])
-    before, after = shifted(middle, ring, 3), shifted(middle, ring, -3)
+    column = jnp.concatenate([box] + [shifted(box, "sub", -by) for by in (1, 2, 3)])
+    left, right = shifted(bundle_last, ring, 1), shifted(bundle_first, ring, -1)
+    other_core = moved_along(column, 0, 1, 1)
 
     inner = ((NEAR_REACH, leaves - NEAR_REACH),)
     outer = ((0, NEAR_REACH), (leaves - NEAR_REACH, leaves))
     half = jax.ShapeDtypeStruct((probe_count, probes.shape[1] // 2), f32)
-    near_inner = pl.pallas_call(
-        functools.partial(near_kernel, groups=inner),
+    near_inner, skeletons, column = pl.pallas_call(
+        functools.partial(inner_kernel, groups=inner),
+        out_shape=(
+            half,
+            jax.ShapeDtypeStruct((pairs, probe_count, 2 * rank), f32),
+            jax.ShapeDtypeStruct(column.shape, f32),
+        ),
+        in_specs=scalars(1) + whole(4),
+        out_specs=tuple(whole(3)),
+        scratch_shapes=near_scratch(items, probe_count, leaf_size),
+        compiler_params=params,
+        cost_estimate=cost(10_000_000_000),
+        name="near_inner",
+    )(items, points, probes, bundle_last, column)
+
+    both = jnp.concatenate([column, other_core])
+    middle = jnp.stack([left[:pairs], skeletons, right[:pairs]])
+    plane = jnp.concatenate([both] + [moved_along(both, 1, 2, by) for by in (1, 2, 3)])
+    before, after = shifted(middle, ring, 3), shifted(middle, ring, -3)
+    planes = [plane] + [moved_along(plane, 3, 2, by) for by in (1, 2, 3)]
+
+    near_outer = pl.pallas_call(
+        functools.partial(near_kernel, groups=outer),
         out_shape=half,
         in_specs=scalars(1) + whole(4),
         out_specs=pl.BlockSpec(memory_space=pltpu.VMEM),
         scratch_shapes=near_scratch(items, probe_count, leaf_size),
         compiler_params=params,
         cost_estimate=cost(10_000_000_000),
-        name="near_inner",
-    )(items, points, probes, box, box)
-
-    near_outer, far_leaf = pl.pallas_call(
-        functools.partial(outer_kernel, groups=outer),
-        out_shape=(half, jax.ShapeDtypeStruct((leaves, probe_count, rank), f32)),
-        in_specs=scalars(3) + whole(7) + hbm(1),
-        out_specs=tuple(whole(2)),
-        scratch_shapes=near_scratch(items, probe_count, leaf_size)
-        + [
+        name="near_outer",
+    )(items, points, probes, left, right)
+
+    far_leaf = pl.pallas_call(
+        far_kernel,
+        out_shape=jax.ShapeDtypeStruct((pairs, probe_count, 2 * rank), f32),
+        in_specs=scalars(2) + whole(3) + hbm(1),
+        out_specs=pl.BlockSpec(memory_space=pltpu.VMEM),
+        scratch_shapes=[
             pltpu.VMEM(((2 * FAR_REACH + 1) * leaves + 2, 2 * probe_count, 2 * rank), bf16),
             like(couple_leaf),
             copy_semaphores(leaves // FAR_STEP),
         ],
         compiler_params=params,
-        cost_estimate=cost(15_000_000_000),
-        name="near_outer_far",
-    )(items, far_list, near_slots, points, probes, left, right, before, middle, after, couple_leaf)
+        cost_estimate=cost(8_000_000_000),
+        name="far",
+    )(far_list, near_slots, before, middle, after, couple_leaf)
 
     gathered = pltpu.VMEM((4 * plane.shape[0],) + plane.shape[1:], f32)
     held = (couple_box, couple_column, transfer_box, transfer_leaf, basis, far_leaf)

time: 99.6 us -> 93.2 us (0.936)
  the two profiles are of different devices: /device:TPU:4 before, /device:TPU:0 now
where the time goes in v4:
time: 93.2 us; the launch traced here: 92.6 us
  Pallas kernels  52 us (56%)
  starting transfers between devices  25.4 us (27%)
  waiting for transfers between devices  9.54 us (10%)
  local copies, waits for them, and re-layouts  4.4 us (5%)
  other arithmetic  1.08 us (1%)
    ppermute x7, starting transfers between devices, shifted(): lax.ppermute(array, axis, [(i, (i + by) % devices) for i in range(devices)])  18.7 us
    pallas_call x1, Pallas kernels, per_device(): pl.pallas_call(functools.partial(near_kernel, groups=outer), out_shape=ha...  15.1 us
    pallas_call x1, Pallas kernels, per_device(): pl.pallas_call(functools.partial(inner_kernel, groups=inner), out_shape=(...  14.8 us
    pallas_call x1, Pallas kernels, per_device(): pl.pallas_call(far_kernel, out_shape=jax.ShapeDtypeStruct((pairs, probe_c...  11.9 us
    ppermute x7, starting transfers between devices, moved_along(): lax.ppermute(array, 'leaf', [(i, target(i)) for i in range(lax.axis_size(...  6.77 us
    ppermute x7, waiting for transfers between devices, moved_along(): lax.ppermute(array, 'leaf', [(i, target(i)) for i in range(lax.axis_size(...  6.16 us
    pallas_call x1, Pallas kernels, per_device(): pl.pallas_call(down_kernel, out_shape=jax.ShapeDtypeStruct(probes.shape,...  5.11 us
    pallas_call x1, Pallas kernels, per_device(): pl.pallas_call(skeleton_kernel, out_shape=(edges, edges, jax.ShapeDtypeSt...  5.02 us
  transfers between devices with their start and end apart: 14, of which 3 were waited for; matrix products, arithmetic and copies ran while one was open for 3% of the time, Pallas kernels for 45%

profile of v4, /device:TPU:0, one launch (start us, length us, event | category | flops | bytes accessed | tf_op | source)
XLA Modules:
  0.0 92.6 jit_solution(9278815390028974589)
XLA Ops:
  0.0 5.0 %skeletons.1 = (f32[34,16,128]{2,1,0:T(8,128)}, f32[34,16,128]{2,1,0:T(8,128)}, f32[1,16,128]{2,1,0:T(8,128)}, s32[9,32]{1,0:T(8,128)}) custom-call(s32[9,32]{1,0:T(8,128)} %bitcast.10, f32[2,8192]{1,0:T(2,128)} %points.5, f32[16,8192]{1,0:T(8,128)} %probes.3, f32[32,64,256]{2,1,0:T(8,128)} %bitcast.7, f32[32,64,64]{2,1,0:T(8,128)} %transfer_in.3, ...), custom_call_target="tpu_custom_call" | custom-call | tf_op jit(solution)/shard_map/skeletons/pallas_call | solution.py:498
  5.0 0.0 copy-start.11
  5.0 0.0 copy-start.10
  5.0 4.2 %collective-permute-start = (f32[1,16,128]{2,1,0:T(8,128)}, f32[1,16,128]{2,1,0:T(8,128)S(1)}, u32[]{:S(2)}, u32[]{:S(2)}) collective-permute-start(f32[1,16,128]{2,1,0:T(8,128)} %get-tuple-element.14), channel_id=1, source_target_pairs={{0,3},{1,0},{2,1},{3,2},{4,7},{5,4},{6,5},{7,6},{8,11},{9,8},{10,9... | collective-permute-start | bytes 24584 | tf_op jit(solution)/shard_map/ppermute | solution.py:439
  9.2 0.0 collective-permute-start.1
  9.2 1.3 %collective-permute-start.2 = (f32[1,16,128]{2,1,0:T(8,128)}, f32[1,16,128]{2,1,0:T(8,128)S(1)}, u32[]{:S(2)}, u32[]{:S(2)}) collective-permute-start(f32[1,16,128]{2,1,0:T(8,128)} %get-tuple-element.14), channel_id=1, source_target_pairs={{0,1},{1,2},{2,3},{3,0},{4,5},{5,6},{6,7},{7,4},{8,9},{9,10},{10,1... | collective-permute-start | bytes 24584 | tf_op jit(solution)/shard_map/ppermute | solution.py:439
  10.5 0.7 constant_dynamic-update-slice_fusion.3
  11.2 0.0 collective-permute-done
  11.2 3.4 %collective-permute-done.1 = f32[1,16,128]{2,1,0:T(8,128)S(1)} collective-permute-done((f32[1,16,128]{2,1,0:T(8,128)}, f32[1,16,128]{2,1,0:T(8,128)S(1)}, u32[]{:S(2)}, u32[]{:S(2)}) %collective-permute-start.1) | collective-permute-done | bytes 8224 | tf_op jit(solution)/shard_map/ppermute | solution.py:439
  14.6 0.0 collective-permute-done.2
  14.6 0.0 copy-start.9
  14.6 0.1 collective-permute-start.3
  14.7 0.5 copy-done.9
  15.2 14.8 %near_inner.1 = (f32[16,4096]{1,0:T(8,128)}, f32[16,16,128]{2,1,0:T(8,128)}, f32[4,16,128]{2,1,0:T(8,128)}) custom-call(s32[9,32]{1,0:T(8,128)} %get-tuple-element.12.items, f32[2,8192]{1,0:T(2,128)} %points.5, f32[16,8192]{1,0:T(8,128)} %probes.3, f32[34,16,128]{2,1,0:T(8,128)} %get-tuple-element.13.bundle, f32[4,16,128]{2,1,0:T(8,128)} %copy-done.9), custom_call_target="tpu_custom_call" | custom-call | flops 10000000000 | bytes 1048576 | tf_op jit(solution)/shard_map/near_inner/pallas_call | solution.py:521
  30.0 0.8 constant_dynamic-update-slice_fusion.5
  30.7 0.0 collective-permute-done.3
  30.7 4.6 %collective-permute-start.4 = (f32[8,16,128]{2,1,0:T(8,128)S(1)}, f32[8,16,128]{2,1,0:T(8,128)S(1)}, u32[]{:S(2)}, u32[]{:S(2)}) collective-permute-start(f32[8,16,128]{2,1,0:T(8,128)S(1)} %get-tuple-element.19), channel_id=1, source_target_pairs={{0,24},{4,28},{8,0},{12,4},{16,8},{20,12},{24,16},{28,20},{32,56},... | collective-permute-start | bytes 196616 | tf_op jit(solution)/shard_map/ppermute | solution.py:473
  35.3 0.0 copy-done.11
  35.3 0.0 collective-permute-start.10
  35.3 0.0 copy-done.10
  35.3 7.2 %collective-permute-start.11 = (f32[34,16,128]{2,1,0:T(8,128)S(1)}, f32[34,16,128]{2,1,0:T(8,128)S(1)}, u32[]{:S(2)}, u32[]{:S(2)}) collective-permute-start(f32[34,16,128]{2,1,0:T(8,128)S(1)} %copy-done.10), channel_id=1, source_target_pairs={{0,127},{1,0},{2,1},{3,2},{4,3},{5,4},{6,5},{7,6},{8,7},{9,8},{10,... | collective-permute-start | bytes 835592 | tf_op jit(solution)/shard_map/ppermute | solution.py:439
  42.5 0.0 collective-permute-start.5
  42.5 0.0 collective-permute-start.6
  42.5 0.0 collective-permute-done.4
  42.5 5.8 %collective-permute-done.5 = f32[8,16,128]{2,1,0:T(8,128)S(1)} collective-permute-done((f32[8,16,128]{2,1,0:T(8,128)S(1)}, f32[8,16,128]{2,1,0:T(8,128)S(1)}, u32[]{:S(2)}, u32[]{:S(2)}) %collective-permute-start.5) | collective-permute-done | bytes 65568 | tf_op jit(solution)/shard_map/ppermute | solution.py:473
  48.4 0.3 collective-permute-done.6
  48.7 0.0 copy-start.3
  48.7 0.1 collective-permute-start.7
  48.8 0.4 collective-permute-start.8
  49.2 1.6 %collective-permute-start.9 = (f32[32,16,128]{2,1,0:T(8,128)S(1)}, f32[32,16,128]{2,1,0:T(8,128)S(1)}, u32[]{:S(2)}, u32[]{:S(2)}) collective-permute-start(f32[32,16,128]{2,1,0:T(8,128)S(1)} %constant_dynamic-update-slice_fusion.6.boxes0), channel_id=1, source_target_pairs={{0,32},{4,36},{8,40},{12,44},{16,48},{20,52},{24,56},{28,60},{32,6... | collective-permute-start | bytes 786440 | tf_op jit(solution)/shard_map/ppermute | solution.py:473
  50.8 0.0 collective-permute-done.10.left
  50.8 0.0 copy-start.7
  50.8 0.0 collective-permute-done.11.right
  50.8 0.0 copy-start.8
  50.9 1.1 %pad_maximum_fusion.middle = f32[3,16,16,128]{3,2,1,0:T(8,128)S(1)} fusion(f32[1,16,16,128]{3,2,1,0:T(8,128)S(1)} %slice_bitcast_fusion, f32[1,16,16,128]{3,2,1,0:T(8,128)} %bitcast.9, f32[1,16,16,128]{3,2,1,0:T(8,128)S(1)} %slice_bitcast_fusion.1), kind=kLoop, calls=%fused_computation | loop fusion | flops 196608 | bytes 786432 | tf_op jit(solution)/shard_map/stack | solution.py:537
  51.9 0.0 copy-start
  52.0 1.2 %collective-permute-start.12 = (f32[3,16,16,128]{3,2,1,0:T(8,128)S(1)}, f32[3,16,16,128]{3,2,1,0:T(8,128)S(1)}, u32[]{:S(2)}, u32[]{:S(2)}) collective-permute-start(f32[3,16,16,128]{3,2,1,0:T(8,128)S(1)} %pad_maximum_fusion.middle), channel_id=1, source_target_pairs={{0,3},{1,4},{2,5},{3,6},{4,7},{5,8},{6,9},{7,10},{8,11},{9,12},{10... | collective-permute-start | bytes 1179656 | tf_op jit(solution)/shard_map/ppermute | solution.py:439
  53.2 4.8 %collective-permute-start.13 = (f32[3,16,16,128]{3,2,1,0:T(8,128)S(1)}, f32[3,16,16,128]{3,2,1,0:T(8,128)S(1)}, u32[]{:S(2)}, u32[]{:S(2)}) collective-permute-start(f32[3,16,16,128]{3,2,1,0:T(8,128)S(1)} %pad_maximum_fusion.middle), channel_id=1, source_target_pairs={{0,125},{1,126},{2,127},{3,0},{4,1},{5,2},{6,3},{7,4},{8,5},{9,6},... | collective-permute-start | bytes 1179656 | tf_op jit(solution)/shard_map/ppermute | solution.py:439
  58.0 0.0 copy-done.7
  58.0 0.0 copy-done.8
  58.0 15.1 %near_outer.1.outer_in = f32[16,4096]{1,0:T(8,128)} custom-call(s32[9,32]{1,0:T(8,128)} %get-tuple-element.12.items, f32[2,8192]{1,0:T(2,128)} %points.5, f32[16,8192]{1,0:T(8,128)} %probes.3, f32[34,16,128]{2,1,0:T(8,128)} %copy-done.7, f32[34,16,128]{2,1,0:T(8,128)} %copy-done.8), custom_call_target="tpu_custom_call" | custom-call | flops 10000000000 | bytes 1048576 | tf_op jit(solution)/shard_map/near_outer/pallas_call | solution.py:542
  73.1 0.0 collective-permute-done.12.before
  73.1 0.0 copy-start.1
  73.1 0.0 collective-permute-done.13.after
  73.2 0.0 copy-done
  73.2 0.7 copy-done.1
  73.9 0.0 copy-start.2
  73.9 0.7 copy-done.2
  74.6 11.9 %far.2.far_in = f32[16,16,128]{2,1,0:T(8,128)} custom-call(s32[32,27]{1,0:T(8,128)} %far.3, s32[9,32]{1,0:T(8,128)} %bitcast.11, f32[3,16,16,128]{3,2,1,0:T(8,128)} %copy-done.1, f32[3,16,16,128]{3,2,1,0:T(8,128)} %copy-done, f32[3,16,16,128]{3,2,1,0:T(8,128)} %copy-done.2, f32[32,27,64,64]{3,2,1,0:T(8,128)} %couples_in.1), custom_call_target="tpu_custom_call" | custom-call | flops 8000000000 | bytes 1048576 | tf_op jit(solution)/shard_map/far/pallas_call | solution.py:553
  86.6 0.0 copy-done.3
  86.6 0.0 collective-permute-done.7.boxes1
  86.6 0.0 copy-start.4
  86.6 0.0 collective-permute-done.8.boxes2
  86.6 0.0 copy-start.5
  86.6 0.0 collective-permute-done.9.boxes3
  86.7 0.0 copy-start.6
  86.7 0.6 copy-done.4
  87.3 0.1 copy-done.5
  87.4 0.1 copy-done.6
  87.5 5.1 %down.1 = f32[16,8192]{1,0:T(8,128)} custom-call(s32[9,32]{1,0:T(8,128)} %bitcast.12, s32[1,27]{1,0:T(1,128)} %box_list.1, s32[1,4]{1,0:T(1,128)} %column_list.1, f32[32,16,128]{2,1,0:T(8,128)} %copy-done.3, f32[32,16,128]{2,1,0:T(8,128)} %copy-done.4, f32[32,16,128]{2,1,0:T(8,128)} %copy-done.5, f32[32,16,128]{2,1,0:T(8,128)} %copy-done.6, ...), custom_call_target="tpu_custom_call" | custom-call | tf_op jit(solution)/shard_map/down/pallas_call | solution.py:571
  (9 shorter events, 0.0 us)
Async XLA Ops:
  5.0 30.3 %copy-start.11 = (f32[34,16,128]{2,1,0:T(8,128)S(1)}, f32[34,16,128]{2,1,0:T(8,128)}, u32[]{:S(2)}) copy-start(f32[34,16,128]{2,1,0:T(8,128)} %get-tuple-element.13.bundle) | copy-start | bytes 835588
  5.0 30.3 %copy-start.10 = (f32[34,16,128]{2,1,0:T(8,128)S(1)}, f32[34,16,128]{2,1,0:T(8,128)}, u32[]{:S(2)}) copy-start(f32[34,16,128]{2,1,0:T(8,128)} %get-tuple-element.17) | copy-start | bytes 835588
  5.0 6.2 %collective-permute-start = (f32[1,16,128]{2,1,0:T(8,128)}, f32[1,16,128]{2,1,0:T(8,128)S(1)}, u32[]{:S(2)}, u32[]{:S(2)}) collective-permute-start(f32[1,16,128]{2,1,0:T(8,128)} %get-tuple-element.14), channel_id=1, source_target_pairs={{0,3},{1,0},{2,1},{3,2},{4,7},{5,4},{6,5},{7,6},{8,11},{9,8},{10,9... | collective-permute-start | bytes 24584 | tf_op jit(solution)/shard_map/ppermute | solution.py:439
  9.2 5.4 %collective-permute-start.1 = (f32[1,16,128]{2,1,0:T(8,128)}, f32[1,16,128]{2,1,0:T(8,128)S(1)}, u32[]{:S(2)}, u32[]{:S(2)}) collective-permute-start(f32[1,16,128]{2,1,0:T(8,128)} %get-tuple-element.14), channel_id=1, source_target_pairs={{0,2},{1,3},{2,0},{3,1},{4,6},{5,7},{6,4},{7,5},{8,10},{9,11},{10,... | collective-permute-start | bytes 24584 | tf_op jit(solution)/shard_map/ppermute | solution.py:439
  9.2 5.4 %collective-permute-start.2 = (f32[1,16,128]{2,1,0:T(8,128)}, f32[1,16,128]{2,1,0:T(8,128)S(1)}, u32[]{:S(2)}, u32[]{:S(2)}) collective-permute-start(f32[1,16,128]{2,1,0:T(8,128)} %get-tuple-element.14), channel_id=1, source_target_pairs={{0,1},{1,2},{2,3},{3,0},{4,5},{5,6},{6,7},{7,4},{8,9},{9,10},{10,1... | collective-permute-start | bytes 24584 | tf_op jit(solution)/shard_map/ppermute | solution.py:439
  14.6 0.6 copy-start.9
  14.6 16.1 %collective-permute-start.3 = (f32[4,16,128]{2,1,0:T(8,128)S(1)}, f32[4,16,128]{2,1,0:T(8,128)S(1)}, u32[]{:S(2)}, u32[]{:S(2)}) collective-permute-start(f32[4,16,128]{2,1,0:T(8,128)S(1)} %constant_dynamic-update-slice_fusion.column), channel_id=1, source_target_pairs={{0,4},{4,0},{8,12},{12,8},{16,20},{20,16},{24,28},{28,24},{32,36},... | collective-permute-start | bytes 98312 | tf_op jit(solution)/shard_map/ppermute | solution.py:473
  30.7 11.8 %collective-permute-start.4 = (f32[8,16,128]{2,1,0:T(8,128)S(1)}, f32[8,16,128]{2,1,0:T(8,128)S(1)}, u32[]{:S(2)}, u32[]{:S(2)}) collective-permute-start(f32[8,16,128]{2,1,0:T(8,128)S(1)} %get-tuple-element.19), channel_id=1, source_target_pairs={{0,24},{4,28},{8,0},{12,4},{16,8},{20,12},{24,16},{28,20},{32,56},... | collective-permute-start | bytes 196616 | tf_op jit(solution)/shard_map/ppermute | solution.py:473
  35.3 15.5 %collective-permute-start.10 = (f32[34,16,128]{2,1,0:T(8,128)S(1)}, f32[34,16,128]{2,1,0:T(8,128)S(1)}, u32[]{:S(2)}, u32[]{:S(2)}) collective-permute-start(f32[34,16,128]{2,1,0:T(8,128)S(1)} %copy-done.11), channel_id=1, source_target_pairs={{0,1},{1,2},{2,3},{3,4},{4,5},{5,6},{6,7},{7,8},{8,9},{9,10},{10,1... | collective-permute-start | bytes 835592 | tf_op jit(solution)/shard_map/ppermute | solution.py:439
  35.3 15.5 %collective-permute-start.11 = (f32[34,16,128]{2,1,0:T(8,128)S(1)}, f32[34,16,128]{2,1,0:T(8,128)S(1)}, u32[]{:S(2)}, u32[]{:S(2)}) collective-permute-start(f32[34,16,128]{2,1,0:T(8,128)S(1)} %copy-done.10), channel_id=1, source_target_pairs={{0,127},{1,0},{2,1},{3,2},{4,3},{5,4},{6,5},{7,6},{8,7},{9,8},{10,... | collective-permute-start | bytes 835592 | tf_op jit(solution)/shard_map/ppermute | solution.py:439
  42.5 5.9 %collective-permute-start.5 = (f32[8,16,128]{2,1,0:T(8,128)S(1)}, f32[8,16,128]{2,1,0:T(8,128)S(1)}, u32[]{:S(2)}, u32[]{:S(2)}) collective-permute-start(f32[8,16,128]{2,1,0:T(8,128)S(1)} %get-tuple-element.19), channel_id=1, source_target_pairs={{0,16},{4,20},{8,24},{12,28},{16,0},{20,4},{24,8},{28,12},{32,48},... | collective-permute-start | bytes 196616 | tf_op jit(solution)/shard_map/ppermute | solution.py:473
  42.5 6.2 %collective-permute-start.6 = (f32[8,16,128]{2,1,0:T(8,128)S(1)}, f32[8,16,128]{2,1,0:T(8,128)S(1)}, u32[]{:S(2)}, u32[]{:S(2)}) collective-permute-start(f32[8,16,128]{2,1,0:T(8,128)S(1)} %get-tuple-element.19), channel_id=1, source_target_pairs={{0,8},{4,12},{8,16},{12,20},{16,24},{20,28},{24,0},{28,4},{32,40},... | collective-permute-start | bytes 196616 | tf_op jit(solution)/shard_map/ppermute | solution.py:473
  48.7 37.9 %copy-start.3 = (f32[32,16,128]{2,1,0:T(8,128)}, f32[32,16,128]{2,1,0:T(8,128)S(1)}, u32[]{:S(2)}) copy-start(f32[32,16,128]{2,1,0:T(8,128)S(1)} %constant_dynamic-update-slice_fusion.6.boxes0) | copy-start | bytes 786436
  48.7 37.9 %collective-permute-start.7 = (f32[32,16,128]{2,1,0:T(8,128)S(1)}, f32[32,16,128]{2,1,0:T(8,128)S(1)}, u32[]{:S(2)}, u32[]{:S(2)}) collective-permute-start(f32[32,16,128]{2,1,0:T(8,128)S(1)} %constant_dynamic-update-slice_fusion.6.boxes0), channel_id=1, source_target_pairs={{0,96},{4,100},{8,104},{12,108},{16,112},{20,116},{24,120},{28,124... | collective-permute-start | bytes 786440 | tf_op jit(solution)/shard_map/ppermute | solution.py:473
  48.8 37.8 %collective-permute-start.8 = (f32[32,16,128]{2,1,0:T(8,128)S(1)}, f32[32,16,128]{2,1,0:T(8,128)S(1)}, u32[]{:S(2)}, u32[]{:S(2)}) collective-permute-start(f32[32,16,128]{2,1,0:T(8,128)S(1)} %constant_dynamic-update-slice_fusion.6.boxes0), channel_id=1, source_target_pairs={{0,64},{4,68},{8,72},{12,76},{16,80},{20,84},{24,88},{28,92},{32,9... | collective-permute-start | bytes 786440 | tf_op jit(solution)/shard_map/ppermute | solution.py:473
  49.2 37.5 %collective-permute-start.9 = (f32[32,16,128]{2,1,0:T(8,128)S(1)}, f32[32,16,128]{2,1,0:T(8,128)S(1)}, u32[]{:S(2)}, u32[]{:S(2)}) collective-permute-start(f32[32,16,128]{2,1,0:T(8,128)S(1)} %constant_dynamic-update-slice_fusion.6.boxes0), channel_id=1, source_target_pairs={{0,32},{4,36},{8,40},{12,44},{16,48},{20,52},{24,56},{28,60},{32,6... | collective-permute-start | bytes 786440 | tf_op jit(solution)/shard_map/ppermute | solution.py:473
  50.8 7.2 %copy-start.7 = (f32[34,16,128]{2,1,0:T(8,128)}, f32[34,16,128]{2,1,0:T(8,128)S(1)}, u32[]{:S(2)}) copy-start(f32[34,16,128]{2,1,0:T(8,128)S(1)} %collective-permute-done.10.left) | copy-start | bytes 835588
  50.8 7.2 %copy-start.8 = (f32[34,16,128]{2,1,0:T(8,128)}, f32[34,16,128]{2,1,0:T(8,128)S(1)}, u32[]{:S(2)}) copy-start(f32[34,16,128]{2,1,0:T(8,128)S(1)} %collective-permute-done.11.right) | copy-start | bytes 835588
  51.9 21.2 %copy-start = (f32[3,16,16,128]{3,2,1,0:T(8,128)}, f32[3,16,16,128]{3,2,1,0:T(8,128)S(1)}, u32[]{:S(2)}) copy-start(f32[3,16,16,128]{3,2,1,0:T(8,128)S(1)} %pad_maximum_fusion.middle) | copy-start | bytes 1179652
  52.0 21.2 %collective-permute-start.12 = (f32[3,16,16,128]{3,2,1,0:T(8,128)S(1)}, f32[3,16,16,128]{3,2,1,0:T(8,128)S(1)}, u32[]{:S(2)}, u32[]{:S(2)}) collective-permute-start(f32[3,16,16,128]{3,2,1,0:T(8,128)S(1)} %pad_maximum_fusion.middle), channel_id=1, source_target_pairs={{0,3},{1,4},{2,5},{3,6},{4,7},{5,8},{6,9},{7,10},{8,11},{9,12},{10... | collective-permute-start | bytes 1179656 | tf_op jit(solution)/shard_map/ppermute | solution.py:439
  53.2 20.0 %collective-permute-start.13 = (f32[3,16,16,128]{3,2,1,0:T(8,128)S(1)}, f32[3,16,16,128]{3,2,1,0:T(8,128)S(1)}, u32[]{:S(2)}, u32[]{:S(2)}) collective-permute-start(f32[3,16,16,128]{3,2,1,0:T(8,128)S(1)} %pad_maximum_fusion.middle), channel_id=1, source_target_pairs={{0,125},{1,126},{2,127},{3,0},{4,1},{5,2},{6,3},{7,4},{8,5},{9,6},... | collective-permute-start | bytes 1179656 | tf_op jit(solution)/shard_map/ppermute | solution.py:439
  73.1 0.7 copy-start.1
  73.9 0.8 copy-start.2
  86.6 0.7 copy-start.4
  86.6 0.8 copy-start.5
  86.7 0.9 copy-start.6

commit v5 on v4

--- a/solution.py
+++ b/solution.py
@@ -12,7 +12,8 @@
 FAR_REACH = 4
 FEATURES = 16
 GROUP = 12
-FAR_STEP = 4
+TAIL_GROUP = 4
+FAR_STEP = 2
 CHUNKS = 4
 
 matern_rate = math.sqrt(3.0) / 0.1
@@ -68,7 +69,7 @@
 
 
 def skeleton_kernel(
-    near, points, probes_in, basis_in, transfer_in, transfer_box, out, out_first, box_out, items,
+    near, points, probes_in, basis_in, transfer_in, transfer_box, out, out_first, items,
     probes, basis, transfer_leaf, semaphores,
 ):
     leaves, rank, leaf_size = basis.shape
@@ -98,9 +99,9 @@
     for side, start in ((out, width - edge), (out_first, 0)):
         for j in range(edge // 128):
             lanes = slice(start + j * 128, start + (j + 1) * 128)
-            side[pairs + j] = probes[:, lanes]
-            side[pairs + edge // 128, j : j + 1, :] = points[0:1, lanes]
-            side[pairs + edge // 128 + 1, j : j + 1, :] = points[1:2, lanes]
+            side[pairs + 1 + j] = probes[:, lanes]
+            side[pairs + 1 + edge // 128, j : j + 1, :] = points[0:1, lanes]
+            side[pairs + 2 + edge // 128, j : j + 1, :] = points[1:2, lanes]
 
     def leaf_probes(c):
         return stacked_halves(probes[:, c * leaf_size : (c + 1) * leaf_size])
@@ -129,45 +130,51 @@
         preferred_element_type=f32,
     )
     box = summed(wide)[:, :rank]
-    box_out[0] = jnp.concatenate([box, product3(box, transfer_box[0])], axis=1)
+    block = jnp.concatenate([box, product3(box, transfer_box[0])], axis=1)
+    out[pairs] = block
+    out_first[pairs] = block
 
 
 def near_kernel(
-    items, points, probes, left, right, out, values, source, target, total, listed, *, groups
+    items, points, probes, side, carried, out, carried_out,
+    values, source, target, total, listed, semaphore, *, begin, end
 ):
     slots, leaves = items.shape
     leaf_size = target.shape[2]
     pieces = leaf_size // 128
     pairs = leaves // 2
     edge_blocks = NEAR_REACH * pieces
+    if len(carried.shape) == 4:
+        handed_on = carried.at[:, pairs]
+    else:
+        handed_on = carried.at[pl.ds(0, carried_out.shape[0])]
+    handing = pltpu.make_async_copy(handed_on, carried_out, semaphore.at[0])
+    handing.start()
 
     count = jnp.int32(0)
-    for begin, end in groups:
-        for c in range(begin, end):
-            for k in range(slots):
-                item = items[k, c]
-                listed[count] = item
-                count = count + jnp.where(item != 0, 1, 0)
-    for u in range(GROUP):
-        listed[count + u] = groups[0][0] + NEAR_REACH * 64
+    for c in range(begin, end):
+        for k in range(slots):
+            item = items[k, c]
+            listed[count] = item
+            count = count + jnp.where(item != 0, 1, 0)
+    for u in range(TAIL_GROUP):
+        listed[count + u] = begin + (begin + NEAR_REACH) * 64
 
     ones = jnp.ones((3, leaf_size), f32)
     pad = jnp.zeros((2, leaf_size), f32)
-    window = sorted({w for begin, end in groups for w in range(begin, end + 2 * NEAR_REACH)})
-    for w in window:
+    for w in range(begin, end + 2 * NEAR_REACH):
         own = NEAR_REACH <= w < NEAR_REACH + leaves
         if own:
             lanes = slice((w - NEAR_REACH) * leaf_size, (w - NEAR_REACH + 1) * leaf_size)
             place, value = points[:, lanes], probes[:, lanes]
         else:
-            side = left if w < NEAR_REACH else right
             first = (w if w < NEAR_REACH else w - NEAR_REACH - leaves) * pieces
             parts = range(first, first + pieces)
-            value = jnp.concatenate([side[pairs + j] for j in parts], axis=1)
+            value = jnp.concatenate([side[pairs + 1 + j] for j in parts], axis=1)
             place = jnp.concatenate(
                 [
                     jnp.concatenate(
-                        [side[pairs + edge_blocks + d, j : j + 1, :] for j in parts], axis=1
+                        [side[pairs + 1 + edge_blocks + d, j : j + 1, :] for j in parts], axis=1
                     )
                     for d in range(2)
                 ],
@@ -185,7 +192,7 @@
         norms = jnp.concatenate([norm1, norm2, rest - norm2], axis=0)
         rows = jnp.concatenate([first, second, first, second, norms, ones, pad], axis=0)
         source[w] = rows.T.astype(bf16)
-        if own and any(begin <= w - NEAR_REACH < end for begin, end in groups):
+        if begin <= w - NEAR_REACH < end:
             target[w - NEAR_REACH] = jnp.concatenate(
                 [-2.0 * first, -2.0 * first, -2.0 * second, -2.0 * second, ones, norms, pad], axis=0
             ).astype(bf16)
@@ -203,17 +210,21 @@
         rest = jnp.dot(both[:16], low, preferred_element_type=f32)
         return c, (wide[:16] + wide[16:] + rest) * (times.astype(f32) * ln2)
 
-    def group(t, carry):
-        for c, term in [tile(t * GROUP + u) for u in range(GROUP)]:
-            total[c] += term
-        return carry
-
-    lax.fori_loop(0, (count + GROUP - 1) // GROUP, group, 0)
-    place = 0
-    for begin, end in groups:
-        for c in range(begin, end):
-            out[:, place * leaf_size : (place + 1) * leaf_size] = total[c]
-            place += 1
+    def group(size, first):
+        def step(t, carry):
+            for c, term in [tile(first + t * size + u) for u in range(size)]:
+                total[c] += term
+            return carry
+
+        return step
+
+    full = count // GROUP
+    lax.fori_loop(0, full, group(GROUP, 0), 0)
+    rest = count - full * GROUP
+    lax.fori_loop(0, (rest + TAIL_GROUP - 1) // TAIL_GROUP, group(TAIL_GROUP, full * GROUP), 0)
+    for c in range(begin, end):
+        out[:, (c - begin) * leaf_size : (c - begin + 1) * leaf_size] = total[c]
+    handing.wait()
 
 
 def fill_table(table, blocks, start):
@@ -271,96 +282,76 @@
     return wide[:16, :rank] + wide[16:, :rank] + wide[:16, rank:]
 
 
-def inner_kernel(
-    items, points, probes, bundle, column, out, skeletons_out, column_out, *scratch, groups
-):
-    skeletons_out[...] = bundle[: skeletons_out.shape[0]]
-    column_out[...] = column[...]
-    near_kernel(items, points, probes, bundle, bundle, out, *scratch, groups=groups)
-
-
-def far_kernel(
-    far, near, before, middle, after, couples_in, out, table, couples, semaphores
-):
-    leaves, slots, rank, _ = couples.shape
-    steps = leaves // FAR_STEP
-
-    def arriving(step):
-        run = pl.ds(step * FAR_STEP, FAR_STEP)
-        return pltpu.make_async_copy(couples_in.at[run], couples.at[run], semaphores.at[step])
-
-    def start(step, carry):
-        arriving(step).start()
-        return carry
-
-    lax.fori_loop(0, steps, start, 0)
+def far_kernel(far, near, before, middle, after, couples, after_this, out, table):
+    step = pl.program_id(0)
+    per_step, slots, rank, _ = couples.shape
+    leaves = far.shape[0]
+    pairs = leaves // 2
     empty = (2 * FAR_REACH + 1) * leaves
     low_lanes = lax.broadcasted_iota(jnp.int32, (32, 2 * rank), 1) < rank
-    for b in range(3):
-        for place, blocks in ((b, before), (3 + b, middle), (6 + b, after)):
-            fill_table(table, blocks.at[b], place * leaves)
-    table[empty] = jnp.zeros_like(table[empty])
-    table[empty + 1] = jnp.zeros_like(table[empty])
+
+    @pl.when(step == 0)
+    def _():
+        for b in range(3):
+            for place, blocks in ((b, before), (3 + b, middle), (6 + b, after)):
+                fill_table(table, blocks.at[b, :pairs], place * leaves)
+        table[empty] = jnp.zeros_like(table[empty])
+        table[empty + 1] = jnp.zeros_like(table[empty])
+
     base = near[0, 0] - FAR_REACH * leaves
 
-    def far_leaf(c):
+    def far_leaf(u):
+        c = step * per_step + u
+
         def picks(start, count):
             rows = [far[c, k] if k < slots else -1 for k in range(start, start + count)]
             rows = [jnp.where(row >= 0, row - base, empty) for row in rows]
             return picked(table, rows, low_lanes)
 
-        return coupled_pairs(picks, couples.at[c])
-
-    def far_step(step, carry):
-        arriving(step).wait()
-        for u in range(0, FAR_STEP, 2):
-            c = step * FAR_STEP + u
-            pair = jnp.concatenate([far_leaf(c), far_leaf(c + 1)], axis=1)
-            out[(step * FAR_STEP + u) // 2] = pair
-        return carry
-
-    lax.fori_loop(0, steps, far_step, 0)
+        return coupled_pairs(picks, couples.at[u])
+
+    for u in range(0, per_step, 2):
+        out[u // 2] = jnp.concatenate([far_leaf(u), far_leaf(u + 1)], axis=1)
 
 
 def down_kernel(
     near, box_list, column_list, boxes0, boxes1, boxes2, boxes3, couple_box_in, couple_column_in,
-    transfer_box_in, transfer_in, basis_in, far_in, inner_in, outer_in, out,
-    gathered, couple_box, couple_column, transfer_box, transfer_leaf, basis, far_leaf,
-    near_inner, near_outer, semaphores,
+    transfer_box_in, far_in, near0_in, near1_in, near2_in, near3_in, transfer_in, basis_in, out,
+    gathered, couple_box, couple_column, transfer_box, far_leaf, near0, near1, near2, near3,
+    transfer_leaf, basis, semaphores,
 ):
     leaves, rank, leaf_size = basis.shape
     slots, column_slots = box_list.shape[1], column_list.shape[1]
+    boxes = gathered.shape[0]
     low_lanes = lax.broadcasted_iota(jnp.int32, (32, 2 * rank), 1) < rank
-    length = boxes0.shape[0]
+    runs, place = [], 0
+    for part in (boxes0, boxes1, boxes2, boxes3):
+        runs.append((part, gathered.at[pl.ds(place, part.shape[0])]))
+        place += part.shape[0]
     arriving = copies(
-        [
-            (boxes, gathered.at[pl.ds(i * length, length)])
-            for i, boxes in enumerate((boxes0, boxes1, boxes2, boxes3))
-        ]
+        runs
         + [
             (couple_box_in, couple_box),
             (couple_column_in, couple_column),
             (transfer_box_in, transfer_box),
             (far_in, far_leaf),
-            (inner_in, near_inner),
-            (outer_in, near_outer),
+            (near0_in, near0),
+            (near1_in, near1),
+            (near2_in, near2),
+            (near3_in, near3),
         ]
         + parts(transfer_in, transfer_leaf)
         + parts(basis_in, basis),
         semaphores,
     )
+    later = 12 + CHUNKS
     for copy in arriving[:7]:
         copy.wait()
 
-    own = near[0, 0] // leaves
-
-    def moved(entry, shift, bits):
-        mask = (1 << bits) - 1
-        return (((entry >> shift) - (own >> shift)) & mask) << shift
+    first = near[0, 0] // leaves - boxes0.shape[0] - boxes1.shape[0] // 2
 
     def box_row(entry):
-        entry = jnp.where(entry >= 0, entry, 0)
-        return moved(entry, 0, 2) + moved(entry, 2, 1) + moved(entry, 3, 2) + moved(entry, 5, 2)
+        return (jnp.where(entry >= 0, entry, 0) - first) & (boxes - 1)
 
     def pick(k):
         entry = box_list[0, k]
@@ -377,10 +368,9 @@
     columns = []
     for k in range(column_slots):
         row = column_list[0, k]
-        start = box_row(row * 4) & ~3
-        block = gathered[start]
+        block = gathered[box_row(row * 4)]
         for j in range(1, 4):
-            block = block + gathered[start + j]
+            block = block + gathered[box_row(row * 4 + j)]
         columns.append(block * jnp.where(row >= 0, 1.0, 0.0))
     pieces = [
         stacked_halves(jnp.where(low_lanes[:16], exchanged(columns[k]), columns[k + 1]))
@@ -389,7 +379,7 @@
     far_column = coupled(jnp.concatenate(pieces, axis=1), couple_column[0])
     down_box = far_box + product3(far_column, transfer_box[0], ((1,), (1,)))
 
-    for copy in arriving[7 : 10 + CHUNKS]:
+    for copy in arriving[7:later]:
         copy.wait()
     high, low = halves(transfer_leaf[...].reshape(leaves * rank, rank))
     both = stacked_halves(down_box)
@@ -399,7 +389,7 @@
     lane = lax.broadcasted_iota(jnp.int32, (16, 4 * rank), 1)
     for m in range(leaves // 4):
         if m % (leaves // 4 // CHUNKS) == 0:
-            arriving[10 + CHUNKS + m // (leaves // 4 // CHUNKS)].wait()
+            arriving[later + m // (leaves // 4 // CHUNKS)].wait()
         down = from_box[:, m * 4 * rank : (m + 1) * 4 * rank]
         down = down + jnp.concatenate([far_leaf[2 * m], far_leaf[2 * m + 1]], axis=1)
         own_rows = [
@@ -412,9 +402,8 @@
         result = wide[:64] + wide[64:] + rest
         for j in range(4):
             c = 4 * m + j
-            inner = NEAR_REACH <= c < leaves - NEAR_REACH
-            place = c - NEAR_REACH if inner else c if c < NEAR_REACH else c - leaves + 2 * NEAR_REACH
-            held = near_inner if inner else near_outer
+            held = (near0, near1, near2, near3)[c // NEAR_REACH]
+            place = c % NEAR_REACH
             near_value = held[:, place * leaf_size : (place + 1) * leaf_size]
             out[:, c * leaf_size : (c + 1) * leaf_size] = near_value + result[16 * j : 16 * j + 16]
 
@@ -443,18 +432,6 @@
     return [pl.BlockSpec(memory_space=pl.ANY)] * count
 
 
-def near_scratch(items, probe_count, leaf_size):
-    slots, leaves = items.shape
-    window = leaves + 2 * NEAR_REACH
-    return [
-        pltpu.VMEM((window, 2 * probe_count, leaf_size), bf16),
-        pltpu.VMEM((window, leaf_size, FEATURES), bf16),
-        pltpu.VMEM((leaves, FEATURES, leaf_size), bf16),
-        pltpu.VMEM((leaves, probe_count, leaf_size), f32),
-        pltpu.SMEM((leaves * slots + 2 * GROUP,), jnp.int32),
-    ]
-
-
 def like(array):
     return pltpu.VMEM(array.shape, array.dtype)
 
@@ -463,14 +440,37 @@
     return pltpu.SemaphoreType.DMA((count,))
 
 
-def moved_along(array, shift, bits, by):
-    mask = (1 << bits) - 1
-
-    def target(i):
-        part = (i >> shift) & mask
-        return i + ((((part - by) & mask) - part) << shift)
-
-    return lax.ppermute(array, "leaf", [(i, target(i)) for i in range(lax.axis_size("leaf"))])
+def near_call(name, begin, items, points, probes, side, carried):
+    slots, leaves = items.shape
+    probe_count = probes.shape[0]
+    leaf_size = probes.shape[1] // leaves
+    window = leaves + 2 * NEAR_REACH
+    if carried.ndim == 4:
+        handed_on = (carried.shape[0],) + carried.shape[2:]
+    else:
+        handed_on = (min(carried.shape[0], 27),) + carried.shape[1:]
+    if name == "near_first":
+        handed_on = (leaves // 2 + 1,) + carried.shape[1:]
+    return pl.pallas_call(
+        functools.partial(near_kernel, begin=begin, end=begin + NEAR_REACH),
+        out_shape=(
+            jax.ShapeDtypeStruct((probe_count, NEAR_REACH * leaf_size), f32),
+            jax.ShapeDtypeStruct(handed_on, f32),
+        ),
+        in_specs=scalars(1) + whole(3) + hbm(1),
+        out_specs=tuple(whole(1) + hbm(1)),
+        scratch_shapes=[
+            pltpu.VMEM((window, 2 * probe_count, leaf_size), bf16),
+            pltpu.VMEM((window, leaf_size, FEATURES), bf16),
+            pltpu.VMEM((leaves, FEATURES, leaf_size), bf16),
+            pltpu.VMEM((leaves, probe_count, leaf_size), f32),
+            pltpu.SMEM((leaves * slots + 2 * GROUP,), jnp.int32),
+            copy_semaphores(1),
+        ],
+        compiler_params=params,
+        cost_estimate=cost(10_000_000_000),
+        name=name,
+    )(items, points, probes, side, carried)
 
 
 def per_device(
@@ -492,92 +492,72 @@
     near_slots = near_list.T
     basis = basis.transpose(0, 2, 1)
     pairs = leaves // 2
-    blocks = pairs + NEAR_REACH * leaf_size // 128 + 2
+    blocks = pairs + 1 + NEAR_REACH * leaf_size // 128 + 2
 
     edges = jax.ShapeDtypeStruct((blocks, probe_count, 2 * rank), f32)
-    bundle_last, bundle_first, box, items = pl.pallas_call(
+    bundle_last, bundle_first, items = pl.pallas_call(
         skeleton_kernel,
-        out_shape=(
-            edges,
-            edges,
-            jax.ShapeDtypeStruct((1, probe_count, 2 * rank), f32),
-            jax.ShapeDtypeStruct(near_slots.shape, jnp.int32),
-        ),
+        out_shape=(edges, edges, jax.ShapeDtypeStruct(near_slots.shape, jnp.int32)),
         in_specs=whole(2) + hbm(3) + whole(1),
-        out_specs=tuple(whole(4)),
+        out_specs=tuple(whole(3)),
         scratch_shapes=[like(probes), like(basis), like(transfer_leaf)]
         + [copy_semaphores(1 + 2 * CHUNKS)],
         compiler_params=params,
         name="skeletons",
     )(near_slots, points, probes, basis, transfer_leaf, transfer_box)
 
-    column = jnp.concatenate([box] + [shifted(box, "sub", -by) for by in (1, 2, 3)])
+    near_leaves = functools.partial(near_call, items=items, points=points, probes=probes)
     left, right = shifted(bundle_last, ring, 1), shifted(bundle_first, ring, -1)
-    other_core = moved_along(column, 0, 1, 1)
-
-    inner = ((NEAR_REACH, leaves - NEAR_REACH),)
-    outer = ((0, NEAR_REACH), (leaves - NEAR_REACH, leaves))
-    half = jax.ShapeDtypeStruct((probe_count, probes.shape[1] // 2), f32)
-    near_inner, skeletons, column = pl.pallas_call(
-        functools.partial(inner_kernel, groups=inner),
-        out_shape=(
-            half,
-            jax.ShapeDtypeStruct((pairs, probe_count, 2 * rank), f32),
-            jax.ShapeDtypeStruct(column.shape, f32),
-        ),
-        in_specs=scalars(1) + whole(4),
-        out_specs=tuple(whole(3)),
-        scratch_shapes=near_scratch(items, probe_count, leaf_size),
-        compiler_params=params,
-        cost_estimate=cost(10_000_000_000),
-        name="near_inner",
-    )(items, points, probes, bundle_last, column)
-
-    both = jnp.concatenate([column, other_core])
-    middle = jnp.stack([left[:pairs], skeletons, right[:pairs]])
-    plane = jnp.concatenate([both] + [moved_along(both, 1, 2, by) for by in (1, 2, 3)])
+    near1, own = near_leaves("near_first", NEAR_REACH, side=bundle_first, carried=bundle_last)
+
+    middle = jnp.stack([left[: pairs + 1], own, right[: pairs + 1]])
     before, after = shifted(middle, ring, 3), shifted(middle, ring, -3)
-    planes = [plane] + [moved_along(plane, 3, 2, by) for by in (1, 2, 3)]
-
-    near_outer = pl.pallas_call(
-        functools.partial(near_kernel, groups=outer),
-        out_shape=half,
-        in_specs=scalars(1) + whole(4),
-        out_specs=pl.BlockSpec(memory_space=pltpu.VMEM),
-        scratch_shapes=near_scratch(items, probe_count, leaf_size),
-        compiler_params=params,
-        cost_estimate=cost(10_000_000_000),
-        name="near_outer",
-    )(items, points, probes, left, right)
-
+    near2, three = near_leaves("near_second", 2 * NEAR_REACH, side=bundle_first, carried=middle)
+
+    nine = jnp.concatenate([before[:, pairs], three, after[:, pairs]])
+    nine_before, nine_after = shifted(nine, ring, 9), shifted(nine, ring, -9)
+    near0, nine = near_leaves("near_third", 0, side=left, carried=nine)
+
+    more = jnp.concatenate([nine_before, nine, nine_after])
+    more_before, more_after = shifted(more, ring, 27), shifted(more, ring, -27)
+    near3, more = near_leaves("near_fourth", leaves - NEAR_REACH, side=right, carried=more)
+
+    count = lax.axis_size(ring)
+    missing = (count - 3 * more.shape[0] - more.shape[0]) // 2
+    inner = jnp.concatenate([more_before[-missing:], more, more_after[:missing]])
+    opposite = shifted(inner, ring, count // 2)
+
+    window = pl.BlockSpec(middle.shape, lambda i: (0, 0, 0, 0))
     far_leaf = pl.pallas_call(
         far_kernel,
+        grid=(leaves // FAR_STEP,),
         out_shape=jax.ShapeDtypeStruct((pairs, probe_count, 2 * rank), f32),
-        in_specs=scalars(2) + whole(3) + hbm(1),
-        out_specs=pl.BlockSpec(memory_space=pltpu.VMEM),
+        in_specs=scalars(2)
+        + [window] * 3
+        + [pl.BlockSpec((FAR_STEP,) + couple_leaf.shape[1:], lambda i: (i, 0, 0, 0))]
+        + hbm(1),
+        out_specs=pl.BlockSpec((FAR_STEP // 2, probe_count, 2 * rank), lambda i: (i, 0, 0)),
         scratch_shapes=[
-            pltpu.VMEM(((2 * FAR_REACH + 1) * leaves + 2, 2 * probe_count, 2 * rank), bf16),
-            like(couple_leaf),
-            copy_semaphores(leaves // FAR_STEP),
+            pltpu.VMEM(((2 * FAR_REACH + 1) * leaves + 2, 2 * probe_count, 2 * rank), bf16)
         ],
         compiler_params=params,
         cost_estimate=cost(8_000_000_000),
         name="far",
-    )(far_list, near_slots, before, middle, after, couple_leaf)
-
-    gathered = pltpu.VMEM((4 * plane.shape[0],) + plane.shape[1:], f32)
-    held = (couple_box, couple_column, transfer_box, transfer_leaf, basis, far_leaf)
-    held += (near_inner, near_outer)
+    )(far_list, near_slots, before, middle, after, couple_leaf, inner)
+
+    held = (couple_box, couple_column, transfer_box, far_leaf, near0, near1, near2, near3)
+    held += (transfer_leaf, basis)
     return pl.pallas_call(
         down_kernel,
         out_shape=jax.ShapeDtypeStruct(probes.shape, f32),
-        in_specs=scalars(3) + hbm(12),
+        in_specs=scalars(3) + hbm(14),
         out_specs=pl.BlockSpec(memory_space=pltpu.VMEM),
-        scratch_shapes=[gathered] + [like(array) for array in held]
-        + [copy_semaphores(10 + 2 * CHUNKS)],
+        scratch_shapes=[pltpu.VMEM((count, probe_count, 2 * rank), f32)]
+        + [like(array) for array in held]
+        + [copy_semaphores(12 + 2 * CHUNKS)],
         compiler_params=params,
         name="down",
-    )(near_slots, box_list, column_list, *planes, *held)
+    )(near_slots, box_list, column_list, more_before, more, more_after, opposite, *held)
 
 
 def solution(mesh):

time: 93.2 us -> 98.6 us (1.058)
  the two profiles are of different devices: /device:TPU:0 before, /device:TPU:3 now
where the time goes in v5:
time: 98.6 us; the launch traced here: 97.8 us
  Pallas kernels  64.4 us (65%)
  starting transfers between devices  23.8 us (24%)
  local copies, waits for them, and re-layouts  4.05 us (4%)
  other arithmetic  2.92 us (3%)
  waiting for transfers between devices  2.26 us (2%)
    pallas_call x4, Pallas kernels, near_call(): pl.pallas_call(functools.partial(near_kernel, begin=begin, end=begin + NE...  34.4 us
    ppermute x9, starting transfers between devices, shifted(): lax.ppermute(array, axis, [(i, (i + by) % devices) for i in range(devices)])  23.8 us
    pallas_call x1, Pallas kernels, per_device(): pl.pallas_call(far_kernel, grid=(leaves // FAR_STEP,), out_shape=jax.Shap...  19.5 us
    pallas_call x1, Pallas kernels, per_device(): pl.pallas_call(down_kernel, out_shape=jax.ShapeDtypeStruct(probes.shape,...  5.26 us
    pallas_call x1, Pallas kernels, per_device(): pl.pallas_call(skeleton_kernel, out_shape=(edges, edges, jax.ShapeDtypeSt...  5.22 us
    ppermute x9, waiting for transfers between devices, shifted(): lax.ppermute(array, axis, [(i, (i + by) % devices) for i in range(devices)])  2.26 us
  transfers between devices with their start and end apart: 9, of which 1 were waited for; matrix products, arithmetic and copies ran while one was open for 3% of the time, Pallas kernels for 55%

profile of v5, /device:TPU:3, one launch (start us, length us, event | category | flops | bytes accessed | tf_op | source)
XLA Modules:
  0.0 97.8 jit_solution(12804146111401061003)
XLA Ops:
  0.0 5.2 %skeletons.1 = (f32[35,16,128]{2,1,0:T(8,128)}, f32[35,16,128]{2,1,0:T(8,128)}, s32[9,32]{1,0:T(8,128)}) custom-call(s32[9,32]{1,0:T(8,128)} %bitcast.14, f32[2,8192]{1,0:T(2,128)} %points.9, f32[16,8192]{1,0:T(8,128)} %probes.7, f32[32,64,256]{2,1,0:T(8,128)} %bitcast.11, f32[32,64,64]{2,1,0:T(8,128)} %transfer_in.3, f32[1,64,64]{2,1,0:T(8,128)} %transfer_box_in.1), custom_call_target="tpu_custom_call" | custom-call | tf_op jit(solution)/shard_map/skeletons/pallas_call | solution.py:498
  5.2 1.7 %collective-permute-start = (f32[35,16,128]{2,1,0:T(8,128)}, f32[35,16,128]{2,1,0:T(8,128)S(1)}, u32[]{:S(2)}, u32[]{:S(2)}) collective-permute-start(f32[35,16,128]{2,1,0:T(8,128)} %get-tuple-element.16.carried), channel_id=1, source_target_pairs={{0,1},{1,2},{2,3},{3,4},{4,5},{5,6},{6,7},{7,8},{8,9},{9,10},{10,1... | collective-permute-start | bytes 860168 | tf_op jit(solution)/shard_map/ppermute | solution.py:428
  6.9 2.8 %collective-permute-start.1 = (f32[35,16,128]{2,1,0:T(8,128)}, f32[35,16,128]{2,1,0:T(8,128)S(1)}, u32[]{:S(2)}, u32[]{:S(2)}) collective-permute-start(f32[35,16,128]{2,1,0:T(8,128)} %get-tuple-element.18.side), channel_id=1, source_target_pairs={{0,127},{1,0},{2,1},{3,2},{4,3},{5,4},{6,5},{7,6},{8,7},{9,8},{10,... | collective-permute-start | bytes 860168 | tf_op jit(solution)/shard_map/ppermute | solution.py:428
  9.7 8.3 %near_first.1 = (f32[16,2048]{1,0:T(8,128)}, f32[17,16,128]{2,1,0:T(8,128)}) custom-call(s32[9,32]{1,0:T(8,128)} %get-tuple-element.17.items, f32[2,8192]{1,0:T(2,128)} %points.9, f32[16,8192]{1,0:T(8,128)} %probes.7, f32[35,16,128]{2,1,0:T(8,128)} %get-tuple-element.18.side, f32[35,16,128]{2,1,0:T(8,128)} %get-tuple-element.16.carried), custom_call_target="tpu_custom_call" | custom-call | flops 10000000000 | bytes 1048576 | tf_op jit(solution)/shard_map/near_first/pallas_call | solution.py:454
  18.0 0.0 collective-permute-done.side
  18.0 0.0 copy-start.6
  18.1 0.0 collective-permute-done.1.side
  18.1 0.0 copy-start.5
  18.1 1.1 %pad_maximum_fusion = f32[3,17,16,128]{3,2,0,1:T(8,128)S(1)} fusion(f32[1,17,16,128]{3,2,0,1:T(8,128)S(1)} %slice_bitcast_fusion, f32[1,17,16,128]{3,2,0,1:T(8,128)} %bitcast.13, f32[1,17,16,128]{3,2,0,1:T(8,128)S(1)} %slice_bitcast_fusion.1), kind=kLoop, calls=%fused_computation | loop fusion | flops 208896 | bytes 835584 | tf_op jit(solution)/shard_map/stack | solution.py:513
  19.2 0.8 copy.13.carried.middle
  20.0 0.0 collective-permute-start.3
  20.0 2.7 %collective-permute-start.2 = (f32[3,17,16,128]{3,2,0,1:T(8,128)S(1)}, f32[3,17,16,128]{3,2,0,1:T(8,128)S(1)}, u32[]{:S(2)}, u32[]{:S(2)}) collective-permute-start(f32[3,17,16,128]{3,2,0,1:T(8,128)S(1)} %pad_maximum_fusion), channel_id=1, source_target_pairs={{0,3},{1,4},{2,5},{3,6},{4,7},{5,8},{6,9},{7,10},{8,11},{9,12},{10... | collective-permute-start | bytes 1253384 | tf_op jit(solution)/shard_map/ppermute | solution.py:428
  22.7 8.3 %near_second.1 = (f32[16,2048]{1,0:T(8,128)}, f32[3,16,128]{2,1,0:T(8,128)}) custom-call(s32[9,32]{1,0:T(8,128)} %get-tuple-element.17.items, f32[2,8192]{1,0:T(2,128)} %points.9, f32[16,8192]{1,0:T(8,128)} %probes.7, f32[35,16,128]{2,1,0:T(8,128)} %get-tuple-element.18.side, f32[3,17,16,128]{3,2,1,0:T(8,128)} %copy.13.carried.middle), custom_call_target="tpu_custom_call" | custom-call | flops 10000000000 | bytes 1048576 | tf_op jit(solution)/shard_map/near_second/pallas_call | solution.py:454
  30.9 0.0 collective-permute-done.3
  30.9 2.2 %collective-permute-done.2 = f32[3,17,16,128]{3,2,0,1:T(8,128)S(1)} collective-permute-done((f32[3,17,16,128]{3,2,0,1:T(8,128)S(1)}, f32[3,17,16,128]{3,2,0,1:T(8,128)S(1)}, u32[]{:S(2)}, u32[]{:S(2)}) %collective-permute-start.2) | collective-permute-done | bytes 417824 | tf_op jit(solution)/shard_map/ppermute | solution.py:428
  33.2 0.7 pad_maximum_fusion.2.carried
  33.9 0.0 copy-start.4
  33.9 4.4 %collective-permute-start.5 = (f32[9,16,128]{2,1,0:T(8,128)S(1)}, f32[9,16,128]{2,1,0:T(8,128)S(1)}, u32[]{:S(2)}, u32[]{:S(2)}) collective-permute-start(f32[9,16,128]{2,1,0:T(8,128)S(1)} %pad_maximum_fusion.2.carried), channel_id=1, source_target_pairs={{0,119},{1,120},{2,121},{3,122},{4,123},{5,124},{6,125},{7,126},{8... | collective-permute-start | bytes 221192 | tf_op jit(solution)/shard_map/ppermute | solution.py:428
  38.3 0.0 collective-permute-start.4
  38.3 0.0 copy-done.6
  38.3 0.0 copy-done.4
  38.3 8.3 %near_third.1 = (f32[16,2048]{1,0:T(8,128)}, f32[9,16,128]{2,1,0:T(8,128)}) custom-call(s32[9,32]{1,0:T(8,128)} %get-tuple-element.17.items, f32[2,8192]{1,0:T(2,128)} %points.9, f32[16,8192]{1,0:T(8,128)} %probes.7, f32[35,16,128]{2,1,0:T(8,128)} %copy-done.6, f32[9,16,128]{2,1,0:T(8,128)} %copy-done.4), custom_call_target="tpu_custom_call" | custom-call | flops 10000000000 | bytes 1048576 | tf_op jit(solution)/shard_map/near_third/pallas_call | solution.py:454
  46.6 0.0 copy-done.5
  46.6 0.8 copy.16.after
  47.4 0.8 copy.14.before
  48.2 0.0 collective-permute-done.4
  48.2 0.9 constant_dynamic-update-slice_fusion.1
  49.1 0.0 collective-permute-done.5
  49.1 0.0 copy-start.7
  49.1 2.5 %collective-permute-start.7 = (f32[27,16,128]{2,1,0:T(8,128)S(1)}, f32[27,16,128]{2,1,0:T(8,128)S(1)}, u32[]{:S(2)}, u32[]{:S(2)}) collective-permute-start(f32[27,16,128]{2,1,0:T(8,128)S(1)} %constant_dynamic-update-slice_fusion.carried), channel_id=1, source_target_pairs={{0,101},{1,102},{2,103},{3,104},{4,105},{5,106},{6,107},{7,108},{8... | collective-permute-start | bytes 663560 | tf_op jit(solution)/shard_map/ppermute | solution.py:428
  51.6 5.1 %collective-permute-start.6 = (f32[27,16,128]{2,1,0:T(8,128)S(1)}, f32[27,16,128]{2,1,0:T(8,128)S(1)}, u32[]{:S(2)}, u32[]{:S(2)}) collective-permute-start(f32[27,16,128]{2,1,0:T(8,128)S(1)} %constant_dynamic-update-slice_fusion.carried), channel_id=1, source_target_pairs={{0,27},{1,28},{2,29},{3,30},{4,31},{5,32},{6,33},{7,34},{8,35},{9,... | collective-permute-start | bytes 663560 | tf_op jit(solution)/shard_map/ppermute | solution.py:428
  56.7 0.0 copy-done.7
  56.7 9.6 %near_fourth.1 = (f32[16,2048]{1,0:T(8,128)}, f32[27,16,128]{2,1,0:T(8,128)}) custom-call(s32[9,32]{1,0:T(8,128)} %get-tuple-element.17.items, f32[2,8192]{1,0:T(2,128)} %points.9, f32[16,8192]{1,0:T(8,128)} %probes.7, f32[35,16,128]{2,1,0:T(8,128)} %copy-done.5, f32[27,16,128]{2,1,0:T(8,128)} %copy-done.7), custom_call_target="tpu_custom_call" | custom-call | flops 10000000000 | bytes 1048576 | tf_op jit(solution)/shard_map/near_fourth/pallas_call | solution.py:454
  66.3 0.0 collective-permute-done.7.boxes2
  66.3 0.0 copy-start.1
  66.4 0.0 collective-permute-done.6.boxes0
  66.4 0.0 copy-start.2
  66.4 1.1 %pad_maximum_fusion.1.after_this = f32[47,16,128]{2,1,0:T(8,128)S(1)} fusion(f32[10,16,128]{2,1,0:T(8,128)S(1)} %slice.29, f32[27,16,128]{2,1,0:T(8,128)} %get-tuple-element.22.boxes1, f32[10,16,128]{2,1,0:T(8,128)S(1)} %slice.28), kind=kLoop, calls=%fused_computation.1 | loop fusion | flops 192512 | bytes 770048 | tf_op jit(solution)/shard_map/concatenate | solution.py:527
  67.5 0.0 copy-start
  67.5 4.7 %collective-permute-start.8 = (f32[47,16,128]{2,1,0:T(8,128)S(1)}, f32[47,16,128]{2,1,0:T(8,128)S(1)}, u32[]{:S(2)}, u32[]{:S(2)}) collective-permute-start(f32[47,16,128]{2,1,0:T(8,128)S(1)} %pad_maximum_fusion.1.after_this), channel_id=1, source_target_pairs={{0,64},{1,65},{2,66},{3,67},{4,68},{5,69},{6,70},{7,71},{8,72},{9,... | collective-permute-start | bytes 1155080 | tf_op jit(solution)/shard_map/ppermute | solution.py:428
  72.2 0.0 copy-done
  72.2 19.5 %far.2.far_in = f32[16,16,128]{2,1,0:T(8,128)} custom-call(s32[32,27]{1,0:T(8,128)} %far.3, s32[9,32]{1,0:T(8,128)} %bitcast.15, f32[3,17,16,128]{3,2,1,0:T(8,128)} %copy.14.before, f32[3,17,16,128]{3,2,1,0:T(8,128)} %copy.13.carried.middle, f32[3,17,16,128]{3,2,1,0:T(8,128)} %copy.16.after, f32[32,27,64,64]{3,2,1,0:T(8,128)} %couples.1, f32[47,16,128]{2,1,0:T(8,128)} %copy-done), custom_call_target="tpu_custom_call" | custom-call | flops 8000000000 | bytes 1048576 | tf_op jit(solution)/shard_map/far/pallas_call | solution.py:531
  91.6 0.0 collective-permute-done.8.boxes3
  91.6 0.0 copy-start.3
  91.7 0.0 copy-done.1
  91.7 0.0 copy-done.2
  91.7 0.7 copy-done.3
  92.4 5.3 %down.1 = f32[16,8192]{1,0:T(8,128)} custom-call(s32[9,32]{1,0:T(8,128)} %bitcast.16, s32[1,27]{1,0:T(1,128)} %box_list.1, s32[1,4]{1,0:T(1,128)} %column_list.1, f32[27,16,128]{2,1,0:T(8,128)} %copy-done.2, f32[27,16,128]{2,1,0:T(8,128)} %get-tuple-element.22.boxes1, f32[27,16,128]{2,1,0:T(8,128)} %copy-done.1, f32[47,16,128]{2,1,0:T(8,128)} %copy-done.3, ...), custom_call_target="tpu_custom_call" | custom-call | tf_op jit(solution)/shard_map/down/pallas_call | solution.py:550
  (8 shorter events, 0.1 us)
Async XLA Ops:
  5.2 12.8 %collective-permute-start = (f32[35,16,128]{2,1,0:T(8,128)}, f32[35,16,128]{2,1,0:T(8,128)S(1)}, u32[]{:S(2)}, u32[]{:S(2)}) collective-permute-start(f32[35,16,128]{2,1,0:T(8,128)} %get-tuple-element.16.carried), channel_id=1, source_target_pairs={{0,1},{1,2},{2,3},{3,4},{4,5},{5,6},{6,7},{7,8},{8,9},{9,10},{10,1... | collective-permute-start | bytes 860168 | tf_op jit(solution)/shard_map/ppermute | solution.py:428
  6.9 11.1 %collective-permute-start.1 = (f32[35,16,128]{2,1,0:T(8,128)}, f32[35,16,128]{2,1,0:T(8,128)S(1)}, u32[]{:S(2)}, u32[]{:S(2)}) collective-permute-start(f32[35,16,128]{2,1,0:T(8,128)} %get-tuple-element.18.side), channel_id=1, source_target_pairs={{0,127},{1,0},{2,1},{3,2},{4,3},{5,4},{6,5},{7,6},{8,7},{9,8},{10,... | collective-permute-start | bytes 860168 | tf_op jit(solution)/shard_map/ppermute | solution.py:428
  18.0 20.3 %copy-start.6 = (f32[35,16,128]{2,1,0:T(8,128)}, f32[35,16,128]{2,1,0:T(8,128)S(1)}, u32[]{:S(2)}) copy-start(f32[35,16,128]{2,1,0:T(8,128)S(1)} %collective-permute-done.side) | copy-start | bytes 860164
  18.1 28.5 %copy-start.5 = (f32[35,16,128]{2,1,0:T(8,128)}, f32[35,16,128]{2,1,0:T(8,128)S(1)}, u32[]{:S(2)}) copy-start(f32[35,16,128]{2,1,0:T(8,128)S(1)} %collective-permute-done.1.side) | copy-start | bytes 860164
  20.0 11.0 %collective-permute-start.3 = (f32[3,17,16,128]{3,2,0,1:T(8,128)S(1)}, f32[3,17,16,128]{3,2,0,1:T(8,128)S(1)}, u32[]{:S(2)}, u32[]{:S(2)}) collective-permute-start(f32[3,17,16,128]{3,2,0,1:T(8,128)S(1)} %pad_maximum_fusion), channel_id=1, source_target_pairs={{0,125},{1,126},{2,127},{3,0},{4,1},{5,2},{6,3},{7,4},{8,5},{9,6},... | collective-permute-start | bytes 1253384 | tf_op jit(solution)/shard_map/ppermute | solution.py:428
  20.0 13.2 %collective-permute-start.2 = (f32[3,17,16,128]{3,2,0,1:T(8,128)S(1)}, f32[3,17,16,128]{3,2,0,1:T(8,128)S(1)}, u32[]{:S(2)}, u32[]{:S(2)}) collective-permute-start(f32[3,17,16,128]{3,2,0,1:T(8,128)S(1)} %pad_maximum_fusion), channel_id=1, source_target_pairs={{0,3},{1,4},{2,5},{3,6},{4,7},{5,8},{6,9},{7,10},{8,11},{9,12},{10... | collective-permute-start | bytes 1253384 | tf_op jit(solution)/shard_map/ppermute | solution.py:428
  33.9 4.4 %copy-start.4 = (f32[9,16,128]{2,1,0:T(8,128)}, f32[9,16,128]{2,1,0:T(8,128)S(1)}, u32[]{:S(2)}) copy-start(f32[9,16,128]{2,1,0:T(8,128)S(1)} %pad_maximum_fusion.2.carried) | copy-start | bytes 221188
  33.9 15.1 %collective-permute-start.5 = (f32[9,16,128]{2,1,0:T(8,128)S(1)}, f32[9,16,128]{2,1,0:T(8,128)S(1)}, u32[]{:S(2)}, u32[]{:S(2)}) collective-permute-start(f32[9,16,128]{2,1,0:T(8,128)S(1)} %pad_maximum_fusion.2.carried), channel_id=1, source_target_pairs={{0,119},{1,120},{2,121},{3,122},{4,123},{5,124},{6,125},{7,126},{8... | collective-permute-start | bytes 221192 | tf_op jit(solution)/shard_map/ppermute | solution.py:428
  38.3 9.9 %collective-permute-start.4 = (f32[9,16,128]{2,1,0:T(8,128)S(1)}, f32[9,16,128]{2,1,0:T(8,128)S(1)}, u32[]{:S(2)}, u32[]{:S(2)}) collective-permute-start(f32[9,16,128]{2,1,0:T(8,128)S(1)} %pad_maximum_fusion.2.carried), channel_id=1, source_target_pairs={{0,9},{1,10},{2,11},{3,12},{4,13},{5,14},{6,15},{7,16},{8,17},{9,1... | collective-permute-start | bytes 221192 | tf_op jit(solution)/shard_map/ppermute | solution.py:428
  49.1 7.6 %copy-start.7 = (f32[27,16,128]{2,1,0:T(8,128)}, f32[27,16,128]{2,1,0:T(8,128)S(1)}, u32[]{:S(2)}) copy-start(f32[27,16,128]{2,1,0:T(8,128)S(1)} %constant_dynamic-update-slice_fusion.carried) | copy-start | bytes 663556
  49.1 17.2 %collective-permute-start.7 = (f32[27,16,128]{2,1,0:T(8,128)S(1)}, f32[27,16,128]{2,1,0:T(8,128)S(1)}, u32[]{:S(2)}, u32[]{:S(2)}) collective-permute-start(f32[27,16,128]{2,1,0:T(8,128)S(1)} %constant_dynamic-update-slice_fusion.carried), channel_id=1, source_target_pairs={{0,101},{1,102},{2,103},{3,104},{4,105},{5,106},{6,107},{7,108},{8... | collective-permute-start | bytes 663560 | tf_op jit(solution)/shard_map/ppermute | solution.py:428
  51.6 14.8 %collective-permute-start.6 = (f32[27,16,128]{2,1,0:T(8,128)S(1)}, f32[27,16,128]{2,1,0:T(8,128)S(1)}, u32[]{:S(2)}, u32[]{:S(2)}) collective-permute-start(f32[27,16,128]{2,1,0:T(8,128)S(1)} %constant_dynamic-update-slice_fusion.carried), channel_id=1, source_target_pairs={{0,27},{1,28},{2,29},{3,30},{4,31},{5,32},{6,33},{7,34},{8,35},{9,... | collective-permute-start | bytes 663560 | tf_op jit(solution)/shard_map/ppermute | solution.py:428
  66.3 25.3 %copy-start.1 = (f32[27,16,128]{2,1,0:T(8,128)}, f32[27,16,128]{2,1,0:T(8,128)S(1)}, u32[]{:S(2)}) copy-start(f32[27,16,128]{2,1,0:T(8,128)S(1)} %collective-permute-done.7.boxes2) | copy-start | bytes 663556
  66.4 25.3 %copy-start.2 = (f32[27,16,128]{2,1,0:T(8,128)}, f32[27,16,128]{2,1,0:T(8,128)S(1)}, u32[]{:S(2)}) copy-start(f32[27,16,128]{2,1,0:T(8,128)S(1)} %collective-permute-done.6.boxes0) | copy-start | bytes 663556
  67.5 4.7 %copy-start = (f32[47,16,128]{2,1,0:T(8,128)}, f32[47,16,128]{2,1,0:T(8,128)S(1)}, u32[]{:S(2)}) copy-start(f32[47,16,128]{2,1,0:T(8,128)S(1)} %pad_maximum_fusion.1.after_this) | copy-start | bytes 1155076
  67.5 24.2 %collective-permute-start.8 = (f32[47,16,128]{2,1,0:T(8,128)S(1)}, f32[47,16,128]{2,1,0:T(8,128)S(1)}, u32[]{:S(2)}, u32[]{:S(2)}) collective-permute-start(f32[47,16,128]{2,1,0:T(8,128)S(1)} %pad_maximum_fusion.1.after_this), channel_id=1, source_target_pairs={{0,64},{1,65},{2,66},{3,67},{4,68},{5,69},{6,70},{7,71},{8,72},{9,... | collective-permute-start | bytes 1155080 | tf_op jit(solution)/shard_map/ppermute | solution.py:428
  91.6 0.8 copy-start.3

commit v6 on v5

--- a/solution.py
+++ b/solution.py
@@ -137,19 +137,15 @@
 
 def near_kernel(
     items, points, probes, side, carried, out, carried_out,
-    values, source, target, total, listed, semaphore, *, begin, end
+    values, source, target, total, listed, *, begin, end
 ):
     slots, leaves = items.shape
     leaf_size = target.shape[2]
     pieces = leaf_size // 128
     pairs = leaves // 2
     edge_blocks = NEAR_REACH * pieces
-    if len(carried.shape) == 4:
-        handed_on = carried.at[:, pairs]
-    else:
-        handed_on = carried.at[pl.ds(0, carried_out.shape[0])]
-    handing = pltpu.make_async_copy(handed_on, carried_out, semaphore.at[0])
-    handing.start()
+    for i in range(carried_out.shape[0]):
+        carried_out[i] = carried[i, pairs] if len(carried.shape) == 4 else carried[i]
 
     count = jnp.int32(0)
     for c in range(begin, end):
@@ -224,7 +220,6 @@
     lax.fori_loop(0, (rest + TAIL_GROUP - 1) // TAIL_GROUP, group(TAIL_GROUP, full * GROUP), 0)
     for c in range(begin, end):
         out[:, (c - begin) * leaf_size : (c - begin + 1) * leaf_size] = total[c]
-    handing.wait()
 
 
 def fill_table(table, blocks, start):
@@ -416,7 +411,8 @@
     return [pl.BlockSpec(memory_space=pltpu.SMEM)] * count
 
 
-params = pltpu.CompilerParams(vmem_limit_bytes=60 * 2**20)
+def params(mebibytes):
+    return pltpu.CompilerParams(vmem_limit_bytes=mebibytes * 2**20)
 
 
 def cost(flops):
@@ -457,17 +453,16 @@
             jax.ShapeDtypeStruct((probe_count, NEAR_REACH * leaf_size), f32),
             jax.ShapeDtypeStruct(handed_on, f32),
         ),
-        in_specs=scalars(1) + whole(3) + hbm(1),
-        out_specs=tuple(whole(1) + hbm(1)),
+        in_specs=scalars(1) + whole(4),
+        out_specs=tuple(whole(2)),
         scratch_shapes=[
             pltpu.VMEM((window, 2 * probe_count, leaf_size), bf16),
             pltpu.VMEM((window, leaf_size, FEATURES), bf16),
             pltpu.VMEM((leaves, FEATURES, leaf_size), bf16),
             pltpu.VMEM((leaves, probe_count, leaf_size), f32),
             pltpu.SMEM((leaves * slots + 2 * GROUP,), jnp.int32),
-            copy_semaphores(1),
         ],
-        compiler_params=params,
+        compiler_params=params(16),
         cost_estimate=cost(10_000_000_000),
         name=name,
     )(items, points, probes, side, carried)
@@ -502,7 +497,7 @@
         out_specs=tuple(whole(3)),
         scratch_shapes=[like(probes), like(basis), like(transfer_leaf)]
         + [copy_semaphores(1 + 2 * CHUNKS)],
-        compiler_params=params,
+        compiler_params=params(60),
         name="skeletons",
     )(near_slots, points, probes, basis, transfer_leaf, transfer_box)
 
@@ -540,7 +535,7 @@
         scratch_shapes=[
             pltpu.VMEM(((2 * FAR_REACH + 1) * leaves + 2, 2 * probe_count, 2 * rank), bf16)
         ],
-        compiler_params=params,
+        compiler_params=params(20),
         cost_estimate=cost(8_000_000_000),
         name="far",
     )(far_list, near_slots, before, middle, after, couple_leaf, inner)
@@ -555,7 +550,7 @@
         scratch_shapes=[pltpu.VMEM((count, probe_count, 2 * rank), f32)]
         + [like(array) for array in held]
         + [copy_semaphores(12 + 2 * CHUNKS)],
-        compiler_params=params,
+        compiler_params=params(40),
         name="down",
     )(near_slots, box_list, column_list, more_before, more, more_after, opposite, *held)
 

time: 98.6 us -> 83.5 us (0.85)
  the two profiles are of different devices: /device:TPU:3 before, /device:TPU:1 now
where the time goes in v6:
time: 83.5 us; the launch traced here: 82.5 us
  Pallas kernels  51.2 us (61%)
  starting transfers between devices  17.5 us (21%)
  waiting for transfers between devices  8.45 us (10%)
  local copies, waits for them, and re-layouts  4.73 us (6%)
    pallas_call x4, Pallas kernels, near_call(): pl.pallas_call(functools.partial(near_kernel, begin=begin, end=begin + NE...  29.1 us
    ppermute x9, starting transfers between devices, shifted(): lax.ppermute(array, axis, [(i, (i + by) % devices) for i in range(devices)])  17.5 us
    pallas_call x1, Pallas kernels, per_device(): pl.pallas_call(far_kernel, grid=(leaves // FAR_STEP,), out_shape=jax.Shap...  10.9 us
    ppermute x9, waiting for transfers between devices, shifted(): lax.ppermute(array, axis, [(i, (i + by) % devices) for i in range(devices)])  8.45 us
    pallas_call x1, Pallas kernels, per_device(): pl.pallas_call(down_kernel, out_shape=jax.ShapeDtypeStruct(probes.shape,...  5.96 us
    pallas_call x1, Pallas kernels, per_device(): pl.pallas_call(skeleton_kernel, out_shape=(edges, edges, jax.ShapeDtypeSt...  5.23 us
    unnamed x46, local copies, waits for them, and re-layouts  4.6 us
  transfers between devices with their start and end apart: 9, of which 3 were waited for; matrix products, arithmetic and copies ran while one was open for 0% of the time, Pallas kernels for 49%

profile of v6, /device:TPU:1, one launch (start us, length us, event | category | flops | bytes accessed | tf_op | source)
XLA Modules:
  0.0 82.5 jit_solution(8704987440765838308)
XLA Ops:
  0.0 5.2 %skeletons.1 = (f32[35,16,128]{2,1,0:T(8,128)}, f32[35,16,128]{2,1,0:T(8,128)}, s32[9,32]{1,0:T(8,128)}) custom-call(s32[9,32]{1,0:T(8,128)} %bitcast.16, f32[2,8192]{1,0:T(2,128)} %points.9, f32[16,8192]{1,0:T(8,128)} %probes.7, f32[32,64,256]{2,1,0:T(8,128)} %bitcast.13, f32[32,64,64]{2,1,0:T(8,128)} %transfer_in.3, f32[1,64,64]{2,1,0:T(8,128)} %transfer_box_in.1), custom_call_target="tpu_custom_call" | custom-call | tf_op jit(solution)/shard_map/skeletons/pallas_call | solution.py:493
  5.2 2.5 %collective-permute-start = (f32[35,16,128]{2,1,0:T(8,128)}, f32[35,16,128]{2,1,0:T(8,128)S(1)}, u32[]{:S(2)}, u32[]{:S(2)}) collective-permute-start(f32[35,16,128]{2,1,0:T(8,128)} %get-tuple-element.16.carried), channel_id=1, source_target_pairs={{0,1},{1,2},{2,3},{3,4},{4,5},{5,6},{6,7},{7,8},{8,9},{9,10},{10,1... | collective-permute-start | bytes 860168 | tf_op jit(solution)/shard_map/ppermute | solution.py:424
  7.8 2.8 %collective-permute-start.1 = (f32[35,16,128]{2,1,0:T(8,128)}, f32[35,16,128]{2,1,0:T(8,128)S(1)}, u32[]{:S(2)}, u32[]{:S(2)}) collective-permute-start(f32[35,16,128]{2,1,0:T(8,128)} %get-tuple-element.18.side), channel_id=1, source_target_pairs={{0,127},{1,0},{2,1},{3,2},{4,3},{5,4},{6,5},{7,6},{8,7},{9,8},{10,... | collective-permute-start | bytes 860168 | tf_op jit(solution)/shard_map/ppermute | solution.py:424
  10.6 0.0 copy-start.3
  10.6 1.0 %copy-done.3 = f32[16,8192]{1,0:T(8,128)S(1)} copy-done((f32[16,8192]{1,0:T(8,128)S(1)}, f32[16,8192]{1,0:T(8,128)}, u32[]{:S(2)}) %copy-start.3) | copy-done | bytes 524312
  11.6 0.0 copy-start.7
  11.6 0.8 %copy-done.7 = f32[2,8192]{1,0:T(2,128)S(1)} copy-done((f32[2,8192]{1,0:T(2,128)S(1)}, f32[2,8192]{1,0:T(2,128)}, u32[]{:S(2)}) %copy-start.7) | copy-done | bytes 65560
  12.4 0.0 copy-start.11
  12.4 1.0 %copy-done.11 = f32[35,16,128]{2,1,0:T(8,128)S(1)} copy-done((f32[35,16,128]{2,1,0:T(8,128)S(1)}, f32[35,16,128]{2,1,0:T(8,128)}, u32[]{:S(2)}) %copy-start.11) | copy-done | bytes 286744
  13.4 0.0 copy-start.13
  13.4 1.0 %copy-done.13 = f32[35,16,128]{2,1,0:T(8,128)S(1)} copy-done((f32[35,16,128]{2,1,0:T(8,128)S(1)}, f32[35,16,128]{2,1,0:T(8,128)}, u32[]{:S(2)}) %copy-start.13) | copy-done | bytes 286744
  14.4 0.7 copy-done.14
  15.1 7.1 %near_first.1 = (f32[16,2048]{1,0:T(8,128)S(1)}, f32[17,16,128]{2,1,0:T(8,128)S(1)}) custom-call(s32[9,32]{1,0:T(8,128)S(1)} %copy-done.14, f32[2,8192]{1,0:T(2,128)S(1)} %copy-done.7, f32[16,8192]{1,0:T(8,128)S(1)} %copy-done.3, f32[35,16,128]{2,1,0:T(8,128)S(1)} %copy-done.11, f32[35,16,128]{2,1,0:T(8,128)S(1)} %copy-done.13), custom_call_target="tpu_custom_call" | custom-call | flops 10000000000 | bytes 1048576 | tf_op jit(solution)/shard_map/near_first/pallas_call | solution.py:450
  22.2 0.0 collective-permute-done.side
  22.2 0.0 collective-permute-done.1.side
  22.3 0.5 collective-permute-start.3
  22.8 2.2 %collective-permute-start.2 = (f32[3,17,16,128]{3,2,0,1:T(8,128)S(1)}, f32[3,17,16,128]{3,2,0,1:T(8,128)S(1)}, u32[]{:S(2)}, u32[]{:S(2)}) collective-permute-start(f32[3,17,16,128]{3,2,0,1:T(8,128)S(1)} %pad_maximum_fusion), channel_id=1, source_target_pairs={{0,3},{1,4},{2,5},{3,6},{4,7},{5,8},{6,9},{7,10},{8,11},{9,12},{10... | collective-permute-start | bytes 1253384 | tf_op jit(solution)/shard_map/ppermute | solution.py:424
  25.1 0.0 copy-done.12
  25.1 7.1 %near_second.1 = (f32[16,2048]{1,0:T(8,128)S(1)}, f32[3,16,128]{2,1,0:T(8,128)S(1)}) custom-call(s32[9,32]{1,0:T(8,128)S(1)} %copy-done.14, f32[2,8192]{1,0:T(2,128)S(1)} %copy-done.7, f32[16,8192]{1,0:T(8,128)S(1)} %copy-done.3, f32[35,16,128]{2,1,0:T(8,128)S(1)} %copy-done.12, f32[3,17,16,128]{3,2,1,0:T(8,128)S(1)} %copy.13.carried.middle), custom_call_target="tpu_custom_call" | custom-call | flops 10000000000 | bytes 1048576 | tf_op jit(solution)/shard_map/near_second/pallas_call | solution.py:450
  32.2 0.1 collective-permute-done.3
  32.3 6.4 %collective-permute-done.2 = f32[3,17,16,128]{3,2,0,1:T(8,128)S(1)} collective-permute-done((f32[3,17,16,128]{3,2,0,1:T(8,128)S(1)}, f32[3,17,16,128]{3,2,0,1:T(8,128)S(1)}, u32[]{:S(2)}, u32[]{:S(2)}) %collective-permute-start.2) | collective-permute-done | bytes 417824 | tf_op jit(solution)/shard_map/ppermute | solution.py:424
  38.7 4.3 %collective-permute-start.5 = (f32[9,16,128]{2,1,0:T(8,128)S(1)}, f32[9,16,128]{2,1,0:T(8,128)S(1)}, u32[]{:S(2)}, u32[]{:S(2)}) collective-permute-start(f32[9,16,128]{2,1,0:T(8,128)S(1)} %pad_maximum_fusion.2.carried), channel_id=1, source_target_pairs={{0,119},{1,120},{2,121},{3,122},{4,123},{5,124},{6,125},{7,126},{8... | collective-permute-start | bytes 221192 | tf_op jit(solution)/shard_map/ppermute | solution.py:424
  42.9 0.0 collective-permute-start.4
  43.0 0.0 slice-start.3
  43.0 7.1 %near_third.1 = (f32[16,2048]{1,0:T(8,128)S(1)}, f32[9,16,128]{2,1,0:T(8,128)S(1)}) custom-call(s32[9,32]{1,0:T(8,128)S(1)} %copy-done.14, f32[2,8192]{1,0:T(2,128)S(1)} %copy-done.7, f32[16,8192]{1,0:T(8,128)S(1)} %copy-done.3, f32[35,16,128]{2,1,0:T(8,128)S(1)} %collective-permute-done.side, f32[9,16,128]{2,1,0:T(8,128)S(1)} %pad_maximum_fusion.2.carried), custom_call_target="tpu_custom_call" | custom-call | flops 10000000000 | bytes 1048576 | tf_op jit(solution)/shard_map/near_third/pallas_call | solution.py:450
  50.1 0.0 copy-start.6
  50.1 0.0 copy-start.8
  50.2 2.0 %collective-permute-done.4 = f32[9,16,128]{2,1,0:T(8,128)S(1)} collective-permute-done((f32[9,16,128]{2,1,0:T(8,128)S(1)}, f32[9,16,128]{2,1,0:T(8,128)S(1)}, u32[]{:S(2)}, u32[]{:S(2)}) %collective-permute-start.4) | collective-permute-done | bytes 73760 | tf_op jit(solution)/shard_map/ppermute | solution.py:424
  52.2 0.0 collective-permute-done.5
  52.2 0.0 slice-start.4
  52.2 0.0 slice-start.5
  52.2 0.0 slice-start.6
  52.2 0.0 copy-start
  52.2 0.0 copy-start.1
  52.3 0.0 copy-start.2
  52.3 0.0 copy-start.4
  52.3 0.0 copy-start.5
  52.3 0.0 copy-start.9
  52.3 0.0 copy-start.10
  52.3 0.3 collective-permute-start.7
  52.6 4.8 %collective-permute-start.6 = (f32[27,16,128]{2,1,0:T(8,128)S(1)}, f32[27,16,128]{2,1,0:T(8,128)S(1)}, u32[]{:S(2)}, u32[]{:S(2)}) collective-permute-start(f32[27,16,128]{2,1,0:T(8,128)S(1)} %constant_dynamic-update-slice_fusion.carried), channel_id=1, source_target_pairs={{0,27},{1,28},{2,29},{3,30},{4,31},{5,32},{6,33},{7,34},{8,35},{9,... | collective-permute-start | bytes 663560 | tf_op jit(solution)/shard_map/ppermute | solution.py:424
  57.4 7.8 %near_fourth.1 = (f32[16,2048]{1,0:T(8,128)S(1)}, f32[27,16,128]{2,1,0:T(8,128)S(1)}) custom-call(s32[9,32]{1,0:T(8,128)S(1)} %copy-done.14, f32[2,8192]{1,0:T(2,128)S(1)} %copy-done.7, f32[16,8192]{1,0:T(8,128)S(1)} %copy-done.3, f32[35,16,128]{2,1,0:T(8,128)S(1)} %collective-permute-done.1.side, f32[27,16,128]{2,1,0:T(8,128)S(1)} %constant_dynamic-update-slice_fusion.carried), custom_call_target="tpu_custom_call" | custom-call | flops 10000000000 | bytes 1048576 | tf_op jit(solution)/shard_map/near_fourth/pallas_call | solution.py:450
  65.1 0.0 collective-permute-done.7.boxes2
  65.2 0.0 collective-permute-done.6.boxes0
  65.2 0.1 collective-permute-start.8
  65.3 0.0 slice-done
  65.3 0.0 slice-done.1
  65.3 0.0 slice-done.2
  65.3 0.0 slice-done.3
  65.4 0.0 copy-done.6
  65.4 0.0 copy-done.8
  65.4 0.0 slice-done.4
  65.4 0.0 slice-done.5
  65.4 0.0 slice-done.6
  65.4 10.9 %far.2.far_in = f32[16,16,128]{2,1,0:T(8,128)S(1)} custom-call(s32[32,27]{1,0:T(8,128)S(1)} %copy-done.8, s32[9,32]{1,0:T(8,128)S(1)} %bitcast.17, f32[3,17,16,128]{3,2,1,0:T(8,128)S(1)} %copy.14.before, f32[3,17,16,128]{3,2,1,0:T(8,128)S(1)} %copy.13.carried.middle, f32[3,17,16,128]{3,2,1,0:T(8,128)S(1)} %copy.16.after, f32[32,27,64,64]{3,2,1,0:T(8,128)S(1)} %bitcast.12, ...), custom_call_target="tpu_custom_call" | custom-call | flops 8000000000 | bytes 1048576 | tf_op jit(solution)/shard_map/far/pallas_call | solution.py:526
  76.3 0.0 collective-permute-done.8.boxes3
  76.4 0.0 copy-done
  76.4 0.0 copy-done.1
  76.4 0.0 copy-done.2
  76.4 0.0 copy-done.4
  76.4 0.0 copy-done.5
  76.4 0.0 copy-done.9
  76.4 0.0 copy-done.10
  76.4 6.0 %down.1 = f32[16,8192]{1,0:T(8,128)} custom-call(s32[9,32]{1,0:T(8,128)S(1)} %bitcast.18, s32[1,27]{1,0:T(1,128)S(1)} %copy-done.9, s32[1,4]{1,0:T(1,128)S(1)} %copy-done.10, f32[27,16,128]{2,1,0:T(8,128)S(1)} %collective-permute-done.6.boxes0, f32[27,16,128]{2,1,0:T(8,128)S(1)} %get-tuple-element.22.boxes1, ...), custom_call_target="tpu_custom_call" | custom-call | tf_op jit(solution)/shard_map/down/pallas_call | solution.py:545
  (21 shorter events, 0.2 us)
Async XLA Ops:
  5.2 16.9 %collective-permute-start = (f32[35,16,128]{2,1,0:T(8,128)}, f32[35,16,128]{2,1,0:T(8,128)S(1)}, u32[]{:S(2)}, u32[]{:S(2)}) collective-permute-start(f32[35,16,128]{2,1,0:T(8,128)} %get-tuple-element.16.carried), channel_id=1, source_target_pairs={{0,1},{1,2},{2,3},{3,4},{4,5},{5,6},{6,7},{7,8},{8,9},{9,10},{10,1... | collective-permute-start | bytes 860168 | tf_op jit(solution)/shard_map/ppermute | solution.py:424
  7.8 14.4 %collective-permute-start.1 = (f32[35,16,128]{2,1,0:T(8,128)}, f32[35,16,128]{2,1,0:T(8,128)S(1)}, u32[]{:S(2)}, u32[]{:S(2)}) collective-permute-start(f32[35,16,128]{2,1,0:T(8,128)} %get-tuple-element.18.side), channel_id=1, source_target_pairs={{0,127},{1,0},{2,1},{3,2},{4,3},{5,4},{6,5},{7,6},{8,7},{9,8},{10,... | collective-permute-start | bytes 860168 | tf_op jit(solution)/shard_map/ppermute | solution.py:424
  10.6 1.0 %copy-start.3 = (f32[16,8192]{1,0:T(8,128)S(1)}, f32[16,8192]{1,0:T(8,128)}, u32[]{:S(2)}) copy-start(f32[16,8192]{1,0:T(8,128)} %probes.7) | copy-start | bytes 1572868
  11.6 0.8 %copy-start.7 = (f32[2,8192]{1,0:T(2,128)S(1)}, f32[2,8192]{1,0:T(2,128)}, u32[]{:S(2)}) copy-start(f32[2,8192]{1,0:T(2,128)} %points.9) | copy-start | bytes 196612
  12.4 1.0 %copy-start.11 = (f32[35,16,128]{2,1,0:T(8,128)S(1)}, f32[35,16,128]{2,1,0:T(8,128)}, u32[]{:S(2)}) copy-start(f32[35,16,128]{2,1,0:T(8,128)} %get-tuple-element.18.side) | copy-start | bytes 860164
  13.4 1.0 %copy-start.13 = (f32[35,16,128]{2,1,0:T(8,128)S(1)}, f32[35,16,128]{2,1,0:T(8,128)}, u32[]{:S(2)}) copy-start(f32[35,16,128]{2,1,0:T(8,128)} %get-tuple-element.16.carried) | copy-start | bytes 860164
  14.4 0.7 copy-start.14
  15.1 10.0 %copy-start.12 = (f32[35,16,128]{2,1,0:T(8,128)S(1)}, f32[35,16,128]{2,1,0:T(8,128)}, u32[]{:S(2)}) copy-start(f32[35,16,128]{2,1,0:T(8,128)} %get-tuple-element.18.side) | copy-start | bytes 860164
  22.3 10.0 %collective-permute-start.3 = (f32[3,17,16,128]{3,2,0,1:T(8,128)S(1)}, f32[3,17,16,128]{3,2,0,1:T(8,128)S(1)}, u32[]{:S(2)}, u32[]{:S(2)}) collective-permute-start(f32[3,17,16,128]{3,2,0,1:T(8,128)S(1)} %pad_maximum_fusion), channel_id=1, source_target_pairs={{0,125},{1,126},{2,127},{3,0},{4,1},{5,2},{6,3},{7,4},{8,5},{9,6},... | collective-permute-start | bytes 1253384 | tf_op jit(solution)/shard_map/ppermute | solution.py:424
  22.8 15.8 %collective-permute-start.2 = (f32[3,17,16,128]{3,2,0,1:T(8,128)S(1)}, f32[3,17,16,128]{3,2,0,1:T(8,128)S(1)}, u32[]{:S(2)}, u32[]{:S(2)}) collective-permute-start(f32[3,17,16,128]{3,2,0,1:T(8,128)S(1)} %pad_maximum_fusion), channel_id=1, source_target_pairs={{0,3},{1,4},{2,5},{3,6},{4,7},{5,8},{6,9},{7,10},{8,11},{9,12},{10... | collective-permute-start | bytes 1253384 | tf_op jit(solution)/shard_map/ppermute | solution.py:424
  38.7 13.5 %collective-permute-start.5 = (f32[9,16,128]{2,1,0:T(8,128)S(1)}, f32[9,16,128]{2,1,0:T(8,128)S(1)}, u32[]{:S(2)}, u32[]{:S(2)}) collective-permute-start(f32[9,16,128]{2,1,0:T(8,128)S(1)} %pad_maximum_fusion.2.carried), channel_id=1, source_target_pairs={{0,119},{1,120},{2,121},{3,122},{4,123},{5,124},{6,125},{7,126},{8... | collective-permute-start | bytes 221192 | tf_op jit(solution)/shard_map/ppermute | solution.py:424
  42.9 9.2 %collective-permute-start.4 = (f32[9,16,128]{2,1,0:T(8,128)S(1)}, f32[9,16,128]{2,1,0:T(8,128)S(1)}, u32[]{:S(2)}, u32[]{:S(2)}) collective-permute-start(f32[9,16,128]{2,1,0:T(8,128)S(1)} %pad_maximum_fusion.2.carried), channel_id=1, source_target_pairs={{0,9},{1,10},{2,11},{3,12},{4,13},{5,14},{6,15},{7,16},{8,17},{9,1... | collective-permute-start | bytes 221192 | tf_op jit(solution)/shard_map/ppermute | solution.py:424
  42.9 22.4 %slice-start = ((s8[28311552]{0:T(1024)(128)(4,1)}), s8[4194304]{0:T(1024)(128)(4,1)S(1)}, s32[]{:S(2)}) async-start(s8[28311552]{0:T(1024)(128)(4,1)} %bitcast.11), calls=%async_computation | async-start | bytes 8388608
  42.9 22.4 %slice-start.1 = ((s8[28311552]{0:T(1024)(128)(4,1)}), s8[4194304]{0:T(1024)(128)(4,1)S(1)}, s32[]{:S(2)}) async-start(s8[28311552]{0:T(1024)(128)(4,1)} %bitcast.11), calls=%async_computation.1 | async-start | bytes 8388608
  43.0 22.4 %slice-start.2 = ((s8[28311552]{0:T(1024)(128)(4,1)}), s8[4194304]{0:T(1024)(128)(4,1)S(1)}, s32[]{:S(2)}) async-start(s8[28311552]{0:T(1024)(128)(4,1)} %bitcast.11), calls=%async_computation.2 | async-start | bytes 8388608
  43.0 22.4 %slice-start.3 = ((s8[28311552]{0:T(1024)(128)(4,1)}), s8[4194304]{0:T(1024)(128)(4,1)S(1)}, s32[]{:S(2)}) async-start(s8[28311552]{0:T(1024)(128)(4,1)} %bitcast.11), calls=%async_computation.3 | async-start | bytes 8388608
  50.1 15.3 %copy-start.6 = (s32[32,9]{0,1:T(8,128)S(1)}, s32[32,9]{0,1:T(8,128)}, u32[]{:S(2)}) copy-start(s32[32,9]{0,1:T(8,128)} %param.20) | copy-start | bytes 3460
  50.1 15.3 %copy-start.8 = (s32[32,27]{1,0:T(8,128)S(1)}, s32[32,27]{1,0:T(8,128)}, u32[]{:S(2)}) copy-start(s32[32,27]{1,0:T(8,128)} %far.3) | copy-start | bytes 10372
  52.2 13.2 %slice-start.4 = ((s8[28311552]{0:T(1024)(128)(4,1)}), s8[4194304]{0:T(1024)(128)(4,1)S(1)}, s32[]{:S(2)}) async-start(s8[28311552]{0:T(1024)(128)(4,1)} %bitcast.11), calls=%async_computation.4 | async-start | bytes 8388608
  52.2 13.2 %slice-start.5 = ((s8[28311552]{0:T(1024)(128)(4,1)}), s8[4194304]{0:T(1024)(128)(4,1)S(1)}, s32[]{:S(2)}) async-start(s8[28311552]{0:T(1024)(128)(4,1)} %bitcast.11), calls=%async_computation.5 | async-start | bytes 8388608
  52.2 13.2 %slice-start.6 = ((s8[28311552]{0:T(1024)(128)(4,1)}), s8[3145728]{0:T(1024)(128)(4,1)S(1)}, s32[]{:S(2)}) async-start(s8[28311552]{0:T(1024)(128)(4,1)} %bitcast.11), calls=%async_computation.6 | async-start | bytes 6291456
  52.2 24.1 %copy-start = (f32[32,256,64]{1,2,0:T(8,128)S(1)}, f32[32,256,64]{1,2,0:T(8,128)}, u32[]{:S(2)}) copy-start(f32[32,256,64]{1,2,0:T(8,128)} %param.14) | copy-start | bytes 6291460
  52.2 24.1 %copy-start.1 = (f32[32,64,64]{2,1,0:T(8,128)S(1)}, f32[32,64,64]{2,1,0:T(8,128)}, u32[]{:S(2)}) copy-start(f32[32,64,64]{2,1,0:T(8,128)} %transfer_in.3) | copy-start | bytes 1572868
  52.3 24.1 %copy-start.2 = (f32[1,27,64,64]{3,2,1,0:T(8,128)S(1)}, f32[1,27,64,64]{3,2,1,0:T(8,128)}, u32[]{:S(2)}) copy-start(f32[1,27,64,64]{3,2,1,0:T(8,128)} %couple_box_in.1) | copy-start | bytes 1327108
  52.3 24.1 %copy-start.4 = (f32[1,64,64]{2,1,0:T(8,128)S(1)}, f32[1,64,64]{2,1,0:T(8,128)}, u32[]{:S(2)}) copy-start(f32[1,64,64]{2,1,0:T(8,128)} %transfer_box_in.1) | copy-start | bytes 49156
  52.3 24.1 %copy-start.5 = (f32[1,4,64,64]{3,2,1,0:T(8,128)S(1)}, f32[1,4,64,64]{3,2,1,0:T(8,128)}, u32[]{:S(2)}) copy-start(f32[1,4,64,64]{3,2,1,0:T(8,128)} %couple_column_in.1) | copy-start | bytes 196612
  52.3 24.1 %copy-start.9 = (s32[1,27]{1,0:T(1,128)S(1)}, s32[1,27]{1,0:T(1,128)}, u32[]{:S(2)}) copy-start(s32[1,27]{1,0:T(1,128)} %box_list.1) | copy-start | bytes 328
  52.3 24.1 %copy-start.10 = (s32[1,4]{1,0:T(1,128)S(1)}, s32[1,4]{1,0:T(1,128)}, u32[]{:S(2)}) copy-start(s32[1,4]{1,0:T(1,128)} %column_list.1) | copy-start | bytes 52
  52.3 12.8 %collective-permute-start.7 = (f32[27,16,128]{2,1,0:T(8,128)S(1)}, f32[27,16,128]{2,1,0:T(8,128)S(1)}, u32[]{:S(2)}, u32[]{:S(2)}) collective-permute-start(f32[27,16,128]{2,1,0:T(8,128)S(1)} %constant_dynamic-update-slice_fusion.carried), channel_id=1, source_target_pairs={{0,101},{1,102},{2,103},{3,104},{4,105},{5,106},{6,107},{7,108},{8... | collective-permute-start | bytes 663560 | tf_op jit(solution)/shard_map/ppermute | solution.py:424
  52.6 12.6 %collective-permute-start.6 = (f32[27,16,128]{2,1,0:T(8,128)S(1)}, f32[27,16,128]{2,1,0:T(8,128)S(1)}, u32[]{:S(2)}, u32[]{:S(2)}) collective-permute-start(f32[27,16,128]{2,1,0:T(8,128)S(1)} %constant_dynamic-update-slice_fusion.carried), channel_id=1, source_target_pairs={{0,27},{1,28},{2,29},{3,30},{4,31},{5,32},{6,33},{7,34},{8,35},{9,... | collective-permute-start | bytes 663560 | tf_op jit(solution)/shard_map/ppermute | solution.py:424
  65.2 11.1 %collective-permute-start.8 = (f32[47,16,128]{2,1,0:T(8,128)S(1)}, f32[47,16,128]{2,1,0:T(8,128)S(1)}, u32[]{:S(2)}, u32[]{:S(2)}) collective-permute-start(f32[47,16,128]{2,1,0:T(8,128)S(1)} %pad_maximum_fusion.1.after_this), channel_id=1, source_target_pairs={{0,64},{1,65},{2,66},{3,67},{4,68},{5,69},{6,70},{7,71},{8,72},{9,... | collective-permute-start | bytes 1155080 | tf_op jit(solution)/shard_map/ppermute | solution.py:424

commit v7 on v6

--- a/solution.py
+++ b/solution.py
@@ -69,7 +69,7 @@
 
 
 def skeleton_kernel(
-    near, points, probes_in, basis_in, transfer_in, transfer_box, out, out_first, items,
+    near, points, probes_in, basis_in, transfer_in, transfer_box, out, out_first, sent, items,
     probes, basis, transfer_leaf, semaphores,
 ):
     leaves, rank, leaf_size = basis.shape
@@ -99,9 +99,9 @@
     for side, start in ((out, width - edge), (out_first, 0)):
         for j in range(edge // 128):
             lanes = slice(start + j * 128, start + (j + 1) * 128)
-            side[pairs + 1 + j] = probes[:, lanes]
-            side[pairs + 1 + edge // 128, j : j + 1, :] = points[0:1, lanes]
-            side[pairs + 2 + edge // 128, j : j + 1, :] = points[1:2, lanes]
+            side[pairs + j] = probes[:, lanes]
+            side[pairs + edge // 128, j : j + 1, :] = points[0:1, lanes]
+            side[pairs + 1 + edge // 128, j : j + 1, :] = points[1:2, lanes]
 
     def leaf_probes(c):
         return stacked_halves(probes[:, c * leaf_size : (c + 1) * leaf_size])
@@ -131,46 +131,44 @@
     )
     box = summed(wide)[:, :rank]
     block = jnp.concatenate([box, product3(box, transfer_box[0])], axis=1)
-    out[pairs] = block
-    out_first[pairs] = block
+    for i in range(sent.shape[0]):
+        sent[i] = block
 
 
 def near_kernel(
-    items, points, probes, side, carried, out, carried_out,
-    values, source, target, total, listed, *, begin, end
+    items, points, probes, left, right, out, values, source, target, total, listed
 ):
     slots, leaves = items.shape
     leaf_size = target.shape[2]
     pieces = leaf_size // 128
     pairs = leaves // 2
     edge_blocks = NEAR_REACH * pieces
-    for i in range(carried_out.shape[0]):
-        carried_out[i] = carried[i, pairs] if len(carried.shape) == 4 else carried[i]
 
     count = jnp.int32(0)
-    for c in range(begin, end):
+    for c in range(leaves):
         for k in range(slots):
             item = items[k, c]
             listed[count] = item
             count = count + jnp.where(item != 0, 1, 0)
     for u in range(TAIL_GROUP):
-        listed[count + u] = begin + (begin + NEAR_REACH) * 64
+        listed[count + u] = NEAR_REACH * 64
 
     ones = jnp.ones((3, leaf_size), f32)
     pad = jnp.zeros((2, leaf_size), f32)
-    for w in range(begin, end + 2 * NEAR_REACH):
+    for w in range(leaves + 2 * NEAR_REACH):
         own = NEAR_REACH <= w < NEAR_REACH + leaves
         if own:
             lanes = slice((w - NEAR_REACH) * leaf_size, (w - NEAR_REACH + 1) * leaf_size)
             place, value = points[:, lanes], probes[:, lanes]
         else:
+            side = left if w < NEAR_REACH else right
             first = (w if w < NEAR_REACH else w - NEAR_REACH - leaves) * pieces
-            parts = range(first, first + pieces)
-            value = jnp.concatenate([side[pairs + 1 + j] for j in parts], axis=1)
+            runs = range(first, first + pieces)
+            value = jnp.concatenate([side[pairs + j] for j in runs], axis=1)
             place = jnp.concatenate(
                 [
                     jnp.concatenate(
-                        [side[pairs + 1 + edge_blocks + d, j : j + 1, :] for j in parts], axis=1
+                        [side[pairs + edge_blocks + d, j : j + 1, :] for j in runs], axis=1
                     )
                     for d in range(2)
                 ],
@@ -188,7 +186,7 @@
         norms = jnp.concatenate([norm1, norm2, rest - norm2], axis=0)
         rows = jnp.concatenate([first, second, first, second, norms, ones, pad], axis=0)
         source[w] = rows.T.astype(bf16)
-        if begin <= w - NEAR_REACH < end:
+        if own:
             target[w - NEAR_REACH] = jnp.concatenate(
                 [-2.0 * first, -2.0 * first, -2.0 * second, -2.0 * second, ones, norms, pad], axis=0
             ).astype(bf16)
@@ -218,8 +216,8 @@
     lax.fori_loop(0, full, group(GROUP, 0), 0)
     rest = count - full * GROUP
     lax.fori_loop(0, (rest + TAIL_GROUP - 1) // TAIL_GROUP, group(TAIL_GROUP, full * GROUP), 0)
-    for c in range(begin, end):
-        out[:, (c - begin) * leaf_size : (c - begin + 1) * leaf_size] = total[c]
+    for c in range(leaves):
+        out[:, c * leaf_size : (c + 1) * leaf_size] = total[c]
 
 
 def fill_table(table, blocks, start):
@@ -277,11 +275,10 @@
     return wide[:16, :rank] + wide[16:, :rank] + wide[:16, rank:]
 
 
-def far_kernel(far, near, before, middle, after, couples, after_this, out, table):
+def far_kernel(far, near, before, middle, after, couples, out, table):
     step = pl.program_id(0)
     per_step, slots, rank, _ = couples.shape
     leaves = far.shape[0]
-    pairs = leaves // 2
     empty = (2 * FAR_REACH + 1) * leaves
     low_lanes = lax.broadcasted_iota(jnp.int32, (32, 2 * rank), 1) < rank
 
@@ -289,7 +286,7 @@
     def _():
         for b in range(3):
             for place, blocks in ((b, before), (3 + b, middle), (6 + b, after)):
-                fill_table(table, blocks.at[b, :pairs], place * leaves)
+                fill_table(table, blocks.at[b], place * leaves)
         table[empty] = jnp.zeros_like(table[empty])
         table[empty + 1] = jnp.zeros_like(table[empty])
 
@@ -310,43 +307,33 @@
 
 
 def down_kernel(
-    near, box_list, column_list, boxes0, boxes1, boxes2, boxes3, couple_box_in, couple_column_in,
-    transfer_box_in, far_in, near0_in, near1_in, near2_in, near3_in, transfer_in, basis_in, out,
-    gathered, couple_box, couple_column, transfer_box, far_leaf, near0, near1, near2, near3,
-    transfer_leaf, basis, semaphores,
+    box_list, column_list, boxes_in, couple_box_in, couple_column_in,
+    transfer_box_in, far_in, near_in, transfer_in, basis_in, out,
+    gathered, couple_box, couple_column, transfer_box, far_leaf, near, transfer_leaf, basis,
+    semaphores,
 ):
     leaves, rank, leaf_size = basis.shape
     slots, column_slots = box_list.shape[1], column_list.shape[1]
-    boxes = gathered.shape[0]
     low_lanes = lax.broadcasted_iota(jnp.int32, (32, 2 * rank), 1) < rank
-    runs, place = [], 0
-    for part in (boxes0, boxes1, boxes2, boxes3):
-        runs.append((part, gathered.at[pl.ds(place, part.shape[0])]))
-        place += part.shape[0]
     arriving = copies(
-        runs
-        + [
+        [
+            (boxes_in, gathered),
             (couple_box_in, couple_box),
             (couple_column_in, couple_column),
             (transfer_box_in, transfer_box),
             (far_in, far_leaf),
-            (near0_in, near0),
-            (near1_in, near1),
-            (near2_in, near2),
-            (near3_in, near3),
+            (near_in, near),
         ]
         + parts(transfer_in, transfer_leaf)
         + parts(basis_in, basis),
         semaphores,
     )
-    later = 12 + CHUNKS
-    for copy in arriving[:7]:
+    later = 6 + CHUNKS
+    for copy in arriving[:4]:
         copy.wait()
 
-    first = near[0, 0] // leaves - boxes0.shape[0] - boxes1.shape[0] // 2
-
     def box_row(entry):
-        return (jnp.where(entry >= 0, entry, 0) - first) & (boxes - 1)
+        return jnp.where(entry >= 0, entry, 0)
 
     def pick(k):
         entry = box_list[0, k]
@@ -374,7 +361,7 @@
     far_column = coupled(jnp.concatenate(pieces, axis=1), couple_column[0])
     down_box = far_box + product3(far_column, transfer_box[0], ((1,), (1,)))
 
-    for copy in arriving[7:later]:
+    for copy in arriving[4:later]:
         copy.wait()
     high, low = halves(transfer_leaf[...].reshape(leaves * rank, rank))
     both = stacked_halves(down_box)
@@ -397,10 +384,8 @@
         result = wide[:64] + wide[64:] + rest
         for j in range(4):
             c = 4 * m + j
-            held = (near0, near1, near2, near3)[c // NEAR_REACH]
-            place = c % NEAR_REACH
-            near_value = held[:, place * leaf_size : (place + 1) * leaf_size]
-            out[:, c * leaf_size : (c + 1) * leaf_size] = near_value + result[16 * j : 16 * j + 16]
+            lanes = slice(c * leaf_size, (c + 1) * leaf_size)
+            out[:, lanes] = near[:, lanes] + result[16 * j : 16 * j + 16]
 
 
 def whole(count):
@@ -434,38 +419,6 @@
 
 def copy_semaphores(count):
     return pltpu.SemaphoreType.DMA((count,))
-
-
-def near_call(name, begin, items, points, probes, side, carried):
-    slots, leaves = items.shape
-    probe_count = probes.shape[0]
-    leaf_size = probes.shape[1] // leaves
-    window = leaves + 2 * NEAR_REACH
-    if carried.ndim == 4:
-        handed_on = (carried.shape[0],) + carried.shape[2:]
-    else:
-        handed_on = (min(carried.shape[0], 27),) + carried.shape[1:]
-    if name == "near_first":
-        handed_on = (leaves // 2 + 1,) + carried.shape[1:]
-    return pl.pallas_call(
-        functools.partial(near_kernel, begin=begin, end=begin + NEAR_REACH),
-        out_shape=(
-            jax.ShapeDtypeStruct((probe_count, NEAR_REACH * leaf_size), f32),
-            jax.ShapeDtypeStruct(handed_on, f32),
-        ),
-        in_specs=scalars(1) + whole(4),
-        out_specs=tuple(whole(2)),
-        scratch_shapes=[
-            pltpu.VMEM((window, 2 * probe_count, leaf_size), bf16),
-            pltpu.VMEM((window, leaf_size, FEATURES), bf16),
-            pltpu.VMEM((leaves, FEATURES, leaf_size), bf16),
-            pltpu.VMEM((leaves, probe_count, leaf_size), f32),
-            pltpu.SMEM((leaves * slots + 2 * GROUP,), jnp.int32),
-        ],
-        compiler_params=params(16),
-        cost_estimate=cost(10_000_000_000),
-        name=name,
-    )(items, points, probes, side, carried)
 
 
 def per_device(
@@ -487,50 +440,57 @@
     near_slots = near_list.T
     basis = basis.transpose(0, 2, 1)
     pairs = leaves // 2
-    blocks = pairs + 1 + NEAR_REACH * leaf_size // 128 + 2
+    blocks = pairs + NEAR_REACH * leaf_size // 128 + 2
+    devices = lax.axis_size(ring)
 
     edges = jax.ShapeDtypeStruct((blocks, probe_count, 2 * rank), f32)
-    bundle_last, bundle_first, items = pl.pallas_call(
+    bundle_last, bundle_first, sent, items = pl.pallas_call(
         skeleton_kernel,
-        out_shape=(edges, edges, jax.ShapeDtypeStruct(near_slots.shape, jnp.int32)),
+        out_shape=(
+            edges,
+            edges,
+            jax.ShapeDtypeStruct((devices, probe_count, 2 * rank), f32),
+            jax.ShapeDtypeStruct(near_slots.shape, jnp.int32),
+        ),
         in_specs=whole(2) + hbm(3) + whole(1),
-        out_specs=tuple(whole(3)),
+        out_specs=tuple(whole(4)),
         scratch_shapes=[like(probes), like(basis), like(transfer_leaf)]
         + [copy_semaphores(1 + 2 * CHUNKS)],
         compiler_params=params(60),
         name="skeletons",
     )(near_slots, points, probes, basis, transfer_leaf, transfer_box)
 
-    near_leaves = functools.partial(near_call, items=items, points=points, probes=probes)
     left, right = shifted(bundle_last, ring, 1), shifted(bundle_first, ring, -1)
-    near1, own = near_leaves("near_first", NEAR_REACH, side=bundle_first, carried=bundle_last)
-
-    middle = jnp.stack([left[: pairs + 1], own, right[: pairs + 1]])
+    boxes = lax.all_to_all(sent, ring, 0, 0, tiled=True)
+    middle = jnp.stack([left[:pairs], bundle_last[:pairs], right[:pairs]])
     before, after = shifted(middle, ring, 3), shifted(middle, ring, -3)
-    near2, three = near_leaves("near_second", 2 * NEAR_REACH, side=bundle_first, carried=middle)
-
-    nine = jnp.concatenate([before[:, pairs], three, after[:, pairs]])
-    nine_before, nine_after = shifted(nine, ring, 9), shifted(nine, ring, -9)
-    near0, nine = near_leaves("near_third", 0, side=left, carried=nine)
-
-    more = jnp.concatenate([nine_before, nine, nine_after])
-    more_before, more_after = shifted(more, ring, 27), shifted(more, ring, -27)
-    near3, more = near_leaves("near_fourth", leaves - NEAR_REACH, side=right, carried=more)
-
-    count = lax.axis_size(ring)
-    missing = (count - 3 * more.shape[0] - more.shape[0]) // 2
-    inner = jnp.concatenate([more_before[-missing:], more, more_after[:missing]])
-    opposite = shifted(inner, ring, count // 2)
-
-    window = pl.BlockSpec(middle.shape, lambda i: (0, 0, 0, 0))
+
+    window = leaves + 2 * NEAR_REACH
+    near_values = pl.pallas_call(
+        near_kernel,
+        out_shape=jax.ShapeDtypeStruct(probes.shape, f32),
+        in_specs=scalars(1) + whole(4),
+        out_specs=pl.BlockSpec(memory_space=pltpu.VMEM),
+        scratch_shapes=[
+            pltpu.VMEM((window, 2 * probe_count, leaf_size), bf16),
+            pltpu.VMEM((window, leaf_size, FEATURES), bf16),
+            pltpu.VMEM((leaves, FEATURES, leaf_size), bf16),
+            pltpu.VMEM((leaves, probe_count, leaf_size), f32),
+            pltpu.SMEM((leaves * near_slots.shape[0] + 2 * GROUP,), jnp.int32),
+        ],
+        compiler_params=params(16),
+        cost_estimate=cost(20_000_000_000),
+        name="near",
+    )(items, points, probes, left, right)
+
+    blocks3 = pl.BlockSpec(middle.shape, lambda i: (0, 0, 0, 0))
     far_leaf = pl.pallas_call(
         far_kernel,
         grid=(leaves // FAR_STEP,),
         out_shape=jax.ShapeDtypeStruct((pairs, probe_count, 2 * rank), f32),
         in_specs=scalars(2)
-        + [window] * 3
-        + [pl.BlockSpec((FAR_STEP,) + couple_leaf.shape[1:], lambda i: (i, 0, 0, 0))]
-        + hbm(1),
+        + [blocks3] * 3
+        + [pl.BlockSpec((FAR_STEP,) + couple_leaf.shape[1:], lambda i: (i, 0, 0, 0))],
         out_specs=pl.BlockSpec((FAR_STEP // 2, probe_count, 2 * rank), lambda i: (i, 0, 0)),
         scratch_shapes=[
             pltpu.VMEM(((2 * FAR_REACH + 1) * leaves + 2, 2 * probe_count, 2 * rank), bf16)
@@ -538,21 +498,19 @@
         compiler_params=params(20),
         cost_estimate=cost(8_000_000_000),
         name="far",
-    )(far_list, near_slots, before, middle, after, couple_leaf, inner)
-
-    held = (couple_box, couple_column, transfer_box, far_leaf, near0, near1, near2, near3)
+    )(far_list, near_slots, before, middle, after, couple_leaf)
+
+    held = (boxes, couple_box, couple_column, transfer_box, far_leaf, near_values)
     held += (transfer_leaf, basis)
     return pl.pallas_call(
         down_kernel,
         out_shape=jax.ShapeDtypeStruct(probes.shape, f32),
-        in_specs=scalars(3) + hbm(14),
+        in_specs=scalars(2) + hbm(8),
         out_specs=pl.BlockSpec(memory_space=pltpu.VMEM),
-        scratch_shapes=[pltpu.VMEM((count, probe_count, 2 * rank), f32)]
-        + [like(array) for array in held]
-        + [copy_semaphores(12 + 2 * CHUNKS)],
+        scratch_shapes=[like(array) for array in held] + [copy_semaphores(6 + 2 * CHUNKS)],
         compiler_params=params(40),
         name="down",
-    )(near_slots, box_list, column_list, more_before, more, more_after, opposite, *held)
+    )(box_list, column_list, *held)
 
 
 def solution(mesh):

time: 83.5 us -> 90.9 us (1.089)
  the two profiles are of different devices: /device:TPU:1 before, /device:TPU:0 now
where the time goes in v7:
time: 90.9 us; the launch traced here: 90.7 us
  Pallas kernels  46.1 us (51%)
  waiting for transfers between devices  19.3 us (21%)
  starting transfers between devices  18.4 us (20%)
  local copies, waits for them, and re-layouts  6.6 us (7%)
    pallas_call x1, Pallas kernels, per_device(): pl.pallas_call(near_kernel, out_shape=jax.ShapeDtypeStruct(probes.shape,...  25.2 us
    ppermute x4, waiting for transfers between devices, shifted(): lax.ppermute(array, axis, [(i, (i + by) % devices) for i in range(devices)])  19.3 us
    ppermute x4, starting transfers between devices, shifted(): lax.ppermute(array, axis, [(i, (i + by) % devices) for i in range(devices)])  12.7 us
    pallas_call x1, Pallas kernels, per_device(): pl.pallas_call(far_kernel, grid=(leaves // FAR_STEP,), out_shape=jax.Shap...  10.9 us
    all_to_all x1, starting transfers between devices, per_device(): boxes = lax.all_to_all(sent, ring, 0, 0, tiled=True)  5.75 us
    unnamed x42, local copies, waits for them, and re-layouts  5.64 us
    pallas_call x1, Pallas kernels, per_device(): pl.pallas_call(skeleton_kernel, out_shape=(edges, edges, jax.ShapeDtypeSt...  5.45 us
    pallas_call x1, Pallas kernels, per_device(): pl.pallas_call(down_kernel, out_shape=jax.ShapeDtypeStruct(probes.shape,...  4.51 us
  transfers between devices with their start and end apart: 5, of which 1 were waited for; matrix products, arithmetic and copies ran while one was open for 1% of the time, Pallas kernels for 40%

profile of v7, /device:TPU:0, one launch (start us, length us, event | category | flops | bytes accessed | tf_op | source)
XLA Modules:
  0.0 90.7 jit_solution(11656164402715964728)
XLA Ops:
  0.0 5.5 %skeletons.1 = (f32[34,16,128]{2,1,0:T(8,128)}, f32[34,16,128]{2,1,0:T(8,128)}, f32[128,16,128]{2,1,0:T(8,128)}, s32[9,32]{1,0:T(8,128)}) custom-call(s32[9,32]{1,0:T(8,128)} %bitcast.12, f32[2,8192]{1,0:T(2,128)} %points.3, f32[16,8192]{1,0:T(8,128)} %probes.1, f32[32,64,256]{2,1,0:T(8,128)} %bitcast.10, f32[32,64,64]{2,1,0:T(8,128)} %transfer_in.3, ...), custom_call_target="tpu_custom_call" | custom-call | tf_op jit(solution)/shard_map/skeletons/pallas_call | solution.py:447
  5.5 8.3 %collective-permute-start.1 = (f32[34,16,128]{2,1,0:T(8,128)}, f32[34,16,128]{2,1,0:T(8,128)S(1)}, u32[]{:S(2)}, u32[]{:S(2)}) collective-permute-start(f32[34,16,128]{2,1,0:T(8,128)} %get-tuple-element.11), channel_id=1, source_target_pairs={{0,127},{1,0},{2,1},{3,2},{4,3},{5,4},{6,5},{7,6},{8,7},{9,8},{10,... | collective-permute-start | bytes 835592 | tf_op jit(solution)/shard_map/ppermute | solution.py:409
  13.7 5.8 %all-to-all-start = ((f32[128,16,128]{2,1,0:T(8,128)}), f32[128,16,128]{2,1,0:T(8,128)}, u32[]{:S(2)}, u32[]{:S(2)}) async-start(f32[128,16,128]{2,1,0:T(8,128)} %get-tuple-element.9), calls=%async_computation | async-start | bytes 2097152 | tf_op jit(solution)/shard_map/all_to_all | solution.py:464
  19.5 1.1 %collective-permute-start = (f32[34,16,128]{2,1,0:T(8,128)}, f32[34,16,128]{2,1,0:T(8,128)S(1)}, u32[]{:S(2)}, u32[]{:S(2)}) collective-permute-start(f32[34,16,128]{2,1,0:T(8,128)} %get-tuple-element.10), channel_id=1, source_target_pairs={{0,1},{1,2},{2,3},{3,4},{4,5},{5,6},{6,7},{7,8},{8,9},{9,10},{10,1... | collective-permute-start | bytes 835592 | tf_op jit(solution)/shard_map/ppermute | solution.py:409
  20.6 0.9 %slice_bitcast_fusion.2 = f32[1,16,16,128]{3,2,1,0:T(8,128)S(1)} fusion(f32[34,16,128]{2,1,0:T(8,128)} %get-tuple-element.10), kind=kLoop, calls=%fused_computation.3 | loop fusion | bytes 262144 | tf_op jit(solution)/shard_map/stack | solution.py:465
  21.5 0.0 collective-permute-done.1.right
  21.6 19.3 %collective-permute-done.left = f32[34,16,128]{2,1,0:T(8,128)S(1)} collective-permute-done((f32[34,16,128]{2,1,0:T(8,128)}, f32[34,16,128]{2,1,0:T(8,128)S(1)}, u32[]{:S(2)}, u32[]{:S(2)}) %collective-permute-start) | collective-permute-done | bytes 278560 | tf_op jit(solution)/shard_map/ppermute | solution.py:409
  40.8 0.0 slice-start
  40.9 1.4 %collective-permute-start.3 = (f32[3,16,16,128]{3,2,1,0:T(8,128)S(1)}, f32[3,16,16,128]{3,2,1,0:T(8,128)S(1)}, u32[]{:S(2)}, u32[]{:S(2)}) collective-permute-start(f32[3,16,16,128]{3,2,1,0:T(8,128)S(1)} %pad_maximum_fusion.middle), channel_id=1, source_target_pairs={{0,125},{1,126},{2,127},{3,0},{4,1},{5,2},{6,3},{7,4},{8,5},{9,6},... | collective-permute-start | bytes 1179656 | tf_op jit(solution)/shard_map/ppermute | solution.py:409
  42.3 1.9 %collective-permute-start.2 = (f32[3,16,16,128]{3,2,1,0:T(8,128)S(1)}, f32[3,16,16,128]{3,2,1,0:T(8,128)S(1)}, u32[]{:S(2)}, u32[]{:S(2)}) collective-permute-start(f32[3,16,16,128]{3,2,1,0:T(8,128)S(1)} %pad_maximum_fusion.middle), channel_id=1, source_target_pairs={{0,3},{1,4},{2,5},{3,6},{4,7},{5,8},{6,9},{7,10},{8,11},{9,12},{10... | collective-permute-start | bytes 1179656 | tf_op jit(solution)/shard_map/ppermute | solution.py:409
  44.2 0.0 copy-start.3
  44.2 1.0 %copy-done.3 = f32[16,8192]{1,0:T(8,128)S(1)} copy-done((f32[16,8192]{1,0:T(8,128)S(1)}, f32[16,8192]{1,0:T(8,128)}, u32[]{:S(2)}) %copy-start.3) | copy-done | bytes 524312
  45.2 0.0 copy-start.8
  45.2 0.8 copy-done.8
  46.1 0.0 copy-start.13
  46.1 0.7 copy-done.13
  46.8 0.0 slice-start.1
  46.8 0.0 slice-start.2
  46.8 0.0 slice-start.3
  46.8 0.0 slice-start.4
  46.8 0.0 slice-start.5
  46.8 0.0 slice-start.6
  46.8 0.0 copy-start.9
  46.8 0.0 copy-start.10
  46.8 25.2 %near.1.near_in = f32[16,8192]{1,0:T(8,128)S(1)} custom-call(s32[9,32]{1,0:T(8,128)S(1)} %copy-done.13, f32[2,8192]{1,0:T(2,128)S(1)} %copy-done.8, f32[16,8192]{1,0:T(8,128)S(1)} %copy-done.3, f32[34,16,128]{2,1,0:T(8,128)S(1)} %collective-permute-done.left, f32[34,16,128]{2,1,0:T(8,128)S(1)} %collective-permute-done.1.right), custom_call_target="tpu_custom_call" | custom-call | flops 20000000000 | bytes 1048576 | tf_op jit(solution)/shard_map/near/pallas_call | solution.py:469
  72.0 0.0 copy-start.4
  72.1 0.8 copy-done.4
  72.8 0.0 copy-start
  72.8 0.0 copy-start.1
  72.8 0.0 copy-start.6
  72.8 0.0 copy-start.7
  72.8 0.0 copy-start.11
  72.9 0.0 copy-start.12
  72.9 0.0 collective-permute-done.3.after
  72.9 0.0 collective-permute-done.2.before
  72.9 0.0 slice-done
  72.9 0.0 slice-done.1
  72.9 0.0 slice-done.2
  72.9 0.0 slice-done.3
  72.9 0.0 slice-done.4
  72.9 0.0 slice-done.5
  73.0 0.0 slice-done.6
  73.0 0.0 copy-done.9
  73.0 0.0 copy-done.10
  73.0 10.9 %far.2.far_in = f32[16,16,128]{2,1,0:T(8,128)S(1)} custom-call(s32[32,27]{1,0:T(8,128)S(1)} %copy-done.10, s32[9,32]{1,0:T(8,128)S(1)} %bitcast.13, f32[3,16,16,128]{3,2,1,0:T(8,128)S(1)} %collective-permute-done.2.before, f32[3,16,16,128]{3,2,1,0:T(8,128)S(1)} %pad_maximum_fusion.middle, f32[3,16,16,128]{3,2,1,0:T(8,128)S(1)} %collective-permute-done.3.after, ...), custom_call_target="tpu_custom_call" | custom-call | flops 8000000000 | bytes 1048576 | tf_op jit(solution)/shard_map/far/pallas_call | solution.py:487
  83.9 0.0 all-to-all-done.boxes_in
  83.9 0.0 copy-done
  83.9 0.0 copy-done.1
  83.9 0.0 copy-done.6
  83.9 0.0 copy-done.7
  84.0 0.0 copy-done.11
  84.0 0.0 copy-done.12
  84.0 0.0 copy-start.2
  84.0 1.2 %copy-done.2 = f32[1,27,64,64]{3,2,1,0:T(8,128)S(1)} copy-done((f32[1,27,64,64]{3,2,1,0:T(8,128)S(1)}, f32[1,27,64,64]{3,2,1,0:T(8,128)}, u32[]{:S(2)}) %copy-start.2) | copy-done | bytes 442392
  85.1 0.0 copy-start.5
  85.2 1.0 %copy-done.5 = f32[16,8192]{1,0:T(8,128)S(1)} copy-done((f32[16,8192]{1,0:T(8,128)S(1)}, f32[16,8192]{1,0:T(8,128)}, u32[]{:S(2)}) %copy-start.5) | copy-done | bytes 524312
  86.2 4.5 %down.1 = f32[16,8192]{1,0:T(8,128)} custom-call(s32[1,27]{1,0:T(1,128)S(1)} %copy-done.11, s32[1,4]{1,0:T(1,128)S(1)} %copy-done.12, f32[128,16,128]{2,1,0:T(8,128)} %all-to-all-done.boxes_in, f32[1,27,64,64]{3,2,1,0:T(8,128)S(1)} %copy-done.2, f32[1,4,64,64]{3,2,1,0:T(8,128)S(1)} %copy-done.7, f32[1,64,64]{2,1,0:T(8,128)S(1)} %copy-done.6, ...), custom_call_target="tpu_custom_call" | custom-call | tf_op jit(solution)/shard_map/down/pallas_call | solution.py:505
  (4 shorter events, 0.0 us)
Async XLA Ops:
  5.5 16.1 %collective-permute-start.1 = (f32[34,16,128]{2,1,0:T(8,128)}, f32[34,16,128]{2,1,0:T(8,128)S(1)}, u32[]{:S(2)}, u32[]{:S(2)}) collective-permute-start(f32[34,16,128]{2,1,0:T(8,128)} %get-tuple-element.11), channel_id=1, source_target_pairs={{0,127},{1,0},{2,1},{3,2},{4,3},{5,4},{6,5},{7,6},{8,7},{9,8},{10,... | collective-permute-start | bytes 835592 | tf_op jit(solution)/shard_map/ppermute | solution.py:409
  13.7 70.2 %all-to-all-start = ((f32[128,16,128]{2,1,0:T(8,128)}), f32[128,16,128]{2,1,0:T(8,128)}, u32[]{:S(2)}, u32[]{:S(2)}) async-start(f32[128,16,128]{2,1,0:T(8,128)} %get-tuple-element.9), calls=%async_computation | async-start | bytes 2097152 | tf_op jit(solution)/shard_map/all_to_all | solution.py:464
  19.5 21.3 %collective-permute-start = (f32[34,16,128]{2,1,0:T(8,128)}, f32[34,16,128]{2,1,0:T(8,128)S(1)}, u32[]{:S(2)}, u32[]{:S(2)}) collective-permute-start(f32[34,16,128]{2,1,0:T(8,128)} %get-tuple-element.10), channel_id=1, source_target_pairs={{0,1},{1,2},{2,3},{3,4},{4,5},{5,6},{6,7},{7,8},{8,9},{9,10},{10,1... | collective-permute-start | bytes 835592 | tf_op jit(solution)/shard_map/ppermute | solution.py:409
  40.8 32.1 %slice-start = ((s8[28311552]{0:T(1024)(128)(4,1)}), s8[4194304]{0:T(1024)(128)(4,1)S(1)}, s32[]{:S(2)}) async-start(s8[28311552]{0:T(1024)(128)(4,1)} %bitcast.8), calls=%async_computation.1 | async-start | bytes 8388608
  40.9 32.0 %collective-permute-start.3 = (f32[3,16,16,128]{3,2,1,0:T(8,128)S(1)}, f32[3,16,16,128]{3,2,1,0:T(8,128)S(1)}, u32[]{:S(2)}, u32[]{:S(2)}) collective-permute-start(f32[3,16,16,128]{3,2,1,0:T(8,128)S(1)} %pad_maximum_fusion.middle), channel_id=1, source_target_pairs={{0,125},{1,126},{2,127},{3,0},{4,1},{5,2},{6,3},{7,4},{8,5},{9,6},... | collective-permute-start | bytes 1179656 | tf_op jit(solution)/shard_map/ppermute | solution.py:409
  42.3 30.6 %collective-permute-start.2 = (f32[3,16,16,128]{3,2,1,0:T(8,128)S(1)}, f32[3,16,16,128]{3,2,1,0:T(8,128)S(1)}, u32[]{:S(2)}, u32[]{:S(2)}) collective-permute-start(f32[3,16,16,128]{3,2,1,0:T(8,128)S(1)} %pad_maximum_fusion.middle), channel_id=1, source_target_pairs={{0,3},{1,4},{2,5},{3,6},{4,7},{5,8},{6,9},{7,10},{8,11},{9,12},{10... | collective-permute-start | bytes 1179656 | tf_op jit(solution)/shard_map/ppermute | solution.py:409
  44.2 1.0 %copy-start.3 = (f32[16,8192]{1,0:T(8,128)S(1)}, f32[16,8192]{1,0:T(8,128)}, u32[]{:S(2)}) copy-start(f32[16,8192]{1,0:T(8,128)} %probes.1) | copy-start | bytes 1572868
  45.2 0.8 copy-start.8
  46.1 0.7 copy-start.13
  46.8 26.1 %slice-start.1 = ((s8[28311552]{0:T(1024)(128)(4,1)}), s8[4194304]{0:T(1024)(128)(4,1)S(1)}, s32[]{:S(2)}) async-start(s8[28311552]{0:T(1024)(128)(4,1)} %bitcast.8), calls=%async_computation.2 | async-start | bytes 8388608
  46.8 26.1 %slice-start.2 = ((s8[28311552]{0:T(1024)(128)(4,1)}), s8[4194304]{0:T(1024)(128)(4,1)S(1)}, s32[]{:S(2)}) async-start(s8[28311552]{0:T(1024)(128)(4,1)} %bitcast.8), calls=%async_computation.3 | async-start | bytes 8388608
  46.8 26.1 %slice-start.3 = ((s8[28311552]{0:T(1024)(128)(4,1)}), s8[4194304]{0:T(1024)(128)(4,1)S(1)}, s32[]{:S(2)}) async-start(s8[28311552]{0:T(1024)(128)(4,1)} %bitcast.8), calls=%async_computation.4 | async-start | bytes 8388608
  46.8 26.2 %slice-start.4 = ((s8[28311552]{0:T(1024)(128)(4,1)}), s8[4194304]{0:T(1024)(128)(4,1)S(1)}, s32[]{:S(2)}) async-start(s8[28311552]{0:T(1024)(128)(4,1)} %bitcast.8), calls=%async_computation.5 | async-start | bytes 8388608
  46.8 26.2 %slice-start.5 = ((s8[28311552]{0:T(1024)(128)(4,1)}), s8[4194304]{0:T(1024)(128)(4,1)S(1)}, s32[]{:S(2)}) async-start(s8[28311552]{0:T(1024)(128)(4,1)} %bitcast.8), calls=%async_computation.6 | async-start | bytes 8388608
  46.8 26.2 %slice-start.6 = ((s8[28311552]{0:T(1024)(128)(4,1)}), s8[3145728]{0:T(1024)(128)(4,1)S(1)}, s32[]{:S(2)}) async-start(s8[28311552]{0:T(1024)(128)(4,1)} %bitcast.8), calls=%async_computation.7 | async-start | bytes 6291456
  46.8 26.2 %copy-start.9 = (s32[32,9]{0,1:T(8,128)S(1)}, s32[32,9]{0,1:T(8,128)}, u32[]{:S(2)}) copy-start(s32[32,9]{0,1:T(8,128)} %param.20) | copy-start | bytes 3460
  46.8 26.2 %copy-start.10 = (s32[32,27]{1,0:T(8,128)S(1)}, s32[32,27]{1,0:T(8,128)}, u32[]{:S(2)}) copy-start(s32[32,27]{1,0:T(8,128)} %far.3) | copy-start | bytes 10372
  72.0 0.8 copy-start.4
  72.8 11.1 %copy-start = (f32[32,256,64]{1,2,0:T(8,128)S(1)}, f32[32,256,64]{1,2,0:T(8,128)}, u32[]{:S(2)}) copy-start(f32[32,256,64]{1,2,0:T(8,128)} %param.14) | copy-start | bytes 6291460
  72.8 11.1 %copy-start.1 = (f32[32,64,64]{2,1,0:T(8,128)S(1)}, f32[32,64,64]{2,1,0:T(8,128)}, u32[]{:S(2)}) copy-start(f32[32,64,64]{2,1,0:T(8,128)} %transfer_in.3) | copy-start | bytes 1572868
  72.8 11.1 %copy-start.6 = (f32[1,64,64]{2,1,0:T(8,128)S(1)}, f32[1,64,64]{2,1,0:T(8,128)}, u32[]{:S(2)}) copy-start(f32[1,64,64]{2,1,0:T(8,128)} %transfer_box_in.1) | copy-start | bytes 49156
  72.8 11.1 %copy-start.7 = (f32[1,4,64,64]{3,2,1,0:T(8,128)S(1)}, f32[1,4,64,64]{3,2,1,0:T(8,128)}, u32[]{:S(2)}) copy-start(f32[1,4,64,64]{3,2,1,0:T(8,128)} %couple_column_in.1) | copy-start | bytes 196612
  72.8 11.1 %copy-start.11 = (s32[1,27]{1,0:T(1,128)S(1)}, s32[1,27]{1,0:T(1,128)}, u32[]{:S(2)}) copy-start(s32[1,27]{1,0:T(1,128)} %box_list.1) | copy-start | bytes 328
  72.9 11.1 %copy-start.12 = (s32[1,4]{1,0:T(1,128)S(1)}, s32[1,4]{1,0:T(1,128)}, u32[]{:S(2)}) copy-start(s32[1,4]{1,0:T(1,128)} %column_list.1) | copy-start | bytes 52
  84.0 1.2 %copy-start.2 = (f32[1,27,64,64]{3,2,1,0:T(8,128)S(1)}, f32[1,27,64,64]{3,2,1,0:T(8,128)}, u32[]{:S(2)}) copy-start(f32[1,27,64,64]{3,2,1,0:T(8,128)} %couple_box_in.1) | copy-start | bytes 1327108
  85.1 1.0 %copy-start.5 = (f32[16,8192]{1,0:T(8,128)S(1)}, f32[16,8192]{1,0:T(8,128)}, u32[]{:S(2)}) copy-start(f32[16,8192]{1,0:T(8,128)} %copy-done.4) | copy-start | bytes 1572868

commit v8 on v7

--- a/solution.py
+++ b/solution.py
@@ -13,7 +13,7 @@
 FEATURES = 16
 GROUP = 12
 TAIL_GROUP = 4
-FAR_STEP = 2
+FAR_STEP = 8
 CHUNKS = 4
 
 matern_rate = math.sqrt(3.0) / 0.1
@@ -69,7 +69,7 @@
 
 
 def skeleton_kernel(
-    near, points, probes_in, basis_in, transfer_in, transfer_box, out, out_first, sent, items,
+    near, far, points, probes_in, basis_in, transfer_in, transfer_box, out, out_first, sent, items,
     probes, basis, transfer_leaf, semaphores,
 ):
     leaves, rank, leaf_size = basis.shape
@@ -91,7 +91,10 @@
         for j in range(k + 1, slots):
             times = times + jnp.where(rows[j] == rows[k], 1, 0)
         place = rows[k] - rows[0] + leaf + NEAR_REACH
-        items[k : k + 1, :] = jnp.where(new, leaf + place * 64 + times * 4096, 0)
+        items[k : k + 1, 0:leaves] = jnp.where(new, leaf + place * 64 + times * 4096, 0)
+    empty = (2 * FAR_REACH + 1) * leaves
+    place = far[...] - (near[0:1, 0:1] - FAR_REACH * leaves)
+    items[slots : slots + leaves, 0 : far.shape[1]] = jnp.where(far[...] >= 0, place, empty)
 
     arriving[0].wait()
     width = probes.shape[1]
@@ -135,11 +138,11 @@
         sent[i] = block
 
 
-def near_kernel(
-    items, points, probes, left, right, out, values, source, target, total, listed
+def near_field(
+    items, points, probes, left, right, out, values, source, target, total, listed, arriving
 ):
-    slots, leaves = items.shape
-    leaf_size = target.shape[2]
+    leaves, _, leaf_size = target.shape
+    slots = items.shape[0] - leaves
     pieces = leaf_size // 128
     pairs = leaves // 2
     edge_blocks = NEAR_REACH * pieces
@@ -153,6 +156,8 @@
     for u in range(TAIL_GROUP):
         listed[count + u] = NEAR_REACH * 64
 
+    for copy in arriving:
+        copy.wait()
     ones = jnp.ones((3, leaf_size), f32)
     pad = jnp.zeros((2, leaf_size), f32)
     for w in range(leaves + 2 * NEAR_REACH):
@@ -275,35 +280,54 @@
     return wide[:16, :rank] + wide[16:, :rank] + wide[:16, rank:]
 
 
-def far_kernel(far, near, before, middle, after, couples, out, table):
-    step = pl.program_id(0)
-    per_step, slots, rank, _ = couples.shape
-    leaves = far.shape[0]
+def field_kernel(
+    items, points_in, probes_in, left, right, before, middle, after, couples_in, out,
+    far_out, points, probes, values, source, target, total, listed, table, couples, semaphores,
+    held_semaphores,
+):
+    leaves, slots, rank, _ = couples.shape
+    steps = leaves // FAR_STEP
+
+    held = copies([(points_in, points), (probes_in, probes)], held_semaphores)
+
+    def arriving(step):
+        run = pl.ds(step * FAR_STEP, FAR_STEP)
+        return pltpu.make_async_copy(couples_in.at[run], couples.at[run], semaphores.at[step])
+
+    def start(step, carry):
+        arriving(step).start()
+        return carry
+
+    lax.fori_loop(0, steps, start, 0)
+    near_field(
+        items, points, probes, left, right, out, values, source, target, total, listed, held
+    )
+
     empty = (2 * FAR_REACH + 1) * leaves
     low_lanes = lax.broadcasted_iota(jnp.int32, (32, 2 * rank), 1) < rank
-
-    @pl.when(step == 0)
-    def _():
-        for b in range(3):
-            for place, blocks in ((b, before), (3 + b, middle), (6 + b, after)):
-                fill_table(table, blocks.at[b], place * leaves)
-        table[empty] = jnp.zeros_like(table[empty])
-        table[empty + 1] = jnp.zeros_like(table[empty])
-
-    base = near[0, 0] - FAR_REACH * leaves
-
-    def far_leaf(u):
-        c = step * per_step + u
-
+    for b in range(3):
+        for place, blocks in ((b, before), (3 + b, middle), (6 + b, after)):
+            fill_table(table, blocks.at[b], place * leaves)
+    table[empty] = jnp.zeros_like(table[empty])
+    table[empty + 1] = jnp.zeros_like(table[empty])
+    first_row = items.shape[0] - leaves
+
+    def far_leaf(c):
         def picks(start, count):
-            rows = [far[c, k] if k < slots else -1 for k in range(start, start + count)]
-            rows = [jnp.where(row >= 0, row - base, empty) for row in rows]
+            listed_here = range(start, start + count)
+            rows = [items[first_row + c, k] if k < slots else empty for k in listed_here]
             return picked(table, rows, low_lanes)
 
-        return coupled_pairs(picks, couples.at[u])
-
-    for u in range(0, per_step, 2):
-        out[u // 2] = jnp.concatenate([far_leaf(u), far_leaf(u + 1)], axis=1)
+        return coupled_pairs(picks, couples.at[c])
+
+    def far_step(step, carry):
+        arriving(step).wait()
+        for u in range(0, FAR_STEP, 2):
+            c = step * FAR_STEP + u
+            far_out[c // 2] = jnp.concatenate([far_leaf(c), far_leaf(c + 1)], axis=1)
+        return carry
+
+    lax.fori_loop(0, steps, far_step, 0)
 
 
 def down_kernel(
@@ -450,55 +474,48 @@
             edges,
             edges,
             jax.ShapeDtypeStruct((devices, probe_count, 2 * rank), f32),
-            jax.ShapeDtypeStruct(near_slots.shape, jnp.int32),
+            jax.ShapeDtypeStruct((near_slots.shape[0] + leaves, 128), jnp.int32),
         ),
-        in_specs=whole(2) + hbm(3) + whole(1),
+        in_specs=whole(3) + hbm(3) + whole(1),
         out_specs=tuple(whole(4)),
         scratch_shapes=[like(probes), like(basis), like(transfer_leaf)]
         + [copy_semaphores(1 + 2 * CHUNKS)],
         compiler_params=params(60),
         name="skeletons",
-    )(near_slots, points, probes, basis, transfer_leaf, transfer_box)
+    )(near_slots, far_list, points, probes, basis, transfer_leaf, transfer_box)
 
     left, right = shifted(bundle_last, ring, 1), shifted(bundle_first, ring, -1)
+    sent, left, right = lax.optimization_barrier((sent, left, right))
     boxes = lax.all_to_all(sent, ring, 0, 0, tiled=True)
     middle = jnp.stack([left[:pairs], bundle_last[:pairs], right[:pairs]])
     before, after = shifted(middle, ring, 3), shifted(middle, ring, -3)
 
     window = leaves + 2 * NEAR_REACH
-    near_values = pl.pallas_call(
-        near_kernel,
-        out_shape=jax.ShapeDtypeStruct(probes.shape, f32),
-        in_specs=scalars(1) + whole(4),
-        out_specs=pl.BlockSpec(memory_space=pltpu.VMEM),
+    near_values, far_leaf = pl.pallas_call(
+        field_kernel,
+        out_shape=(
+            jax.ShapeDtypeStruct(probes.shape, f32),
+            jax.ShapeDtypeStruct((pairs, probe_count, 2 * rank), f32),
+        ),
+        in_specs=scalars(1) + hbm(2) + whole(5) + hbm(1),
+        out_specs=tuple(whole(2)),
         scratch_shapes=[
+            like(points),
+            like(probes),
             pltpu.VMEM((window, 2 * probe_count, leaf_size), bf16),
             pltpu.VMEM((window, leaf_size, FEATURES), bf16),
             pltpu.VMEM((leaves, FEATURES, leaf_size), bf16),
             pltpu.VMEM((leaves, probe_count, leaf_size), f32),
             pltpu.SMEM((leaves * near_slots.shape[0] + 2 * GROUP,), jnp.int32),
+            pltpu.VMEM(((2 * FAR_REACH + 1) * leaves + 2, 2 * probe_count, 2 * rank), bf16),
+            like(couple_leaf),
+            copy_semaphores(leaves // FAR_STEP),
+            copy_semaphores(2),
         ],
-        compiler_params=params(16),
-        cost_estimate=cost(20_000_000_000),
-        name="near",
-    )(items, points, probes, left, right)
-
-    blocks3 = pl.BlockSpec(middle.shape, lambda i: (0, 0, 0, 0))
-    far_leaf = pl.pallas_call(
-        far_kernel,
-        grid=(leaves // FAR_STEP,),
-        out_shape=jax.ShapeDtypeStruct((pairs, probe_count, 2 * rank), f32),
-        in_specs=scalars(2)
-        + [blocks3] * 3
-        + [pl.BlockSpec((FAR_STEP,) + couple_leaf.shape[1:], lambda i: (i, 0, 0, 0))],
-        out_specs=pl.BlockSpec((FAR_STEP // 2, probe_count, 2 * rank), lambda i: (i, 0, 0)),
-        scratch_shapes=[
-            pltpu.VMEM(((2 * FAR_REACH + 1) * leaves + 2, 2 * probe_count, 2 * rank), bf16)
-        ],
-        compiler_params=params(20),
-        cost_estimate=cost(8_000_000_000),
-        name="far",
-    )(far_list, near_slots, before, middle, after, couple_leaf)
+        compiler_params=params(60),
+        cost_estimate=cost(30_000_000_000),
+        name="near_far",
+    )(items, points, probes, left, right, before, middle, after, couple_leaf)
 
     held = (boxes, couple_box, couple_column, transfer_box, far_leaf, near_values)
     held += (transfer_leaf, basis)
@@ -508,7 +525,7 @@
         in_specs=scalars(2) + hbm(8),
         out_specs=pl.BlockSpec(memory_space=pltpu.VMEM),
         scratch_shapes=[like(array) for array in held] + [copy_semaphores(6 + 2 * CHUNKS)],
-        compiler_params=params(40),
+        compiler_params=params(60),
         name="down",
     )(box_list, column_list, *held)
 

time: 90.9 us -> 86.2 us (0.948)
  the two profiles are of different devices: /device:TPU:0 before, /device:TPU:65 now
where the time goes in v8:
time: 86.2 us; the launch traced here: 85.1 us
  Pallas kernels  46.9 us (54%)
  starting transfers between devices  21 us (24%)
  waiting for transfers between devices  14.5 us (17%)
  local copies, waits for them, and re-layouts  2.68 us (3%)
    pallas_call x1, Pallas kernels, per_device(): pl.pallas_call(field_kernel, out_shape=(jax.ShapeDtypeStruct(probes.shape...  36.4 us
    all_to_all x1, starting transfers between devices, per_device(): boxes = lax.all_to_all(sent, ring, 0, 0, tiled=True)  14.6 us
    ppermute x4, waiting for transfers between devices, shifted(): lax.ppermute(array, axis, [(i, (i + by) % devices) for i in range(devices)])  14.5 us
    ppermute x4, starting transfers between devices, shifted(): lax.ppermute(array, axis, [(i, (i + by) % devices) for i in range(devices)])  6.39 us
    pallas_call x1, Pallas kernels, per_device(): pl.pallas_call(skeleton_kernel, out_shape=(edges, edges, jax.ShapeDtypeSt...  5.51 us
    pallas_call x1, Pallas kernels, per_device(): pl.pallas_call(down_kernel, out_shape=jax.ShapeDtypeStruct(probes.shape,...  4.94 us
  transfers between devices with their start and end apart: 5, of which 2 were waited for; matrix products, arithmetic and copies ran while one was open for 1% of the time, Pallas kernels for 43%

profile of v8, /device:TPU:65, one launch (start us, length us, event | category | flops | bytes accessed | tf_op | source)
XLA Modules:
  0.0 85.1 jit_solution(11903273616644425858)
XLA Ops:
  0.0 5.5 %skeletons.1 = (f32[34,16,128]{2,1,0:T(8,128)}, f32[34,16,128]{2,1,0:T(8,128)}, f32[128,16,128]{2,1,0:T(8,128)}, s32[41,128]{1,0:T(8,128)}) custom-call(s32[9,32]{1,0:T(8,128)} %bitcast.10, s32[32,27]{1,0:T(8,128)} %far.1, f32[2,8192]{1,0:T(2,128)} %points_in.1, f32[16,8192]{1,0:T(8,128)} %probes_in.3, f32[32,64,256]{2,1,0:T(8,128)} %bitcast.8, ...), custom_call_target="tpu_custom_call" | custom-call | tf_op jit(solution)/shard_map/skeletons/pallas_call | solution.py:471
  5.5 0.1 collective-permute-start.1
  5.6 1.5 %collective-permute-start = (f32[34,16,128]{2,1,0:T(8,128)}, f32[34,16,128]{2,1,0:T(8,128)S(1)}, u32[]{:S(2)}, u32[]{:S(2)}) collective-permute-start(f32[34,16,128]{2,1,0:T(8,128)} %get-tuple-element.15), channel_id=1, source_target_pairs={{0,1},{1,2},{2,3},{3,4},{4,5},{5,6},{6,7},{7,8},{8,9},{9,10},{10,1... | collective-permute-start | bytes 835592 | tf_op jit(solution)/shard_map/ppermute | solution.py:433
  7.1 0.9 %slice_bitcast_fusion.1 = f32[1,16,16,128]{3,2,1,0:T(8,128)S(1)} fusion(f32[34,16,128]{2,1,0:T(8,128)} %get-tuple-element.15), kind=kLoop, calls=%fused_computation.2 | loop fusion | bytes 262144 | tf_op jit(solution)/shard_map/stack | solution.py:490
  8.0 5.3 %collective-permute-done.1.right = f32[34,16,128]{2,1,0:T(8,128)S(1)} collective-permute-done((f32[34,16,128]{2,1,0:T(8,128)}, f32[34,16,128]{2,1,0:T(8,128)S(1)}, u32[]{:S(2)}, u32[]{:S(2)}) %collective-permute-start.1) | collective-permute-done | bytes 278560 | tf_op jit(solution)/shard_map/ppermute | solution.py:433
  13.3 0.0 copy-start.2
  13.3 0.0 collective-permute-done.left
  13.4 0.0 copy-start.3
  13.4 0.0 copy-start.1
  13.4 4.6 %collective-permute-start.3 = (f32[3,16,16,128]{3,2,1,0:T(8,128)S(1)}, f32[3,16,16,128]{3,2,1,0:T(8,128)S(1)}, u32[]{:S(2)}, u32[]{:S(2)}) collective-permute-start(f32[3,16,16,128]{3,2,1,0:T(8,128)S(1)} %pad_maximum_fusion.middle), channel_id=1, source_target_pairs={{0,125},{1,126},{2,127},{3,0},{4,1},{5,2},{6,3},{7,4},{8,5},{9,6},... | collective-permute-start | bytes 1179656 | tf_op jit(solution)/shard_map/ppermute | solution.py:433
  18.0 0.3 collective-permute-start.2
  18.3 14.6 %all-to-all-start = ((f32[128,16,128]{2,1,0:T(8,128)}), f32[128,16,128]{2,1,0:T(8,128)S(1)}, u32[]{:S(2)}, u32[]{:S(2)}) async-start(f32[128,16,128]{2,1,0:T(8,128)} %get-tuple-element.17), calls=%async_computation | async-start | bytes 2097152 | tf_op jit(solution)/shard_map/all_to_all | solution.py:489
  32.9 0.0 collective-permute-done.3.after
  32.9 0.0 copy-start.4
  32.9 9.1 %collective-permute-done.2.before = f32[3,16,16,128]{3,2,1,0:T(8,128)S(1)} collective-permute-done((f32[3,16,16,128]{3,2,1,0:T(8,128)S(1)}, f32[3,16,16,128]{3,2,1,0:T(8,128)S(1)}, u32[]{:S(2)}, u32[]{:S(2)}) %collective-permute-start.2) | collective-permute-done | bytes 393248 | tf_op jit(solution)/shard_map/ppermute | solution.py:433
  42.0 0.0 copy-start.5
  42.0 0.0 copy-done.2
  42.0 0.0 copy-done.3
  42.0 0.0 copy-done.1
  42.0 0.0 copy-done.4
  42.0 0.7 copy-done.5
  42.8 36.4 %near_far.1 = (f32[16,8192]{1,0:T(8,128)}, f32[16,16,128]{2,1,0:T(8,128)}) custom-call(s32[41,128]{1,0:T(8,128)} %get-tuple-element.18.items, f32[2,8192]{1,0:T(2,128)} %points_in.1, f32[16,8192]{1,0:T(8,128)} %probes_in.3, f32[34,16,128]{2,1,0:T(8,128)} %copy-done.3, f32[34,16,128]{2,1,0:T(8,128)} %copy-done.2, f32[3,16,16,128]{3,2,1,0:T(8,128)} %copy-done.5, ...), custom_call_target="tpu_custom_call" | custom-call | flops 30000001024 | bytes 1048576 | tf_op jit(solution)/shard_map/near_far/pallas_call | solution.py:494
  79.2 0.0 all-to-all-done.boxes_in
  79.2 0.0 copy-start
  79.2 1.0 %copy-done = f32[128,16,128]{2,1,0:T(8,128)} copy-done((f32[128,16,128]{2,1,0:T(8,128)}, f32[128,16,128]{2,1,0:T(8,128)S(1)}, u32[]{:S(2)}) %copy-start) | copy-done | bytes 1048600
  80.2 4.9 %down.1 = f32[16,8192]{1,0:T(8,128)} custom-call(s32[1,27]{1,0:T(1,128)} %box_list.1, s32[1,4]{1,0:T(1,128)} %column_list.1, f32[128,16,128]{2,1,0:T(8,128)} %copy-done, f32[1,27,64,64]{3,2,1,0:T(8,128)} %couple_box_in.1, f32[1,4,64,64]{3,2,1,0:T(8,128)} %couple_column_in.1, f32[1,64,64]{2,1,0:T(8,128)} %transfer_box_in.1, ...), custom_call_target="tpu_custom_call" | custom-call | tf_op jit(solution)/shard_map/down/pallas_call | solution.py:522
  (2 shorter events, 0.0 us)
Async XLA Ops:
  5.5 7.8 %collective-permute-start.1 = (f32[34,16,128]{2,1,0:T(8,128)}, f32[34,16,128]{2,1,0:T(8,128)S(1)}, u32[]{:S(2)}, u32[]{:S(2)}) collective-permute-start(f32[34,16,128]{2,1,0:T(8,128)} %get-tuple-element.16), channel_id=1, source_target_pairs={{0,127},{1,0},{2,1},{3,2},{4,3},{5,4},{6,5},{7,6},{8,7},{9,8},{10,... | collective-permute-start | bytes 835592 | tf_op jit(solution)/shard_map/ppermute | solution.py:433
  5.6 7.8 %collective-permute-start = (f32[34,16,128]{2,1,0:T(8,128)}, f32[34,16,128]{2,1,0:T(8,128)S(1)}, u32[]{:S(2)}, u32[]{:S(2)}) collective-permute-start(f32[34,16,128]{2,1,0:T(8,128)} %get-tuple-element.15), channel_id=1, source_target_pairs={{0,1},{1,2},{2,3},{3,4},{4,5},{5,6},{6,7},{7,8},{8,9},{9,10},{10,1... | collective-permute-start | bytes 835592 | tf_op jit(solution)/shard_map/ppermute | solution.py:433
  13.3 28.7 %copy-start.2 = (f32[34,16,128]{2,1,0:T(8,128)}, f32[34,16,128]{2,1,0:T(8,128)S(1)}, u32[]{:S(2)}) copy-start(f32[34,16,128]{2,1,0:T(8,128)S(1)} %collective-permute-done.1.right) | copy-start | bytes 835588
  13.4 28.6 %copy-start.3 = (f32[34,16,128]{2,1,0:T(8,128)}, f32[34,16,128]{2,1,0:T(8,128)S(1)}, u32[]{:S(2)}) copy-start(f32[34,16,128]{2,1,0:T(8,128)S(1)} %collective-permute-done.left) | copy-start | bytes 835588
  13.4 28.6 %copy-start.1 = (f32[3,16,16,128]{3,2,1,0:T(8,128)}, f32[3,16,16,128]{3,2,1,0:T(8,128)S(1)}, u32[]{:S(2)}) copy-start(f32[3,16,16,128]{3,2,1,0:T(8,128)S(1)} %pad_maximum_fusion.middle) | copy-start | bytes 1179652
  13.4 19.4 %collective-permute-start.3 = (f32[3,16,16,128]{3,2,1,0:T(8,128)S(1)}, f32[3,16,16,128]{3,2,1,0:T(8,128)S(1)}, u32[]{:S(2)}, u32[]{:S(2)}) collective-permute-start(f32[3,16,16,128]{3,2,1,0:T(8,128)S(1)} %pad_maximum_fusion.middle), channel_id=1, source_target_pairs={{0,125},{1,126},{2,127},{3,0},{4,1},{5,2},{6,3},{7,4},{8,5},{9,6},... | collective-permute-start | bytes 1179656 | tf_op jit(solution)/shard_map/ppermute | solution.py:433
  18.0 24.0 %collective-permute-start.2 = (f32[3,16,16,128]{3,2,1,0:T(8,128)S(1)}, f32[3,16,16,128]{3,2,1,0:T(8,128)S(1)}, u32[]{:S(2)}, u32[]{:S(2)}) collective-permute-start(f32[3,16,16,128]{3,2,1,0:T(8,128)S(1)} %pad_maximum_fusion.middle), channel_id=1, source_target_pairs={{0,3},{1,4},{2,5},{3,6},{4,7},{5,8},{6,9},{7,10},{8,11},{9,12},{10... | collective-permute-start | bytes 1179656 | tf_op jit(solution)/shard_map/ppermute | solution.py:433
  18.3 60.9 %all-to-all-start = ((f32[128,16,128]{2,1,0:T(8,128)}), f32[128,16,128]{2,1,0:T(8,128)S(1)}, u32[]{:S(2)}, u32[]{:S(2)}) async-start(f32[128,16,128]{2,1,0:T(8,128)} %get-tuple-element.17), calls=%async_computation | async-start | bytes 2097152 | tf_op jit(solution)/shard_map/all_to_all | solution.py:489
  32.9 9.1 %copy-start.4 = (f32[3,16,16,128]{3,2,1,0:T(8,128)}, f32[3,16,16,128]{3,2,1,0:T(8,128)S(1)}, u32[]{:S(2)}) copy-start(f32[3,16,16,128]{3,2,1,0:T(8,128)S(1)} %collective-permute-done.3.after) | copy-start | bytes 1179652
  42.0 0.7 copy-start.5
  79.2 1.0 %copy-start = (f32[128,16,128]{2,1,0:T(8,128)}, f32[128,16,128]{2,1,0:T(8,128)S(1)}, u32[]{:S(2)}) copy-start(f32[128,16,128]{2,1,0:T(8,128)S(1)} %all-to-all-done.boxes_in) | copy-start | bytes 3145732

commit v9 on v8

--- a/solution.py
+++ b/solution.py
@@ -13,7 +13,7 @@
 FEATURES = 16
 GROUP = 12
 TAIL_GROUP = 4
-FAR_STEP = 8
+FAR_STEP = 4
 CHUNKS = 4
 
 matern_rate = math.sqrt(3.0) / 0.1
@@ -139,7 +139,7 @@
 
 
 def near_field(
-    items, points, probes, left, right, out, values, source, target, total, listed, arriving
+    items, points, probes, left, right, out, values, source, target, total, listed, arriving, groups
 ):
     leaves, _, leaf_size = target.shape
     slots = items.shape[0] - leaves
@@ -148,19 +148,21 @@
     edge_blocks = NEAR_REACH * pieces
 
     count = jnp.int32(0)
-    for c in range(leaves):
+    served = [c for begin, end in groups for c in range(begin, end)]
+    for c in served:
         for k in range(slots):
             item = items[k, c]
             listed[count] = item
             count = count + jnp.where(item != 0, 1, 0)
     for u in range(TAIL_GROUP):
-        listed[count + u] = NEAR_REACH * 64
+        listed[count + u] = served[0] + (served[0] + NEAR_REACH) * 64
 
     for copy in arriving:
         copy.wait()
     ones = jnp.ones((3, leaf_size), f32)
     pad = jnp.zeros((2, leaf_size), f32)
-    for w in range(leaves + 2 * NEAR_REACH):
+    window = {c + j for c in served for j in range(2 * NEAR_REACH + 1)}
+    for w in sorted(window):
         own = NEAR_REACH <= w < NEAR_REACH + leaves
         if own:
             lanes = slice((w - NEAR_REACH) * leaf_size, (w - NEAR_REACH + 1) * leaf_size)
@@ -191,7 +193,7 @@
         norms = jnp.concatenate([norm1, norm2, rest - norm2], axis=0)
         rows = jnp.concatenate([first, second, first, second, norms, ones, pad], axis=0)
         source[w] = rows.T.astype(bf16)
-        if own:
+        if w - NEAR_REACH in served:
             target[w - NEAR_REACH] = jnp.concatenate(
                 [-2.0 * first, -2.0 * first, -2.0 * second, -2.0 * second, ones, norms, pad], axis=0
             ).astype(bf16)
@@ -221,8 +223,8 @@
     lax.fori_loop(0, full, group(GROUP, 0), 0)
     rest = count - full * GROUP
     lax.fori_loop(0, (rest + TAIL_GROUP - 1) // TAIL_GROUP, group(TAIL_GROUP, full * GROUP), 0)
-    for c in range(leaves):
-        out[:, c * leaf_size : (c + 1) * leaf_size] = total[c]
+    for place, c in enumerate(served):
+        out[:, place * leaf_size : (place + 1) * leaf_size] = total[c]
 
 
 def fill_table(table, blocks, start):
@@ -280,10 +282,20 @@
     return wide[:16, :rank] + wide[16:, :rank] + wide[:16, rank:]
 
 
+def inner_kernel(
+    items, points_in, probes_in, out,
+    points, probes, values, source, target, total, listed, held_semaphores, *, groups
+):
+    held = copies([(points_in, points), (probes_in, probes)], held_semaphores)
+    near_field(
+        items, points, probes, None, None, out, values, source, target, total, listed, held, groups
+    )
+
+
 def field_kernel(
     items, points_in, probes_in, left, right, before, middle, after, couples_in, out,
-    far_out, points, probes, values, source, target, total, listed, table, couples, semaphores,
-    held_semaphores,
+    far_out, points, probes, values, source, target, total, listed, held_semaphores, table, couples,
+    semaphores, *, groups
 ):
     leaves, slots, rank, _ = couples.shape
     steps = leaves // FAR_STEP
@@ -300,7 +312,7 @@
 
     lax.fori_loop(0, steps, start, 0)
     near_field(
-        items, points, probes, left, right, out, values, source, target, total, listed, held
+        items, points, probes, left, right, out, values, source, target, total, listed, held, groups
     )
 
     empty = (2 * FAR_REACH + 1) * leaves
@@ -332,8 +344,8 @@
 
 def down_kernel(
     box_list, column_list, boxes_in, couple_box_in, couple_column_in,
-    transfer_box_in, far_in, near_in, transfer_in, basis_in, out,
-    gathered, couple_box, couple_column, transfer_box, far_leaf, near, transfer_leaf, basis,
+    transfer_box_in, far_in, inner_in, outer_in, transfer_in, basis_in, out,
+    gathered, couple_box, couple_column, transfer_box, far_leaf, inner, outer, transfer_leaf, basis,
     semaphores,
 ):
     leaves, rank, leaf_size = basis.shape
@@ -346,13 +358,14 @@
             (couple_column_in, couple_column),
             (transfer_box_in, transfer_box),
             (far_in, far_leaf),
-            (near_in, near),
+            (inner_in, inner),
+            (outer_in, outer),
         ]
         + parts(transfer_in, transfer_leaf)
         + parts(basis_in, basis),
         semaphores,
     )
-    later = 6 + CHUNKS
+    later = 7 + CHUNKS
     for copy in arriving[:4]:
         copy.wait()
 
@@ -408,8 +421,12 @@
         result = wide[:64] + wide[64:] + rest
         for j in range(4):
             c = 4 * m + j
+            held, place = outer, c if c < NEAR_REACH else c - leaves + 2 * NEAR_REACH
+            if NEAR_REACH <= c < leaves - NEAR_REACH:
+                held, place = inner, c - NEAR_REACH
+            near_value = held[:, place * leaf_size : (place + 1) * leaf_size]
             lanes = slice(c * leaf_size, (c + 1) * leaf_size)
-            out[:, lanes] = near[:, lanes] + result[16 * j : 16 * j + 16]
+            out[:, lanes] = near_value + result[16 * j : 16 * j + 16]
 
 
 def whole(count):
@@ -485,46 +502,61 @@
     )(near_slots, far_list, points, probes, basis, transfer_leaf, transfer_box)
 
     left, right = shifted(bundle_last, ring, 1), shifted(bundle_first, ring, -1)
-    sent, left, right = lax.optimization_barrier((sent, left, right))
-    boxes = lax.all_to_all(sent, ring, 0, 0, tiled=True)
+
+    window = leaves + 2 * NEAR_REACH
+    near_scratch = [
+        like(points),
+        like(probes),
+        pltpu.VMEM((window, 2 * probe_count, leaf_size), bf16),
+        pltpu.VMEM((window, leaf_size, FEATURES), bf16),
+        pltpu.VMEM((leaves, FEATURES, leaf_size), bf16),
+        pltpu.VMEM((leaves, probe_count, leaf_size), f32),
+        pltpu.SMEM((leaves * near_slots.shape[0] + 2 * GROUP,), jnp.int32),
+        copy_semaphores(2),
+    ]
+    inner = ((NEAR_REACH, leaves - NEAR_REACH),)
+    outer = ((0, NEAR_REACH), (leaves - NEAR_REACH, leaves))
+    half = jax.ShapeDtypeStruct((probe_count, probes.shape[1] // 2), f32)
+    near_inner = pl.pallas_call(
+        functools.partial(inner_kernel, groups=inner),
+        out_shape=half,
+        in_specs=scalars(1) + hbm(2),
+        out_specs=pl.BlockSpec(memory_space=pltpu.VMEM),
+        scratch_shapes=near_scratch,
+        compiler_params=params(60),
+        cost_estimate=cost(10_000_000_000),
+        name="near_inner",
+    )(items, points, probes)
+
+    sent, left, right, near_inner = lax.optimization_barrier((sent, left, right, near_inner))
     middle = jnp.stack([left[:pairs], bundle_last[:pairs], right[:pairs]])
     before, after = shifted(middle, ring, 3), shifted(middle, ring, -3)
-
-    window = leaves + 2 * NEAR_REACH
-    near_values, far_leaf = pl.pallas_call(
-        field_kernel,
-        out_shape=(
-            jax.ShapeDtypeStruct(probes.shape, f32),
-            jax.ShapeDtypeStruct((pairs, probe_count, 2 * rank), f32),
-        ),
+    boxes = lax.all_to_all(sent, ring, 0, 0, tiled=True)
+
+    near_outer, far_leaf = pl.pallas_call(
+        functools.partial(field_kernel, groups=outer),
+        out_shape=(half, jax.ShapeDtypeStruct((pairs, probe_count, 2 * rank), f32)),
         in_specs=scalars(1) + hbm(2) + whole(5) + hbm(1),
         out_specs=tuple(whole(2)),
-        scratch_shapes=[
-            like(points),
-            like(probes),
-            pltpu.VMEM((window, 2 * probe_count, leaf_size), bf16),
-            pltpu.VMEM((window, leaf_size, FEATURES), bf16),
-            pltpu.VMEM((leaves, FEATURES, leaf_size), bf16),
-            pltpu.VMEM((leaves, probe_count, leaf_size), f32),
-            pltpu.SMEM((leaves * near_slots.shape[0] + 2 * GROUP,), jnp.int32),
+        scratch_shapes=near_scratch
+        + [
             pltpu.VMEM(((2 * FAR_REACH + 1) * leaves + 2, 2 * probe_count, 2 * rank), bf16),
             like(couple_leaf),
             copy_semaphores(leaves // FAR_STEP),
-            copy_semaphores(2),
         ],
         compiler_params=params(60),
-        cost_estimate=cost(30_000_000_000),
+        cost_estimate=cost(20_000_000_000),
         name="near_far",
     )(items, points, probes, left, right, before, middle, after, couple_leaf)
 
-    held = (boxes, couple_box, couple_column, transfer_box, far_leaf, near_values)
+    held = (boxes, couple_box, couple_column, transfer_box, far_leaf, near_inner, near_outer)
     held += (transfer_leaf, basis)
     return pl.pallas_call(
         down_kernel,
         out_shape=jax.ShapeDtypeStruct(probes.shape, f32),
-        in_specs=scalars(2) + hbm(8),
+        in_specs=scalars(2) + hbm(9),
         out_specs=pl.BlockSpec(memory_space=pltpu.VMEM),
-        scratch_shapes=[like(array) for array in held] + [copy_semaphores(6 + 2 * CHUNKS)],
+        scratch_shapes=[like(array) for array in held] + [copy_semaphores(7 + 2 * CHUNKS)],
         compiler_params=params(60),
         name="down",
     )(box_list, column_list, *held)

time: 86.2 us -> 77.2 us (0.90)
  the two profiles are of different devices: /device:TPU:65 before, /device:TPU:64 now
where the time goes in v9:
time: 77.2 us; the launch traced here: 77.6 us
  Pallas kernels  50.3 us (65%)
  starting transfers between devices  22.3 us (29%)
  local copies, waits for them, and re-layouts  2.67 us (3%)
  waiting for transfers between devices  2.13 us (3%)
    pallas_call x1, Pallas kernels, per_device(): pl.pallas_call(functools.partial(field_kernel, groups=outer), out_shape=(...  25 us
    pallas_call x1, Pallas kernels, per_device(): pl.pallas_call(functools.partial(inner_kernel, groups=inner), out_shape=h...  14.9 us
    ppermute x4, starting transfers between devices, shifted(): lax.ppermute(array, axis, [(i, (i + by) % devices) for i in range(devices)])  13 us
    all_to_all x1, starting transfers between devices, per_device(): boxes = lax.all_to_all(sent, ring, 0, 0, tiled=True)  9.28 us
    pallas_call x1, Pallas kernels, per_device(): pl.pallas_call(skeleton_kernel, out_shape=(edges, edges, jax.ShapeDtypeSt...  5.51 us
    pallas_call x1, Pallas kernels, per_device(): pl.pallas_call(down_kernel, out_shape=jax.ShapeDtypeStruct(probes.shape,...  4.95 us
    ppermute x4, waiting for transfers between devices, shifted(): lax.ppermute(array, axis, [(i, (i + by) % devices) for i in range(devices)])  2.13 us
    unnamed x12, local copies, waits for them, and re-layouts  1.73 us
  transfers between devices with their start and end apart: 5, of which 1 were waited for; matrix products, arithmetic and copies ran while one was open for 1% of the time, Pallas kernels for 51%

profile of v9, /device:TPU:64, one launch (start us, length us, event | category | flops | bytes accessed | tf_op | source)
XLA Modules:
  0.0 77.6 jit_solution(10129041158092580980)
XLA Ops:
  0.0 5.5 %skeletons.1 = (f32[34,16,128]{2,1,0:T(8,128)}, f32[34,16,128]{2,1,0:T(8,128)}, f32[128,16,128]{2,1,0:T(8,128)}, s32[41,128]{1,0:T(8,128)}) custom-call(s32[9,32]{1,0:T(8,128)} %bitcast.10, s32[32,27]{1,0:T(8,128)} %far.1, f32[2,8192]{1,0:T(2,128)} %points_in.3, f32[16,8192]{1,0:T(8,128)} %probes_in.5, f32[32,64,256]{2,1,0:T(8,128)} %bitcast.8, ...), custom_call_target="tpu_custom_call" | custom-call | tf_op jit(solution)/shard_map/skeletons/pallas_call | solution.py:488
  5.5 0.2 collective-permute-start.1
  5.7 1.9 %collective-permute-start = (f32[34,16,128]{2,1,0:T(8,128)}, f32[34,16,128]{2,1,0:T(8,128)S(1)}, u32[]{:S(2)}, u32[]{:S(2)}) collective-permute-start(f32[34,16,128]{2,1,0:T(8,128)} %get-tuple-element.16), channel_id=1, source_target_pairs={{0,1},{1,2},{2,3},{3,4},{4,5},{5,6},{6,7},{7,8},{8,9},{9,10},{10,1... | collective-permute-start | bytes 835592 | tf_op jit(solution)/shard_map/ppermute | solution.py:450
  7.6 14.9 %near_inner.1.inner_in = f32[16,4096]{1,0:T(8,128)} custom-call(s32[41,128]{1,0:T(8,128)} %get-tuple-element.18.items, f32[2,8192]{1,0:T(2,128)} %points_in.3, f32[16,8192]{1,0:T(8,128)} %probes_in.5), custom_call_target="tpu_custom_call" | custom-call | flops 10000000000 | bytes 1048576 | tf_op jit(solution)/shard_map/near_inner/pallas_call | solution.py:520
  22.5 0.9 %slice_bitcast_fusion.1 = f32[1,16,16,128]{3,2,1,0:T(8,128)S(1)} fusion(f32[34,16,128]{2,1,0:T(8,128)} %get-tuple-element.16), kind=kLoop, calls=%fused_computation.2 | loop fusion | bytes 262144 | tf_op jit(solution)/shard_map/stack | solution.py:532
  23.4 0.0 collective-permute-done.1.right
  23.4 0.0 copy-start.2
  23.4 0.0 collective-permute-done.left
  23.5 0.0 copy-start.3
  23.5 0.0 copy-start.1
  23.5 10.9 %collective-permute-start.3 = (f32[3,16,16,128]{3,2,1,0:T(8,128)S(1)}, f32[3,16,16,128]{3,2,1,0:T(8,128)S(1)}, u32[]{:S(2)}, u32[]{:S(2)}) collective-permute-start(f32[3,16,16,128]{3,2,1,0:T(8,128)S(1)} %pad_maximum_fusion.middle), channel_id=1, source_target_pairs={{0,125},{1,126},{2,127},{3,0},{4,1},{5,2},{6,3},{7,4},{8,5},{9,6},... | collective-permute-start | bytes 1179656 | tf_op jit(solution)/shard_map/ppermute | solution.py:450
  34.5 0.0 collective-permute-start.2
  34.5 9.3 %all-to-all-start = ((f32[128,16,128]{2,1,0:T(8,128)}), f32[128,16,128]{2,1,0:T(8,128)S(1)}, u32[]{:S(2)}, u32[]{:S(2)}) async-start(f32[128,16,128]{2,1,0:T(8,128)} %get-tuple-element.19), calls=%async_computation | async-start | bytes 2097152 | tf_op jit(solution)/shard_map/all_to_all | solution.py:534
  43.8 0.0 collective-permute-done.3.after
  43.8 0.0 copy-start.4
  43.8 2.1 %collective-permute-done.2.before = f32[3,16,16,128]{3,2,1,0:T(8,128)S(1)} collective-permute-done((f32[3,16,16,128]{3,2,1,0:T(8,128)S(1)}, f32[3,16,16,128]{3,2,1,0:T(8,128)S(1)}, u32[]{:S(2)}, u32[]{:S(2)}) %collective-permute-start.2) | collective-permute-done | bytes 393248 | tf_op jit(solution)/shard_map/ppermute | solution.py:450
  45.9 0.0 copy-done.2
  45.9 0.0 copy-done.3
  45.9 0.0 copy-done.1
  45.9 0.0 copy-done.4
  45.9 0.0 copy-start.5
  46.0 0.7 copy-done.5
  46.7 25.0 %near_far.1 = (f32[16,4096]{1,0:T(8,128)}, f32[16,16,128]{2,1,0:T(8,128)}) custom-call(s32[41,128]{1,0:T(8,128)} %get-tuple-element.18.items, f32[2,8192]{1,0:T(2,128)} %points_in.3, f32[16,8192]{1,0:T(8,128)} %probes_in.5, f32[34,16,128]{2,1,0:T(8,128)} %copy-done.3, f32[34,16,128]{2,1,0:T(8,128)} %copy-done.2, f32[3,16,16,128]{3,2,1,0:T(8,128)} %copy-done.5, ...), custom_call_target="tpu_custom_call" | custom-call | flops 20000000000 | bytes 1048576 | tf_op jit(solution)/shard_map/near_far/pallas_call | solution.py:536
  71.7 0.0 all-to-all-done.boxes_in
  71.7 0.0 copy-start
  71.7 1.0 %copy-done = f32[128,16,128]{2,1,0:T(8,128)} copy-done((f32[128,16,128]{2,1,0:T(8,128)}, f32[128,16,128]{2,1,0:T(8,128)S(1)}, u32[]{:S(2)}) %copy-start) | copy-done | bytes 1048600
  72.7 4.9 %down.1 = f32[16,8192]{1,0:T(8,128)} custom-call(s32[1,27]{1,0:T(1,128)} %box_list.1, s32[1,4]{1,0:T(1,128)} %column_list.1, f32[128,16,128]{2,1,0:T(8,128)} %copy-done, f32[1,27,64,64]{3,2,1,0:T(8,128)} %couple_box_in.1, f32[1,4,64,64]{3,2,1,0:T(8,128)} %couple_column_in.1, f32[1,64,64]{2,1,0:T(8,128)} %transfer_box_in.1, ...), custom_call_target="tpu_custom_call" | custom-call | tf_op jit(solution)/shard_map/down/pallas_call | solution.py:554
  (2 shorter events, 0.0 us)
Async XLA Ops:
  5.5 17.9 %collective-permute-start.1 = (f32[34,16,128]{2,1,0:T(8,128)}, f32[34,16,128]{2,1,0:T(8,128)S(1)}, u32[]{:S(2)}, u32[]{:S(2)}) collective-permute-start(f32[34,16,128]{2,1,0:T(8,128)} %get-tuple-element.17), channel_id=1, source_target_pairs={{0,127},{1,0},{2,1},{3,2},{4,3},{5,4},{6,5},{7,6},{8,7},{9,8},{10,... | collective-permute-start | bytes 835592 | tf_op jit(solution)/shard_map/ppermute | solution.py:450
  5.7 17.8 %collective-permute-start = (f32[34,16,128]{2,1,0:T(8,128)}, f32[34,16,128]{2,1,0:T(8,128)S(1)}, u32[]{:S(2)}, u32[]{:S(2)}) collective-permute-start(f32[34,16,128]{2,1,0:T(8,128)} %get-tuple-element.16), channel_id=1, source_target_pairs={{0,1},{1,2},{2,3},{3,4},{4,5},{5,6},{6,7},{7,8},{8,9},{9,10},{10,1... | collective-permute-start | bytes 835592 | tf_op jit(solution)/shard_map/ppermute | solution.py:450
  23.4 22.5 %copy-start.2 = (f32[34,16,128]{2,1,0:T(8,128)}, f32[34,16,128]{2,1,0:T(8,128)S(1)}, u32[]{:S(2)}) copy-start(f32[34,16,128]{2,1,0:T(8,128)S(1)} %collective-permute-done.1.right) | copy-start | bytes 835588
  23.5 22.5 %copy-start.3 = (f32[34,16,128]{2,1,0:T(8,128)}, f32[34,16,128]{2,1,0:T(8,128)S(1)}, u32[]{:S(2)}) copy-start(f32[34,16,128]{2,1,0:T(8,128)S(1)} %collective-permute-done.left) | copy-start | bytes 835588
  23.5 22.4 %copy-start.1 = (f32[3,16,16,128]{3,2,1,0:T(8,128)}, f32[3,16,16,128]{3,2,1,0:T(8,128)S(1)}, u32[]{:S(2)}) copy-start(f32[3,16,16,128]{3,2,1,0:T(8,128)S(1)} %pad_maximum_fusion.middle) | copy-start | bytes 1179652
  23.5 20.2 %collective-permute-start.3 = (f32[3,16,16,128]{3,2,1,0:T(8,128)S(1)}, f32[3,16,16,128]{3,2,1,0:T(8,128)S(1)}, u32[]{:S(2)}, u32[]{:S(2)}) collective-permute-start(f32[3,16,16,128]{3,2,1,0:T(8,128)S(1)} %pad_maximum_fusion.middle), channel_id=1, source_target_pairs={{0,125},{1,126},{2,127},{3,0},{4,1},{5,2},{6,3},{7,4},{8,5},{9,6},... | collective-permute-start | bytes 1179656 | tf_op jit(solution)/shard_map/ppermute | solution.py:450
  34.5 11.4 %collective-permute-start.2 = (f32[3,16,16,128]{3,2,1,0:T(8,128)S(1)}, f32[3,16,16,128]{3,2,1,0:T(8,128)S(1)}, u32[]{:S(2)}, u32[]{:S(2)}) collective-permute-start(f32[3,16,16,128]{3,2,1,0:T(8,128)S(1)} %pad_maximum_fusion.middle), channel_id=1, source_target_pairs={{0,3},{1,4},{2,5},{3,6},{4,7},{5,8},{6,9},{7,10},{8,11},{9,12},{10... | collective-permute-start | bytes 1179656 | tf_op jit(solution)/shard_map/ppermute | solution.py:450
  34.5 37.2 %all-to-all-start = ((f32[128,16,128]{2,1,0:T(8,128)}), f32[128,16,128]{2,1,0:T(8,128)S(1)}, u32[]{:S(2)}, u32[]{:S(2)}) async-start(f32[128,16,128]{2,1,0:T(8,128)} %get-tuple-element.19), calls=%async_computation | async-start | bytes 2097152 | tf_op jit(solution)/shard_map/all_to_all | solution.py:534
  43.8 2.1 %copy-start.4 = (f32[3,16,16,128]{3,2,1,0:T(8,128)}, f32[3,16,16,128]{3,2,1,0:T(8,128)S(1)}, u32[]{:S(2)}) copy-start(f32[3,16,16,128]{3,2,1,0:T(8,128)S(1)} %collective-permute-done.3.after) | copy-start | bytes 1179652
  45.9 0.7 copy-start.5
  71.7 1.0 %copy-start = (f32[128,16,128]{2,1,0:T(8,128)}, f32[128,16,128]{2,1,0:T(8,128)S(1)}, u32[]{:S(2)}) copy-start(f32[128,16,128]{2,1,0:T(8,128)S(1)} %all-to-all-done.boxes_in) | copy-start | bytes 3145732

commit v10 on v9

--- a/solution.py
+++ b/solution.py
@@ -11,7 +11,7 @@
 NEAR_REACH = 8
 FAR_REACH = 4
 FEATURES = 16
-GROUP = 12
+GROUP = 16
 TAIL_GROUP = 4
 FAR_STEP = 4
 CHUNKS = 4
@@ -69,7 +69,7 @@
 
 
 def skeleton_kernel(
-    near, far, points, probes_in, basis_in, transfer_in, transfer_box, out, out_first, sent, items,
+    near, far, points, probes_in, basis_in, transfer_in, transfer_box, out, out_first, own, box_out, items,
     probes, basis, transfer_leaf, semaphores,
 ):
     leaves, rank, leaf_size = basis.shape
@@ -123,6 +123,7 @@
         pair = jnp.where(low_lanes, even, exchanged(odd))
         out[m] = pair
         out_first[m] = pair
+        own[m] = pair
         skeletons.append(pair)
     for copy in arriving[1 + CHUNKS :]:
         copy.wait()
@@ -134,8 +135,7 @@
     )
     box = summed(wide)[:, :rank]
     block = jnp.concatenate([box, product3(box, transfer_box[0])], axis=1)
-    for i in range(sent.shape[0]):
-        sent[i] = block
+    box_out[...] = block
 
 
 def near_field(
@@ -283,25 +283,34 @@
 
 
 def inner_kernel(
-    items, points_in, probes_in, out,
-    points, probes, values, source, target, total, listed, held_semaphores, *, groups
+    items, box, points_in, probes_in, out, sent_out,
+    points, probes, values, source, target, total, listed, held_semaphores, sent, sent_semaphore,
+    *, groups
 ):
     held = copies([(points_in, points), (probes_in, probes)], held_semaphores)
+    for i in range(sent.shape[0]):
+        sent[i] = box[...]
+    (sending,) = copies([(sent, sent_out)], sent_semaphore)
     near_field(
         items, points, probes, None, None, out, values, source, target, total, listed, held, groups
     )
+    sending.wait()
 
 
 def field_kernel(
-    items, points_in, probes_in, left, right, before, middle, after, couples_in, out,
+    items, points_in, probes_in, left, right, before_in, middle_in, after_in, couples_in, out,
     far_out, points, probes, values, source, target, total, listed, held_semaphores, table, couples,
-    semaphores, *, groups
+    semaphores, before, middle, after, window_semaphores, *, groups
 ):
     leaves, slots, rank, _ = couples.shape
     steps = leaves // FAR_STEP
 
     held = copies([(points_in, points), (probes_in, probes)], held_semaphores)
 
+    window = copies(
+        [(before_in, before), (middle_in, middle), (after_in, after)], window_semaphores
+    )
+
     def arriving(step):
         run = pl.ds(step * FAR_STEP, FAR_STEP)
         return pltpu.make_async_copy(couples_in.at[run], couples.at[run], semaphores.at[step])
@@ -317,6 +326,8 @@
 
     empty = (2 * FAR_REACH + 1) * leaves
     low_lanes = lax.broadcasted_iota(jnp.int32, (32, 2 * rank), 1) < rank
+    for copy in window:
+        copy.wait()
     for b in range(3):
         for place, blocks in ((b, before), (3 + b, middle), (6 + b, after)):
             fill_table(table, blocks.at[b], place * leaves)
@@ -482,19 +493,19 @@
     basis = basis.transpose(0, 2, 1)
     pairs = leaves // 2
     blocks = pairs + NEAR_REACH * leaf_size // 128 + 2
-    devices = lax.axis_size(ring)
 
     edges = jax.ShapeDtypeStruct((blocks, probe_count, 2 * rank), f32)
-    bundle_last, bundle_first, sent, items = pl.pallas_call(
+    bundle_last, bundle_first, own, box, items = pl.pallas_call(
         skeleton_kernel,
         out_shape=(
             edges,
             edges,
-            jax.ShapeDtypeStruct((devices, probe_count, 2 * rank), f32),
+            jax.ShapeDtypeStruct((pairs, probe_count, 2 * rank), f32),
+            jax.ShapeDtypeStruct((probe_count, 2 * rank), f32),
             jax.ShapeDtypeStruct((near_slots.shape[0] + leaves, 128), jnp.int32),
         ),
         in_specs=whole(3) + hbm(3) + whole(1),
-        out_specs=tuple(whole(4)),
+        out_specs=tuple(whole(5)),
         scratch_shapes=[like(probes), like(basis), like(transfer_leaf)]
         + [copy_semaphores(1 + 2 * CHUNKS)],
         compiler_params=params(60),
@@ -517,33 +528,36 @@
     inner = ((NEAR_REACH, leaves - NEAR_REACH),)
     outer = ((0, NEAR_REACH), (leaves - NEAR_REACH, leaves))
     half = jax.ShapeDtypeStruct((probe_count, probes.shape[1] // 2), f32)
-    near_inner = pl.pallas_call(
+    copies_of_box = (lax.axis_size(ring), probe_count, 2 * rank)
+    near_inner, sent = pl.pallas_call(
         functools.partial(inner_kernel, groups=inner),
-        out_shape=half,
-        in_specs=scalars(1) + hbm(2),
-        out_specs=pl.BlockSpec(memory_space=pltpu.VMEM),
-        scratch_shapes=near_scratch,
+        out_shape=(half, jax.ShapeDtypeStruct(copies_of_box, f32)),
+        in_specs=scalars(1) + whole(1) + hbm(2),
+        out_specs=tuple(whole(1) + hbm(1)),
+        scratch_shapes=near_scratch + [pltpu.VMEM(copies_of_box, f32), copy_semaphores(1)],
         compiler_params=params(60),
         cost_estimate=cost(10_000_000_000),
         name="near_inner",
-    )(items, points, probes)
-
-    sent, left, right, near_inner = lax.optimization_barrier((sent, left, right, near_inner))
-    middle = jnp.stack([left[:pairs], bundle_last[:pairs], right[:pairs]])
+    )(items, box, points, probes)
+
+    sent, left, right, own = lax.optimization_barrier((sent, left, right, own))
+    middle = jnp.stack([left[:pairs], own, right[:pairs]])
     before, after = shifted(middle, ring, 3), shifted(middle, ring, -3)
     boxes = lax.all_to_all(sent, ring, 0, 0, tiled=True)
 
     near_outer, far_leaf = pl.pallas_call(
         functools.partial(field_kernel, groups=outer),
         out_shape=(half, jax.ShapeDtypeStruct((pairs, probe_count, 2 * rank), f32)),
-        in_specs=scalars(1) + hbm(2) + whole(5) + hbm(1),
+        in_specs=scalars(1) + hbm(2) + whole(2) + hbm(4),
         out_specs=tuple(whole(2)),
         scratch_shapes=near_scratch
         + [
             pltpu.VMEM(((2 * FAR_REACH + 1) * leaves + 2, 2 * probe_count, 2 * rank), bf16),
             like(couple_leaf),
             copy_semaphores(leaves // FAR_STEP),
-        ],
+        ]
+        + [like(middle)] * 3
+        + [copy_semaphores(3)],
         compiler_params=params(60),
         cost_estimate=cost(20_000_000_000),
         name="near_far",

time: 77.2 us -> 72.4 us (0.938)
  the two profiles are of different devices: /device:TPU:64 before, /device:TPU:0 now
where the time goes in v10:
time: 72.4 us; the launch traced here: 71.1 us
  Pallas kernels  48.8 us (67%)
  starting transfers between devices  16.9 us (23%)
  waiting for transfers between devices  3.48 us (5%)
  local copies, waits for them, and re-layouts  1.75 us (2%)
    pallas_call x1, Pallas kernels, per_device(): pl.pallas_call(functools.partial(field_kernel, groups=outer), out_shape=(...  22.5 us
    pallas_call x1, Pallas kernels, per_device(): pl.pallas_call(functools.partial(inner_kernel, groups=inner), out_shape=(...  16.3 us
    ppermute x4, starting transfers between devices, shifted(): lax.ppermute(array, axis, [(i, (i + by) % devices) for i in range(devices)])  11.7 us
    all_to_all x1, starting transfers between devices, per_device(): boxes = lax.all_to_all(sent, ring, 0, 0, tiled=True)  5.18 us
    pallas_call x1, Pallas kernels, per_device(): pl.pallas_call(skeleton_kernel, out_shape=(edges, edges, jax.ShapeDtypeSt...  5.07 us
    pallas_call x1, Pallas kernels, per_device(): pl.pallas_call(down_kernel, out_shape=jax.ShapeDtypeStruct(probes.shape,...  4.95 us
    ppermute x4, waiting for transfers between devices, shifted(): lax.ppermute(array, axis, [(i, (i + by) % devices) for i in range(devices)])  3.48 us
    unnamed x14, local copies, waits for them, and re-layouts  1.73 us
  transfers between devices with their start and end apart: 5, of which 2 were waited for; matrix products, arithmetic and copies ran while one was open for 0% of the time, Pallas kernels for 55%

profile of v10, /device:TPU:0, one launch (start us, length us, event | category | flops | bytes accessed | tf_op | source)
XLA Modules:
  0.0 71.1 jit_solution(15379762716570580565)
XLA Ops:
  0.0 5.1 %skeletons.1 = (f32[34,16,128]{2,1,0:T(8,128)}, f32[34,16,128]{2,1,0:T(8,128)}, f32[16,16,128]{2,1,0:T(8,128)}, f32[16,128]{1,0:T(8,128)}, s32[41,128]{1,0:T(8,128)}) custom-call(s32[9,32]{1,0:T(8,128)} %bitcast.10, s32[32,27]{1,0:T(8,128)} %far.1, f32[2,8192]{1,0:T(2,128)} %points_in.3, f32[16,8192]{1,0:T(8,128)} %probes_in.5, f32[32,64,256]{2,1,0:T(8,128)} %bitcast.7, ...), custom_call_target="tpu_custom_call" | custom-call | tf_op jit(solution)/shard_map/skeletons/pallas_call | solution.py:498
  5.1 0.0 copy-start.2
  5.1 2.1 %collective-permute-start = (f32[34,16,128]{2,1,0:T(8,128)}, f32[34,16,128]{2,1,0:T(8,128)S(1)}, u32[]{:S(2)}, u32[]{:S(2)}) collective-permute-start(f32[34,16,128]{2,1,0:T(8,128)} %get-tuple-element.21), channel_id=1, source_target_pairs={{0,1},{1,2},{2,3},{3,4},{4,5},{5,6},{6,7},{7,8},{8,9},{9,10},{10,1... | collective-permute-start | bytes 835592 | tf_op jit(solution)/shard_map/ppermute | solution.py:461
  7.2 6.3 %collective-permute-start.1 = (f32[34,16,128]{2,1,0:T(8,128)}, f32[34,16,128]{2,1,0:T(8,128)S(1)}, u32[]{:S(2)}, u32[]{:S(2)}) collective-permute-start(f32[34,16,128]{2,1,0:T(8,128)} %get-tuple-element.22), channel_id=1, source_target_pairs={{0,127},{1,0},{2,1},{3,2},{4,3},{5,4},{6,5},{7,6},{8,7},{9,8},{10,... | collective-permute-start | bytes 835592 | tf_op jit(solution)/shard_map/ppermute | solution.py:461
  13.5 16.3 %near_inner.1 = (f32[16,4096]{1,0:T(8,128)}, f32[128,16,128]{2,1,0:T(8,128)}) custom-call(s32[41,128]{1,0:T(8,128)} %get-tuple-element.18.items, f32[16,128]{1,0:T(8,128)} %get-tuple-element.19.box, f32[2,8192]{1,0:T(2,128)} %points_in.3, f32[16,8192]{1,0:T(8,128)} %probes_in.5), custom_call_target="tpu_custom_call" | custom-call | flops 10000000000 | bytes 1048576 | tf_op jit(solution)/shard_map/near_inner/pallas_call | solution.py:532
  29.8 0.0 collective-permute-done.left
  29.8 0.0 copy-start.3
  29.8 0.0 collective-permute-done.1.right
  29.8 0.0 copy-start.4
  29.9 0.0 copy-done.2
  29.9 0.0 copy-start.1
  29.9 0.1 collective-permute-start.3
  30.0 3.2 %collective-permute-start.2 = (f32[3,16,16,128]{3,2,1,0:T(8,128)S(1)}, f32[3,16,16,128]{3,2,1,0:T(8,128)S(1)}, u32[]{:S(2)}, u32[]{:S(2)}) collective-permute-start(f32[3,16,16,128]{3,2,1,0:T(8,128)S(1)} %pad_maximum_fusion.middle_in), channel_id=1, source_target_pairs={{0,3},{1,4},{2,5},{3,6},{4,7},{5,8},{6,9},{7,10},{8,11},{9,12},{10... | collective-permute-start | bytes 1179656 | tf_op jit(solution)/shard_map/ppermute | solution.py:461
  33.2 5.2 %all-to-all-start = ((f32[128,16,128]{2,1,0:T(8,128)}), f32[128,16,128]{2,1,0:T(8,128)S(1)}, u32[]{:S(2)}, u32[]{:S(2)}) async-start(f32[128,16,128]{2,1,0:T(8,128)} %get-tuple-element.24), calls=%async_computation | async-start | bytes 2097152 | tf_op jit(solution)/shard_map/all_to_all | solution.py:546
  38.4 0.6 collective-permute-done.3.after_in
  39.0 0.0 copy-start.5
  39.0 2.9 %collective-permute-done.2.before_in = f32[3,16,16,128]{3,2,1,0:T(8,128)S(1)} collective-permute-done((f32[3,16,16,128]{3,2,1,0:T(8,128)S(1)}, f32[3,16,16,128]{3,2,1,0:T(8,128)S(1)}, u32[]{:S(2)}, u32[]{:S(2)}) %collective-permute-start.2) | collective-permute-done | bytes 393248 | tf_op jit(solution)/shard_map/ppermute | solution.py:461
  41.9 0.0 copy-done.3
  41.9 0.0 copy-done.4
  41.9 0.0 copy-done.1
  41.9 0.0 copy-done.5
  41.9 0.0 copy-start.6
  41.9 0.7 %copy-done.6 = f32[3,16,16,128]{3,2,1,0:T(8,128)} copy-done((f32[3,16,16,128]{3,2,1,0:T(8,128)}, f32[3,16,16,128]{3,2,1,0:T(8,128)S(1)}, u32[]{:S(2)}) %copy-start.6) | copy-done | bytes 393240
  42.7 22.5 %near_far.1 = (f32[16,4096]{1,0:T(8,128)}, f32[16,16,128]{2,1,0:T(8,128)}) custom-call(s32[41,128]{1,0:T(8,128)} %get-tuple-element.18.items, f32[2,8192]{1,0:T(2,128)} %points_in.3, f32[16,8192]{1,0:T(8,128)} %probes_in.5, f32[34,16,128]{2,1,0:T(8,128)} %copy-done.3, f32[34,16,128]{2,1,0:T(8,128)} %copy-done.4, f32[3,16,16,128]{3,2,1,0:T(8,128)} %copy-done.6, ...), custom_call_target="tpu_custom_call" | custom-call | flops 20000000000 | bytes 1048576 | tf_op jit(solution)/shard_map/near_far/pallas_call | solution.py:548
  65.2 0.0 all-to-all-done.boxes_in
  65.2 0.0 copy-start
  65.2 1.0 %copy-done = f32[128,16,128]{2,1,0:T(8,128)} copy-done((f32[128,16,128]{2,1,0:T(8,128)}, f32[128,16,128]{2,1,0:T(8,128)S(1)}, u32[]{:S(2)}) %copy-start) | copy-done | bytes 1048600
  66.2 4.9 %down.1 = f32[16,8192]{1,0:T(8,128)} custom-call(s32[1,27]{1,0:T(1,128)} %box_list.1, s32[1,4]{1,0:T(1,128)} %column_list.1, f32[128,16,128]{2,1,0:T(8,128)} %copy-done, f32[1,27,64,64]{3,2,1,0:T(8,128)} %couple_box_in.1, f32[1,4,64,64]{3,2,1,0:T(8,128)} %couple_column_in.1, f32[1,64,64]{2,1,0:T(8,128)} %transfer_box_in.1, ...), custom_call_target="tpu_custom_call" | custom-call | tf_op jit(solution)/shard_map/down/pallas_call | solution.py:568
  (2 shorter events, 0.0 us)
Async XLA Ops:
  5.1 24.8 %copy-start.2 = (f32[16,16,128]{2,1,0:T(8,128)S(1)}, f32[16,16,128]{2,1,0:T(8,128)}, u32[]{:S(2)}) copy-start(f32[16,16,128]{2,1,0:T(8,128)} %get-tuple-element.27) | copy-start | bytes 393220
  5.1 24.7 %collective-permute-start = (f32[34,16,128]{2,1,0:T(8,128)}, f32[34,16,128]{2,1,0:T(8,128)S(1)}, u32[]{:S(2)}, u32[]{:S(2)}) collective-permute-start(f32[34,16,128]{2,1,0:T(8,128)} %get-tuple-element.21), channel_id=1, source_target_pairs={{0,1},{1,2},{2,3},{3,4},{4,5},{5,6},{6,7},{7,8},{8,9},{9,10},{10,1... | collective-permute-start | bytes 835592 | tf_op jit(solution)/shard_map/ppermute | solution.py:461
  7.2 22.7 %collective-permute-start.1 = (f32[34,16,128]{2,1,0:T(8,128)}, f32[34,16,128]{2,1,0:T(8,128)S(1)}, u32[]{:S(2)}, u32[]{:S(2)}) collective-permute-start(f32[34,16,128]{2,1,0:T(8,128)} %get-tuple-element.22), channel_id=1, source_target_pairs={{0,127},{1,0},{2,1},{3,2},{4,3},{5,4},{6,5},{7,6},{8,7},{9,8},{10,... | collective-permute-start | bytes 835592 | tf_op jit(solution)/shard_map/ppermute | solution.py:461
  29.8 12.1 %copy-start.3 = (f32[34,16,128]{2,1,0:T(8,128)}, f32[34,16,128]{2,1,0:T(8,128)S(1)}, u32[]{:S(2)}) copy-start(f32[34,16,128]{2,1,0:T(8,128)S(1)} %collective-permute-done.left) | copy-start | bytes 835588
  29.8 12.1 %copy-start.4 = (f32[34,16,128]{2,1,0:T(8,128)}, f32[34,16,128]{2,1,0:T(8,128)S(1)}, u32[]{:S(2)}) copy-start(f32[34,16,128]{2,1,0:T(8,128)S(1)} %collective-permute-done.1.right) | copy-start | bytes 835588
  29.9 12.0 %copy-start.1 = (f32[3,16,16,128]{3,2,1,0:T(8,128)}, f32[3,16,16,128]{3,2,1,0:T(8,128)S(1)}, u32[]{:S(2)}) copy-start(f32[3,16,16,128]{3,2,1,0:T(8,128)S(1)} %pad_maximum_fusion.middle_in) | copy-start | bytes 1179652
  29.9 9.1 %collective-permute-start.3 = (f32[3,16,16,128]{3,2,1,0:T(8,128)S(1)}, f32[3,16,16,128]{3,2,1,0:T(8,128)S(1)}, u32[]{:S(2)}, u32[]{:S(2)}) collective-permute-start(f32[3,16,16,128]{3,2,1,0:T(8,128)S(1)} %pad_maximum_fusion.middle_in), channel_id=1, source_target_pairs={{0,125},{1,126},{2,127},{3,0},{4,1},{5,2},{6,3},{7,4},{8,5},{9,6},... | collective-permute-start | bytes 1179656 | tf_op jit(solution)/shard_map/ppermute | solution.py:461
  30.0 11.9 %collective-permute-start.2 = (f32[3,16,16,128]{3,2,1,0:T(8,128)S(1)}, f32[3,16,16,128]{3,2,1,0:T(8,128)S(1)}, u32[]{:S(2)}, u32[]{:S(2)}) collective-permute-start(f32[3,16,16,128]{3,2,1,0:T(8,128)S(1)} %pad_maximum_fusion.middle_in), channel_id=1, source_target_pairs={{0,3},{1,4},{2,5},{3,6},{4,7},{5,8},{6,9},{7,10},{8,11},{9,12},{10... | collective-permute-start | bytes 1179656 | tf_op jit(solution)/shard_map/ppermute | solution.py:461
  33.2 31.9 %all-to-all-start = ((f32[128,16,128]{2,1,0:T(8,128)}), f32[128,16,128]{2,1,0:T(8,128)S(1)}, u32[]{:S(2)}, u32[]{:S(2)}) async-start(f32[128,16,128]{2,1,0:T(8,128)} %get-tuple-element.24), calls=%async_computation | async-start | bytes 2097152 | tf_op jit(solution)/shard_map/all_to_all | solution.py:546
  39.0 2.9 %copy-start.5 = (f32[3,16,16,128]{3,2,1,0:T(8,128)}, f32[3,16,16,128]{3,2,1,0:T(8,128)S(1)}, u32[]{:S(2)}) copy-start(f32[3,16,16,128]{3,2,1,0:T(8,128)S(1)} %collective-permute-done.3.after_in) | copy-start | bytes 1179652
  41.9 0.7 %copy-start.6 = (f32[3,16,16,128]{3,2,1,0:T(8,128)}, f32[3,16,16,128]{3,2,1,0:T(8,128)S(1)}, u32[]{:S(2)}) copy-start(f32[3,16,16,128]{3,2,1,0:T(8,128)S(1)} %collective-permute-done.2.before_in) | copy-start | bytes 1179652
  65.2 1.0 %copy-start = (f32[128,16,128]{2,1,0:T(8,128)}, f32[128,16,128]{2,1,0:T(8,128)S(1)}, u32[]{:S(2)}) copy-start(f32[128,16,128]{2,1,0:T(8,128)S(1)} %all-to-all-done.boxes_in) | copy-start | bytes 3145732

commit v11 on v10

--- a/solution.py
+++ b/solution.py
@@ -70,13 +70,10 @@
 
 def skeleton_kernel(
     near, far, points, probes_in, basis_in, transfer_in, transfer_box, out, out_first, own, box_out, items,
-    probes, basis, transfer_leaf, semaphores,
+    probes, basis, transfer_leaf, semaphores, later_semaphore,
 ):
     leaves, rank, leaf_size = basis.shape
-    arriving = copies(
-        [(probes_in, probes)] + parts(basis_in, basis) + parts(transfer_in, transfer_leaf),
-        semaphores,
-    )
+    arriving = copies([(probes_in, probes)] + parts(basis_in, basis), semaphores)
     slots = near.shape[0]
     pairs = leaves // 2
     low_lanes = lax.broadcasted_iota(jnp.int32, (16, 2 * rank), 1) < rank
@@ -116,6 +113,8 @@
     for m in range(pairs):
         if m % (pairs // CHUNKS) == 0:
             arriving[1 + m // (pairs // CHUNKS)].wait()
+        if m == 0:
+            later = copies([(transfer_in, transfer_leaf)], later_semaphore)
         left = jnp.concatenate([leaf_probes(2 * m), leaf_probes(2 * m + 1)], axis=0)
         right = jnp.concatenate([stacked_halves(basis[2 * m]), stacked_halves(basis[2 * m + 1])], axis=0)
         wide = contract(left, right, ((1,), (1,)))
@@ -125,8 +124,7 @@
         out_first[m] = pair
         own[m] = pair
         skeletons.append(pair)
-    for copy in arriving[1 + CHUNKS :]:
-        copy.wait()
+    later[0].wait()
     high, low = halves(transfer_leaf[...].reshape(leaves * rank, rank))
     wide = jnp.dot(
         stacked_halves(jnp.concatenate(skeletons, axis=1)),
@@ -354,9 +352,9 @@
 
 
 def down_kernel(
-    box_list, column_list, boxes_in, couple_box_in, couple_column_in,
+    box_list, column_list, gathered, couple_box_in, couple_column_in,
     transfer_box_in, far_in, inner_in, outer_in, transfer_in, basis_in, out,
-    gathered, couple_box, couple_column, transfer_box, far_leaf, inner, outer, transfer_leaf, basis,
+    couple_box, couple_column, transfer_box, far_leaf, inner, outer, transfer_leaf, basis,
     semaphores,
 ):
     leaves, rank, leaf_size = basis.shape
@@ -364,7 +362,6 @@
     low_lanes = lax.broadcasted_iota(jnp.int32, (32, 2 * rank), 1) < rank
     arriving = copies(
         [
-            (boxes_in, gathered),
             (couple_box_in, couple_box),
             (couple_column_in, couple_column),
             (transfer_box_in, transfer_box),
@@ -376,8 +373,8 @@
         + parts(basis_in, basis),
         semaphores,
     )
-    later = 7 + CHUNKS
-    for copy in arriving[:4]:
+    later = 6 + CHUNKS
+    for copy in arriving[:3]:
         copy.wait()
 
     def box_row(entry):
@@ -409,7 +406,7 @@
     far_column = coupled(jnp.concatenate(pieces, axis=1), couple_column[0])
     down_box = far_box + product3(far_column, transfer_box[0], ((1,), (1,)))
 
-    for copy in arriving[4:later]:
+    for copy in arriving[3:later]:
         copy.wait()
     high, low = halves(transfer_leaf[...].reshape(leaves * rank, rank))
     both = stacked_halves(down_box)
@@ -507,7 +504,7 @@
         in_specs=whole(3) + hbm(3) + whole(1),
         out_specs=tuple(whole(5)),
         scratch_shapes=[like(probes), like(basis), like(transfer_leaf)]
-        + [copy_semaphores(1 + 2 * CHUNKS)],
+        + [copy_semaphores(1 + CHUNKS), copy_semaphores(1)],
         compiler_params=params(60),
         name="skeletons",
     )(near_slots, far_list, points, probes, basis, transfer_leaf, transfer_box)
@@ -563,17 +560,17 @@
         name="near_far",
     )(items, points, probes, left, right, before, middle, after, couple_leaf)
 
-    held = (boxes, couple_box, couple_column, transfer_box, far_leaf, near_inner, near_outer)
+    held = (couple_box, couple_column, transfer_box, far_leaf, near_inner, near_outer)
     held += (transfer_leaf, basis)
     return pl.pallas_call(
         down_kernel,
         out_shape=jax.ShapeDtypeStruct(probes.shape, f32),
-        in_specs=scalars(2) + hbm(9),
+        in_specs=scalars(2) + whole(1) + hbm(8),
         out_specs=pl.BlockSpec(memory_space=pltpu.VMEM),
-        scratch_shapes=[like(array) for array in held] + [copy_semaphores(7 + 2 * CHUNKS)],
+        scratch_shapes=[like(array) for array in held] + [copy_semaphores(6 + 2 * CHUNKS)],
         compiler_params=params(60),
         name="down",
-    )(box_list, column_list, *held)
+    )(box_list, column_list, boxes, *held)
 
 
 def solution(mesh):

time: 72.4 us -> 72.2 us (level)
  the two profiles are of different devices: /device:TPU:0 before, /device:TPU:1 now
where the time goes in v11:
time: 72.2 us; the launch traced here: 72 us
  Pallas kernels  48.4 us (67%)
  starting transfers between devices  19.5 us (27%)
  waiting for transfers between devices  2.09 us (3%)
  local copies, waits for them, and re-layouts  1.75 us (2%)
    pallas_call x1, Pallas kernels, per_device(): pl.pallas_call(functools.partial(field_kernel, groups=outer), out_shape=(...  23.8 us
    pallas_call x1, Pallas kernels, per_device(): pl.pallas_call(functools.partial(inner_kernel, groups=inner), out_shape=(...  14.4 us
    all_to_all x1, starting transfers between devices, per_device(): boxes = lax.all_to_all(sent, ring, 0, 0, tiled=True)  11.4 us
    ppermute x4, starting transfers between devices, shifted(): lax.ppermute(array, axis, [(i, (i + by) % devices) for i in range(devices)])  8.07 us
    pallas_call x1, Pallas kernels, per_device(): pl.pallas_call(down_kernel, out_shape=jax.ShapeDtypeStruct(probes.shape,...  5.19 us
    pallas_call x1, Pallas kernels, per_device(): pl.pallas_call(skeleton_kernel, out_shape=(edges, edges, jax.ShapeDtypeSt...  5.04 us
    ppermute x4, waiting for transfers between devices, shifted(): lax.ppermute(array, axis, [(i, (i + by) % devices) for i in range(devices)])  2.09 us
    unnamed x14, local copies, waits for them, and re-layouts  1.73 us
  transfers between devices with their start and end apart: 5, of which 1 were waited for; matrix products, arithmetic and copies ran while one was open for 0% of the time, Pallas kernels for 53%

profile of v11, /device:TPU:1, one launch (start us, length us, event | category | flops | bytes accessed | tf_op | source)
XLA Modules:
  0.0 72.0 jit_solution(10717855011147101504)
XLA Ops:
  0.0 5.0 %skeletons.1 = (f32[34,16,128]{2,1,0:T(8,128)}, f32[34,16,128]{2,1,0:T(8,128)}, f32[16,16,128]{2,1,0:T(8,128)}, f32[16,128]{1,0:T(8,128)}, s32[41,128]{1,0:T(8,128)}) custom-call(s32[9,32]{1,0:T(8,128)} %bitcast.10, s32[32,27]{1,0:T(8,128)} %far.1, f32[2,8192]{1,0:T(2,128)} %points_in.3, f32[16,8192]{1,0:T(8,128)} %probes_in.5, f32[32,64,256]{2,1,0:T(8,128)} %bitcast.7, ...), custom_call_target="tpu_custom_call" | custom-call | tf_op jit(solution)/shard_map/skeletons/pallas_call | solution.py:495
  5.1 0.0 copy-start.2
  5.1 2.5 %collective-permute-start = (f32[34,16,128]{2,1,0:T(8,128)}, f32[34,16,128]{2,1,0:T(8,128)S(1)}, u32[]{:S(2)}, u32[]{:S(2)}) collective-permute-start(f32[34,16,128]{2,1,0:T(8,128)} %get-tuple-element.21), channel_id=1, source_target_pairs={{0,1},{1,2},{2,3},{3,4},{4,5},{5,6},{6,7},{7,8},{8,9},{9,10},{10,1... | collective-permute-start | bytes 835592 | tf_op jit(solution)/shard_map/ppermute | solution.py:458
  7.6 2.8 %collective-permute-start.1 = (f32[34,16,128]{2,1,0:T(8,128)}, f32[34,16,128]{2,1,0:T(8,128)S(1)}, u32[]{:S(2)}, u32[]{:S(2)}) collective-permute-start(f32[34,16,128]{2,1,0:T(8,128)} %get-tuple-element.22), channel_id=1, source_target_pairs={{0,127},{1,0},{2,1},{3,2},{4,3},{5,4},{6,5},{7,6},{8,7},{9,8},{10,... | collective-permute-start | bytes 835592 | tf_op jit(solution)/shard_map/ppermute | solution.py:458
  10.4 14.4 %near_inner.1 = (f32[16,4096]{1,0:T(8,128)}, f32[128,16,128]{2,1,0:T(8,128)}) custom-call(s32[41,128]{1,0:T(8,128)} %get-tuple-element.18.items, f32[16,128]{1,0:T(8,128)} %get-tuple-element.19.box, f32[2,8192]{1,0:T(2,128)} %points_in.3, f32[16,8192]{1,0:T(8,128)} %probes_in.5), custom_call_target="tpu_custom_call" | custom-call | flops 10000000000 | bytes 1048576 | tf_op jit(solution)/shard_map/near_inner/pallas_call | solution.py:529
  24.8 0.0 collective-permute-done.left
  24.8 0.0 copy-start.3
  24.8 0.0 collective-permute-done.1.right
  24.8 0.0 copy-start.4
  24.8 0.0 copy-done.2
  24.9 0.0 copy-start.1
  24.9 0.1 collective-permute-start.3
  25.0 2.7 %collective-permute-start.2 = (f32[3,16,16,128]{3,2,1,0:T(8,128)S(1)}, f32[3,16,16,128]{3,2,1,0:T(8,128)S(1)}, u32[]{:S(2)}, u32[]{:S(2)}) collective-permute-start(f32[3,16,16,128]{3,2,1,0:T(8,128)S(1)} %pad_maximum_fusion.middle_in), channel_id=1, source_target_pairs={{0,3},{1,4},{2,5},{3,6},{4,7},{5,8},{6,9},{7,10},{8,11},{9,12},{10... | collective-permute-start | bytes 1179656 | tf_op jit(solution)/shard_map/ppermute | solution.py:458
  27.6 11.4 %all-to-all-start = ((f32[128,16,128]{2,1,0:T(8,128)}), f32[128,16,128]{2,1,0:T(8,128)S(1)}, u32[]{:S(2)}, u32[]{:S(2)}) async-start(f32[128,16,128]{2,1,0:T(8,128)} %get-tuple-element.24), calls=%async_computation | async-start | bytes 2097152 | tf_op jit(solution)/shard_map/all_to_all | solution.py:543
  39.1 0.0 collective-permute-done.3.after_in
  39.1 0.0 copy-start.5
  39.1 2.1 %collective-permute-done.2.before_in = f32[3,16,16,128]{3,2,1,0:T(8,128)S(1)} collective-permute-done((f32[3,16,16,128]{3,2,1,0:T(8,128)S(1)}, f32[3,16,16,128]{3,2,1,0:T(8,128)S(1)}, u32[]{:S(2)}, u32[]{:S(2)}) %collective-permute-start.2) | collective-permute-done | bytes 393248 | tf_op jit(solution)/shard_map/ppermute | solution.py:458
  41.2 0.0 copy-done.3
  41.2 0.0 copy-done.4
  41.2 0.0 copy-done.1
  41.2 0.0 copy-done.5
  41.2 0.0 copy-start.6
  41.2 0.7 %copy-done.6 = f32[3,16,16,128]{3,2,1,0:T(8,128)} copy-done((f32[3,16,16,128]{3,2,1,0:T(8,128)}, f32[3,16,16,128]{3,2,1,0:T(8,128)S(1)}, u32[]{:S(2)}) %copy-start.6) | copy-done | bytes 393240
  42.0 23.8 %near_far.1 = (f32[16,4096]{1,0:T(8,128)}, f32[16,16,128]{2,1,0:T(8,128)}) custom-call(s32[41,128]{1,0:T(8,128)} %get-tuple-element.18.items, f32[2,8192]{1,0:T(2,128)} %points_in.3, f32[16,8192]{1,0:T(8,128)} %probes_in.5, f32[34,16,128]{2,1,0:T(8,128)} %copy-done.3, f32[34,16,128]{2,1,0:T(8,128)} %copy-done.4, f32[3,16,16,128]{3,2,1,0:T(8,128)} %copy-done.6, ...), custom_call_target="tpu_custom_call" | custom-call | flops 20000000000 | bytes 1048576 | tf_op jit(solution)/shard_map/near_far/pallas_call | solution.py:545
  65.8 0.0 all-to-all-done.gathered
  65.8 0.0 copy-start
  65.8 1.0 %copy-done = f32[128,16,128]{2,1,0:T(8,128)} copy-done((f32[128,16,128]{2,1,0:T(8,128)}, f32[128,16,128]{2,1,0:T(8,128)S(1)}, u32[]{:S(2)}) %copy-start) | copy-done | bytes 1048600
  66.8 5.2 %down.1 = f32[16,8192]{1,0:T(8,128)} custom-call(s32[1,27]{1,0:T(1,128)} %box_list.1, s32[1,4]{1,0:T(1,128)} %column_list.1, f32[128,16,128]{2,1,0:T(8,128)} %copy-done, f32[1,27,64,64]{3,2,1,0:T(8,128)} %couple_box_in.1, f32[1,4,64,64]{3,2,1,0:T(8,128)} %couple_column_in.1, f32[1,64,64]{2,1,0:T(8,128)} %transfer_box_in.1, ...), custom_call_target="tpu_custom_call" | custom-call | tf_op jit(solution)/shard_map/down/pallas_call | solution.py:565
  (2 shorter events, 0.0 us)
Async XLA Ops:
  5.1 19.8 %copy-start.2 = (f32[16,16,128]{2,1,0:T(8,128)S(1)}, f32[16,16,128]{2,1,0:T(8,128)}, u32[]{:S(2)}) copy-start(f32[16,16,128]{2,1,0:T(8,128)} %get-tuple-element.27) | copy-start | bytes 393220
  5.1 19.7 %collective-permute-start = (f32[34,16,128]{2,1,0:T(8,128)}, f32[34,16,128]{2,1,0:T(8,128)S(1)}, u32[]{:S(2)}, u32[]{:S(2)}) collective-permute-start(f32[34,16,128]{2,1,0:T(8,128)} %get-tuple-element.21), channel_id=1, source_target_pairs={{0,1},{1,2},{2,3},{3,4},{4,5},{5,6},{6,7},{7,8},{8,9},{9,10},{10,1... | collective-permute-start | bytes 835592 | tf_op jit(solution)/shard_map/ppermute | solution.py:458
  7.6 17.2 %collective-permute-start.1 = (f32[34,16,128]{2,1,0:T(8,128)}, f32[34,16,128]{2,1,0:T(8,128)S(1)}, u32[]{:S(2)}, u32[]{:S(2)}) collective-permute-start(f32[34,16,128]{2,1,0:T(8,128)} %get-tuple-element.22), channel_id=1, source_target_pairs={{0,127},{1,0},{2,1},{3,2},{4,3},{5,4},{6,5},{7,6},{8,7},{9,8},{10,... | collective-permute-start | bytes 835592 | tf_op jit(solution)/shard_map/ppermute | solution.py:458
  24.8 16.4 %copy-start.3 = (f32[34,16,128]{2,1,0:T(8,128)}, f32[34,16,128]{2,1,0:T(8,128)S(1)}, u32[]{:S(2)}) copy-start(f32[34,16,128]{2,1,0:T(8,128)S(1)} %collective-permute-done.left) | copy-start | bytes 835588
  24.8 16.4 %copy-start.4 = (f32[34,16,128]{2,1,0:T(8,128)}, f32[34,16,128]{2,1,0:T(8,128)S(1)}, u32[]{:S(2)}) copy-start(f32[34,16,128]{2,1,0:T(8,128)S(1)} %collective-permute-done.1.right) | copy-start | bytes 835588
  24.9 16.3 %copy-start.1 = (f32[3,16,16,128]{3,2,1,0:T(8,128)}, f32[3,16,16,128]{3,2,1,0:T(8,128)S(1)}, u32[]{:S(2)}) copy-start(f32[3,16,16,128]{3,2,1,0:T(8,128)S(1)} %pad_maximum_fusion.middle_in) | copy-start | bytes 1179652
  24.9 14.2 %collective-permute-start.3 = (f32[3,16,16,128]{3,2,1,0:T(8,128)S(1)}, f32[3,16,16,128]{3,2,1,0:T(8,128)S(1)}, u32[]{:S(2)}, u32[]{:S(2)}) collective-permute-start(f32[3,16,16,128]{3,2,1,0:T(8,128)S(1)} %pad_maximum_fusion.middle_in), channel_id=1, source_target_pairs={{0,125},{1,126},{2,127},{3,0},{4,1},{5,2},{6,3},{7,4},{8,5},{9,6},... | collective-permute-start | bytes 1179656 | tf_op jit(solution)/shard_map/ppermute | solution.py:458
  25.0 16.2 %collective-permute-start.2 = (f32[3,16,16,128]{3,2,1,0:T(8,128)S(1)}, f32[3,16,16,128]{3,2,1,0:T(8,128)S(1)}, u32[]{:S(2)}, u32[]{:S(2)}) collective-permute-start(f32[3,16,16,128]{3,2,1,0:T(8,128)S(1)} %pad_maximum_fusion.middle_in), channel_id=1, source_target_pairs={{0,3},{1,4},{2,5},{3,6},{4,7},{5,8},{6,9},{7,10},{8,11},{9,12},{10... | collective-permute-start | bytes 1179656 | tf_op jit(solution)/shard_map/ppermute | solution.py:458
  27.6 38.1 %all-to-all-start = ((f32[128,16,128]{2,1,0:T(8,128)}), f32[128,16,128]{2,1,0:T(8,128)S(1)}, u32[]{:S(2)}, u32[]{:S(2)}) async-start(f32[128,16,128]{2,1,0:T(8,128)} %get-tuple-element.24), calls=%async_computation | async-start | bytes 2097152 | tf_op jit(solution)/shard_map/all_to_all | solution.py:543
  39.1 2.1 %copy-start.5 = (f32[3,16,16,128]{3,2,1,0:T(8,128)}, f32[3,16,16,128]{3,2,1,0:T(8,128)S(1)}, u32[]{:S(2)}) copy-start(f32[3,16,16,128]{3,2,1,0:T(8,128)S(1)} %collective-permute-done.3.after_in) | copy-start | bytes 1179652
  41.2 0.7 %copy-start.6 = (f32[3,16,16,128]{3,2,1,0:T(8,128)}, f32[3,16,16,128]{3,2,1,0:T(8,128)S(1)}, u32[]{:S(2)}) copy-start(f32[3,16,16,128]{3,2,1,0:T(8,128)S(1)} %collective-permute-done.2.before_in) | copy-start | bytes 1179652
  65.8 1.0 %copy-start = (f32[128,16,128]{2,1,0:T(8,128)}, f32[128,16,128]{2,1,0:T(8,128)S(1)}, u32[]{:S(2)}) copy-start(f32[128,16,128]{2,1,0:T(8,128)S(1)} %all-to-all-done.gathered) | copy-start | bytes 3145732

commit v12 on v10

--- a/solution.py
+++ b/solution.py
@@ -70,13 +70,10 @@
 
 def skeleton_kernel(
     near, far, points, probes_in, basis_in, transfer_in, transfer_box, out, out_first, own, box_out, items,
-    probes, basis, transfer_leaf, semaphores,
+    probes, basis, transfer_leaf, semaphores, later_semaphore,
 ):
     leaves, rank, leaf_size = basis.shape
-    arriving = copies(
-        [(probes_in, probes)] + parts(basis_in, basis) + parts(transfer_in, transfer_leaf),
-        semaphores,
-    )
+    arriving = copies([(probes_in, probes)] + parts(basis_in, basis), semaphores)
     slots = near.shape[0]
     pairs = leaves // 2
     low_lanes = lax.broadcasted_iota(jnp.int32, (16, 2 * rank), 1) < rank
@@ -116,6 +113,8 @@
     for m in range(pairs):
         if m % (pairs // CHUNKS) == 0:
             arriving[1 + m // (pairs // CHUNKS)].wait()
+        if m == 0:
+            later = copies([(transfer_in, transfer_leaf)], later_semaphore)
         left = jnp.concatenate([leaf_probes(2 * m), leaf_probes(2 * m + 1)], axis=0)
         right = jnp.concatenate([stacked_halves(basis[2 * m]), stacked_halves(basis[2 * m + 1])], axis=0)
         wide = contract(left, right, ((1,), (1,)))
@@ -125,8 +124,7 @@
         out_first[m] = pair
         own[m] = pair
         skeletons.append(pair)
-    for copy in arriving[1 + CHUNKS :]:
-        copy.wait()
+    later[0].wait()
     high, low = halves(transfer_leaf[...].reshape(leaves * rank, rank))
     wide = jnp.dot(
         stacked_halves(jnp.concatenate(skeletons, axis=1)),
@@ -507,7 +505,7 @@
         in_specs=whole(3) + hbm(3) + whole(1),
         out_specs=tuple(whole(5)),
         scratch_shapes=[like(probes), like(basis), like(transfer_leaf)]
-        + [copy_semaphores(1 + 2 * CHUNKS)],
+        + [copy_semaphores(1 + CHUNKS), copy_semaphores(1)],
         compiler_params=params(60),
         name="skeletons",
     )(near_slots, far_list, points, probes, basis, transfer_leaf, transfer_box)
@@ -558,7 +556,7 @@
         ]
         + [like(middle)] * 3
         + [copy_semaphores(3)],
-        compiler_params=params(60),
+        compiler_params=params(63),
         cost_estimate=cost(20_000_000_000),
         name="near_far",
     )(items, points, probes, left, right, before, middle, after, couple_leaf)

time: 72.4 us -> 70.1 us (0.968)
  waiting for transfers between devices: 3.48 us -> 2.24 us
  local copies, waits for them, and re-layouts: 1.75 us -> 0.79 us
    ppermute x4, waiting for transfers between devices: 3.48 us -> 2.23 us  [shifted(): lax.ppermute(array, axis, [(i, (i + by) % devices) for i in range(devices)])]
    unnamed x14 -> x10, local copies, waits for them, and re-layouts: 1.73 us -> 0.77 us
  transfers between devices with their start and end apart: 5 -> 5, of which waited for: 2 -> 1; matrix products, arithmetic and copies ran while one was open for 0% -> 0% of each run, Pallas kernels for 55% -> 56%
where the time goes in v12:
time: 70.1 us; the launch traced here: 69.5 us
  Pallas kernels  48.8 us (70%)
  starting transfers between devices  17.4 us (25%)
  waiting for transfers between devices  2.24 us (3%)
  local copies, waits for them, and re-layouts  0.79 us (1%)
    pallas_call x1, Pallas kernels, per_device(): pl.pallas_call(functools.partial(field_kernel, groups=outer), out_shape=(...  22.5 us
    pallas_call x1, Pallas kernels, per_device(): pl.pallas_call(functools.partial(inner_kernel, groups=inner), out_shape=(...  16.3 us
    ppermute x4, starting transfers between devices, shifted(): lax.ppermute(array, axis, [(i, (i + by) % devices) for i in range(devices)])  11.7 us
    all_to_all x1, starting transfers between devices, per_device(): boxes = lax.all_to_all(sent, ring, 0, 0, tiled=True)  5.75 us
    pallas_call x1, Pallas kernels, per_device(): pl.pallas_call(skeleton_kernel, out_shape=(edges, edges, jax.ShapeDtypeSt...  5.03 us
    pallas_call x1, Pallas kernels, per_device(): pl.pallas_call(down_kernel, out_shape=jax.ShapeDtypeStruct(probes.shape,...  4.95 us
    ppermute x4, waiting for transfers between devices, shifted(): lax.ppermute(array, axis, [(i, (i + by) % devices) for i in range(devices)])  2.23 us
  transfers between devices with their start and end apart: 5, of which 1 were waited for; matrix products, arithmetic and copies ran while one was open for 0% of the time, Pallas kernels for 56%

profile of v12, /device:TPU:0, one launch (start us, length us, event | category | flops | bytes accessed | tf_op | source)
XLA Modules:
  0.0 69.5 jit_solution(15179510608842885304)
XLA Ops:
  0.0 5.0 %skeletons.1 = (f32[34,16,128]{2,1,0:T(8,128)}, f32[34,16,128]{2,1,0:T(8,128)}, f32[16,16,128]{2,1,0:T(8,128)}, f32[16,128]{1,0:T(8,128)}, s32[41,128]{1,0:T(8,128)}) custom-call(s32[9,32]{1,0:T(8,128)} %bitcast.10, s32[32,27]{1,0:T(8,128)} %far.1, f32[2,8192]{1,0:T(2,128)} %points_in.3, f32[16,8192]{1,0:T(8,128)} %probes_in.5, f32[32,64,256]{2,1,0:T(8,128)} %bitcast.7, ...), custom_call_target="tpu_custom_call" | custom-call | tf_op jit(solution)/shard_map/skeletons/pallas_call | solution.py:496
  5.0 0.0 copy-start.1
  5.1 2.1 %collective-permute-start = (f32[34,16,128]{2,1,0:T(8,128)}, f32[34,16,128]{2,1,0:T(8,128)S(1)}, u32[]{:S(2)}, u32[]{:S(2)}) collective-permute-start(f32[34,16,128]{2,1,0:T(8,128)} %get-tuple-element.21), channel_id=1, source_target_pairs={{0,1},{1,2},{2,3},{3,4},{4,5},{5,6},{6,7},{7,8},{8,9},{9,10},{10,1... | collective-permute-start | bytes 835592 | tf_op jit(solution)/shard_map/ppermute | solution.py:459
  7.1 6.3 %collective-permute-start.1 = (f32[34,16,128]{2,1,0:T(8,128)}, f32[34,16,128]{2,1,0:T(8,128)S(1)}, u32[]{:S(2)}, u32[]{:S(2)}) collective-permute-start(f32[34,16,128]{2,1,0:T(8,128)} %get-tuple-element.22), channel_id=1, source_target_pairs={{0,127},{1,0},{2,1},{3,2},{4,3},{5,4},{6,5},{7,6},{8,7},{9,8},{10,... | collective-permute-start | bytes 835592 | tf_op jit(solution)/shard_map/ppermute | solution.py:459
  13.4 16.3 %near_inner.1 = (f32[16,4096]{1,0:T(8,128)}, f32[128,16,128]{2,1,0:T(8,128)}) custom-call(s32[41,128]{1,0:T(8,128)} %get-tuple-element.18.items, f32[16,128]{1,0:T(8,128)} %get-tuple-element.19.box, f32[2,8192]{1,0:T(2,128)} %points_in.3, f32[16,8192]{1,0:T(8,128)} %probes_in.5), custom_call_target="tpu_custom_call" | custom-call | flops 10000000000 | bytes 1048576 | tf_op jit(solution)/shard_map/near_inner/pallas_call | solution.py:530
  29.7 0.0 collective-permute-done.left
  29.8 0.0 copy-start.2
  29.8 0.0 collective-permute-done.1.right
  29.8 0.0 copy-start.3
  29.8 0.0 copy-done.1
  29.9 0.0 copy-start
  29.9 0.1 collective-permute-start.3
  30.0 3.2 %collective-permute-start.2 = (f32[3,16,16,128]{3,2,1,0:T(8,128)S(1)}, f32[3,16,16,128]{3,2,1,0:T(8,128)}, u32[]{:S(2)}, u32[]{:S(2)}) collective-permute-start(f32[3,16,16,128]{3,2,1,0:T(8,128)S(1)} %pad_maximum_fusion.middle_in), channel_id=1, source_target_pairs={{0,3},{1,4},{2,5},{3,6},{4,7},{5,8},{6,9},{7,10},{8,11},{9,12},{10... | collective-permute-start | bytes 1179656 | tf_op jit(solution)/shard_map/ppermute | solution.py:459
  33.2 5.8 %all-to-all-start = ((f32[128,16,128]{2,1,0:T(8,128)}), f32[128,16,128]{2,1,0:T(8,128)}, u32[]{:S(2)}, u32[]{:S(2)}) async-start(f32[128,16,128]{2,1,0:T(8,128)} %get-tuple-element.24), calls=%async_computation | async-start | bytes 2097152 | tf_op jit(solution)/shard_map/all_to_all | solution.py:544
  39.0 0.0 collective-permute-done.3.after_in
  39.0 0.0 copy-start.4
  39.0 0.8 %copy-done.4 = f32[3,16,16,128]{3,2,1,0:T(8,128)} copy-done((f32[3,16,16,128]{3,2,1,0:T(8,128)}, f32[3,16,16,128]{3,2,1,0:T(8,128)S(1)}, u32[]{:S(2)}) %copy-start.4) | copy-done | bytes 393240
  39.7 2.2 %collective-permute-done.2.before_in = f32[3,16,16,128]{3,2,1,0:T(8,128)} collective-permute-done((f32[3,16,16,128]{3,2,1,0:T(8,128)S(1)}, f32[3,16,16,128]{3,2,1,0:T(8,128)}, u32[]{:S(2)}, u32[]{:S(2)}) %collective-permute-start.2) | collective-permute-done | bytes 393248 | tf_op jit(solution)/shard_map/ppermute | solution.py:459
  42.0 0.0 copy-done.2
  42.0 0.0 copy-done.3
  42.0 0.0 copy-done
  42.0 22.5 %near_far.1 = (f32[16,4096]{1,0:T(8,128)}, f32[16,16,128]{2,1,0:T(8,128)}) custom-call(s32[41,128]{1,0:T(8,128)} %get-tuple-element.18.items, f32[2,8192]{1,0:T(2,128)} %points_in.3, f32[16,8192]{1,0:T(8,128)} %probes_in.5, f32[34,16,128]{2,1,0:T(8,128)} %copy-done.2, f32[34,16,128]{2,1,0:T(8,128)} %copy-done.3, ...), custom_call_target="tpu_custom_call" | custom-call | flops 20000000000 | bytes 1048576 | tf_op jit(solution)/shard_map/near_far/pallas_call | solution.py:546
  64.5 0.0 all-to-all-done.boxes_in
  64.5 5.0 %down.1 = f32[16,8192]{1,0:T(8,128)} custom-call(s32[1,27]{1,0:T(1,128)} %box_list.1, s32[1,4]{1,0:T(1,128)} %column_list.1, f32[128,16,128]{2,1,0:T(8,128)} %all-to-all-done.boxes_in, f32[1,27,64,64]{3,2,1,0:T(8,128)} %couple_box_in.1, f32[1,4,64,64]{3,2,1,0:T(8,128)} %couple_column_in.1, f32[1,64,64]{2,1,0:T(8,128)} %transfer_box_in.1, ...), custom_call_target="tpu_custom_call" | custom-call | tf_op jit(solution)/shard_map/down/pallas_call | solution.py:566
  (2 shorter events, 0.0 us)
Async XLA Ops:
  5.0 24.8 %copy-start.1 = (f32[16,16,128]{2,1,0:T(8,128)S(1)}, f32[16,16,128]{2,1,0:T(8,128)}, u32[]{:S(2)}) copy-start(f32[16,16,128]{2,1,0:T(8,128)} %get-tuple-element.27) | copy-start | bytes 393220
  5.1 24.7 %collective-permute-start = (f32[34,16,128]{2,1,0:T(8,128)}, f32[34,16,128]{2,1,0:T(8,128)S(1)}, u32[]{:S(2)}, u32[]{:S(2)}) collective-permute-start(f32[34,16,128]{2,1,0:T(8,128)} %get-tuple-element.21), channel_id=1, source_target_pairs={{0,1},{1,2},{2,3},{3,4},{4,5},{5,6},{6,7},{7,8},{8,9},{9,10},{10,1... | collective-permute-start | bytes 835592 | tf_op jit(solution)/shard_map/ppermute | solution.py:459
  7.1 22.6 %collective-permute-start.1 = (f32[34,16,128]{2,1,0:T(8,128)}, f32[34,16,128]{2,1,0:T(8,128)S(1)}, u32[]{:S(2)}, u32[]{:S(2)}) collective-permute-start(f32[34,16,128]{2,1,0:T(8,128)} %get-tuple-element.22), channel_id=1, source_target_pairs={{0,127},{1,0},{2,1},{3,2},{4,3},{5,4},{6,5},{7,6},{8,7},{9,8},{10,... | collective-permute-start | bytes 835592 | tf_op jit(solution)/shard_map/ppermute | solution.py:459
  29.8 12.2 %copy-start.2 = (f32[34,16,128]{2,1,0:T(8,128)}, f32[34,16,128]{2,1,0:T(8,128)S(1)}, u32[]{:S(2)}) copy-start(f32[34,16,128]{2,1,0:T(8,128)S(1)} %collective-permute-done.left) | copy-start | bytes 835588
  29.8 12.2 %copy-start.3 = (f32[34,16,128]{2,1,0:T(8,128)}, f32[34,16,128]{2,1,0:T(8,128)S(1)}, u32[]{:S(2)}) copy-start(f32[34,16,128]{2,1,0:T(8,128)S(1)} %collective-permute-done.1.right) | copy-start | bytes 835588
  29.9 12.1 %copy-start = (f32[3,16,16,128]{3,2,1,0:T(8,128)}, f32[3,16,16,128]{3,2,1,0:T(8,128)S(1)}, u32[]{:S(2)}) copy-start(f32[3,16,16,128]{3,2,1,0:T(8,128)S(1)} %pad_maximum_fusion.middle_in) | copy-start | bytes 1179652
  29.9 9.1 %collective-permute-start.3 = (f32[3,16,16,128]{3,2,1,0:T(8,128)S(1)}, f32[3,16,16,128]{3,2,1,0:T(8,128)S(1)}, u32[]{:S(2)}, u32[]{:S(2)}) collective-permute-start(f32[3,16,16,128]{3,2,1,0:T(8,128)S(1)} %pad_maximum_fusion.middle_in), channel_id=1, source_target_pairs={{0,125},{1,126},{2,127},{3,0},{4,1},{5,2},{6,3},{7,4},{8,5},{9,6},... | collective-permute-start | bytes 1179656 | tf_op jit(solution)/shard_map/ppermute | solution.py:459
  30.0 12.0 %collective-permute-start.2 = (f32[3,16,16,128]{3,2,1,0:T(8,128)S(1)}, f32[3,16,16,128]{3,2,1,0:T(8,128)}, u32[]{:S(2)}, u32[]{:S(2)}) collective-permute-start(f32[3,16,16,128]{3,2,1,0:T(8,128)S(1)} %pad_maximum_fusion.middle_in), channel_id=1, source_target_pairs={{0,3},{1,4},{2,5},{3,6},{4,7},{5,8},{6,9},{7,10},{8,11},{9,12},{10... | collective-permute-start | bytes 1179656 | tf_op jit(solution)/shard_map/ppermute | solution.py:459
  33.2 31.3 %all-to-all-start = ((f32[128,16,128]{2,1,0:T(8,128)}), f32[128,16,128]{2,1,0:T(8,128)}, u32[]{:S(2)}, u32[]{:S(2)}) async-start(f32[128,16,128]{2,1,0:T(8,128)} %get-tuple-element.24), calls=%async_computation | async-start | bytes 2097152 | tf_op jit(solution)/shard_map/all_to_all | solution.py:544
  39.0 0.8 %copy-start.4 = (f32[3,16,16,128]{3,2,1,0:T(8,128)}, f32[3,16,16,128]{3,2,1,0:T(8,128)S(1)}, u32[]{:S(2)}) copy-start(f32[3,16,16,128]{3,2,1,0:T(8,128)S(1)} %collective-permute-done.3.after_in) | copy-start | bytes 1179652

commit v13 on v12

--- a/solution.py
+++ b/solution.py
@@ -14,7 +14,7 @@
 GROUP = 16
 TAIL_GROUP = 4
 FAR_STEP = 4
-CHUNKS = 4
+CHUNKS = 8
 
 matern_rate = math.sqrt(3.0) / 0.1
 coordinate_scale = matern_rate * math.log2(math.e)

time: 70.1 us -> 71.9 us (1.026)
  starting transfers between devices: 17.4 us -> 19.1 us
  waiting for transfers between devices: 2.24 us -> 0.85 us
  Pallas kernels: 48.8 us -> 50 us
    pallas_call x1, Pallas kernels: 16.3 us -> 14.4 us  [per_device(): pl.pallas_call(functools.partial(inner_kernel, groups=inner), out_shape=(...]
    all_to_all x1, starting transfers between devices: 5.75 us -> 7.37 us  [per_device(): boxes = lax.all_to_all(sent, ring, 0, 0, tiled=True)]
    ppermute x4, waiting for transfers between devices: 2.23 us -> 0.85 us  [shifted(): lax.ppermute(array, axis, [(i, (i + by) % devices) for i in range(devices)])]
    pallas_call x1, Pallas kernels: 22.5 us -> 23.8 us  [per_device(): pl.pallas_call(functools.partial(field_kernel, groups=outer), out_shape=(...]
    pallas_call x1, Pallas kernels: 5.03 us -> 6.05 us  [per_device(): pl.pallas_call(skeleton_kernel, out_shape=(edges, edges, jax.ShapeDtypeSt...]
    pallas_call x1, Pallas kernels: 4.95 us -> 5.73 us  [per_device(): pl.pallas_call(down_kernel, out_shape=jax.ShapeDtypeStruct(probes.shape,...]
  transfers between devices with their start and end apart: 5 -> 5, of which waited for: 1 -> 1; matrix products, arithmetic and copies ran while one was open for 0% -> 0% of each run, Pallas kernels for 56% -> 54%
where the time goes in v13:
time: 71.9 us; the launch traced here: 70.8 us
  Pallas kernels  50 us (70%)
  starting transfers between devices  19.1 us (27%)
  waiting for transfers between devices  0.85 us (1%)
  local copies, waits for them, and re-layouts  0.79 us (1%)
    pallas_call x1, Pallas kernels, per_device(): pl.pallas_call(functools.partial(field_kernel, groups=outer), out_shape=(...  23.8 us
    pallas_call x1, Pallas kernels, per_device(): pl.pallas_call(functools.partial(inner_kernel, groups=inner), out_shape=(...  14.4 us
    ppermute x4, starting transfers between devices, shifted(): lax.ppermute(array, axis, [(i, (i + by) % devices) for i in range(devices)])  11.7 us
    all_to_all x1, starting transfers between devices, per_device(): boxes = lax.all_to_all(sent, ring, 0, 0, tiled=True)  7.37 us
    pallas_call x1, Pallas kernels, per_device(): pl.pallas_call(skeleton_kernel, out_shape=(edges, edges, jax.ShapeDtypeSt...  6.05 us
    pallas_call x1, Pallas kernels, per_device(): pl.pallas_call(down_kernel, out_shape=jax.ShapeDtypeStruct(probes.shape,...  5.73 us
  transfers between devices with their start and end apart: 5, of which 1 were waited for; matrix products, arithmetic and copies ran while one was open for 0% of the time, Pallas kernels for 54%

profile of v13, /device:TPU:0, one launch (start us, length us, event | category | flops | bytes accessed | tf_op | source)
XLA Modules:
  0.0 70.8 jit_solution(5171981805278479848)
XLA Ops:
  0.0 6.1 %skeletons.1 = (f32[34,16,128]{2,1,0:T(8,128)}, f32[34,16,128]{2,1,0:T(8,128)}, f32[16,16,128]{2,1,0:T(8,128)}, f32[16,128]{1,0:T(8,128)}, s32[41,128]{1,0:T(8,128)}) custom-call(s32[9,32]{1,0:T(8,128)} %bitcast.10, s32[32,27]{1,0:T(8,128)} %far.1, f32[2,8192]{1,0:T(2,128)} %points_in.3, f32[16,8192]{1,0:T(8,128)} %probes_in.5, f32[32,64,256]{2,1,0:T(8,128)} %bitcast.7, ...), custom_call_target="tpu_custom_call" | custom-call | tf_op jit(solution)/shard_map/skeletons/pallas_call | solution.py:496
  6.1 0.0 copy-start.1
  6.1 2.1 %collective-permute-start = (f32[34,16,128]{2,1,0:T(8,128)}, f32[34,16,128]{2,1,0:T(8,128)S(1)}, u32[]{:S(2)}, u32[]{:S(2)}) collective-permute-start(f32[34,16,128]{2,1,0:T(8,128)} %get-tuple-element.21), channel_id=1, source_target_pairs={{0,1},{1,2},{2,3},{3,4},{4,5},{5,6},{6,7},{7,8},{8,9},{9,10},{10,1... | collective-permute-start | bytes 835592 | tf_op jit(solution)/shard_map/ppermute | solution.py:459
  8.1 6.3 %collective-permute-start.1 = (f32[34,16,128]{2,1,0:T(8,128)}, f32[34,16,128]{2,1,0:T(8,128)S(1)}, u32[]{:S(2)}, u32[]{:S(2)}) collective-permute-start(f32[34,16,128]{2,1,0:T(8,128)} %get-tuple-element.22), channel_id=1, source_target_pairs={{0,127},{1,0},{2,1},{3,2},{4,3},{5,4},{6,5},{7,6},{8,7},{9,8},{10,... | collective-permute-start | bytes 835592 | tf_op jit(solution)/shard_map/ppermute | solution.py:459
  14.4 14.4 %near_inner.1 = (f32[16,4096]{1,0:T(8,128)}, f32[128,16,128]{2,1,0:T(8,128)}) custom-call(s32[41,128]{1,0:T(8,128)} %get-tuple-element.18.items, f32[16,128]{1,0:T(8,128)} %get-tuple-element.19.box, f32[2,8192]{1,0:T(2,128)} %points_in.3, f32[16,8192]{1,0:T(8,128)} %probes_in.5), custom_call_target="tpu_custom_call" | custom-call | flops 10000000000 | bytes 1048576 | tf_op jit(solution)/shard_map/near_inner/pallas_call | solution.py:530
  28.8 0.0 collective-permute-done.left
  28.8 0.0 copy-start.2
  28.8 0.0 collective-permute-done.1.right
  28.9 0.0 copy-start.3
  28.9 0.0 copy-done.1
  28.9 0.0 copy-start
  28.9 0.8 %collective-permute-start.3 = (f32[3,16,16,128]{3,2,1,0:T(8,128)S(1)}, f32[3,16,16,128]{3,2,1,0:T(8,128)S(1)}, u32[]{:S(2)}, u32[]{:S(2)}) collective-permute-start(f32[3,16,16,128]{3,2,1,0:T(8,128)S(1)} %pad_maximum_fusion.middle_in), channel_id=1, source_target_pairs={{0,125},{1,126},{2,127},{3,0},{4,1},{5,2},{6,3},{7,4},{8,5},{9,6},... | collective-permute-start | bytes 1179656 | tf_op jit(solution)/shard_map/ppermute | solution.py:459
  29.7 2.6 %collective-permute-start.2 = (f32[3,16,16,128]{3,2,1,0:T(8,128)S(1)}, f32[3,16,16,128]{3,2,1,0:T(8,128)}, u32[]{:S(2)}, u32[]{:S(2)}) collective-permute-start(f32[3,16,16,128]{3,2,1,0:T(8,128)S(1)} %pad_maximum_fusion.middle_in), channel_id=1, source_target_pairs={{0,3},{1,4},{2,5},{3,6},{4,7},{5,8},{6,9},{7,10},{8,11},{9,12},{10... | collective-permute-start | bytes 1179656 | tf_op jit(solution)/shard_map/ppermute | solution.py:459
  32.3 7.4 %all-to-all-start = ((f32[128,16,128]{2,1,0:T(8,128)}), f32[128,16,128]{2,1,0:T(8,128)}, u32[]{:S(2)}, u32[]{:S(2)}) async-start(f32[128,16,128]{2,1,0:T(8,128)} %get-tuple-element.24), calls=%async_computation | async-start | bytes 2097152 | tf_op jit(solution)/shard_map/all_to_all | solution.py:544
  39.6 0.0 collective-permute-done.3.after_in
  39.7 0.0 copy-start.4
  39.7 0.8 %copy-done.4 = f32[3,16,16,128]{3,2,1,0:T(8,128)} copy-done((f32[3,16,16,128]{3,2,1,0:T(8,128)}, f32[3,16,16,128]{3,2,1,0:T(8,128)S(1)}, u32[]{:S(2)}) %copy-start.4) | copy-done | bytes 393240
  40.4 0.8 %collective-permute-done.2.before_in = f32[3,16,16,128]{3,2,1,0:T(8,128)} collective-permute-done((f32[3,16,16,128]{3,2,1,0:T(8,128)S(1)}, f32[3,16,16,128]{3,2,1,0:T(8,128)}, u32[]{:S(2)}, u32[]{:S(2)}) %collective-permute-start.2) | collective-permute-done | bytes 393248 | tf_op jit(solution)/shard_map/ppermute | solution.py:459
  41.3 0.0 copy-done.2
  41.3 0.0 copy-done.3
  41.3 0.0 copy-done
  41.3 23.8 %near_far.1 = (f32[16,4096]{1,0:T(8,128)}, f32[16,16,128]{2,1,0:T(8,128)}) custom-call(s32[41,128]{1,0:T(8,128)} %get-tuple-element.18.items, f32[2,8192]{1,0:T(2,128)} %points_in.3, f32[16,8192]{1,0:T(8,128)} %probes_in.5, f32[34,16,128]{2,1,0:T(8,128)} %copy-done.2, f32[34,16,128]{2,1,0:T(8,128)} %copy-done.3, ...), custom_call_target="tpu_custom_call" | custom-call | flops 20000000000 | bytes 1048576 | tf_op jit(solution)/shard_map/near_far/pallas_call | solution.py:546
  65.1 0.0 all-to-all-done.boxes_in
  65.1 5.7 %down.1 = f32[16,8192]{1,0:T(8,128)} custom-call(s32[1,27]{1,0:T(1,128)} %box_list.1, s32[1,4]{1,0:T(1,128)} %column_list.1, f32[128,16,128]{2,1,0:T(8,128)} %all-to-all-done.boxes_in, f32[1,27,64,64]{3,2,1,0:T(8,128)} %couple_box_in.1, f32[1,4,64,64]{3,2,1,0:T(8,128)} %couple_column_in.1, f32[1,64,64]{2,1,0:T(8,128)} %transfer_box_in.1, ...), custom_call_target="tpu_custom_call" | custom-call | tf_op jit(solution)/shard_map/down/pallas_call | solution.py:566
  (2 shorter events, 0.0 us)
Async XLA Ops:
  6.1 22.8 %copy-start.1 = (f32[16,16,128]{2,1,0:T(8,128)S(1)}, f32[16,16,128]{2,1,0:T(8,128)}, u32[]{:S(2)}) copy-start(f32[16,16,128]{2,1,0:T(8,128)} %get-tuple-element.27) | copy-start | bytes 393220
  6.1 22.8 %collective-permute-start = (f32[34,16,128]{2,1,0:T(8,128)}, f32[34,16,128]{2,1,0:T(8,128)S(1)}, u32[]{:S(2)}, u32[]{:S(2)}) collective-permute-start(f32[34,16,128]{2,1,0:T(8,128)} %get-tuple-element.21), channel_id=1, source_target_pairs={{0,1},{1,2},{2,3},{3,4},{4,5},{5,6},{6,7},{7,8},{8,9},{9,10},{10,1... | collective-permute-start | bytes 835592 | tf_op jit(solution)/shard_map/ppermute | solution.py:459
  8.1 20.7 %collective-permute-start.1 = (f32[34,16,128]{2,1,0:T(8,128)}, f32[34,16,128]{2,1,0:T(8,128)S(1)}, u32[]{:S(2)}, u32[]{:S(2)}) collective-permute-start(f32[34,16,128]{2,1,0:T(8,128)} %get-tuple-element.22), channel_id=1, source_target_pairs={{0,127},{1,0},{2,1},{3,2},{4,3},{5,4},{6,5},{7,6},{8,7},{9,8},{10,... | collective-permute-start | bytes 835592 | tf_op jit(solution)/shard_map/ppermute | solution.py:459
  28.8 12.4 %copy-start.2 = (f32[34,16,128]{2,1,0:T(8,128)}, f32[34,16,128]{2,1,0:T(8,128)S(1)}, u32[]{:S(2)}) copy-start(f32[34,16,128]{2,1,0:T(8,128)S(1)} %collective-permute-done.left) | copy-start | bytes 835588
  28.9 12.4 %copy-start.3 = (f32[34,16,128]{2,1,0:T(8,128)}, f32[34,16,128]{2,1,0:T(8,128)S(1)}, u32[]{:S(2)}) copy-start(f32[34,16,128]{2,1,0:T(8,128)S(1)} %collective-permute-done.1.right) | copy-start | bytes 835588
  28.9 12.3 %copy-start = (f32[3,16,16,128]{3,2,1,0:T(8,128)}, f32[3,16,16,128]{3,2,1,0:T(8,128)S(1)}, u32[]{:S(2)}) copy-start(f32[3,16,16,128]{3,2,1,0:T(8,128)S(1)} %pad_maximum_fusion.middle_in) | copy-start | bytes 1179652
  28.9 10.7 %collective-permute-start.3 = (f32[3,16,16,128]{3,2,1,0:T(8,128)S(1)}, f32[3,16,16,128]{3,2,1,0:T(8,128)S(1)}, u32[]{:S(2)}, u32[]{:S(2)}) collective-permute-start(f32[3,16,16,128]{3,2,1,0:T(8,128)S(1)} %pad_maximum_fusion.middle_in), channel_id=1, source_target_pairs={{0,125},{1,126},{2,127},{3,0},{4,1},{5,2},{6,3},{7,4},{8,5},{9,6},... | collective-permute-start | bytes 1179656 | tf_op jit(solution)/shard_map/ppermute | solution.py:459
  29.7 11.5 %collective-permute-start.2 = (f32[3,16,16,128]{3,2,1,0:T(8,128)S(1)}, f32[3,16,16,128]{3,2,1,0:T(8,128)}, u32[]{:S(2)}, u32[]{:S(2)}) collective-permute-start(f32[3,16,16,128]{3,2,1,0:T(8,128)S(1)} %pad_maximum_fusion.middle_in), channel_id=1, source_target_pairs={{0,3},{1,4},{2,5},{3,6},{4,7},{5,8},{6,9},{7,10},{8,11},{9,12},{10... | collective-permute-start | bytes 1179656 | tf_op jit(solution)/shard_map/ppermute | solution.py:459
  32.3 32.8 %all-to-all-start = ((f32[128,16,128]{2,1,0:T(8,128)}), f32[128,16,128]{2,1,0:T(8,128)}, u32[]{:S(2)}, u32[]{:S(2)}) async-start(f32[128,16,128]{2,1,0:T(8,128)} %get-tuple-element.24), calls=%async_computation | async-start | bytes 2097152 | tf_op jit(solution)/shard_map/all_to_all | solution.py:544
  39.7 0.8 %copy-start.4 = (f32[3,16,16,128]{3,2,1,0:T(8,128)}, f32[3,16,16,128]{3,2,1,0:T(8,128)S(1)}, u32[]{:S(2)}) copy-start(f32[3,16,16,128]{3,2,1,0:T(8,128)S(1)} %collective-permute-done.3.after_in) | copy-start | bytes 1179652
